TPU v7x, 256 devices: a whole 4x4x8 slice. The times are simulated.
256 devices in a mesh: filt: 8 (over x_lo, y), sx: 4 (over x_hi, core), sy: 8 (over z).
Axes of the slice: x: 4 (x_hi: 2, x_lo: 2; x = x_hi * 2 + x_lo), y: 4, z: 8, core: 2. Of those that a mesh axis runs over, the one named last changes fastest.
Arguments:
- activations: bfloat16 [8, 1, 32, 32, 2048], P('filt', None, 'sx', 'sy'), may hold values from -6 to 6
- weights: bfloat16 [8, 27, 32768], P('filt'), may hold values from -0.0546875 to 0.0546875
- out_grad: bfloat16 [8, 1, 32, 32, 2048], P('filt', None, 'sx', 'sy'), may hold values from -6 to 6
Outputs:
- outputs: bfloat16 [8, 1, 32, 32, 2048], P('filt', None, 'sx', 'sy')
- input_grad: bfloat16 [8, 1, 32, 32, 2048], P('filt', None, 'sx', 'sy')
- weight_grad: float32 [8, 27, 32768], P('filt', None, ('sx', 'sy'))
All inputs are finite; a program needn't handle non-finite values.
Results may differ from a plain program's by a relative error of at most 0.02.
Values may be sent and summed in bfloat16 or wider, within the bound.
No kernel may reach another device: no remote copies, remote signals or barrier semaphores. Data moves between devices by JAX's collectives and lax.ppermute only.
A program may use at most 128 MiB of HBM per device.

v0:
```python
import math

import jax
import jax.numpy as jnp
from jax import lax
from jax.experimental import pallas as pl
from jax.experimental.pallas import tpu as pltpu
from jax.sharding import PartitionSpec as P

BF = jnp.bfloat16
F32 = jnp.float32
LEAK = 0.2
SCALE = 1.0 / math.sqrt(32768.0)
PIECE = (8, 4, 16, 128)


def call(kernel, outs, ins, scratch=(), flops=0, nbytes=0):
    return pl.pallas_call(
        kernel,
        out_shape=outs,
        in_specs=[
            pl.BlockSpec(memory_space=pltpu.VMEM if space is None else space)
            for _, space in ins
        ],
        out_specs=jax.tree.map(lambda _: pl.BlockSpec(memory_space=pltpu.VMEM), outs),
        scratch_shapes=list(scratch),
        compiler_params=pltpu.CompilerParams(vmem_limit_bytes=48 << 20),
        cost_estimate=pl.CostEstimate(flops=flops, bytes_accessed=nbytes, transcendentals=0),
    )(*[array for array, _ in ins])


def shape(dims, dtype=BF):
    return jax.ShapeDtypeStruct(dims, dtype)


def down(v):
    rows = lax.broadcasted_iota(jnp.int32, v.shape, 0)
    return jnp.where(rows == 0, 0.0, pltpu.roll(v, 1, 0))


def up(v):
    rows = lax.broadcasted_iota(jnp.int32, v.shape, 0)
    return jnp.where(rows == v.shape[0] - 1, 0.0, pltpu.roll(v, v.shape[0] - 1, 0))


def to_pairs(field_ref, pair_ref, wide):
    for x in range(8):
        rows = field_ref[x].astype(F32)
        for t in range(16):
            wide[pl.ds(x * 64 + t, 4, stride=16), :] = rows[:, t * 128 : (t + 1) * 128]
    pair_ref[...] = wide[...].reshape(PIECE).astype(BF)


def from_pairs(wide, field_ref):
    for x in range(8):
        parts = [wide[pl.ds(x * 64 + t, 4, stride=16), :] for t in range(16)]
        field_ref[x] = jnp.concatenate(parts, axis=1).astype(BF)


def prepare_field(field):
    def kernel(field_ref, pair_ref, wide):
        to_pairs(field_ref, pair_ref, wide)

    return call(
        kernel, shape(PIECE), [(field, None)], [pltpu.VMEM((512, 128), F32)], 0, 400_000
    )


def prepare_weights(weights):
    def kernel(w_ref, fore_ref, back_ref, tall, even, odd):
        def spread(t, carry):
            lanes = pl.ds(pl.multiple_of(t * 128, 128), 128)
            tall[pl.ds(t, 27, stride=256), :] = w_ref[:, lanes].astype(F32)
            return carry

        lax.fori_loop(0, 256, spread, 0, unroll=8)

        def place(ij, carry):
            taps = [tall[pl.ds(pl.multiple_of((ij * 3 + k) * 256, 256), 256), :] for k in range(3)]
            zero = jnp.zeros((256, 64), F32)
            for par in range(2):
                lanes = slice(par * 64, par * 64 + 64)
                even[pl.ds(par, 256, stride=2), :] = jnp.concatenate(
                    [taps[0][:, lanes], taps[1][:, lanes]], axis=1
                )
                odd[pl.ds(par, 256, stride=2), :] = jnp.concatenate([taps[2][:, lanes], zero], axis=1)
            fore_ref[ij, :, 0:128] = even[...].astype(BF)
            fore_ref[ij, :, 128:256] = odd[...].astype(BF)
            for c in range(4):
                rows = slice(c * 128, c * 128 + 128)
                back_ref[ij, 0:128, rows] = even[rows, :].T.astype(BF)
                back_ref[ij, 128:256, rows] = odd[rows, :].T.astype(BF)
            return carry

        lax.fori_loop(0, 9, place, 0)

    return call(
        kernel,
        (shape((9, 512, 256)), shape((9, 256, 512))),
        [(weights, None)],
        [pltpu.VMEM((27 * 256, 128), F32), pltpu.VMEM((512, 128), F32), pltpu.VMEM((512, 128), F32)],
        0,
        8_000_000,
    )


def forward(coords, pieces, y_before, y_after, x_before, x_after, fore, grad):
    def kernel(
        co, p0, p1, p2, p3, p4, p5, p6, p7, yb, ya, xb, xa, fore_ref, grad_ref,
        field_ref, out_ref, pre_ref, slots, total, wide, sems,
    ):
        col, row = co[0], co[1]
        copies = []
        for s, piece in enumerate((p0, p1, p2, p3, p4, p5, p6, p7)):
            owner = (col ^ (s // 4)) * 4 + ((row - s) & 3)
            copies.append(pltpu.make_async_copy(piece, slots.at[owner], sems.at[s]))
        for copy in copies:
            copy.start()

        def place(x, y, take):
            for q in range(4):
                a, b = take(2 * q), take(2 * q + 1)
                lanes = slice(q * 128, q * 128 + 128)
                field_ref[x, y * 32 : y * 32 + 16, lanes] = jnp.concatenate([a[:, :64], b[:, :64]], axis=1)
                field_ref[x, y * 32 + 16 : y * 32 + 32, lanes] = jnp.concatenate([a[:, 64:], b[:, 64:]], axis=1)

        def slot(owner):
            return ((owner // 4) ^ col) * 4 + ((row - owner) & 3)

        for y in range(6):
            place(0, y, lambda f: xb[slot(f), y])
            place(9, y, lambda f: xa[slot(f), y])
        for copy in copies:
            copy.wait()

        def place_x(x, carry):
            place(x + 1, 0, lambda f: yb[slot(f), x])
            place(x + 1, 5, lambda f: ya[slot(f), x])
            for y in range(4):
                place(x + 1, y + 1, lambda f: slots[f, x, y])
            return carry

        lax.fori_loop(0, 8, place_x, 0)

        def multiply(h, carry):
            acc = jnp.zeros((256, 256), F32)
            for i in range(3):
                for j in range(3):
                    rows = [field_ref[2 * h + u + i, j * 32 : j * 32 + 128, :] for u in range(2)]
                    acc = acc + jnp.dot(
                        jnp.concatenate(rows, axis=0), fore_ref[i * 3 + j], preferred_element_type=F32
                    )
            total[pl.ds(pl.multiple_of(h * 256, 256), 256), :] = acc
            return carry

        lax.fori_loop(0, 4, multiply, 0)

        def finish(x, carry):
            for y in range(4):
                start = pl.multiple_of(x * 128 + y * 32, 32)
                even, odd = total[pl.ds(start, 16), :], total[pl.ds(start + 16, 16), :]
                pre = (
                    jnp.concatenate([down(odd[:, 0:64]), even[:, 0:64]], axis=1)
                    + jnp.concatenate([even[:, 64:128], odd[:, 64:128]], axis=1)
                    + jnp.concatenate([odd[:, 128:192], up(even[:, 128:192])], axis=1)
                )
                e = jnp.exp(-jnp.abs(pre))
                soft = jnp.maximum(pre, 0.0) + jnp.log1p(e)
                slope = jnp.where(pre >= 0, 1.0, e) / (1.0 + e)
                value = LEAK * pre + (1.0 - LEAK) * (soft - math.log(2.0))
                wide[pl.ds(pl.multiple_of(x * 64 + y * 16, 16), 16), :] = value
                g = grad_ref[x, y].astype(F32)
                pre_ref[x, y] = (g * (LEAK + (1.0 - LEAK) * slope)).astype(BF)
            return carry

        lax.fori_loop(0, 8, finish, 0)
        from_pairs(wide, out_ref)

    return call(
        kernel,
        (shape((10, 192, 512)), shape((8, 4, 2048)), shape(PIECE)),
        [(coords, pltpu.SMEM)]
        + [(piece, pl.ANY) for piece in pieces]
        + [(a, None) for a in (y_before, y_after, x_before, x_after, fore, grad)],
        [
            pltpu.VMEM((8,) + PIECE, BF),
            pltpu.VMEM((1024, 256), F32),
            pltpu.VMEM((512, 128), F32),
            pltpu.SemaphoreType.DMA((8,)),
        ],
        5_000_000_000,
        6_000_000,
    )


def stacked_depth(v):
    even, odd = v[:, :64], v[:, 64:]
    zero = jnp.zeros((16, 64), F32)
    return (
        (jnp.concatenate([odd, even], axis=1), jnp.concatenate([down(odd), zero], axis=1)),
        (jnp.concatenate([up(even), odd], axis=1), jnp.concatenate([even, zero], axis=1)),
    )


def filter_grad(coords, field, pre_grad):
    def kernel(co, field_ref, pre_ref, keep_ref, send_ref, first, second, turned):
        core = co[2]

        def place(x, carry):
            for y in range(4):
                low, high = stacked_depth(pre_ref[x, y].astype(F32))
                first[y * 32 : y * 32 + 16, :] = low[0]
                second[y * 32 : y * 32 + 16, :] = low[1]
                first[y * 32 + 16 : y * 32 + 32, :] = high[0]
                second[y * 32 + 16 : y * 32 + 32, :] = high[1]
            lanes = pl.ds(pl.multiple_of(x * 128, 128), 128)
            turned[0:128, lanes] = first[...].T.astype(BF)
            turned[128:192, lanes] = second[...].T[0:64].astype(BF)
            return carry

        lax.fori_loop(0, 8, place, 0)

        def multiply(ij, carry):
            i, j = ij // 3, ij % 3
            start = pl.multiple_of(j * 32, 32)
            for half in range(2):
                lanes = slice(half * 256, half * 256 + 256)
                rows = [field_ref[x + i, pl.ds(start, 128), lanes] for x in range(8)]
                got = jnp.dot(
                    turned[...], jnp.concatenate(rows, axis=0), preferred_element_type=F32
                ) * SCALE
                left, right = got[:, :128], got[:, 128:]
                keep_ref[half, ij] = jnp.where(core == 0, left, right)
                send_ref[half, ij] = jnp.where(core == 0, right, left).astype(BF)
            return carry

        lax.fori_loop(0, 9, multiply, 0)

    return call(
        kernel,
        (shape((2, 9, 192, 128), F32), shape((2, 9, 192, 128))),
        [(coords, pltpu.SMEM), (field, None), (pre_grad, None)],
        [pltpu.VMEM((128, 128), F32), pltpu.VMEM((128, 128), F32), pltpu.VMEM((192, 1024), BF)],
        5_000_000_000,
        6_000_000,
    )


def add_cores(coords, keep, got):
    def kernel(co, keep_ref, got_ref, stay_ref, send_ref):
        far = co[3]
        stay_ref[...] = keep_ref[far] + got_ref[far].astype(F32)
        send_ref[...] = (keep_ref[1 - far] + got_ref[1 - far].astype(F32)).astype(BF)

    return call(
        kernel,
        (shape((9, 192, 128), F32), shape((9, 192, 128))),
        [(coords, pltpu.SMEM), (keep, None), (got, None)],
        (),
        0,
        4_000_000,
    )


def add_far(coords, stay, got):
    def kernel(co, stay_ref, got_ref, *outs):
        out_ref, total, turned = outs
        sy = co[4]
        total[...] = (stay_ref[...] + got_ref[...].astype(F32)).reshape(1728, 128)
        for t in range(14):
            width = min(128, 1728 - t * 128)
            turned[:, t * 128 : t * 128 + width] = total[t * 128 : t * 128 + width, :].T.astype(BF)
        for s in range(8):
            out_ref[(s - sy) & 7] = turned[s * 16 : s * 16 + 16, :]

    return call(
        kernel,
        shape((8, 16, 1728)),
        [(coords, pltpu.SMEM), (stay, None), (got, None)],
        [pltpu.VMEM((1728, 128), F32), pltpu.VMEM((128, 1728), BF)],
        0,
        2_000_000,
    )


def add_regions(parts):
    def kernel(*refs):
        ins, (out_ref, total, pairs) = refs[:8], refs[8:]
        for t in range(14):
            width = min(128, 1728 - t * 128)
            lanes = slice(t * 128, t * 128 + width)
            s = ins[0][:, lanes].astype(F32)
            for ref in ins[1:]:
                s = s + ref[:, lanes].astype(F32)
            total[:, 0:width] = s
            even, odd = total[pl.ds(0, 8, stride=2), :], total[pl.ds(1, 8, stride=2), :]
            for u in range(width // 64):
                pick = slice(u * 64, u * 64 + 64)
                at = (2 * t + u) * 8
                pairs[at : at + 8, :] = jnp.concatenate([even[:, pick], odd[:, pick]], axis=1)
        for cp in range(8):
            out_ref[:, cp * 128 : cp * 128 + 128] = pairs[pl.ds(cp, 27, stride=8), :]

    return call(
        kernel,
        shape((27, 1024), F32),
        [(part, None) for part in parts],
        [pltpu.VMEM((16, 128), F32), pltpu.VMEM((216, 128), F32)],
        0,
        600_000,
    )


def input_grad_parts(coords, pre_grad, y_before, y_after, x_before, x_after, back):
    def kernel(co, pre_ref, yb, ya, xb, xa, back_ref, out_ref, rim, total):
        col, row = co[0], co[1]

        def place(x, y, v):
            low, high = stacked_depth(v.astype(F32))
            for half in range(2):
                lanes = slice(half * 128, half * 128 + 128)
                rim[x, y * 32 : y * 32 + 16, lanes] = low[half].astype(BF)
                rim[x, y * 32 + 16 : y * 32 + 32, lanes] = high[half].astype(BF)

        for y in range(6):
            place(0, y, xb[y])
            place(9, y, xa[y])

        def place_x(x, carry):
            place(x + 1, 0, yb[x])
            place(x + 1, 5, ya[x])
            for y in range(4):
                place(x + 1, y + 1, pre_ref[x, y])
            return carry

        lax.fori_loop(0, 8, place_x, 0)

        def multiply(h, carry):
            for n in range(2):
                lanes = slice(n * 256, n * 256 + 256)
                acc = jnp.zeros((256, 256), F32)
                for i in range(3):
                    for j in range(3):
                        at = (2 - j) * 32
                        rows = [rim[2 * h + u + 2 - i, at : at + 128, :] for u in range(2)]
                        acc = acc + jnp.dot(
                            jnp.concatenate(rows, axis=0),
                            back_ref[i * 3 + j, :, lanes],
                            preferred_element_type=F32,
                        )
                total[:, lanes] = acc
            for u in range(2):
                for y in range(4):
                    at = u * 128 + y * 32
                    for f in range(8):
                        lanes = slice(f * 64, f * 64 + 64)
                        pair = jnp.concatenate(
                            [total[at : at + 16, lanes], total[at + 16 : at + 32, lanes]], axis=1
                        )
                        slot = ((f // 4) ^ col) * 4 + ((f - row) & 3)
                        out_ref[slot, 2 * h + u, y] = pair.astype(BF)
            return carry

        lax.fori_loop(0, 4, multiply, 0)

    return call(
        kernel,
        shape((8,) + PIECE),
        [(coords, pltpu.SMEM)]
        + [(a, None) for a in (pre_grad, y_before, y_after, x_before, x_after, back)],
        [pltpu.VMEM((10, 192, 256), BF), pltpu.VMEM((256, 512), F32)],
        5_000_000_000,
        5_000_000,
    )


def add_blocks(parts):
    def kernel(*refs):
        ins, (out_ref, wide) = refs[:8], refs[8:]
        s = ins[0][...].astype(F32)
        for ref in ins[1:]:
            s = s + ref[...].astype(F32)
        wide[...] = s.reshape(512, 128)
        from_pairs(wide, out_ref)

    return call(
        kernel,
        shape((8, 4, 2048)),
        [(part, None) for part in parts],
        [pltpu.VMEM((512, 128), F32)],
        0,
        1_200_000,
    )


def along_filt(slot):
    return [(f, ((f // 4) ^ (slot // 4)) * 4 + (f + slot) % 4) for f in range(8)]


ORDER = (2, 6, 1, 3, 5, 7, 4)


def rims(field, y_dim, join):
    ups = [(i, i + 1) for i in range(7)]
    downs = [(i + 1, i) for i in range(7)]
    first, last = join(3), join(0)
    y_before = lax.ppermute(first, "sy", ups)
    y_after = lax.ppermute(last, "sy", downs)
    x_last = field(7, y_before, y_after)
    x_first = field(0, y_before, y_after)
    x_before = lax.ppermute(x_last, "sx", ups[:3])
    x_after = lax.ppermute(x_first, "sx", downs[:3])
    return y_before, y_after, x_before, x_after


def per_device(activations, weights, out_grad):
    filt, sx, sy = (lax.axis_index(a) for a in ("filt", "sx", "sy"))
    coords = jnp.stack([filt // 4, filt % 4, sx % 2, sx // 2, sy, 0, 0, 0]).astype(jnp.int32)
    own = prepare_field(activations[0, 0])
    pieces = {0: own}
    for s in ORDER:
        pieces[s] = lax.ppermute(own, "filt", along_filt(s))
    pieces = [pieces[s] for s in range(8)]
    fore, back = prepare_weights(weights[0])
    grad = prepare_field(out_grad[0, 0])

    halos = rims(
        lambda x, yb, ya: jnp.concatenate(
            [yb[:, x : x + 1], jnp.stack([p[x] for p in pieces]), ya[:, x : x + 1]], axis=1
        ),
        1,
        lambda y: jnp.stack([p[:, y] for p in pieces]),
    )
    field, outputs, pre_grad = forward(coords, pieces, *halos, fore, grad)

    grad_halos = rims(
        lambda x, yb, ya: jnp.concatenate([yb[x : x + 1], pre_grad[x], ya[x : x + 1]], axis=0),
        1,
        lambda y: pre_grad[:, y],
    )
    keep, send = filter_grad(coords, field, pre_grad)
    got = lax.ppermute(send, "sx", [(i, i ^ 1) for i in range(4)])
    stay, send = add_cores(coords, keep, got)
    got = lax.ppermute(send, "sx", [(i, i ^ 2) for i in range(4)])

    parts = input_grad_parts(coords, pre_grad, *grad_halos, back)
    sums = {0: parts[0]}
    for s in ORDER:
        sums[s] = lax.ppermute(parts[s], "filt", along_filt(s))

    turned = add_far(coords, stay, got)
    regions = [turned[0]]
    for d in range(1, 8):
        regions.append(lax.ppermute(turned[d], "sy", [(i, (i + d) % 8) for i in range(8)]))

    input_grad = add_blocks([sums[s] for s in range(8)])
    weight_grad = add_regions(regions)
    return outputs[None, None], input_grad[None, None], weight_grad[None]


def solution(mesh):
    in_specs = (
        P("filt", None, "sx", "sy", None),
        P("filt", None, None),
        P("filt", None, "sx", "sy", None),
    )
    out_specs = (
        P("filt", None, "sx", "sy", None),
        P("filt", None, "sx", "sy", None),
        P("filt", None, ("sx", "sy")),
    )
    return jax.shard_map(
        per_device, mesh=mesh, in_specs=in_specs, out_specs=out_specs, check_vma=False
    )
```

profile of v0, /device:TPU:1, one launch (start us, length us, event | category | flops | bytes accessed | tf_op | source)
XLA Modules:
  0.0 145.0 jit_solution(17734935144949605240)
XLA Ops:
  0.7 1.0 copy-done.1
  1.7 0.1 shard_map.58.p0
  1.8 4.6 %collective-permute-start.6 = (bf16[8,4,16,128]{3,2,0,1:T(8,128)(2,1)S(1)}, bf16[8,4,16,128]{3,2,0,1:T(8,128)(2,1)S(1)}, u32[]{:S(2)}, u32[]{:S(2)}) collective-permute-start(bf16[8,4,16,128]{3,2,0,1:T(8,128)(2,1)S(1)} %copy.6), channel_id=1, source_target_pairs={{0,224},{32,128},{64,160},{96,192},{128,96},{160,0},{192,32},{224,... | collective-permute-start | bytes 393224 | tf_op jit(solution)/shard_map/ppermute | solution.py:422
  6.4 0.3 collective-permute-start.5
  6.7 1.6 %collective-permute-start.4 = (bf16[8,4,16,128]{3,2,0,1:T(8,128)(2,1)S(1)}, bf16[8,4,16,128]{3,2,0,1:T(8,128)(2,1)S(1)}, u32[]{:S(2)}, u32[]{:S(2)}) collective-permute-start(bf16[8,4,16,128]{3,2,0,1:T(8,128)(2,1)S(1)} %copy.6), channel_id=1, source_target_pairs={{0,160},{32,192},{64,224},{96,128},{128,32},{160,64},{192,96},{224... | collective-permute-start | bytes 393224 | tf_op jit(solution)/shard_map/ppermute | solution.py:422
  8.3 0.3 collective-permute-start.3
  8.6 1.6 %collective-permute-start = (bf16[8,4,16,128]{3,2,0,1:T(8,128)(2,1)S(1)}, bf16[8,4,16,128]{3,2,0,1:T(8,128)(2,1)S(1)}, u32[]{:S(2)}, u32[]{:S(2)}) collective-permute-start(bf16[8,4,16,128]{3,2,0,1:T(8,128)(2,1)S(1)} %copy.6), channel_id=1, source_target_pairs={{0,32},{32,64},{64,96},{96,0},{128,160},{160,192},{192,224},{224,1... | collective-permute-start | bytes 393224 | tf_op jit(solution)/shard_map/ppermute | solution.py:422
  10.2 9.6 %collective-permute-done = bf16[8,4,16,128]{3,2,0,1:T(8,128)(2,1)S(1)} collective-permute-done((bf16[8,4,16,128]{3,2,0,1:T(8,128)(2,1)S(1)}, bf16[8,4,16,128]{3,2,0,1:T(8,128)(2,1)S(1)}, u32[]{:S(2)}, u32[]{:S(2)}) %collective-permute-start) | collective-permute-done | bytes 131104 | tf_op jit(solution)/shard_map/ppermute | solution.py:422
  19.8 0.8 collective-permute-start.1
  20.6 5.3 %collective-permute-done.1 = bf16[8,4,16,128]{3,2,0,1:T(8,128)(2,1)S(1)} collective-permute-done((bf16[8,4,16,128]{3,2,0,1:T(8,128)(2,1)S(1)}, bf16[8,4,16,128]{3,2,0,1:T(8,128)(2,1)S(1)}, u32[]{:S(2)}, u32[]{:S(2)}) %collective-permute-start.1) | collective-permute-done | bytes 131104 | tf_op jit(solution)/shard_map/ppermute | solution.py:422
  25.9 0.3 collective-permute-start.2
  26.2 3.5 %collective-permute-done.2 = bf16[8,4,16,128]{3,2,0,1:T(8,128)(2,1)S(1)} collective-permute-done((bf16[8,4,16,128]{3,2,0,1:T(8,128)(2,1)S(1)}, bf16[8,4,16,128]{3,2,0,1:T(8,128)(2,1)S(1)}, u32[]{:S(2)}, u32[]{:S(2)}) %collective-permute-start.2) | collective-permute-done | bytes 131104 | tf_op jit(solution)/shard_map/ppermute | solution.py:422
  29.7 0.0 collective-permute-done.3
  29.8 0.0 collective-permute-done.4
  29.8 0.0 collective-permute-done.6
  29.8 1.3 collective-permute-start.8
  31.3 4.2 %collective-permute-start.7 = (bf16[8,8,16,128]{3,2,0,1:T(8,128)(2,1)S(1)}, bf16[8,8,16,128]{3,2,0,1:T(8,128)(2,1)S(1)}, u32[]{:S(2)}, u32[]{:S(2)}) collective-permute-start(bf16[8,8,16,128]{3,2,0,1:T(8,128)(2,1)S(1)} %constant_dynamic-update-slice_fusion), channel_id=1, source_target_pairs={{0,1},{1,2},{2,3},{3,4},{4,5},{5,6},{6,7},{8,9},{9,10},{10,11},{11... | collective-permute-start | bytes 786440 | tf_op jit(solution)/shard_map/ppermute | solution.py:407
  35.6 1.6 %collective-permute-done.8.ya = bf16[8,8,16,128]{3,2,1,0:T(8,128)(2,1)S(1)} collective-permute-done((bf16[8,8,16,128]{3,2,1,0:T(8,128)(2,1)S(1)}, bf16[8,8,16,128]{3,2,1,0:T(8,128)(2,1)S(1)}, u32[]{:S(2)}, u32[]{:S(2)}) %collective-permute-start.8) | collective-permute-done | bytes 262176 | tf_op jit(solution)/shard_map/ppermute | solution.py:408
  37.2 1.6 %collective-permute-done.7 = bf16[8,8,16,128]{3,2,0,1:T(8,128)(2,1)S(1)} collective-permute-done((bf16[8,8,16,128]{3,2,0,1:T(8,128)(2,1)S(1)}, bf16[8,8,16,128]{3,2,0,1:T(8,128)(2,1)S(1)}, u32[]{:S(2)}, u32[]{:S(2)}) %collective-permute-start.7) | collective-permute-done | bytes 262176 | tf_op jit(solution)/shard_map/ppermute | solution.py:407
  38.7 0.7 pad_maximum_fusion
  39.4 7.7 %collective-permute-start.9 = (bf16[8,6,16,128]{3,2,0,1:T(8,128)(2,1)}, bf16[8,6,16,128]{3,2,0,1:T(8,128)(2,1)}, u32[]{:S(2)}, u32[]{:S(2)}) collective-permute-start(bf16[8,6,16,128]{3,2,0,1:T(8,128)(2,1)} %pad_maximum_fusion), channel_id=1, source_target_pairs={{0,8},{8,16},{16,24},{1,9},{9,17},{17,25},{2,10},{10,18},{18,26},{... | collective-permute-start | bytes 589832 | tf_op jit(solution)/shard_map/ppermute | solution.py:411
  47.1 0.7 pad_maximum_fusion.1
  47.8 1.9 %collective-permute-start.10 = (bf16[8,6,16,128]{3,2,1,0:T(8,128)(2,1)}, bf16[8,6,16,128]{3,2,1,0:T(8,128)(2,1)S(1)}, u32[]{:S(2)}, u32[]{:S(2)}) collective-permute-start(bf16[8,6,16,128]{3,2,1,0:T(8,128)(2,1)} %pad_maximum_fusion.1), channel_id=1, source_target_pairs={{8,0},{16,8},{24,16},{9,1},{17,9},{25,17},{10,2},{18,10},{26,18},{... | collective-permute-start | bytes 589832 | tf_op jit(solution)/shard_map/ppermute | solution.py:412
  49.8 0.1 shard_map.60.grad_ref
  49.9 7.7 %shard_map.59 = (bf16[9,512,256]{2,1,0:T(8,128)(2,1)S(1)}, bf16[9,256,512]{2,1,0:T(8,128)(2,1)}) custom-call(bf16[27,32768]{1,0:T(8,128)(2,1)S(1)} %bitcast.119), custom_call_target="tpu_custom_call" | custom-call | bytes 8000000 | tf_op jit(solution)/shard_map/pallas_call | solution.py:18
  57.7 1.5 %copy-done.4 = bf16[9,512,256]{2,1,0:T(8,128)(2,1)} copy-done((bf16[9,512,256]{2,1,0:T(8,128)(2,1)}, bf16[9,512,256]{2,1,0:T(8,128)(2,1)S(1)}, u32[]{:S(2)}) %copy-start.4) | copy-done | bytes 2359320
  59.1 0.1 stack.35.co
  59.3 0.9 copy.23.p4
  60.2 0.9 copy.22.p3
  61.1 0.9 copy.21.p2
  62.0 0.9 copy.20.p1
  63.0 0.9 copy.28.xb
  63.9 9.1 %shard_map.61 = (bf16[10,192,512]{2,1,0:T(8,128)(2,1)S(1)}, bf16[8,4,2048]{2,1,0:T(4,128)(2,1)}, bf16[8,4,16,128]{3,2,1,0:T(8,128)(2,1)S(1)}) custom-call(s32[8]{0:T(128)S(1)} %stack.35.co, bf16[8,4,16,128]{3,2,1,0:T(8,128)(2,1)S(1)} %shard_map.58.p0, bf16[8,4,16,128]{3,2,1,0:T(8,128)(2,1)S(1)} %copy.20.p1, bf16[8,4,16,128]{3,2,1,0:T(8,128)(2,1)S(1)} %copy.21.p2, ...), custom_call_target="tpu_custom_call" | custom-call | flops 5000000000 | bytes 6000000 | tf_op jit(solution)/shard_map/pallas_call | solution.py:18
  73.1 1.3 collective-permute-start.12
  74.4 5.4 %shard_map.64 = (f32[2,9,192,128]{3,2,1,0:T(8,128)S(1)}, bf16[2,9,192,128]{3,2,1,0:T(8,128)(2,1)S(1)}) custom-call(s32[8]{0:T(128)S(1)} %stack.35.co, bf16[10,192,512]{2,1,0:T(8,128)(2,1)S(1)} %get-tuple-element.16.field_ref, bf16[8,4,16,128]{3,2,1,0:T(8,128)(2,1)S(1)} %get-tuple-element.14.pre_ref), custom_call_target="tpu_custom_call" | custom-call | flops 5000000000 | bytes 6000000 | tf_op jit(solution)/shard_map/pallas_call | solution.py:18
  79.9 0.1 collective-permute-start.22
  80.0 4.9 %collective-permute-start.11 = (bf16[8,16,128]{2,1,0:T(8,128)(2,1)S(1)}, bf16[8,16,128]{2,1,0:T(8,128)(2,1)S(1)}, u32[]{:S(2)}, u32[]{:S(2)}) collective-permute-start(bf16[8,16,128]{2,1,0:T(8,128)(2,1)S(1)} %get-tuple-element.47), channel_id=1, source_target_pairs={{0,1},{1,2},{2,3},{3,4},{4,5},{5,6},{6,7},{8,9},{9,10},{10,11},{11... | collective-permute-start | bytes 98312 | tf_op jit(solution)/shard_map/ppermute | solution.py:407
  84.9 1.0 collective-permute-done.11.yb
  85.9 6.0 %collective-permute-start.13 = (bf16[6,16,128]{2,1,0:T(8,128)(2,1)S(1)}, bf16[6,16,128]{2,1,0:T(8,128)(2,1)S(1)}, u32[]{:S(2)}, u32[]{:S(2)}) collective-permute-start(bf16[6,16,128]{2,1,0:T(8,128)(2,1)S(1)} %pad_maximum_fusion.2), channel_id=1, source_target_pairs={{0,8},{8,16},{16,24},{1,9},{9,17},{17,25},{2,10},{10,18},{18,26},{... | collective-permute-start | bytes 73736 | tf_op jit(solution)/shard_map/ppermute | solution.py:411
  91.9 1.9 %collective-permute-start.14 = (bf16[6,16,128]{2,1,0:T(8,128)(2,1)S(1)}, bf16[6,16,128]{2,1,0:T(8,128)(2,1)S(1)}, u32[]{:S(2)}, u32[]{:S(2)}) collective-permute-start(bf16[6,16,128]{2,1,0:T(8,128)(2,1)S(1)} %pad_maximum_fusion.3), channel_id=1, source_target_pairs={{8,0},{16,8},{24,16},{9,1},{17,9},{25,17},{10,2},{18,10},{26,18},{... | collective-permute-start | bytes 73736 | tf_op jit(solution)/shard_map/ppermute | solution.py:412
  93.8 0.7 shard_map.65
  94.5 0.2 collective-permute-start.23
  94.7 3.8 %collective-permute-done.14.xa = bf16[6,16,128]{2,1,0:T(8,128)(2,1)S(1)} collective-permute-done((bf16[6,16,128]{2,1,0:T(8,128)(2,1)S(1)}, bf16[6,16,128]{2,1,0:T(8,128)(2,1)S(1)}, u32[]{:S(2)}, u32[]{:S(2)}) %collective-permute-start.14) | collective-permute-done | bytes 24608 | tf_op jit(solution)/shard_map/ppermute | solution.py:412
  98.5 4.7 %shard_map.62 = bf16[8,8,4,16,128]{4,3,2,1,0:T(8,128)(2,1)S(1)} custom-call(s32[8]{0:T(128)S(1)} %stack.35.co, bf16[8,4,16,128]{3,2,1,0:T(8,128)(2,1)S(1)} %get-tuple-element.14.pre_ref, bf16[8,16,128]{2,1,0:T(8,128)(2,1)S(1)} %collective-permute-done.11.yb, bf16[8,16,128]{2,1,0:T(8,128)(2,1)S(1)} %collective-permute-done.12.ya, ...), custom_call_target="tpu_custom_call" | custom-call | flops 5000000000 | bytes 5000000 | tf_op jit(solution)/shard_map/pallas_call | solution.py:18
  103.3 0.2 slice_bitcast_fusion
  103.5 1.3 collective-permute-start.21
  104.8 2.0 %collective-permute-start.20 = (bf16[8,4,16,128]{3,2,1,0:T(8,128)(2,1)S(1)}, bf16[8,4,16,128]{3,2,1,0:T(8,128)(2,1)S(1)}, u32[]{:S(2)}, u32[]{:S(2)}) collective-permute-start(bf16[8,4,16,128]{3,2,1,0:T(8,128)(2,1)S(1)} %get-tuple-element.25), channel_id=1, source_target_pairs={{0,192},{32,224},{64,128},{96,160},{128,64},{160,96},{192,0},{224,... | collective-permute-start | bytes 393224 | tf_op jit(solution)/shard_map/ppermute | solution.py:449
  106.8 1.1 collective-permute-start.18
  107.9 2.8 %collective-permute-start.17 = (bf16[8,4,16,128]{3,2,1,0:T(8,128)(2,1)S(1)}, bf16[8,4,16,128]{3,2,1,0:T(8,128)(2,1)S(1)}, u32[]{:S(2)}, u32[]{:S(2)}) collective-permute-start(bf16[8,4,16,128]{3,2,1,0:T(8,128)(2,1)S(1)} %get-tuple-element.28), channel_id=1, source_target_pairs={{0,96},{32,0},{64,32},{96,64},{128,224},{160,128},{192,160},{224,1... | collective-permute-start | bytes 393224 | tf_op jit(solution)/shard_map/ppermute | solution.py:449
  110.7 0.8 shard_map.66
  111.5 1.0 collective-permute-start.16
  112.5 1.2 collective-permute-done.20.refs_6_
  113.7 2.5 %collective-permute-done.19.refs_5_ = bf16[8,4,16,128]{3,2,1,0:T(8,128)(2,1)S(1)} collective-permute-done((bf16[8,4,16,128]{3,2,1,0:T(8,128)(2,1)S(1)}, bf16[8,4,16,128]{3,2,1,0:T(8,128)(2,1)S(1)}, u32[]{:S(2)}, u32[]{:S(2)}) %collective-permute-start.19) | collective-permute-done | bytes 131104 | tf_op jit(solution)/shard_map/ppermute | solution.py:449
  116.3 7.9 %collective-permute-start.30 = (bf16[16,1728]{1,0:T(8,128)(2,1)S(1)}, bf16[16,1728]{1,0:T(8,128)(2,1)S(1)}, u32[]{:S(2)}, u32[]{:S(2)}) collective-permute-start(bf16[16,1728]{1,0:T(8,128)(2,1)S(1)} %get-tuple-element.32), channel_id=1, source_target_pairs={{0,7},{1,0},{2,1},{3,2},{4,3},{5,4},{6,5},{7,6},{8,15},{9,8},{10,9... | collective-permute-start | bytes 165896 | tf_op jit(solution)/shard_map/ppermute | solution.py:454
  124.1 2.8 %collective-permute-start.29 = (bf16[16,1728]{1,0:T(8,128)(2,1)S(1)}, bf16[16,1728]{1,0:T(8,128)(2,1)S(1)}, u32[]{:S(2)}, u32[]{:S(2)}) collective-permute-start(bf16[16,1728]{1,0:T(8,128)(2,1)S(1)} %get-tuple-element.33), channel_id=1, source_target_pairs={{0,6},{1,7},{2,0},{3,1},{4,2},{5,3},{6,4},{7,5},{8,14},{9,15},{10,... | collective-permute-start | bytes 165896 | tf_op jit(solution)/shard_map/ppermute | solution.py:454
  126.9 0.8 collective-permute-start.28
  127.8 4.1 %collective-permute-start.27 = (bf16[16,1728]{1,0:T(8,128)(2,1)S(1)}, bf16[16,1728]{1,0:T(8,128)(2,1)S(1)}, u32[]{:S(2)}, u32[]{:S(2)}) collective-permute-start(bf16[16,1728]{1,0:T(8,128)(2,1)S(1)} %get-tuple-element.35), channel_id=1, source_target_pairs={{0,4},{1,5},{2,6},{3,7},{4,0},{5,1},{6,2},{7,3},{8,12},{9,13},{10,... | collective-permute-start | bytes 165896 | tf_op jit(solution)/shard_map/ppermute | solution.py:454
  131.9 3.3 %collective-permute-start.25 = (bf16[16,1728]{1,0:T(8,128)(2,1)S(1)}, bf16[16,1728]{1,0:T(8,128)(2,1)S(1)}, u32[]{:S(2)}, u32[]{:S(2)}) collective-permute-start(bf16[16,1728]{1,0:T(8,128)(2,1)S(1)} %get-tuple-element.37), channel_id=1, source_target_pairs={{0,2},{1,3},{2,4},{3,5},{4,6},{5,7},{6,0},{7,1},{8,10},{9,11},{10,... | collective-permute-start | bytes 165896 | tf_op jit(solution)/shard_map/ppermute | solution.py:454
  135.2 0.5 collective-permute-start.24
  135.7 0.9 shard_map.63
  136.6 3.7 %collective-permute-done.26.refs_3_ = bf16[16,1728]{1,0:T(8,128)(2,1)S(1)} collective-permute-done((bf16[16,1728]{1,0:T(8,128)(2,1)S(1)}, bf16[16,1728]{1,0:T(8,128)(2,1)S(1)}, u32[]{:S(2)}, u32[]{:S(2)}) %collective-permute-start.26) | collective-permute-done | bytes 55328 | tf_op jit(solution)/shard_map/ppermute | solution.py:454
  140.4 3.8 %collective-permute-done.24.refs_1_ = bf16[16,1728]{1,0:T(8,128)(2,1)S(1)} collective-permute-done((bf16[16,1728]{1,0:T(8,128)(2,1)S(1)}, bf16[16,1728]{1,0:T(8,128)(2,1)S(1)}, u32[]{:S(2)}, u32[]{:S(2)}) %collective-permute-start.24) | collective-permute-done | bytes 55328 | tf_op jit(solution)/shard_map/ppermute | solution.py:454
  144.1 0.2 shard_map.67
  144.3 0.8 copy.31
  (79 shorter events, 0.5 us)
Async XLA Ops:
  0.6 49.3 %copy-start = (bf16[1,27,32768]{2,1,0:T(8,128)(2,1)S(1)}, bf16[1,27,32768]{2,1,0:T(8,128)(2,1)}, u32[]{:S(2)}) copy-start(bf16[1,27,32768]{2,1,0:T(8,128)(2,1)} %param.4) | copy-start | bytes 5308420
  0.6 1.1 copy-start.1
  1.7 48.1 %copy-start.2 = (bf16[1,1,8,4,2048]{4,3,2,1,0:T(4,128)(2,1)S(1)}, bf16[1,1,8,4,2048]{4,3,2,1,0:T(4,128)(2,1)}, u32[]{:S(2)}) copy-start(bf16[1,1,8,4,2048]{4,3,2,1,0:T(4,128)(2,1)} %param.5) | copy-start | bytes 393220
  1.8 28.0 %collective-permute-start.6 = (bf16[8,4,16,128]{3,2,0,1:T(8,128)(2,1)S(1)}, bf16[8,4,16,128]{3,2,0,1:T(8,128)(2,1)S(1)}, u32[]{:S(2)}, u32[]{:S(2)}) collective-permute-start(bf16[8,4,16,128]{3,2,0,1:T(8,128)(2,1)S(1)} %copy.6), channel_id=1, source_target_pairs={{0,224},{32,128},{64,160},{96,192},{128,96},{160,0},{192,32},{224,... | collective-permute-start | bytes 393224 | tf_op jit(solution)/shard_map/ppermute | solution.py:422
  6.4 23.4 %collective-permute-start.5 = (bf16[8,4,16,128]{3,2,0,1:T(8,128)(2,1)S(1)}, bf16[8,4,16,128]{3,2,0,1:T(8,128)(2,1)S(1)}, u32[]{:S(2)}, u32[]{:S(2)}) collective-permute-start(bf16[8,4,16,128]{3,2,0,1:T(8,128)(2,1)S(1)} %copy.6), channel_id=1, source_target_pairs={{0,192},{32,224},{64,128},{96,160},{128,64},{160,96},{192,0},{224,... | collective-permute-start | bytes 393224 | tf_op jit(solution)/shard_map/ppermute | solution.py:422
  6.7 23.1 %collective-permute-start.4 = (bf16[8,4,16,128]{3,2,0,1:T(8,128)(2,1)S(1)}, bf16[8,4,16,128]{3,2,0,1:T(8,128)(2,1)S(1)}, u32[]{:S(2)}, u32[]{:S(2)}) collective-permute-start(bf16[8,4,16,128]{3,2,0,1:T(8,128)(2,1)S(1)} %copy.6), channel_id=1, source_target_pairs={{0,160},{32,192},{64,224},{96,128},{128,32},{160,64},{192,96},{224... | collective-permute-start | bytes 393224 | tf_op jit(solution)/shard_map/ppermute | solution.py:422
  8.3 21.4 %collective-permute-start.3 = (bf16[8,4,16,128]{3,2,0,1:T(8,128)(2,1)S(1)}, bf16[8,4,16,128]{3,2,0,1:T(8,128)(2,1)S(1)}, u32[]{:S(2)}, u32[]{:S(2)}) collective-permute-start(bf16[8,4,16,128]{3,2,0,1:T(8,128)(2,1)S(1)} %copy.6), channel_id=1, source_target_pairs={{0,128},{32,160},{64,192},{96,224},{128,0},{160,32},{192,64},{224,... | collective-permute-start | bytes 393224 | tf_op jit(solution)/shard_map/ppermute | solution.py:422
  8.6 11.2 %collective-permute-start = (bf16[8,4,16,128]{3,2,0,1:T(8,128)(2,1)S(1)}, bf16[8,4,16,128]{3,2,0,1:T(8,128)(2,1)S(1)}, u32[]{:S(2)}, u32[]{:S(2)}) collective-permute-start(bf16[8,4,16,128]{3,2,0,1:T(8,128)(2,1)S(1)} %copy.6), channel_id=1, source_target_pairs={{0,32},{32,64},{64,96},{96,0},{128,160},{160,192},{192,224},{224,1... | collective-permute-start | bytes 393224 | tf_op jit(solution)/shard_map/ppermute | solution.py:422
  19.8 27.3 %copy-start.7 = (bf16[8,4,16,128]{3,2,0,1:T(8,128)(2,1)}, bf16[8,4,16,128]{3,2,0,1:T(8,128)(2,1)S(1)}, u32[]{:S(2)}) copy-start(bf16[8,4,16,128]{3,2,0,1:T(8,128)(2,1)S(1)} %collective-permute-done) | copy-start | bytes 393220
  19.8 6.1 %collective-permute-start.1 = (bf16[8,4,16,128]{3,2,0,1:T(8,128)(2,1)S(1)}, bf16[8,4,16,128]{3,2,0,1:T(8,128)(2,1)S(1)}, u32[]{:S(2)}, u32[]{:S(2)}) collective-permute-start(bf16[8,4,16,128]{3,2,0,1:T(8,128)(2,1)S(1)} %copy.6), channel_id=1, source_target_pairs={{0,64},{32,96},{64,0},{96,32},{128,192},{160,224},{192,128},{224,1... | collective-permute-start | bytes 393224 | tf_op jit(solution)/shard_map/ppermute | solution.py:422
  25.9 23.8 %copy-start.9 = (bf16[8,4,16,128]{3,2,0,1:T(8,128)(2,1)}, bf16[8,4,16,128]{3,2,0,1:T(8,128)(2,1)S(1)}, u32[]{:S(2)}) copy-start(bf16[8,4,16,128]{3,2,0,1:T(8,128)(2,1)S(1)} %collective-permute-done.1) | copy-start | bytes 393220
  25.9 3.8 %collective-permute-start.2 = (bf16[8,4,16,128]{3,2,0,1:T(8,128)(2,1)S(1)}, bf16[8,4,16,128]{3,2,0,1:T(8,128)(2,1)S(1)}, u32[]{:S(2)}, u32[]{:S(2)}) collective-permute-start(bf16[8,4,16,128]{3,2,0,1:T(8,128)(2,1)S(1)} %copy.6), channel_id=1, source_target_pairs={{0,96},{32,0},{64,32},{96,64},{128,224},{160,128},{192,160},{224,1... | collective-permute-start | bytes 393224 | tf_op jit(solution)/shard_map/ppermute | solution.py:422
  29.7 20.0 %copy-start.10 = (bf16[8,4,16,128]{3,2,0,1:T(8,128)(2,1)}, bf16[8,4,16,128]{3,2,0,1:T(8,128)(2,1)S(1)}, u32[]{:S(2)}) copy-start(bf16[8,4,16,128]{3,2,0,1:T(8,128)(2,1)S(1)} %collective-permute-done.2) | copy-start | bytes 393220
  29.7 18.1 %copy-start.8 = (bf16[8,4,16,128]{3,2,0,1:T(8,128)(2,1)}, bf16[8,4,16,128]{3,2,0,1:T(8,128)(2,1)S(1)}, u32[]{:S(2)}) copy-start(bf16[8,4,16,128]{3,2,0,1:T(8,128)(2,1)S(1)} %collective-permute-done.3) | copy-start | bytes 393220
  29.8 20.0 %copy-start.5 = (bf16[8,4,16,128]{3,2,0,1:T(8,128)(2,1)}, bf16[8,4,16,128]{3,2,0,1:T(8,128)(2,1)S(1)}, u32[]{:S(2)}) copy-start(bf16[8,4,16,128]{3,2,0,1:T(8,128)(2,1)S(1)} %collective-permute-done.4) | copy-start | bytes 393220
  29.8 7.3 %collective-permute-start.8 = (bf16[8,8,16,128]{3,2,1,0:T(8,128)(2,1)S(1)}, bf16[8,8,16,128]{3,2,1,0:T(8,128)(2,1)S(1)}, u32[]{:S(2)}, u32[]{:S(2)}) collective-permute-start(bf16[8,8,16,128]{3,2,1,0:T(8,128)(2,1)S(1)} %constant_dynamic-update-slice_fusion.8), channel_id=1, source_target_pairs={{1,0},{2,1},{3,2},{4,3},{5,4},{6,5},{7,6},{9,8},{10,9},{11,10},{12... | collective-permute-start | bytes 786440 | tf_op jit(solution)/shard_map/ppermute | solution.py:408
  31.3 7.5 %collective-permute-start.7 = (bf16[8,8,16,128]{3,2,0,1:T(8,128)(2,1)S(1)}, bf16[8,8,16,128]{3,2,0,1:T(8,128)(2,1)S(1)}, u32[]{:S(2)}, u32[]{:S(2)}) collective-permute-start(bf16[8,8,16,128]{3,2,0,1:T(8,128)(2,1)S(1)} %constant_dynamic-update-slice_fusion), channel_id=1, source_target_pairs={{0,1},{1,2},{2,3},{3,4},{4,5},{5,6},{6,7},{8,9},{9,10},{10,11},{11... | collective-permute-start | bytes 786440 | tf_op jit(solution)/shard_map/ppermute | solution.py:407
  39.4 23.5 %collective-permute-start.9 = (bf16[8,6,16,128]{3,2,0,1:T(8,128)(2,1)}, bf16[8,6,16,128]{3,2,0,1:T(8,128)(2,1)}, u32[]{:S(2)}, u32[]{:S(2)}) collective-permute-start(bf16[8,6,16,128]{3,2,0,1:T(8,128)(2,1)} %pad_maximum_fusion), channel_id=1, source_target_pairs={{0,8},{8,16},{16,24},{1,9},{9,17},{17,25},{2,10},{10,18},{18,26},{... | collective-permute-start | bytes 589832 | tf_op jit(solution)/shard_map/ppermute | solution.py:411
  47.8 16.1 %collective-permute-start.10 = (bf16[8,6,16,128]{3,2,1,0:T(8,128)(2,1)}, bf16[8,6,16,128]{3,2,1,0:T(8,128)(2,1)S(1)}, u32[]{:S(2)}, u32[]{:S(2)}) collective-permute-start(bf16[8,6,16,128]{3,2,1,0:T(8,128)(2,1)} %pad_maximum_fusion.1), channel_id=1, source_target_pairs={{8,0},{16,8},{24,16},{9,1},{17,9},{25,17},{10,2},{18,10},{26,18},{... | collective-permute-start | bytes 589832 | tf_op jit(solution)/shard_map/ppermute | solution.py:412
  49.9 9.4 %copy-start.6 = (bf16[8,4,16,128]{3,2,0,1:T(8,128)(2,1)S(1)}, bf16[8,4,16,128]{3,2,0,1:T(8,128)(2,1)}, u32[]{:S(2)}) copy-start(bf16[8,4,16,128]{3,2,0,1:T(8,128)(2,1)} %copy-done.5) | copy-start | bytes 393220
  57.7 1.5 %copy-start.4 = (bf16[9,512,256]{2,1,0:T(8,128)(2,1)}, bf16[9,512,256]{2,1,0:T(8,128)(2,1)S(1)}, u32[]{:S(2)}) copy-start(bf16[9,512,256]{2,1,0:T(8,128)(2,1)S(1)} %get-tuple-element.12.fore_ref) | copy-start | bytes 7077892
  73.1 11.8 %collective-permute-start.12 = (bf16[8,16,128]{2,1,0:T(8,128)(2,1)S(1)}, bf16[8,16,128]{2,1,0:T(8,128)(2,1)S(1)}, u32[]{:S(2)}, u32[]{:S(2)}) collective-permute-start(bf16[8,16,128]{2,1,0:T(8,128)(2,1)S(1)} %get-tuple-element.46), channel_id=1, source_target_pairs={{1,0},{2,1},{3,2},{4,3},{5,4},{6,5},{7,6},{9,8},{10,9},{11,10},{12... | collective-permute-start | bytes 98312 | tf_op jit(solution)/shard_map/ppermute | solution.py:408
  79.8 18.7 %copy-start.3 = (bf16[9,256,512]{2,1,0:T(8,128)(2,1)S(1)}, bf16[9,256,512]{2,1,0:T(8,128)(2,1)}, u32[]{:S(2)}) copy-start(bf16[9,256,512]{2,1,0:T(8,128)(2,1)} %get-tuple-element.15.back_ref) | copy-start | bytes 7077892
  79.9 14.0 %collective-permute-start.22 = (bf16[2,9,192,128]{3,2,1,0:T(8,128)(2,1)S(1)}, bf16[2,9,192,128]{3,2,1,0:T(8,128)(2,1)S(1)}, u32[]{:S(2)}, u32[]{:S(2)}) collective-permute-start(bf16[2,9,192,128]{3,2,1,0:T(8,128)(2,1)S(1)} %get-tuple-element.18), channel_id=1, source_target_pairs={{0,8},{8,0},{16,24},{24,16},{1,9},{9,1},{17,25},{25,17},{2,10},{10... | collective-permute-start | bytes 2654216 | tf_op jit(solution)/shard_map/ppermute | solution.py:442
  80.0 5.9 %collective-permute-start.11 = (bf16[8,16,128]{2,1,0:T(8,128)(2,1)S(1)}, bf16[8,16,128]{2,1,0:T(8,128)(2,1)S(1)}, u32[]{:S(2)}, u32[]{:S(2)}) collective-permute-start(bf16[8,16,128]{2,1,0:T(8,128)(2,1)S(1)} %get-tuple-element.47), channel_id=1, source_target_pairs={{0,1},{1,2},{2,3},{3,4},{4,5},{5,6},{6,7},{8,9},{9,10},{10,11},{11... | collective-permute-start | bytes 98312 | tf_op jit(solution)/shard_map/ppermute | solution.py:407
  85.9 8.8 %collective-permute-start.13 = (bf16[6,16,128]{2,1,0:T(8,128)(2,1)S(1)}, bf16[6,16,128]{2,1,0:T(8,128)(2,1)S(1)}, u32[]{:S(2)}, u32[]{:S(2)}) collective-permute-start(bf16[6,16,128]{2,1,0:T(8,128)(2,1)S(1)} %pad_maximum_fusion.2), channel_id=1, source_target_pairs={{0,8},{8,16},{16,24},{1,9},{9,17},{17,25},{2,10},{10,18},{18,26},{... | collective-permute-start | bytes 73736 | tf_op jit(solution)/shard_map/ppermute | solution.py:411
  91.9 6.7 %collective-permute-start.14 = (bf16[6,16,128]{2,1,0:T(8,128)(2,1)S(1)}, bf16[6,16,128]{2,1,0:T(8,128)(2,1)S(1)}, u32[]{:S(2)}, u32[]{:S(2)}) collective-permute-start(bf16[6,16,128]{2,1,0:T(8,128)(2,1)S(1)} %pad_maximum_fusion.3), channel_id=1, source_target_pairs={{8,0},{16,8},{24,16},{9,1},{17,9},{25,17},{10,2},{18,10},{26,18},{... | collective-permute-start | bytes 73736 | tf_op jit(solution)/shard_map/ppermute | solution.py:412
  94.5 13.4 %collective-permute-start.23 = (bf16[9,192,128]{2,1,0:T(8,128)(2,1)S(1)}, bf16[9,192,128]{2,1,0:T(8,128)(2,1)S(1)}, u32[]{:S(2)}, u32[]{:S(2)}) collective-permute-start(bf16[9,192,128]{2,1,0:T(8,128)(2,1)S(1)} %get-tuple-element.20), channel_id=1, source_target_pairs={{0,16},{8,24},{16,0},{24,8},{1,17},{9,25},{17,1},{25,9},{2,18},{10... | collective-permute-start | bytes 1327112 | tf_op jit(solution)/shard_map/ppermute | solution.py:444
  103.5 8.0 %collective-permute-start.21 = (bf16[8,4,16,128]{3,2,1,0:T(8,128)(2,1)S(1)}, bf16[8,4,16,128]{3,2,1,0:T(8,128)(2,1)S(1)}, u32[]{:S(2)}, u32[]{:S(2)}) collective-permute-start(bf16[8,4,16,128]{3,2,1,0:T(8,128)(2,1)S(1)} %get-tuple-element.24), channel_id=1, source_target_pairs={{0,224},{32,128},{64,160},{96,192},{128,96},{160,0},{192,32},{224,... | collective-permute-start | bytes 393224 | tf_op jit(solution)/shard_map/ppermute | solution.py:449
  104.8 8.9 %collective-permute-start.20 = (bf16[8,4,16,128]{3,2,1,0:T(8,128)(2,1)S(1)}, bf16[8,4,16,128]{3,2,1,0:T(8,128)(2,1)S(1)}, u32[]{:S(2)}, u32[]{:S(2)}) collective-permute-start(bf16[8,4,16,128]{3,2,1,0:T(8,128)(2,1)S(1)} %get-tuple-element.25), channel_id=1, source_target_pairs={{0,192},{32,224},{64,128},{96,160},{128,64},{160,96},{192,0},{224,... | collective-permute-start | bytes 393224 | tf_op jit(solution)/shard_map/ppermute | solution.py:449
  106.8 9.4 %collective-permute-start.19 = (bf16[8,4,16,128]{3,2,1,0:T(8,128)(2,1)S(1)}, bf16[8,4,16,128]{3,2,1,0:T(8,128)(2,1)S(1)}, u32[]{:S(2)}, u32[]{:S(2)}) collective-permute-start(bf16[8,4,16,128]{3,2,1,0:T(8,128)(2,1)S(1)} %get-tuple-element.26), channel_id=1, source_target_pairs={{0,160},{32,192},{64,224},{96,128},{128,32},{160,64},{192,96},{224... | collective-permute-start | bytes 393224 | tf_op jit(solution)/shard_map/ppermute | solution.py:449
  106.8 17.3 %collective-permute-start.18 = (bf16[8,4,16,128]{3,2,1,0:T(8,128)(2,1)S(1)}, bf16[8,4,16,128]{3,2,1,0:T(8,128)(2,1)S(1)}, u32[]{:S(2)}, u32[]{:S(2)}) collective-permute-start(bf16[8,4,16,128]{3,2,1,0:T(8,128)(2,1)S(1)} %get-tuple-element.27), channel_id=1, source_target_pairs={{0,128},{32,160},{64,192},{96,224},{128,0},{160,32},{192,64},{224,... | collective-permute-start | bytes 393224 | tf_op jit(solution)/shard_map/ppermute | solution.py:449
  107.9 19.0 %collective-permute-start.17 = (bf16[8,4,16,128]{3,2,1,0:T(8,128)(2,1)S(1)}, bf16[8,4,16,128]{3,2,1,0:T(8,128)(2,1)S(1)}, u32[]{:S(2)}, u32[]{:S(2)}) collective-permute-start(bf16[8,4,16,128]{3,2,1,0:T(8,128)(2,1)S(1)} %get-tuple-element.28), channel_id=1, source_target_pairs={{0,96},{32,0},{64,32},{96,64},{128,224},{160,128},{192,160},{224,1... | collective-permute-start | bytes 393224 | tf_op jit(solution)/shard_map/ppermute | solution.py:449
  111.5 16.3 %collective-permute-start.16 = (bf16[8,4,16,128]{3,2,1,0:T(8,128)(2,1)S(1)}, bf16[8,4,16,128]{3,2,1,0:T(8,128)(2,1)S(1)}, u32[]{:S(2)}, u32[]{:S(2)}) collective-permute-start(bf16[8,4,16,128]{3,2,1,0:T(8,128)(2,1)S(1)} %get-tuple-element.29), channel_id=1, source_target_pairs={{0,64},{32,96},{64,0},{96,32},{128,192},{160,224},{192,128},{224,1... | collective-permute-start | bytes 393224 | tf_op jit(solution)/shard_map/ppermute | solution.py:449
  113.7 18.2 %collective-permute-start.15 = (bf16[8,4,16,128]{3,2,1,0:T(8,128)(2,1)S(1)}, bf16[8,4,16,128]{3,2,1,0:T(8,128)(2,1)S(1)}, u32[]{:S(2)}, u32[]{:S(2)}) collective-permute-start(bf16[8,4,16,128]{3,2,1,0:T(8,128)(2,1)S(1)} %get-tuple-element.30), channel_id=1, source_target_pairs={{0,32},{32,64},{64,96},{96,0},{128,160},{160,192},{192,224},{224,1... | collective-permute-start | bytes 393224 | tf_op jit(solution)/shard_map/ppermute | solution.py:449
  116.3 15.6 %collective-permute-start.30 = (bf16[16,1728]{1,0:T(8,128)(2,1)S(1)}, bf16[16,1728]{1,0:T(8,128)(2,1)S(1)}, u32[]{:S(2)}, u32[]{:S(2)}) collective-permute-start(bf16[16,1728]{1,0:T(8,128)(2,1)S(1)} %get-tuple-element.32), channel_id=1, source_target_pairs={{0,7},{1,0},{2,1},{3,2},{4,3},{5,4},{6,5},{7,6},{8,15},{9,8},{10,9... | collective-permute-start | bytes 165896 | tf_op jit(solution)/shard_map/ppermute | solution.py:454
  124.1 11.0 %collective-permute-start.29 = (bf16[16,1728]{1,0:T(8,128)(2,1)S(1)}, bf16[16,1728]{1,0:T(8,128)(2,1)S(1)}, u32[]{:S(2)}, u32[]{:S(2)}) collective-permute-start(bf16[16,1728]{1,0:T(8,128)(2,1)S(1)} %get-tuple-element.33), channel_id=1, source_target_pairs={{0,6},{1,7},{2,0},{3,1},{4,2},{5,3},{6,4},{7,5},{8,14},{9,15},{10,... | collective-permute-start | bytes 165896 | tf_op jit(solution)/shard_map/ppermute | solution.py:454
  126.9 9.7 %collective-permute-start.28 = (bf16[16,1728]{1,0:T(8,128)(2,1)S(1)}, bf16[16,1728]{1,0:T(8,128)(2,1)S(1)}, u32[]{:S(2)}, u32[]{:S(2)}) collective-permute-start(bf16[16,1728]{1,0:T(8,128)(2,1)S(1)} %get-tuple-element.34), channel_id=1, source_target_pairs={{0,5},{1,6},{2,7},{3,0},{4,1},{5,2},{6,3},{7,4},{8,13},{9,14},{10,... | collective-permute-start | bytes 165896 | tf_op jit(solution)/shard_map/ppermute | solution.py:454
  127.8 8.9 %collective-permute-start.27 = (bf16[16,1728]{1,0:T(8,128)(2,1)S(1)}, bf16[16,1728]{1,0:T(8,128)(2,1)S(1)}, u32[]{:S(2)}, u32[]{:S(2)}) collective-permute-start(bf16[16,1728]{1,0:T(8,128)(2,1)S(1)} %get-tuple-element.35), channel_id=1, source_target_pairs={{0,4},{1,5},{2,6},{3,7},{4,0},{5,1},{6,2},{7,3},{8,12},{9,13},{10,... | collective-permute-start | bytes 165896 | tf_op jit(solution)/shard_map/ppermute | solution.py:454
  131.9 8.5 %collective-permute-start.26 = (bf16[16,1728]{1,0:T(8,128)(2,1)S(1)}, bf16[16,1728]{1,0:T(8,128)(2,1)S(1)}, u32[]{:S(2)}, u32[]{:S(2)}) collective-permute-start(bf16[16,1728]{1,0:T(8,128)(2,1)S(1)} %get-tuple-element.36), channel_id=1, source_target_pairs={{0,3},{1,4},{2,5},{3,6},{4,7},{5,0},{6,1},{7,2},{8,11},{9,12},{10,... | collective-permute-start | bytes 165896 | tf_op jit(solution)/shard_map/ppermute | solution.py:454
  131.9 8.5 %collective-permute-start.25 = (bf16[16,1728]{1,0:T(8,128)(2,1)S(1)}, bf16[16,1728]{1,0:T(8,128)(2,1)S(1)}, u32[]{:S(2)}, u32[]{:S(2)}) collective-permute-start(bf16[16,1728]{1,0:T(8,128)(2,1)S(1)} %get-tuple-element.37), channel_id=1, source_target_pairs={{0,2},{1,3},{2,4},{3,5},{4,6},{5,7},{6,0},{7,1},{8,10},{9,11},{10,... | collective-permute-start | bytes 165896 | tf_op jit(solution)/shard_map/ppermute | solution.py:454
  135.2 8.9 %collective-permute-start.24 = (bf16[16,1728]{1,0:T(8,128)(2,1)S(1)}, bf16[16,1728]{1,0:T(8,128)(2,1)S(1)}, u32[]{:S(2)}, u32[]{:S(2)}) collective-permute-start(bf16[16,1728]{1,0:T(8,128)(2,1)S(1)} %get-tuple-element.38), channel_id=1, source_target_pairs={{0,1},{1,2},{2,3},{3,4},{4,5},{5,6},{6,7},{7,0},{8,9},{9,10},{10,1... | collective-permute-start | bytes 165896 | tf_op jit(solution)/shard_map/ppermute | solution.py:454
where the time goes:
time: 146 us; the launch traced here: 145 us
  starting transfers between devices  66.5 us (46%)
  waiting for transfers between devices  37.6 us (26%)
  Pallas kernels  29.8 us (20%)
  local copies, waits for them, and re-layouts  8.58 us (6%)
    pallas_call x10, Pallas kernels, call(): pl.pallas_call(kernel, out_shape=outs, in_specs=[pl.BlockSpec(memory_spac...  29.8 us
    ppermute x7, starting transfers between devices, per_device(): lax.ppermute(turned[d], 'sy', [(i, (i + d) % 8) for i in range(8)])  19.4 us
    ppermute x7, waiting for transfers between devices, per_device(): pieces[s] = lax.ppermute(own, 'filt', along_filt(s))  18.4 us
    ppermute x2, starting transfers between devices, rims(): x_before = lax.ppermute(x_last, 'sx', ups[:3])  13.7 us
    ppermute x7, starting transfers between devices, per_device(): pieces[s] = lax.ppermute(own, 'filt', along_filt(s))  9.42 us
    ppermute x2, starting transfers between devices, rims(): y_before = lax.ppermute(first, 'sy', ups)  9.07 us
    ppermute x7, starting transfers between devices, per_device(): sums[s] = lax.ppermute(parts[s], 'filt', along_filt(s))  8.19 us
    ppermute x7, waiting for transfers between devices, per_device(): lax.ppermute(turned[d], 'sy', [(i, (i + d) % 8) for i in range(8)])  7.49 us
  transfers between devices with their start and end apart: 31, of which 11 were waited for; matrix products, arithmetic and copies ran while one was open for 4% of the time, Pallas kernels for 14%

commit v1 on v0

--- a/solution.py
+++ b/solution.py
@@ -64,6 +64,49 @@
     return call(
         kernel, shape(PIECE), [(field, None)], [pltpu.VMEM((512, 128), F32)], 0, 400_000
     )
+
+
+def prepare_gather(field):
+    def kernel(field_ref, edge_ref, middle_ref, wide):
+        for x in range(8):
+            rows = field_ref[x].astype(F32)
+            for t in range(16):
+                wide[pl.ds(x * 16 + t, 4, stride=128), :] = rows[:, t * 128 : (t + 1) * 128]
+        for y, (ref, at) in enumerate(((edge_ref, 0), (middle_ref, 0), (middle_ref, 1), (edge_ref, 1))):
+            row = wide[y * 128 : y * 128 + 128, :].reshape(8, 16, 128).astype(BF)
+            for f in range(8):
+                ref[f, at] = row
+
+    out = shape((8, 2, 8, 16, 128))
+    return call(kernel, (out, out), [(field, None)], [pltpu.VMEM((512, 128), F32)], 0, 1_300_000)
+
+
+def gather_edges(edge, middle, y_before, y_after):
+    def kernel(edge_ref, middle_ref, yb, ya, last_ref, first_ref):
+        for out_ref, x in ((last_ref, 7), (first_ref, 0)):
+            for f in range(8):
+                out_ref[f, 0] = yb[f, x]
+                out_ref[f, 1] = edge_ref[f, 0, x]
+                out_ref[f, 2] = middle_ref[f, 0, x]
+                out_ref[f, 3] = middle_ref[f, 1, x]
+                out_ref[f, 4] = edge_ref[f, 1, x]
+                out_ref[f, 5] = ya[f, x]
+
+    out = shape((8, 6, 16, 128))
+    ins = [(a, None) for a in (edge, middle, y_before, y_after)]
+    return call(kernel, (out, out), ins, (), 0, 400_000)
+
+
+def grad_edges(pre_grad, y_before, y_after):
+    def kernel(pre_ref, yb, ya, last_ref, first_ref):
+        for out_ref, x in ((last_ref, 7), (first_ref, 0)):
+            out_ref[0] = yb[x]
+            out_ref[1:5] = pre_ref[x]
+            out_ref[5] = ya[x]
+
+    out = shape((6, 16, 128))
+    ins = [(a, None) for a in (pre_grad, y_before, y_after)]
+    return call(kernel, (out, out), ins, (), 0, 50_000)
 
 
 def prepare_weights(weights):
@@ -104,18 +147,16 @@
     )
 
 
-def forward(coords, pieces, y_before, y_after, x_before, x_after, fore, grad):
+def masked(v, inside):
+    return jnp.where(inside, v, jnp.zeros_like(v))
+
+
+def forward(coords, edge, middle, y_before, y_after, x_before, x_after, fore, grad):
     def kernel(
-        co, p0, p1, p2, p3, p4, p5, p6, p7, yb, ya, xb, xa, fore_ref, grad_ref,
-        field_ref, out_ref, pre_ref, slots, total, wide, sems,
+        co, edge_ref, middle_ref, yb, ya, xb, xa, fore_ref, grad_ref,
+        field_ref, out_ref, pre_ref, first_ref, last_ref, total, wide,
     ):
-        col, row = co[0], co[1]
-        copies = []
-        for s, piece in enumerate((p0, p1, p2, p3, p4, p5, p6, p7)):
-            owner = (col ^ (s // 4)) * 4 + ((row - s) & 3)
-            copies.append(pltpu.make_async_copy(piece, slots.at[owner], sems.at[s]))
-        for copy in copies:
-            copy.start()
+        y_low, y_high, x_low, x_high = co[4] > 0, co[4] < 7, co[5] > 0, co[5] < 3
 
         def place(x, y, take):
             for q in range(4):
@@ -124,20 +165,18 @@
                 field_ref[x, y * 32 : y * 32 + 16, lanes] = jnp.concatenate([a[:, :64], b[:, :64]], axis=1)
                 field_ref[x, y * 32 + 16 : y * 32 + 32, lanes] = jnp.concatenate([a[:, 64:], b[:, 64:]], axis=1)
 
-        def slot(owner):
-            return ((owner // 4) ^ col) * 4 + ((row - owner) & 3)
-
         for y in range(6):
-            place(0, y, lambda f: xb[slot(f), y])
-            place(9, y, lambda f: xa[slot(f), y])
-        for copy in copies:
-            copy.wait()
+            beside = {0: y_low, 5: y_high}.get(y, True)
+            place(0, y, lambda f: masked(xb[f, y], jnp.logical_and(x_low, beside)))
+            place(9, y, lambda f: masked(xa[f, y], jnp.logical_and(x_high, beside)))
 
         def place_x(x, carry):
-            place(x + 1, 0, lambda f: yb[slot(f), x])
-            place(x + 1, 5, lambda f: ya[slot(f), x])
-            for y in range(4):
-                place(x + 1, y + 1, lambda f: slots[f, x, y])
+            place(x + 1, 0, lambda f: masked(yb[f, x], y_low))
+            place(x + 1, 5, lambda f: masked(ya[f, x], y_high))
+            place(x + 1, 1, lambda f: edge_ref[f, 0, x])
+            place(x + 1, 2, lambda f: middle_ref[f, 0, x])
+            place(x + 1, 3, lambda f: middle_ref[f, 1, x])
+            place(x + 1, 4, lambda f: edge_ref[f, 1, x])
             return carry
 
         lax.fori_loop(0, 8, place_x, 0)
@@ -170,7 +209,12 @@
                 value = LEAK * pre + (1.0 - LEAK) * (soft - math.log(2.0))
                 wide[pl.ds(pl.multiple_of(x * 64 + y * 16, 16), 16), :] = value
                 g = grad_ref[x, y].astype(F32)
-                pre_ref[x, y] = (g * (LEAK + (1.0 - LEAK) * slope)).astype(BF)
+                turned = (g * (LEAK + (1.0 - LEAK) * slope)).astype(BF)
+                pre_ref[x, y] = turned
+                if y == 0:
+                    first_ref[x] = turned
+                if y == 3:
+                    last_ref[x] = turned
             return carry
 
         lax.fori_loop(0, 8, finish, 0)
@@ -178,16 +222,19 @@
 
     return call(
         kernel,
-        (shape((10, 192, 512)), shape((8, 4, 2048)), shape(PIECE)),
+        (
+            shape((10, 192, 512)),
+            shape((8, 4, 2048)),
+            shape(PIECE),
+            shape((8, 16, 128)),
+            shape((8, 16, 128)),
+        ),
         [(coords, pltpu.SMEM)]
-        + [(piece, pl.ANY) for piece in pieces]
-        + [(a, None) for a in (y_before, y_after, x_before, x_after, fore, grad)],
-        [
-            pltpu.VMEM((8,) + PIECE, BF),
-            pltpu.VMEM((1024, 256), F32),
-            pltpu.VMEM((512, 128), F32),
-            pltpu.SemaphoreType.DMA((8,)),
+        + [
+            (a, None)
+            for a in (edge, middle, y_before, y_after, x_before, x_after, fore, grad)
         ],
+        [pltpu.VMEM((1024, 256), F32), pltpu.VMEM((512, 128), F32)],
         5_000_000_000,
         6_000_000,
     )
@@ -262,21 +309,19 @@
     )
 
 
-def add_far(coords, stay, got):
-    def kernel(co, stay_ref, got_ref, *outs):
-        out_ref, total, turned = outs
-        sy = co[4]
+def add_far(stay, got):
+    def kernel(stay_ref, got_ref, out_ref, total, turned):
         total[...] = (stay_ref[...] + got_ref[...].astype(F32)).reshape(1728, 128)
         for t in range(14):
             width = min(128, 1728 - t * 128)
             turned[:, t * 128 : t * 128 + width] = total[t * 128 : t * 128 + width, :].T.astype(BF)
         for s in range(8):
-            out_ref[(s - sy) & 7] = turned[s * 16 : s * 16 + 16, :]
+            out_ref[s] = turned[s * 16 : s * 16 + 16, :]
 
     return call(
         kernel,
         shape((8, 16, 1728)),
-        [(coords, pltpu.SMEM), (stay, None), (got, None)],
+        [(stay, None), (got, None)],
         [pltpu.VMEM((1728, 128), F32), pltpu.VMEM((128, 1728), BF)],
         0,
         2_000_000,
@@ -284,14 +329,13 @@
 
 
 def add_regions(parts):
-    def kernel(*refs):
-        ins, (out_ref, total, pairs) = refs[:8], refs[8:]
+    def kernel(parts_ref, out_ref, total, pairs):
         for t in range(14):
             width = min(128, 1728 - t * 128)
             lanes = slice(t * 128, t * 128 + width)
-            s = ins[0][:, lanes].astype(F32)
-            for ref in ins[1:]:
-                s = s + ref[:, lanes].astype(F32)
+            s = parts_ref[0, :, lanes].astype(F32)
+            for d in range(1, 8):
+                s = s + parts_ref[d, :, lanes].astype(F32)
             total[:, 0:width] = s
             even, odd = total[pl.ds(0, 8, stride=2), :], total[pl.ds(1, 8, stride=2), :]
             for u in range(width // 64):
@@ -304,7 +348,7 @@
     return call(
         kernel,
         shape((27, 1024), F32),
-        [(part, None) for part in parts],
+        [(parts, None)],
         [pltpu.VMEM((16, 128), F32), pltpu.VMEM((216, 128), F32)],
         0,
         600_000,
@@ -313,7 +357,7 @@
 
 def input_grad_parts(coords, pre_grad, y_before, y_after, x_before, x_after, back):
     def kernel(co, pre_ref, yb, ya, xb, xa, back_ref, out_ref, rim, total):
-        col, row = co[0], co[1]
+        y_low, y_high, x_low, x_high = co[4] > 0, co[4] < 7, co[5] > 0, co[5] < 3
 
         def place(x, y, v):
             low, high = stacked_depth(v.astype(F32))
@@ -323,12 +367,13 @@
                 rim[x, y * 32 + 16 : y * 32 + 32, lanes] = high[half].astype(BF)
 
         for y in range(6):
-            place(0, y, xb[y])
-            place(9, y, xa[y])
+            beside = {0: y_low, 5: y_high}.get(y, True)
+            place(0, y, masked(xb[y], jnp.logical_and(x_low, beside)))
+            place(9, y, masked(xa[y], jnp.logical_and(x_high, beside)))
 
         def place_x(x, carry):
-            place(x + 1, 0, yb[x])
-            place(x + 1, 5, ya[x])
+            place(x + 1, 0, masked(yb[x], y_low))
+            place(x + 1, 5, masked(ya[x], y_high))
             for y in range(4):
                 place(x + 1, y + 1, pre_ref[x, y])
             return carry
@@ -357,8 +402,7 @@
                         pair = jnp.concatenate(
                             [total[at : at + 16, lanes], total[at + 16 : at + 32, lanes]], axis=1
                         )
-                        slot = ((f // 4) ^ col) * 4 + ((f - row) & 3)
-                        out_ref[slot, 2 * h + u, y] = pair.astype(BF)
+                        out_ref[f, 2 * h + u, y] = pair.astype(BF)
             return carry
 
         lax.fori_loop(0, 4, multiply, 0)
@@ -375,85 +419,63 @@
 
 
 def add_blocks(parts):
-    def kernel(*refs):
-        ins, (out_ref, wide) = refs[:8], refs[8:]
-        s = ins[0][...].astype(F32)
-        for ref in ins[1:]:
-            s = s + ref[...].astype(F32)
+    def kernel(parts_ref, out_ref, wide):
+        s = parts_ref[0].astype(F32)
+        for f in range(1, 8):
+            s = s + parts_ref[f].astype(F32)
         wide[...] = s.reshape(512, 128)
         from_pairs(wide, out_ref)
 
     return call(
         kernel,
         shape((8, 4, 2048)),
-        [(part, None) for part in parts],
+        [(parts, None)],
         [pltpu.VMEM((512, 128), F32)],
         0,
         1_200_000,
     )
 
 
-def along_filt(slot):
-    return [(f, ((f // 4) ^ (slot // 4)) * 4 + (f + slot) % 4) for f in range(8)]
-
-
-ORDER = (2, 6, 1, 3, 5, 7, 4)
-
-
-def rims(field, y_dim, join):
-    ups = [(i, i + 1) for i in range(7)]
-    downs = [(i + 1, i) for i in range(7)]
-    first, last = join(3), join(0)
-    y_before = lax.ppermute(first, "sy", ups)
-    y_after = lax.ppermute(last, "sy", downs)
-    x_last = field(7, y_before, y_after)
-    x_first = field(0, y_before, y_after)
-    x_before = lax.ppermute(x_last, "sx", ups[:3])
-    x_after = lax.ppermute(x_first, "sx", downs[:3])
-    return y_before, y_after, x_before, x_after
+def both_ways(last, first, axis, size):
+    return (
+        lax.ppermute(last, axis, [(i, (i + 1) % size) for i in range(size)]),
+        lax.ppermute(first, axis, [((i + 1) % size, i) for i in range(size)]),
+    )
+
+
+def exchange(parts, axis):
+    return lax.all_to_all(parts, axis, 0, 0)
 
 
 def per_device(activations, weights, out_grad):
     filt, sx, sy = (lax.axis_index(a) for a in ("filt", "sx", "sy"))
-    coords = jnp.stack([filt // 4, filt % 4, sx % 2, sx // 2, sy, 0, 0, 0]).astype(jnp.int32)
-    own = prepare_field(activations[0, 0])
-    pieces = {0: own}
-    for s in ORDER:
-        pieces[s] = lax.ppermute(own, "filt", along_filt(s))
-    pieces = [pieces[s] for s in range(8)]
+    coords = jnp.stack([filt // 4, filt % 4, sx % 2, sx // 2, sy, sx, 0, 0]).astype(jnp.int32)
+    edge, middle = prepare_gather(activations[0, 0])
+    edge = exchange(edge, "filt")
+    middle, edge = lax.optimization_barrier((middle, edge))
+    y_before, y_after = both_ways(edge[:, 1], edge[:, 0], "sy", 8)
+    middle = exchange(middle, "filt")
+    middle, weights, out_grad = lax.optimization_barrier((middle, weights, out_grad))
+    x_last, x_first = gather_edges(edge, middle, y_before, y_after)
+    x_before, x_after = both_ways(x_last, x_first, "sx", 4)
     fore, back = prepare_weights(weights[0])
     grad = prepare_field(out_grad[0, 0])
-
-    halos = rims(
-        lambda x, yb, ya: jnp.concatenate(
-            [yb[:, x : x + 1], jnp.stack([p[x] for p in pieces]), ya[:, x : x + 1]], axis=1
-        ),
-        1,
-        lambda y: jnp.stack([p[:, y] for p in pieces]),
-    )
-    field, outputs, pre_grad = forward(coords, pieces, *halos, fore, grad)
-
-    grad_halos = rims(
-        lambda x, yb, ya: jnp.concatenate([yb[x : x + 1], pre_grad[x], ya[x : x + 1]], axis=0),
-        1,
-        lambda y: pre_grad[:, y],
-    )
+    field, outputs, pre_grad, g_first, g_last = forward(
+        coords, edge, middle, y_before, y_after, x_before, x_after, fore, grad
+    )
+
+    gy_before, gy_after = both_ways(g_last, g_first, "sy", 8)
     keep, send = filter_grad(coords, field, pre_grad)
     got = lax.ppermute(send, "sx", [(i, i ^ 1) for i in range(4)])
+    gx_before, gx_after = both_ways(*grad_edges(pre_grad, gy_before, gy_after), "sx", 4)
     stay, send = add_cores(coords, keep, got)
+    send, pre_grad = lax.optimization_barrier((send, pre_grad))
     got = lax.ppermute(send, "sx", [(i, i ^ 2) for i in range(4)])
 
-    parts = input_grad_parts(coords, pre_grad, *grad_halos, back)
-    sums = {0: parts[0]}
-    for s in ORDER:
-        sums[s] = lax.ppermute(parts[s], "filt", along_filt(s))
-
-    turned = add_far(coords, stay, got)
-    regions = [turned[0]]
-    for d in range(1, 8):
-        regions.append(lax.ppermute(turned[d], "sy", [(i, (i + d) % 8) for i in range(8)]))
-
-    input_grad = add_blocks([sums[s] for s in range(8)])
+    parts = input_grad_parts(coords, pre_grad, gy_before, gy_after, gx_before, gx_after, back)
+    parts = exchange(parts, "filt")
+    regions = exchange(add_far(stay, got), "sy")
+    input_grad = add_blocks(parts)
     weight_grad = add_regions(regions)
     return outputs[None, None], input_grad[None, None], weight_grad[None]
 

time: 146 us -> 134 us (0.918)
  starting transfers between devices: 66.5 us -> 33.3 us
  blocking collectives: 0 us -> 14.4 us
  waiting for transfers between devices: 37.6 us -> 49.1 us
  local copies, waits for them, and re-layouts: 8.58 us -> 4.05 us
  Pallas kernels: 29.8 us -> 31.8 us
    ppermute x29 -> x8, starting transfers between devices: 66.2 us -> 18.1 us  [the longest x4 9.8 us: both_ways(): lax.ppermute(last, axis, [(i, (i + 1) % size) for i in range(size)])]
    ppermute x29 -> x8, waiting for transfers between devices: 37.6 us -> 11.4 us  [the longest x4 6.82 us: both_ways(): lax.ppermute(first, axis, [((i + 1) % size, i) for i in range(size)])]
    ppermute x1, waiting for transfers between devices: 0.01 us -> 21.4 us  [per_device(): got = lax.ppermute(send, 'sx', [(i, i ^ 2) for i in range(4)])]
    all_to_all x0 -> x3, waiting for transfers between devices: none -> 16.3 us  [exchange(): return lax.all_to_all(parts, axis, 0, 0)]
    all_to_all x0 -> x1, blocking collectives: none -> 14.4 us  [exchange(): return lax.all_to_all(parts, axis, 0, 0)]
    all_to_all x0 -> x3, starting transfers between devices: none -> 12.5 us  [exchange(): return lax.all_to_all(parts, axis, 0, 0)]
    ppermute x9 -> x0, local copies, waits for them, and re-layouts: 4.65 us -> none  [the longest x7 3.69 us: per_device(): pieces[s] = lax.ppermute(own, 'filt', along_filt(s))]
    pallas_call x10 -> x12, Pallas kernels: 29.8 us -> 31.8 us  [call(): pl.pallas_call(kernel, out_shape=outs, in_specs=[pl.BlockSpec(memory_spac...]
  transfers between devices with their start and end apart: 31 -> 13, of which waited for: 11 -> 8; matrix products, arithmetic and copies ran while one was open for 4% -> 1% of each run, Pallas kernels for 14% -> 8%
where the time goes in v1:
time: 134 us; the launch traced here: 133 us
  waiting for transfers between devices  49.1 us (37%)
  starting transfers between devices  33.3 us (25%)
  Pallas kernels  31.8 us (24%)
  blocking collectives  14.4 us (11%)
  local copies, waits for them, and re-layouts  4.05 us (3%)
    pallas_call x12, Pallas kernels, call(): pl.pallas_call(kernel, out_shape=outs, in_specs=[pl.BlockSpec(memory_spac...  31.8 us
    ppermute x1, waiting for transfers between devices, per_device(): got = lax.ppermute(send, 'sx', [(i, i ^ 2) for i in range(4)])  21.4 us
    all_to_all x3, waiting for transfers between devices, exchange(): return lax.all_to_all(parts, axis, 0, 0)  16.3 us
    all_to_all x1, blocking collectives, exchange(): return lax.all_to_all(parts, axis, 0, 0)  14.4 us
    all_to_all x3, starting transfers between devices, exchange(): return lax.all_to_all(parts, axis, 0, 0)  12.5 us
    ppermute x4, starting transfers between devices, both_ways(): lax.ppermute(last, axis, [(i, (i + 1) % size) for i in range(size)])  9.8 us
    ppermute x4, starting transfers between devices, both_ways(): lax.ppermute(first, axis, [((i + 1) % size, i) for i in range(size)])  8.27 us
    ppermute x4, waiting for transfers between devices, both_ways(): lax.ppermute(first, axis, [((i + 1) % size, i) for i in range(size)])  6.82 us
  transfers between devices with their start and end apart: 13, of which 8 were waited for; matrix products, arithmetic and copies ran while one was open for 1% of the time, Pallas kernels for 8%

profile of v1, /device:TPU:1, one launch (start us, length us, event | category | flops | bytes accessed | tf_op | source)
XLA Modules:
  0.0 133.3 jit_solution(8544019019193104482)
XLA Ops:
  0.6 0.0 copy-start.2
  0.6 0.9 copy-done.2
  1.5 0.2 shard_map.58
  1.8 0.0 copy-start.1
  1.8 14.4 %all_to_all.20.edge_ref = bf16[8,2,8,16,128]{4,3,2,1,0:T(8,128)(2,1)S(1)} all-to-all(bf16[8,2,8,16,128]{4,3,2,1,0:T(8,128)(2,1)S(1)} %get-tuple-element.28), channel_id=1, replica_groups=mesh['filt'=8,'sx'=4,'sy'=8] {'filt'}, dimensions={0} | all-to-all | bytes 1048576 | tf_op jit(solution)/shard_map/all_to_all | solution.py:447
  16.1 0.0 copy-done.1
  16.1 0.0 copy-start.3
  16.1 0.0 copy-start
  16.1 3.6 %all-to-all-start.1 = ((bf16[8,2,8,16,128]{4,3,2,1,0:T(8,128)(2,1)}), bf16[8,2,8,16,128]{4,3,2,1,0:T(8,128)(2,1)S(1)}, u32[]{:S(2)}, u32[]{:S(2)}) async-start(bf16[8,2,8,16,128]{4,3,2,1,0:T(8,128)(2,1)} %copy-done.1), calls=%async_computation.1 | async-start | bytes 1048576 | tf_op jit(solution)/shard_map/all_to_all | solution.py:447
  19.8 0.9 slice_bitcast_fusion
  20.6 5.6 %collective-permute-start.1 = (bf16[8,8,16,128]{3,2,1,0:T(8,128)(2,1)}, bf16[8,8,16,128]{3,2,1,0:T(8,128)(2,1)S(1)}, u32[]{:S(2)}, u32[]{:S(2)}) collective-permute-start(bf16[8,8,16,128]{3,2,1,0:T(8,128)(2,1)} %get-tuple-element.57), channel_id=1, source_target_pairs={{1,0},{2,1},{3,2},{4,3},{5,4},{6,5},{7,6},{0,7},{9,8},{10,9},{11,1... | collective-permute-start | bytes 786440 | tf_op jit(solution)/shard_map/ppermute | solution.py:442
  26.2 0.0 collective-permute-start
  26.2 0.6 all-to-all-done.1.middle_ref
  26.8 3.0 %collective-permute-done.1.ya = bf16[8,8,16,128]{3,2,1,0:T(8,128)(2,1)S(1)} collective-permute-done((bf16[8,8,16,128]{3,2,1,0:T(8,128)(2,1)}, bf16[8,8,16,128]{3,2,1,0:T(8,128)(2,1)S(1)}, u32[]{:S(2)}, u32[]{:S(2)}) %collective-permute-start.1) | collective-permute-done | bytes 262176 | tf_op jit(solution)/shard_map/ppermute | solution.py:442
  29.8 3.1 %collective-permute-done.yb = bf16[8,8,16,128]{3,2,1,0:T(8,128)(2,1)} collective-permute-done((bf16[8,8,16,128]{3,2,1,0:T(8,128)(2,1)}, bf16[8,8,16,128]{3,2,1,0:T(8,128)(2,1)}, u32[]{:S(2)}, u32[]{:S(2)}) %collective-permute-start) | collective-permute-done | bytes 262176 | tf_op jit(solution)/shard_map/ppermute | solution.py:441
  33.0 1.7 %shard_map.59 = (bf16[8,6,16,128]{3,2,1,0:T(8,128)(2,1)}, bf16[8,6,16,128]{3,2,1,0:T(8,128)(2,1)}) custom-call(bf16[8,2,8,16,128]{4,3,2,1,0:T(8,128)(2,1)S(1)} %all_to_all.20.edge_ref, bf16[8,2,8,16,128]{4,3,2,1,0:T(8,128)(2,1)S(1)} %all-to-all-done.1.middle_ref, bf16[8,8,16,128]{3,2,1,0:T(8,128)(2,1)} %collective-permute-done.yb, ...), custom_call_target="tpu_custom_call" | custom-call | bytes 400000 | tf_op jit(solution)/shard_map/pallas_call | solution.py:18
  34.7 6.2 %collective-permute-start.2 = (bf16[8,6,16,128]{3,2,1,0:T(8,128)(2,1)}, bf16[8,6,16,128]{3,2,1,0:T(8,128)(2,1)}, u32[]{:S(2)}, u32[]{:S(2)}) collective-permute-start(bf16[8,6,16,128]{3,2,1,0:T(8,128)(2,1)} %get-tuple-element.32), channel_id=1, source_target_pairs={{0,8},{8,16},{16,24},{24,0},{1,9},{9,17},{17,25},{25,1},{2,10},{10... | collective-permute-start | bytes 589832 | tf_op jit(solution)/shard_map/ppermute | solution.py:441
  40.9 0.0 collective-permute-start.3
  40.9 0.1 stack.27.co
  40.9 0.0 copy-done.3
  40.9 0.1 shard_map.61.grad_ref
  41.0 0.0 copy-done
  41.0 7.8 %shard_map.60 = (bf16[9,512,256]{2,1,0:T(8,128)(2,1)S(1)}, bf16[9,256,512]{2,1,0:T(8,128)(2,1)}) custom-call(bf16[27,32768]{1,0:T(8,128)(2,1)S(1)} %bitcast.16), custom_call_target="tpu_custom_call" | custom-call | bytes 8000000 | tf_op jit(solution)/shard_map/pallas_call | solution.py:18
  48.8 0.0 copy-start.5
  48.8 1.4 %copy-done.5 = bf16[9,512,256]{2,1,0:T(8,128)(2,1)} copy-done((bf16[9,512,256]{2,1,0:T(8,128)(2,1)}, bf16[9,512,256]{2,1,0:T(8,128)(2,1)S(1)}, u32[]{:S(2)}) %copy-start.5) | copy-done | bytes 2359320
  50.3 0.0 collective-permute-done.2.xb
  50.3 0.0 collective-permute-done.3.xa
  50.3 7.9 %shard_map.62 = (bf16[10,192,512]{2,1,0:T(8,128)(2,1)S(1)}, bf16[8,4,2048]{2,1,0:T(4,128)(2,1)}, bf16[8,4,16,128]{3,2,1,0:T(8,128)(2,1)S(1)}, bf16[8,16,128]{2,1,0:T(8,128)(2,1)S(1)}, bf16[8,16,128]{2,1,0:T(8,128)(2,1)S(1)}) custom-call(s32[8]{0:T(128)S(1)} %stack.27.co, bf16[8,2,8,16,128]{4,3,2,1,0:T(8,128)(2,1)S(1)} %all_to_all.20.edge_ref, ...), custom_call_target="tpu_custom_call" | custom-call | flops 5000000000 | bytes 6000000 | tf_op jit(solution)/shard_map/pallas_call | solution.py:18
  58.2 5.5 %shard_map.63 = (f32[2,9,192,128]{3,2,1,0:T(8,128)S(1)}, bf16[2,9,192,128]{3,2,1,0:T(8,128)(2,1)S(1)}) custom-call(s32[8]{0:T(128)S(1)} %stack.27.co, bf16[10,192,512]{2,1,0:T(8,128)(2,1)S(1)} %get-tuple-element.38.field_ref, bf16[8,4,16,128]{3,2,1,0:T(8,128)(2,1)S(1)} %get-tuple-element.43.pre_ref), custom_call_target="tpu_custom_call" | custom-call | flops 5000000000 | bytes 6000000 | tf_op jit(solution)/shard_map/pallas_call | solution.py:18
  63.7 0.0 copy-start.4
  63.7 1.0 collective-permute-start.4
  64.7 0.0 collective-permute-start.5
  64.7 2.7 %collective-permute-start.6 = (bf16[8,16,128]{2,1,0:T(8,128)(2,1)S(1)}, bf16[8,16,128]{2,1,0:T(8,128)(2,1)S(1)}, u32[]{:S(2)}, u32[]{:S(2)}) collective-permute-start(bf16[8,16,128]{2,1,0:T(8,128)(2,1)S(1)} %get-tuple-element.45), channel_id=1, source_target_pairs={{1,0},{2,1},{3,2},{4,3},{5,4},{6,5},{7,6},{0,7},{9,8},{10,9},{11,1... | collective-permute-start | bytes 98312 | tf_op jit(solution)/shard_map/ppermute | solution.py:442
  67.3 1.3 collective-permute-done.5.yb
  68.6 0.0 collective-permute-done.6.ya
  68.7 3.6 %collective-permute-start.7 = (bf16[6,16,128]{2,1,0:T(8,128)(2,1)S(1)}, bf16[6,16,128]{2,1,0:T(8,128)(2,1)S(1)}, u32[]{:S(2)}, u32[]{:S(2)}) collective-permute-start(bf16[6,16,128]{2,1,0:T(8,128)(2,1)S(1)} %get-tuple-element.46), channel_id=1, source_target_pairs={{0,8},{8,16},{16,24},{24,0},{1,9},{9,17},{17,25},{25,1},{2,10},{10... | collective-permute-start | bytes 73736 | tf_op jit(solution)/shard_map/ppermute | solution.py:441
  72.3 0.0 collective-permute-start.8
  72.3 0.0 collective-permute-done.4.got_ref
  72.3 0.7 shard_map.64
  73.0 0.2 collective-permute-done.7.xb
  73.2 3.8 %collective-permute-done.8.xa = bf16[6,16,128]{2,1,0:T(8,128)(2,1)S(1)} collective-permute-done((bf16[6,16,128]{2,1,0:T(8,128)(2,1)S(1)}, bf16[6,16,128]{2,1,0:T(8,128)(2,1)S(1)}, u32[]{:S(2)}, u32[]{:S(2)}) %collective-permute-start.8) | collective-permute-done | bytes 24608 | tf_op jit(solution)/shard_map/ppermute | solution.py:442
  77.0 0.0 copy-done.4
  77.0 5.7 %shard_map.66 = bf16[8,8,4,16,128]{4,3,2,1,0:T(8,128)(2,1)} custom-call(s32[8]{0:T(128)S(1)} %stack.27.co, bf16[8,4,16,128]{3,2,1,0:T(8,128)(2,1)S(1)} %get-tuple-element.43.pre_ref, bf16[8,16,128]{2,1,0:T(8,128)(2,1)S(1)} %collective-permute-done.5.yb, bf16[8,16,128]{2,1,0:T(8,128)(2,1)S(1)} %collective-permute-done.6.ya, ...), custom_call_target="tpu_custom_call" | custom-call | flops 5000000000 | bytes 5000000 | tf_op jit(solution)/shard_map/pallas_call | solution.py:18
  82.8 4.7 %all-to-all-start.2 = ((bf16[8,8,4,16,128]{4,3,2,1,0:T(8,128)(2,1)}), bf16[8,8,4,16,128]{4,3,2,1,0:T(8,128)(2,1)S(1)}, u32[]{:S(2)}, u32[]{:S(2)}) async-start(bf16[8,8,4,16,128]{4,3,2,1,0:T(8,128)(2,1)} %shard_map.66), calls=%async_computation.2 | async-start | bytes 2097152 | tf_op jit(solution)/shard_map/all_to_all | solution.py:447
  87.5 1.7 %collective-permute-start.9 = (bf16[9,192,128]{2,1,0:T(8,128)(2,1)S(1)}, bf16[9,192,128]{2,1,0:T(8,128)(2,1)S(1)}, u32[]{:S(2)}, u32[]{:S(2)}) collective-permute-start(bf16[9,192,128]{2,1,0:T(8,128)(2,1)S(1)} %get-tuple-element.50), channel_id=1, source_target_pairs={{0,16},{8,24},{16,0},{24,8},{1,17},{9,25},{17,1},{25,9},{2,18},{10... | collective-permute-start | bytes 1327112 | tf_op jit(solution)/shard_map/ppermute | solution.py:473
  89.3 21.4 %collective-permute-done.9.got_ref = bf16[9,192,128]{2,1,0:T(8,128)(2,1)S(1)} collective-permute-done((bf16[9,192,128]{2,1,0:T(8,128)(2,1)S(1)}, bf16[9,192,128]{2,1,0:T(8,128)(2,1)S(1)}, u32[]{:S(2)}, u32[]{:S(2)}) %collective-permute-start.9) | collective-permute-done | bytes 442400 | tf_op jit(solution)/shard_map/ppermute | solution.py:473
  110.6 1.0 shard_map.68
  111.7 0.0 all-to-all-done.2.parts_ref
  111.7 4.2 %all-to-all-start.3 = ((bf16[8,16,1728]{2,1,0:T(8,128)(2,1)}), bf16[8,16,1728]{2,1,0:T(8,128)(2,1)S(1)}, u32[]{:S(2)}, u32[]{:S(2)}) async-start(bf16[8,16,1728]{2,1,0:T(8,128)(2,1)} %shard_map.68), calls=%async_computation.3 | async-start | bytes 917504 | tf_op jit(solution)/shard_map/all_to_all | solution.py:447
  115.8 0.9 shard_map.67
  116.7 15.6 %all-to-all-done.3.parts_ref = bf16[8,16,1728]{2,1,0:T(8,128)(2,1)S(1)} async-done(((bf16[8,16,1728]{2,1,0:T(8,128)(2,1)}), bf16[8,16,1728]{2,1,0:T(8,128)(2,1)S(1)}, u32[]{:S(2)}, u32[]{:S(2)}) %all-to-all-start.3) | async-done | bytes 442400 | tf_op jit(solution)/shard_map/all_to_all | solution.py:447
  132.4 0.2 shard_map.69
  132.5 0.8 copy.12
  (2 shorter events, 0.0 us)
Async XLA Ops:
  0.6 0.9 copy-start.2
  1.8 14.4 %copy-start.1 = (bf16[8,2,8,16,128]{4,3,2,1,0:T(8,128)(2,1)}, bf16[8,2,8,16,128]{4,3,2,1,0:T(8,128)(2,1)S(1)}, u32[]{:S(2)}) copy-start(bf16[8,2,8,16,128]{4,3,2,1,0:T(8,128)(2,1)S(1)} %get-tuple-element.30) | copy-start | bytes 1572868
  16.1 24.8 %copy-start.3 = (bf16[1,1,8,4,2048]{4,3,2,1,0:T(4,128)(2,1)S(1)}, bf16[1,1,8,4,2048]{4,3,2,1,0:T(4,128)(2,1)}, u32[]{:S(2)}) copy-start(bf16[1,1,8,4,2048]{4,3,2,1,0:T(4,128)(2,1)} %param.5) | copy-start | bytes 393220
  16.1 24.9 %copy-start = (bf16[1,27,32768]{2,1,0:T(8,128)(2,1)S(1)}, bf16[1,27,32768]{2,1,0:T(8,128)(2,1)}, u32[]{:S(2)}) copy-start(bf16[1,27,32768]{2,1,0:T(8,128)(2,1)} %param.4) | copy-start | bytes 5308420
  16.1 10.7 %all-to-all-start.1 = ((bf16[8,2,8,16,128]{4,3,2,1,0:T(8,128)(2,1)}), bf16[8,2,8,16,128]{4,3,2,1,0:T(8,128)(2,1)S(1)}, u32[]{:S(2)}, u32[]{:S(2)}) async-start(bf16[8,2,8,16,128]{4,3,2,1,0:T(8,128)(2,1)} %copy-done.1), calls=%async_computation.1 | async-start | bytes 1048576 | tf_op jit(solution)/shard_map/all_to_all | solution.py:447
  20.6 9.2 %collective-permute-start.1 = (bf16[8,8,16,128]{3,2,1,0:T(8,128)(2,1)}, bf16[8,8,16,128]{3,2,1,0:T(8,128)(2,1)S(1)}, u32[]{:S(2)}, u32[]{:S(2)}) collective-permute-start(bf16[8,8,16,128]{3,2,1,0:T(8,128)(2,1)} %get-tuple-element.57), channel_id=1, source_target_pairs={{1,0},{2,1},{3,2},{4,3},{5,4},{6,5},{7,6},{0,7},{9,8},{10,9},{11,1... | collective-permute-start | bytes 786440 | tf_op jit(solution)/shard_map/ppermute | solution.py:442
  26.2 6.7 %collective-permute-start = (bf16[8,8,16,128]{3,2,1,0:T(8,128)(2,1)}, bf16[8,8,16,128]{3,2,1,0:T(8,128)(2,1)}, u32[]{:S(2)}, u32[]{:S(2)}) collective-permute-start(bf16[8,8,16,128]{3,2,1,0:T(8,128)(2,1)} %get-tuple-element.58), channel_id=1, source_target_pairs={{0,1},{1,2},{2,3},{3,4},{4,5},{5,6},{6,7},{7,0},{8,9},{9,10},{10,1... | collective-permute-start | bytes 786440 | tf_op jit(solution)/shard_map/ppermute | solution.py:441
  34.7 15.6 %collective-permute-start.2 = (bf16[8,6,16,128]{3,2,1,0:T(8,128)(2,1)}, bf16[8,6,16,128]{3,2,1,0:T(8,128)(2,1)}, u32[]{:S(2)}, u32[]{:S(2)}) collective-permute-start(bf16[8,6,16,128]{3,2,1,0:T(8,128)(2,1)} %get-tuple-element.32), channel_id=1, source_target_pairs={{0,8},{8,16},{16,24},{24,0},{1,9},{9,17},{17,25},{25,1},{2,10},{10... | collective-permute-start | bytes 589832 | tf_op jit(solution)/shard_map/ppermute | solution.py:441
  40.9 9.4 %collective-permute-start.3 = (bf16[8,6,16,128]{3,2,1,0:T(8,128)(2,1)}, bf16[8,6,16,128]{3,2,1,0:T(8,128)(2,1)}, u32[]{:S(2)}, u32[]{:S(2)}) collective-permute-start(bf16[8,6,16,128]{3,2,1,0:T(8,128)(2,1)} %get-tuple-element.33), channel_id=1, source_target_pairs={{8,0},{16,8},{24,16},{0,24},{9,1},{17,9},{25,17},{1,25},{10,2},{18... | collective-permute-start | bytes 589832 | tf_op jit(solution)/shard_map/ppermute | solution.py:442
  48.8 1.4 %copy-start.5 = (bf16[9,512,256]{2,1,0:T(8,128)(2,1)}, bf16[9,512,256]{2,1,0:T(8,128)(2,1)S(1)}, u32[]{:S(2)}) copy-start(bf16[9,512,256]{2,1,0:T(8,128)(2,1)S(1)} %get-tuple-element.35.fore_ref) | copy-start | bytes 7077892
  63.7 13.4 %copy-start.4 = (bf16[9,256,512]{2,1,0:T(8,128)(2,1)S(1)}, bf16[9,256,512]{2,1,0:T(8,128)(2,1)}, u32[]{:S(2)}) copy-start(bf16[9,256,512]{2,1,0:T(8,128)(2,1)} %get-tuple-element.48.back_ref) | copy-start | bytes 7077892
  63.7 8.6 %collective-permute-start.4 = (bf16[2,9,192,128]{3,2,1,0:T(8,128)(2,1)S(1)}, bf16[2,9,192,128]{3,2,1,0:T(8,128)(2,1)S(1)}, u32[]{:S(2)}, u32[]{:S(2)}) collective-permute-start(bf16[2,9,192,128]{3,2,1,0:T(8,128)(2,1)S(1)} %get-tuple-element.41), channel_id=1, source_target_pairs={{0,8},{8,0},{16,24},{24,16},{1,9},{9,1},{17,25},{25,17},{2,10},{10... | collective-permute-start | bytes 2654216 | tf_op jit(solution)/shard_map/ppermute | solution.py:469
  64.7 4.0 %collective-permute-start.5 = (bf16[8,16,128]{2,1,0:T(8,128)(2,1)S(1)}, bf16[8,16,128]{2,1,0:T(8,128)(2,1)S(1)}, u32[]{:S(2)}, u32[]{:S(2)}) collective-permute-start(bf16[8,16,128]{2,1,0:T(8,128)(2,1)S(1)} %get-tuple-element.44), channel_id=1, source_target_pairs={{0,1},{1,2},{2,3},{3,4},{4,5},{5,6},{6,7},{7,0},{8,9},{9,10},{10,1... | collective-permute-start | bytes 98312 | tf_op jit(solution)/shard_map/ppermute | solution.py:441
  64.7 4.0 %collective-permute-start.6 = (bf16[8,16,128]{2,1,0:T(8,128)(2,1)S(1)}, bf16[8,16,128]{2,1,0:T(8,128)(2,1)S(1)}, u32[]{:S(2)}, u32[]{:S(2)}) collective-permute-start(bf16[8,16,128]{2,1,0:T(8,128)(2,1)S(1)} %get-tuple-element.45), channel_id=1, source_target_pairs={{1,0},{2,1},{3,2},{4,3},{5,4},{6,5},{7,6},{0,7},{9,8},{10,9},{11,1... | collective-permute-start | bytes 98312 | tf_op jit(solution)/shard_map/ppermute | solution.py:442
  68.7 4.6 %collective-permute-start.7 = (bf16[6,16,128]{2,1,0:T(8,128)(2,1)S(1)}, bf16[6,16,128]{2,1,0:T(8,128)(2,1)S(1)}, u32[]{:S(2)}, u32[]{:S(2)}) collective-permute-start(bf16[6,16,128]{2,1,0:T(8,128)(2,1)S(1)} %get-tuple-element.46), channel_id=1, source_target_pairs={{0,8},{8,16},{16,24},{24,0},{1,9},{9,17},{17,25},{25,1},{2,10},{10... | collective-permute-start | bytes 73736 | tf_op jit(solution)/shard_map/ppermute | solution.py:441
  72.3 4.8 %collective-permute-start.8 = (bf16[6,16,128]{2,1,0:T(8,128)(2,1)S(1)}, bf16[6,16,128]{2,1,0:T(8,128)(2,1)S(1)}, u32[]{:S(2)}, u32[]{:S(2)}) collective-permute-start(bf16[6,16,128]{2,1,0:T(8,128)(2,1)S(1)} %get-tuple-element.47), channel_id=1, source_target_pairs={{8,0},{16,8},{24,16},{0,24},{9,1},{17,9},{25,17},{1,25},{10,2},{18... | collective-permute-start | bytes 73736 | tf_op jit(solution)/shard_map/ppermute | solution.py:442
  82.8 28.9 %all-to-all-start.2 = ((bf16[8,8,4,16,128]{4,3,2,1,0:T(8,128)(2,1)}), bf16[8,8,4,16,128]{4,3,2,1,0:T(8,128)(2,1)S(1)}, u32[]{:S(2)}, u32[]{:S(2)}) async-start(bf16[8,8,4,16,128]{4,3,2,1,0:T(8,128)(2,1)} %shard_map.66), calls=%async_computation.2 | async-start | bytes 2097152 | tf_op jit(solution)/shard_map/all_to_all | solution.py:447
  87.5 23.1 %collective-permute-start.9 = (bf16[9,192,128]{2,1,0:T(8,128)(2,1)S(1)}, bf16[9,192,128]{2,1,0:T(8,128)(2,1)S(1)}, u32[]{:S(2)}, u32[]{:S(2)}) collective-permute-start(bf16[9,192,128]{2,1,0:T(8,128)(2,1)S(1)} %get-tuple-element.50), channel_id=1, source_target_pairs={{0,16},{8,24},{16,0},{24,8},{1,17},{9,25},{17,1},{25,9},{2,18},{10... | collective-permute-start | bytes 1327112 | tf_op jit(solution)/shard_map/ppermute | solution.py:473
  111.7 20.7 %all-to-all-start.3 = ((bf16[8,16,1728]{2,1,0:T(8,128)(2,1)}), bf16[8,16,1728]{2,1,0:T(8,128)(2,1)S(1)}, u32[]{:S(2)}, u32[]{:S(2)}) async-start(bf16[8,16,1728]{2,1,0:T(8,128)(2,1)} %shard_map.68), calls=%async_computation.3 | async-start | bytes 917504 | tf_op jit(solution)/shard_map/all_to_all | solution.py:447

commit v2 on v1

--- a/solution.py
+++ b/solution.py
@@ -67,33 +67,37 @@
 
 
 def prepare_gather(field):
-    def kernel(field_ref, edge_ref, middle_ref, wide):
+    def kernel(field_ref, out_ref, wide):
         for x in range(8):
             rows = field_ref[x].astype(F32)
             for t in range(16):
                 wide[pl.ds(x * 16 + t, 4, stride=128), :] = rows[:, t * 128 : (t + 1) * 128]
-        for y, (ref, at) in enumerate(((edge_ref, 0), (middle_ref, 0), (middle_ref, 1), (edge_ref, 1))):
+        for y in range(4):
             row = wide[y * 128 : y * 128 + 128, :].reshape(8, 16, 128).astype(BF)
             for f in range(8):
-                ref[f, at] = row
-
-    out = shape((8, 2, 8, 16, 128))
-    return call(kernel, (out, out), [(field, None)], [pltpu.VMEM((512, 128), F32)], 0, 1_300_000)
-
-
-def gather_edges(edge, middle, y_before, y_after):
-    def kernel(edge_ref, middle_ref, yb, ya, last_ref, first_ref):
+                out_ref[f, y] = row
+
+    return call(
+        kernel,
+        shape((8, 4, 8, 16, 128)),
+        [(field, None)],
+        [pltpu.VMEM((512, 128), F32)],
+        0,
+        1_300_000,
+    )
+
+
+def gather_edges(cells, y_before, y_after):
+    def kernel(cells_ref, yb, ya, last_ref, first_ref):
         for out_ref, x in ((last_ref, 7), (first_ref, 0)):
             for f in range(8):
                 out_ref[f, 0] = yb[f, x]
-                out_ref[f, 1] = edge_ref[f, 0, x]
-                out_ref[f, 2] = middle_ref[f, 0, x]
-                out_ref[f, 3] = middle_ref[f, 1, x]
-                out_ref[f, 4] = edge_ref[f, 1, x]
                 out_ref[f, 5] = ya[f, x]
+                for y in range(4):
+                    out_ref[f, y + 1] = cells_ref[f, y, x]
 
     out = shape((8, 6, 16, 128))
-    ins = [(a, None) for a in (edge, middle, y_before, y_after)]
+    ins = [(a, None) for a in (cells, y_before, y_after)]
     return call(kernel, (out, out), ins, (), 0, 400_000)
 
 
@@ -151,9 +155,9 @@
     return jnp.where(inside, v, jnp.zeros_like(v))
 
 
-def forward(coords, edge, middle, y_before, y_after, x_before, x_after, fore, grad):
+def forward(coords, cells, y_before, y_after, x_before, x_after, fore, grad):
     def kernel(
-        co, edge_ref, middle_ref, yb, ya, xb, xa, fore_ref, grad_ref,
+        co, cells_ref, yb, ya, xb, xa, fore_ref, grad_ref,
         field_ref, out_ref, pre_ref, first_ref, last_ref, total, wide,
     ):
         y_low, y_high, x_low, x_high = co[4] > 0, co[4] < 7, co[5] > 0, co[5] < 3
@@ -173,10 +177,8 @@
         def place_x(x, carry):
             place(x + 1, 0, lambda f: masked(yb[f, x], y_low))
             place(x + 1, 5, lambda f: masked(ya[f, x], y_high))
-            place(x + 1, 1, lambda f: edge_ref[f, 0, x])
-            place(x + 1, 2, lambda f: middle_ref[f, 0, x])
-            place(x + 1, 3, lambda f: middle_ref[f, 1, x])
-            place(x + 1, 4, lambda f: edge_ref[f, 1, x])
+            for y in range(4):
+                place(x + 1, y + 1, lambda f: cells_ref[f, y, x])
             return carry
 
         lax.fori_loop(0, 8, place_x, 0)
@@ -232,7 +234,7 @@
         [(coords, pltpu.SMEM)]
         + [
             (a, None)
-            for a in (edge, middle, y_before, y_after, x_before, x_after, fore, grad)
+            for a in (cells, y_before, y_after, x_before, x_after, fore, grad)
         ],
         [pltpu.VMEM((1024, 256), F32), pltpu.VMEM((512, 128), F32)],
         5_000_000_000,
@@ -450,29 +452,29 @@
 def per_device(activations, weights, out_grad):
     filt, sx, sy = (lax.axis_index(a) for a in ("filt", "sx", "sy"))
     coords = jnp.stack([filt // 4, filt % 4, sx % 2, sx // 2, sy, sx, 0, 0]).astype(jnp.int32)
-    edge, middle = prepare_gather(activations[0, 0])
-    edge = exchange(edge, "filt")
-    middle, edge = lax.optimization_barrier((middle, edge))
-    y_before, y_after = both_ways(edge[:, 1], edge[:, 0], "sy", 8)
-    middle = exchange(middle, "filt")
-    middle, weights, out_grad = lax.optimization_barrier((middle, weights, out_grad))
-    x_last, x_first = gather_edges(edge, middle, y_before, y_after)
-    x_before, x_after = both_ways(x_last, x_first, "sx", 4)
+    cells = prepare_gather(activations[0, 0])
+    cells, weights, out_grad = lax.optimization_barrier((cells, weights, out_grad))
+    cells = exchange(cells, "filt")
     fore, back = prepare_weights(weights[0])
     grad = prepare_field(out_grad[0, 0])
+    cells, fore, back, grad = lax.optimization_barrier((cells, fore, back, grad))
+    y_before, y_after = both_ways(cells[:, 3], cells[:, 0], "sy", 8)
+    x_last, x_first = gather_edges(cells, y_before, y_after)
+    x_before, x_after = both_ways(x_last, x_first, "sx", 4)
     field, outputs, pre_grad, g_first, g_last = forward(
-        coords, edge, middle, y_before, y_after, x_before, x_after, fore, grad
+        coords, cells, y_before, y_after, x_before, x_after, fore, grad
     )
 
     gy_before, gy_after = both_ways(g_last, g_first, "sy", 8)
     keep, send = filter_grad(coords, field, pre_grad)
     got = lax.ppermute(send, "sx", [(i, i ^ 1) for i in range(4)])
+    got, gy_before, gy_after = lax.optimization_barrier((got, gy_before, gy_after))
+    stay, send = add_cores(coords, keep, got)
     gx_before, gx_after = both_ways(*grad_edges(pre_grad, gy_before, gy_after), "sx", 4)
-    stay, send = add_cores(coords, keep, got)
-    send, pre_grad = lax.optimization_barrier((send, pre_grad))
     got = lax.ppermute(send, "sx", [(i, i ^ 2) for i in range(4)])
 
     parts = input_grad_parts(coords, pre_grad, gy_before, gy_after, gx_before, gx_after, back)
+    parts, got = lax.optimization_barrier((parts, got))
     parts = exchange(parts, "filt")
     regions = exchange(add_far(stay, got), "sy")
     input_grad = add_blocks(parts)

time: 134 us -> 116 us (0.87)
  the two profiles are of different devices: /device:TPU:1 before, /device:TPU:2 now
where the time goes in v2:
time: 116 us
  waiting for transfers between devices  33.2 us (29%)
  starting transfers between devices  30.4 us (26%)
  Pallas kernels  30 us (26%)
  blocking collectives  18.3 us (16%)
  local copies, waits for them, and re-layouts  3.39 us (3%)
    pallas_call x12, Pallas kernels, call(): pl.pallas_call(kernel, out_shape=outs, in_specs=[pl.BlockSpec(memory_spac...  30 us
    all_to_all x1, blocking collectives, exchange(): return lax.all_to_all(parts, axis, 0, 0)  18.3 us
    ppermute x4, starting transfers between devices, both_ways(): lax.ppermute(first, axis, [((i + 1) % size, i) for i in range(size)])  15.6 us
    all_to_all x2, waiting for transfers between devices, exchange(): return lax.all_to_all(parts, axis, 0, 0)  14.3 us
    all_to_all x2, starting transfers between devices, exchange(): return lax.all_to_all(parts, axis, 0, 0)  10.6 us
    ppermute x4, waiting for transfers between devices, both_ways(): lax.ppermute(last, axis, [(i, (i + 1) % size) for i in range(size)])  8.56 us
    ppermute x4, waiting for transfers between devices, both_ways(): lax.ppermute(first, axis, [((i + 1) % size, i) for i in range(size)])  5.64 us
    ppermute x1, waiting for transfers between devices, per_device(): got = lax.ppermute(send, 'sx', [(i, i ^ 2) for i in range(4)])  4.68 us
  transfers between devices with their start and end apart: 12, of which 8 were waited for; matrix products, arithmetic and copies ran while one was open for 1% of the time, Pallas kernels for 13%

profile of v2, /device:TPU:2, one launch (start us, length us, event | category | flops | bytes accessed | tf_op | source)
XLA Modules:
  0.0 115.9 jit_solution(10657739806682888758)
XLA Ops:
  0.6 0.0 copy-start
  0.6 0.0 copy-start.1
  0.7 1.0 copy-done.1
  1.7 0.0 copy-start.2
  1.7 1.2 %shard_map.58 = bf16[8,4,8,16,128]{4,3,2,1,0:T(8,128)(2,1)} custom-call(bf16[8,4,2048]{2,1,0:T(4,128)(2,1)S(1)} %bitcast.18), custom_call_target="tpu_custom_call" | custom-call | bytes 1300000 | tf_op jit(solution)/shard_map/pallas_call | solution.py:18
  2.9 5.9 %all-to-all-start = ((bf16[8,4,8,16,128]{4,3,2,1,0:T(8,128)(2,1)}), bf16[8,4,8,16,128]{4,3,2,1,0:T(8,128)(2,1)S(1)}, u32[]{:S(2)}, u32[]{:S(2)}) async-start(bf16[8,4,8,16,128]{4,3,2,1,0:T(8,128)(2,1)} %shard_map.58), calls=%async_computation | async-start | bytes 2097152 | tf_op jit(solution)/shard_map/all_to_all | solution.py:449
  8.8 0.0 copy-done.2
  8.8 0.1 shard_map.60.grad_ref
  8.9 0.0 copy-done
  8.9 7.8 %shard_map.59 = (bf16[9,512,256]{2,1,0:T(8,128)(2,1)S(1)}, bf16[9,256,512]{2,1,0:T(8,128)(2,1)}) custom-call(bf16[27,32768]{1,0:T(8,128)(2,1)S(1)} %bitcast.16), custom_call_target="tpu_custom_call" | custom-call | bytes 8000000 | tf_op jit(solution)/shard_map/pallas_call | solution.py:18
  16.7 0.0 copy-start.4
  16.7 1.4 %copy-done.4 = bf16[9,512,256]{2,1,0:T(8,128)(2,1)} copy-done((bf16[9,512,256]{2,1,0:T(8,128)(2,1)}, bf16[9,512,256]{2,1,0:T(8,128)(2,1)S(1)}, u32[]{:S(2)}) %copy-start.4) | copy-done | bytes 2359320
  18.2 4.9 %all-to-all-done.cells_ref = bf16[8,4,8,16,128]{4,3,2,1,0:T(8,128)(2,1)S(1)} async-done(((bf16[8,4,8,16,128]{4,3,2,1,0:T(8,128)(2,1)}), bf16[8,4,8,16,128]{4,3,2,1,0:T(8,128)(2,1)S(1)}, u32[]{:S(2)}, u32[]{:S(2)}) %all-to-all-start) | async-done | bytes 1048608 | tf_op jit(solution)/shard_map/all_to_all | solution.py:449
  23.1 5.9 %collective-permute-start.1 = (bf16[8,8,16,128]{3,2,1,0:T(8,128)(2,1)S(1)}, bf16[8,8,16,128]{3,2,1,0:T(8,128)(2,1)S(1)}, u32[]{:S(2)}, u32[]{:S(2)}) collective-permute-start(bf16[8,8,16,128]{3,2,1,0:T(8,128)(2,1)S(1)} %get-tuple-element.63), channel_id=1, source_target_pairs={{1,0},{2,1},{3,2},{4,3},{5,4},{6,5},{7,6},{0,7},{9,8},{10,9},{11,1... | collective-permute-start | bytes 786440 | tf_op jit(solution)/shard_map/ppermute | solution.py:444
  29.1 0.0 collective-permute-start
  29.1 5.4 %collective-permute-done.1.ya = bf16[8,8,16,128]{3,2,1,0:T(8,128)(2,1)S(1)} collective-permute-done((bf16[8,8,16,128]{3,2,1,0:T(8,128)(2,1)S(1)}, bf16[8,8,16,128]{3,2,1,0:T(8,128)(2,1)S(1)}, u32[]{:S(2)}, u32[]{:S(2)}) %collective-permute-start.1) | collective-permute-done | bytes 262176 | tf_op jit(solution)/shard_map/ppermute | solution.py:444
  34.5 3.4 %collective-permute-done.yb = bf16[8,8,16,128]{3,2,1,0:T(8,128)(2,1)S(1)} collective-permute-done((bf16[8,8,16,128]{3,2,1,0:T(8,128)(2,1)S(1)}, bf16[8,8,16,128]{3,2,1,0:T(8,128)(2,1)S(1)}, u32[]{:S(2)}, u32[]{:S(2)}) %collective-permute-start) | collective-permute-done | bytes 262176 | tf_op jit(solution)/shard_map/ppermute | solution.py:443
  37.9 0.1 collective-permute-start.2
  38.0 3.2 %collective-permute-start.3 = (bf16[8,6,16,128]{3,2,1,0:T(8,128)(2,1)S(1)}, bf16[8,6,16,128]{3,2,1,0:T(8,128)(2,1)S(1)}, u32[]{:S(2)}, u32[]{:S(2)}) collective-permute-start(bf16[8,6,16,128]{3,2,1,0:T(8,128)(2,1)S(1)} %get-tuple-element.37), channel_id=1, source_target_pairs={{8,0},{16,8},{24,16},{0,24},{9,1},{17,9},{25,17},{1,25},{10,2},{18... | collective-permute-start | bytes 589832 | tf_op jit(solution)/shard_map/ppermute | solution.py:444
  41.2 0.1 stack.27.co
  41.3 3.3 %collective-permute-done.2.xb = bf16[8,6,16,128]{3,2,1,0:T(8,128)(2,1)S(1)} collective-permute-done((bf16[8,6,16,128]{3,2,1,0:T(8,128)(2,1)S(1)}, bf16[8,6,16,128]{3,2,1,0:T(8,128)(2,1)S(1)}, u32[]{:S(2)}, u32[]{:S(2)}) %collective-permute-start.2) | collective-permute-done | bytes 196640 | tf_op jit(solution)/shard_map/ppermute | solution.py:443
  44.6 0.2 collective-permute-done.3.xa
  44.8 7.6 %shard_map.62 = (bf16[10,192,512]{2,1,0:T(8,128)(2,1)S(1)}, bf16[8,4,2048]{2,1,0:T(4,128)(2,1)}, bf16[8,4,16,128]{3,2,1,0:T(8,128)(2,1)S(1)}, bf16[8,16,128]{2,1,0:T(8,128)(2,1)S(1)}, bf16[8,16,128]{2,1,0:T(8,128)(2,1)S(1)}) custom-call(s32[8]{0:T(128)S(1)} %stack.27.co, bf16[8,4,8,16,128]{4,3,2,1,0:T(8,128)(2,1)S(1)} %all-to-all-done.cells_ref, ...), custom_call_target="tpu_custom_call" | custom-call | flops 5000000000 | bytes 6000000 | tf_op jit(solution)/shard_map/pallas_call | solution.py:18
  52.5 5.4 %shard_map.63 = (f32[2,9,192,128]{3,2,1,0:T(8,128)S(1)}, bf16[2,9,192,128]{3,2,1,0:T(8,128)(2,1)S(1)}) custom-call(s32[8]{0:T(128)S(1)} %stack.27.co, bf16[10,192,512]{2,1,0:T(8,128)(2,1)S(1)} %get-tuple-element.42.field_ref, bf16[8,4,16,128]{3,2,1,0:T(8,128)(2,1)S(1)} %get-tuple-element.41.pre_ref), custom_call_target="tpu_custom_call" | custom-call | flops 5000000000 | bytes 6000000 | tf_op jit(solution)/shard_map/pallas_call | solution.py:18
  57.9 0.0 copy-start.3
  57.9 2.1 %collective-permute-start.4 = (bf16[2,9,192,128]{3,2,1,0:T(8,128)(2,1)S(1)}, bf16[2,9,192,128]{3,2,1,0:T(8,128)(2,1)S(1)}, u32[]{:S(2)}, u32[]{:S(2)}) collective-permute-start(bf16[2,9,192,128]{3,2,1,0:T(8,128)(2,1)S(1)} %get-tuple-element.43), channel_id=1, source_target_pairs={{0,8},{8,0},{16,24},{24,16},{1,9},{9,1},{17,25},{25,17},{2,10},{10... | collective-permute-start | bytes 2654216 | tf_op jit(solution)/shard_map/ppermute | solution.py:470
  60.0 0.0 collective-permute-start.5
  60.0 3.2 %collective-permute-start.6 = (bf16[8,16,128]{2,1,0:T(8,128)(2,1)S(1)}, bf16[8,16,128]{2,1,0:T(8,128)(2,1)S(1)}, u32[]{:S(2)}, u32[]{:S(2)}) collective-permute-start(bf16[8,16,128]{2,1,0:T(8,128)(2,1)S(1)} %get-tuple-element.45), channel_id=1, source_target_pairs={{1,0},{2,1},{3,2},{4,3},{5,4},{6,5},{7,6},{0,7},{9,8},{10,9},{11,1... | collective-permute-start | bytes 98312 | tf_op jit(solution)/shard_map/ppermute | solution.py:444
  63.2 1.9 %collective-permute-done.5.yb = bf16[8,16,128]{2,1,0:T(8,128)(2,1)S(1)} collective-permute-done((bf16[8,16,128]{2,1,0:T(8,128)(2,1)S(1)}, bf16[8,16,128]{2,1,0:T(8,128)(2,1)S(1)}, u32[]{:S(2)}, u32[]{:S(2)}) %collective-permute-start.5) | collective-permute-done | bytes 32800 | tf_op jit(solution)/shard_map/ppermute | solution.py:443
  65.1 0.0 collective-permute-done.6.ya
  65.1 0.0 collective-permute-done.4.got_ref
  65.1 0.1 collective-permute-start.7
  65.2 3.2 %collective-permute-start.8 = (bf16[6,16,128]{2,1,0:T(8,128)(2,1)S(1)}, bf16[6,16,128]{2,1,0:T(8,128)(2,1)S(1)}, u32[]{:S(2)}, u32[]{:S(2)}) collective-permute-start(bf16[6,16,128]{2,1,0:T(8,128)(2,1)S(1)} %get-tuple-element.49), channel_id=1, source_target_pairs={{8,0},{16,8},{24,16},{0,24},{9,1},{17,9},{25,17},{1,25},{10,2},{18... | collective-permute-start | bytes 73736 | tf_op jit(solution)/shard_map/ppermute | solution.py:444
  68.4 0.7 shard_map.66
  69.2 1.9 %collective-permute-start.9 = (bf16[9,192,128]{2,1,0:T(8,128)(2,1)S(1)}, bf16[9,192,128]{2,1,0:T(8,128)(2,1)S(1)}, u32[]{:S(2)}, u32[]{:S(2)}) collective-permute-start(bf16[9,192,128]{2,1,0:T(8,128)(2,1)S(1)} %get-tuple-element.53), channel_id=1, source_target_pairs={{0,16},{8,24},{16,0},{24,8},{1,17},{9,25},{17,1},{25,9},{2,18},{10... | collective-permute-start | bytes 1327112 | tf_op jit(solution)/shard_map/ppermute | solution.py:474
  71.1 0.0 collective-permute-done.7.xb
  71.1 0.0 collective-permute-done.8.xa
  71.1 0.0 copy-done.3
  71.1 5.8 %shard_map.65 = bf16[8,8,4,16,128]{4,3,2,1,0:T(8,128)(2,1)} custom-call(s32[8]{0:T(128)S(1)} %stack.27.co, bf16[8,4,16,128]{3,2,1,0:T(8,128)(2,1)S(1)} %get-tuple-element.41.pre_ref, bf16[8,16,128]{2,1,0:T(8,128)(2,1)S(1)} %collective-permute-done.5.yb, bf16[8,16,128]{2,1,0:T(8,128)(2,1)S(1)} %collective-permute-done.6.ya, ...), custom_call_target="tpu_custom_call" | custom-call | flops 5000000000 | bytes 5000000 | tf_op jit(solution)/shard_map/pallas_call | solution.py:18
  76.8 4.7 %collective-permute-done.9.got_ref = bf16[9,192,128]{2,1,0:T(8,128)(2,1)S(1)} collective-permute-done((bf16[9,192,128]{2,1,0:T(8,128)(2,1)S(1)}, bf16[9,192,128]{2,1,0:T(8,128)(2,1)S(1)}, u32[]{:S(2)}, u32[]{:S(2)}) %collective-permute-start.9) | collective-permute-done | bytes 442400 | tf_op jit(solution)/shard_map/ppermute | solution.py:474
  81.5 0.3 shard_map.68
  81.8 18.3 %all_to_all.15.parts_ref = bf16[8,16,1728]{2,1,0:T(8,128)(2,1)S(1)} all-to-all(bf16[8,16,1728]{2,1,0:T(8,128)(2,1)S(1)} %shard_map.68), channel_id=1, replica_groups=mesh['filt'=8,'sx'=4,'sy'=8] {'sy'}, dimensions={0} | all-to-all | bytes 884736 | tf_op jit(solution)/shard_map/all_to_all | solution.py:449
  100.1 4.7 %all-to-all-start.1 = ((bf16[8,8,4,16,128]{4,3,2,1,0:T(8,128)(2,1)}), bf16[8,8,4,16,128]{4,3,2,1,0:T(8,128)(2,1)S(1)}, u32[]{:S(2)}, u32[]{:S(2)}) async-start(bf16[8,8,4,16,128]{4,3,2,1,0:T(8,128)(2,1)} %shard_map.65), calls=%async_computation.1 | async-start | bytes 2097152 | tf_op jit(solution)/shard_map/all_to_all | solution.py:449
  104.7 0.2 shard_map.69
  104.9 0.8 copy.12
  105.7 9.3 %all-to-all-done.1.parts_ref = bf16[8,8,4,16,128]{4,3,2,1,0:T(8,128)(2,1)S(1)} async-done(((bf16[8,8,4,16,128]{4,3,2,1,0:T(8,128)(2,1)}), bf16[8,8,4,16,128]{4,3,2,1,0:T(8,128)(2,1)S(1)}, u32[]{:S(2)}, u32[]{:S(2)}) %all-to-all-start.1) | async-done | bytes 1048608 | tf_op jit(solution)/shard_map/all_to_all | solution.py:449
  115.0 0.9 shard_map.67
  (4 shorter events, 0.1 us)
Async XLA Ops:
  0.6 8.3 %copy-start = (bf16[1,27,32768]{2,1,0:T(8,128)(2,1)S(1)}, bf16[1,27,32768]{2,1,0:T(8,128)(2,1)}, u32[]{:S(2)}) copy-start(bf16[1,27,32768]{2,1,0:T(8,128)(2,1)} %param.4) | copy-start | bytes 5308420
  0.6 1.1 copy-start.1
  1.7 7.2 %copy-start.2 = (bf16[1,1,8,4,2048]{4,3,2,1,0:T(4,128)(2,1)S(1)}, bf16[1,1,8,4,2048]{4,3,2,1,0:T(4,128)(2,1)}, u32[]{:S(2)}) copy-start(bf16[1,1,8,4,2048]{4,3,2,1,0:T(4,128)(2,1)} %param.5) | copy-start | bytes 393220
  2.9 20.2 %all-to-all-start = ((bf16[8,4,8,16,128]{4,3,2,1,0:T(8,128)(2,1)}), bf16[8,4,8,16,128]{4,3,2,1,0:T(8,128)(2,1)S(1)}, u32[]{:S(2)}, u32[]{:S(2)}) async-start(bf16[8,4,8,16,128]{4,3,2,1,0:T(8,128)(2,1)} %shard_map.58), calls=%async_computation | async-start | bytes 2097152 | tf_op jit(solution)/shard_map/all_to_all | solution.py:449
  16.7 1.4 %copy-start.4 = (bf16[9,512,256]{2,1,0:T(8,128)(2,1)}, bf16[9,512,256]{2,1,0:T(8,128)(2,1)S(1)}, u32[]{:S(2)}) copy-start(bf16[9,512,256]{2,1,0:T(8,128)(2,1)S(1)} %get-tuple-element.38.fore_ref) | copy-start | bytes 7077892
  23.1 11.3 %collective-permute-start.1 = (bf16[8,8,16,128]{3,2,1,0:T(8,128)(2,1)S(1)}, bf16[8,8,16,128]{3,2,1,0:T(8,128)(2,1)S(1)}, u32[]{:S(2)}, u32[]{:S(2)}) collective-permute-start(bf16[8,8,16,128]{3,2,1,0:T(8,128)(2,1)S(1)} %get-tuple-element.63), channel_id=1, source_target_pairs={{1,0},{2,1},{3,2},{4,3},{5,4},{6,5},{7,6},{0,7},{9,8},{10,9},{11,1... | collective-permute-start | bytes 786440 | tf_op jit(solution)/shard_map/ppermute | solution.py:444
  29.1 8.8 %collective-permute-start = (bf16[8,8,16,128]{3,2,1,0:T(8,128)(2,1)S(1)}, bf16[8,8,16,128]{3,2,1,0:T(8,128)(2,1)S(1)}, u32[]{:S(2)}, u32[]{:S(2)}) collective-permute-start(bf16[8,8,16,128]{3,2,1,0:T(8,128)(2,1)S(1)} %get-tuple-element.64), channel_id=1, source_target_pairs={{0,1},{1,2},{2,3},{3,4},{4,5},{5,6},{6,7},{7,0},{8,9},{9,10},{10,1... | collective-permute-start | bytes 786440 | tf_op jit(solution)/shard_map/ppermute | solution.py:443
  37.9 6.7 %collective-permute-start.2 = (bf16[8,6,16,128]{3,2,1,0:T(8,128)(2,1)S(1)}, bf16[8,6,16,128]{3,2,1,0:T(8,128)(2,1)S(1)}, u32[]{:S(2)}, u32[]{:S(2)}) collective-permute-start(bf16[8,6,16,128]{3,2,1,0:T(8,128)(2,1)S(1)} %get-tuple-element.36), channel_id=1, source_target_pairs={{0,8},{8,16},{16,24},{24,0},{1,9},{9,17},{17,25},{25,1},{2,10},{10... | collective-permute-start | bytes 589832 | tf_op jit(solution)/shard_map/ppermute | solution.py:443
  38.0 6.8 %collective-permute-start.3 = (bf16[8,6,16,128]{3,2,1,0:T(8,128)(2,1)S(1)}, bf16[8,6,16,128]{3,2,1,0:T(8,128)(2,1)S(1)}, u32[]{:S(2)}, u32[]{:S(2)}) collective-permute-start(bf16[8,6,16,128]{3,2,1,0:T(8,128)(2,1)S(1)} %get-tuple-element.37), channel_id=1, source_target_pairs={{8,0},{16,8},{24,16},{0,24},{9,1},{17,9},{25,17},{1,25},{10,2},{18... | collective-permute-start | bytes 589832 | tf_op jit(solution)/shard_map/ppermute | solution.py:444
  57.9 13.2 %copy-start.3 = (bf16[9,256,512]{2,1,0:T(8,128)(2,1)S(1)}, bf16[9,256,512]{2,1,0:T(8,128)(2,1)}, u32[]{:S(2)}) copy-start(bf16[9,256,512]{2,1,0:T(8,128)(2,1)} %get-tuple-element.50.back_ref) | copy-start | bytes 7077892
  57.9 7.2 %collective-permute-start.4 = (bf16[2,9,192,128]{3,2,1,0:T(8,128)(2,1)S(1)}, bf16[2,9,192,128]{3,2,1,0:T(8,128)(2,1)S(1)}, u32[]{:S(2)}, u32[]{:S(2)}) collective-permute-start(bf16[2,9,192,128]{3,2,1,0:T(8,128)(2,1)S(1)} %get-tuple-element.43), channel_id=1, source_target_pairs={{0,8},{8,0},{16,24},{24,16},{1,9},{9,1},{17,25},{25,17},{2,10},{10... | collective-permute-start | bytes 2654216 | tf_op jit(solution)/shard_map/ppermute | solution.py:470
  60.0 5.1 %collective-permute-start.5 = (bf16[8,16,128]{2,1,0:T(8,128)(2,1)S(1)}, bf16[8,16,128]{2,1,0:T(8,128)(2,1)S(1)}, u32[]{:S(2)}, u32[]{:S(2)}) collective-permute-start(bf16[8,16,128]{2,1,0:T(8,128)(2,1)S(1)} %get-tuple-element.44), channel_id=1, source_target_pairs={{0,1},{1,2},{2,3},{3,4},{4,5},{5,6},{6,7},{7,0},{8,9},{9,10},{10,1... | collective-permute-start | bytes 98312 | tf_op jit(solution)/shard_map/ppermute | solution.py:443
  60.0 5.1 %collective-permute-start.6 = (bf16[8,16,128]{2,1,0:T(8,128)(2,1)S(1)}, bf16[8,16,128]{2,1,0:T(8,128)(2,1)S(1)}, u32[]{:S(2)}, u32[]{:S(2)}) collective-permute-start(bf16[8,16,128]{2,1,0:T(8,128)(2,1)S(1)} %get-tuple-element.45), channel_id=1, source_target_pairs={{1,0},{2,1},{3,2},{4,3},{5,4},{6,5},{7,6},{0,7},{9,8},{10,9},{11,1... | collective-permute-start | bytes 98312 | tf_op jit(solution)/shard_map/ppermute | solution.py:444
  65.1 6.0 %collective-permute-start.7 = (bf16[6,16,128]{2,1,0:T(8,128)(2,1)S(1)}, bf16[6,16,128]{2,1,0:T(8,128)(2,1)S(1)}, u32[]{:S(2)}, u32[]{:S(2)}) collective-permute-start(bf16[6,16,128]{2,1,0:T(8,128)(2,1)S(1)} %get-tuple-element.48), channel_id=1, source_target_pairs={{0,8},{8,16},{16,24},{24,0},{1,9},{9,17},{17,25},{25,1},{2,10},{10... | collective-permute-start | bytes 73736 | tf_op jit(solution)/shard_map/ppermute | solution.py:443
  65.2 5.9 %collective-permute-start.8 = (bf16[6,16,128]{2,1,0:T(8,128)(2,1)S(1)}, bf16[6,16,128]{2,1,0:T(8,128)(2,1)S(1)}, u32[]{:S(2)}, u32[]{:S(2)}) collective-permute-start(bf16[6,16,128]{2,1,0:T(8,128)(2,1)S(1)} %get-tuple-element.49), channel_id=1, source_target_pairs={{8,0},{16,8},{24,16},{0,24},{9,1},{17,9},{25,17},{1,25},{10,2},{18... | collective-permute-start | bytes 73736 | tf_op jit(solution)/shard_map/ppermute | solution.py:444
  69.2 12.3 %collective-permute-start.9 = (bf16[9,192,128]{2,1,0:T(8,128)(2,1)S(1)}, bf16[9,192,128]{2,1,0:T(8,128)(2,1)S(1)}, u32[]{:S(2)}, u32[]{:S(2)}) collective-permute-start(bf16[9,192,128]{2,1,0:T(8,128)(2,1)S(1)} %get-tuple-element.53), channel_id=1, source_target_pairs={{0,16},{8,24},{16,0},{24,8},{1,17},{9,25},{17,1},{25,9},{2,18},{10... | collective-permute-start | bytes 1327112 | tf_op jit(solution)/shard_map/ppermute | solution.py:474
  100.1 14.9 %all-to-all-start.1 = ((bf16[8,8,4,16,128]{4,3,2,1,0:T(8,128)(2,1)}), bf16[8,8,4,16,128]{4,3,2,1,0:T(8,128)(2,1)S(1)}, u32[]{:S(2)}, u32[]{:S(2)}) async-start(bf16[8,8,4,16,128]{4,3,2,1,0:T(8,128)(2,1)} %shard_map.65), calls=%async_computation.1 | async-start | bytes 2097152 | tf_op jit(solution)/shard_map/all_to_all | solution.py:449

commit v3 on v2

v3 whole, which is shorter than its diff:
```python
import math

import jax
import jax.numpy as jnp
from jax import lax
from jax.experimental import pallas as pl
from jax.experimental.pallas import tpu as pltpu
from jax.sharding import PartitionSpec as P

BF = jnp.bfloat16
F32 = jnp.float32
LEAK = 0.2
SCALE = 1.0 / math.sqrt(32768.0)
PIECE = (8, 4, 16, 128)


def call(kernel, outs, ins, scratch=(), flops=0, nbytes=0):
    return pl.pallas_call(
        kernel,
        out_shape=outs,
        in_specs=[
            pl.BlockSpec(memory_space=pltpu.VMEM if space is None else space)
            for _, space in ins
        ],
        out_specs=jax.tree.map(lambda _: pl.BlockSpec(memory_space=pltpu.VMEM), outs),
        scratch_shapes=list(scratch),
        compiler_params=pltpu.CompilerParams(vmem_limit_bytes=48 << 20),
        cost_estimate=pl.CostEstimate(flops=flops, bytes_accessed=nbytes, transcendentals=0),
    )(*[array for array, _ in ins])


def shape(dims, dtype=BF):
    return jax.ShapeDtypeStruct(dims, dtype)


def down(v):
    rows = lax.broadcasted_iota(jnp.int32, v.shape, 0)
    return jnp.where(rows == 0, 0.0, pltpu.roll(v, 1, 0))


def up(v):
    rows = lax.broadcasted_iota(jnp.int32, v.shape, 0)
    return jnp.where(rows == v.shape[0] - 1, 0.0, pltpu.roll(v, v.shape[0] - 1, 0))


def to_pairs(field_ref, pair_ref, wide):
    for x in range(8):
        rows = field_ref[x].astype(F32)
        for t in range(16):
            wide[pl.ds(x * 64 + t, 4, stride=16), :] = rows[:, t * 128 : (t + 1) * 128]
    pair_ref[...] = wide[...].reshape(PIECE).astype(BF)


def from_pairs(wide, field_ref, layers):
    for n, x in enumerate(layers):
        parts = [wide[pl.ds(n * 64 + t, 4, stride=16), :] for t in range(16)]
        field_ref[x] = jnp.concatenate(parts, axis=1).astype(BF)


def prepare_field(field):
    def kernel(field_ref, pair_ref, wide):
        to_pairs(field_ref, pair_ref, wide)

    return call(
        kernel, shape(PIECE), [(field, None)], [pltpu.VMEM((512, 128), F32)], 0, 400_000
    )


def prepare_gather(field):
    def kernel(field_ref, out_ref, wide):
        for x in range(8):
            rows = field_ref[x].astype(F32)
            for t in range(16):
                wide[pl.ds(x * 16 + t, 4, stride=128), :] = rows[:, t * 128 : (t + 1) * 128]
        for y in range(4):
            row = wide[y * 128 : y * 128 + 128, :].reshape(8, 16, 128).astype(BF)
            for f in range(8):
                out_ref[f, y] = row

    return call(
        kernel,
        shape((8, 4, 8, 16, 128)),
        [(field, None)],
        [pltpu.VMEM((512, 128), F32)],
        0,
        1_300_000,
    )


def gather_edges(cells, y_before, y_after):
    def kernel(cells_ref, yb, ya, last_ref, first_ref):
        for out_ref, x in ((last_ref, 7), (first_ref, 0)):
            for f in range(8):
                out_ref[f, 0] = yb[f, x]
                out_ref[f, 5] = ya[f, x]
                for y in range(4):
                    out_ref[f, y + 1] = cells_ref[f, y, x]

    out = shape((8, 6, 16, 128))
    ins = [(a, None) for a in (cells, y_before, y_after)]
    return call(kernel, (out, out), ins, (), 0, 400_000)


def grad_edges(pre_grad, y_before, y_after):
    def kernel(pre_ref, yb, ya, last_ref, first_ref):
        for out_ref, x in ((last_ref, 7), (first_ref, 0)):
            out_ref[0] = yb[x]
            out_ref[1:5] = pre_ref[x]
            out_ref[5] = ya[x]

    out = shape((6, 16, 128))
    ins = [(a, None) for a in (pre_grad, y_before, y_after)]
    return call(kernel, (out, out), ins, (), 0, 50_000)


def prepare_weights(weights):
    def kernel(w_ref, fore_ref, back_ref, tall, even, odd):
        def spread(t, carry):
            lanes = pl.ds(pl.multiple_of(t * 128, 128), 128)
            tall[pl.ds(t, 27, stride=256), :] = w_ref[:, lanes].astype(F32)
            return carry

        lax.fori_loop(0, 256, spread, 0, unroll=8)

        def place(ij, carry):
            taps = [tall[pl.ds(pl.multiple_of((ij * 3 + k) * 256, 256), 256), :] for k in range(3)]
            zero = jnp.zeros((256, 64), F32)
            for par in range(2):
                lanes = slice(par * 64, par * 64 + 64)
                even[pl.ds(par, 256, stride=2), :] = jnp.concatenate(
                    [taps[0][:, lanes], taps[1][:, lanes]], axis=1
                )
                odd[pl.ds(par, 256, stride=2), :] = jnp.concatenate([taps[2][:, lanes], zero], axis=1)
            fore_ref[ij, :, 0:128] = even[...].astype(BF)
            fore_ref[ij, :, 128:256] = odd[...].astype(BF)
            for c in range(4):
                rows = slice(c * 128, c * 128 + 128)
                back_ref[ij, 0:128, rows] = even[rows, :].T.astype(BF)
                back_ref[ij, 128:256, rows] = odd[rows, :].T.astype(BF)
            return carry

        lax.fori_loop(0, 9, place, 0)

    return call(
        kernel,
        (shape((9, 512, 256)), shape((9, 256, 512))),
        [(weights, None)],
        [pltpu.VMEM((27 * 256, 128), F32), pltpu.VMEM((512, 128), F32), pltpu.VMEM((512, 128), F32)],
        0,
        8_000_000,
    )


def masked(v, inside):
    return jnp.where(inside, v, jnp.zeros_like(v))


def place_cell(field_ref, x, y, take):
    for q in range(4):
        a, b = take(2 * q), take(2 * q + 1)
        lanes = slice(q * 128, q * 128 + 128)
        field_ref[x, y * 32 : y * 32 + 16, lanes] = jnp.concatenate([a[:, :64], b[:, :64]], axis=1)
        field_ref[x, y * 32 + 16 : y * 32 + 32, lanes] = jnp.concatenate([a[:, 64:], b[:, 64:]], axis=1)


def convolved(rows, fore_ref):
    acc = jnp.zeros((256, 256), F32)
    for i in range(3):
        for j in range(3):
            acc = acc + jnp.dot(
                jnp.concatenate([rows(u, i, j * 32) for u in range(2)], axis=0),
                fore_ref[i * 3 + j],
                preferred_element_type=F32,
            )
    return acc


def finish_cell(total, start, grad):
    even, odd = total[pl.ds(start, 16), :], total[pl.ds(start + 16, 16), :]
    pre = (
        jnp.concatenate([down(odd[:, 0:64]), even[:, 0:64]], axis=1)
        + jnp.concatenate([even[:, 64:128], odd[:, 64:128]], axis=1)
        + jnp.concatenate([odd[:, 128:192], up(even[:, 128:192])], axis=1)
    )
    e = jnp.exp(-jnp.abs(pre))
    soft = jnp.maximum(pre, 0.0) + jnp.log1p(e)
    slope = jnp.where(pre >= 0, 1.0, e) / (1.0 + e)
    value = LEAK * pre + (1.0 - LEAK) * (soft - math.log(2.0))
    return value, (grad.astype(F32) * (LEAK + (1.0 - LEAK) * slope)).astype(BF)


def forward_inner(coords, cells, y_before, y_after, fore, grad):
    def kernel(co, cells_ref, yb, ya, fore_ref, grad_ref, field_ref, out_ref, pre_ref, total, wide):
        y_low, y_high = co[4] > 0, co[4] < 7

        def place(x, carry):
            place_cell(field_ref, x, 0, lambda f: masked(yb[f, x], y_low))
            place_cell(field_ref, x, 5, lambda f: masked(ya[f, x], y_high))
            for y in range(4):
                place_cell(field_ref, x, y + 1, lambda f: cells_ref[f, y, x])
            return carry

        lax.fori_loop(0, 8, place, 0)

        def multiply(h, carry):
            start = pl.multiple_of(h * 256, 256)
            total[pl.ds(start, 256), :] = convolved(
                lambda u, i, at: field_ref[2 * h + u + i, at : at + 128, :], fore_ref
            )
            return carry

        lax.fori_loop(0, 3, multiply, 0)

        def finish(x, carry):
            for y in range(4):
                start = pl.multiple_of(x * 128 + y * 32, 32)
                value, turned = finish_cell(total, start, grad_ref[x + 1, y])
                wide[pl.ds(pl.multiple_of(x * 64 + y * 16, 16), 16), :] = value
                pre_ref[x, y] = turned
            return carry

        lax.fori_loop(0, 6, finish, 0)
        from_pairs(wide, out_ref, range(6))

    return call(
        kernel,
        (shape((8, 192, 512)), shape((6, 4, 2048)), shape((6, 4, 16, 128))),
        [(coords, pltpu.SMEM)] + [(a, None) for a in (cells, y_before, y_after, fore, grad)],
        [pltpu.VMEM((768, 256), F32), pltpu.VMEM((384, 128), F32)],
        4_000_000_000,
        6_000_000,
    )


def forward_outer(coords, field, x_before, x_after, fore, grad, out_inner, pre_inner):
    def kernel(
        co, field_ref, xb, xa, fore_ref, grad_ref, out_in, pre_in,
        rim_ref, out_ref, pre_ref, first_ref, last_ref, total, wide,
    ):
        y_low, y_high, x_low, x_high = co[4] > 0, co[4] < 7, co[5] > 0, co[5] < 3
        for y in range(6):
            beside = {0: y_low, 5: y_high}.get(y, True)
            place_cell(rim_ref, 0, y, lambda f: masked(xb[f, y], jnp.logical_and(x_low, beside)))
            place_cell(rim_ref, 1, y, lambda f: masked(xa[f, y], jnp.logical_and(x_high, beside)))

        def rows(u, i, at):
            if u == 0:
                return (field_ref[i - 1] if i else rim_ref[0])[at : at + 128, :]
            return (field_ref[6 + i] if i < 2 else rim_ref[1])[at : at + 128, :]

        total[...] = convolved(rows, fore_ref)
        for n, x in enumerate((0, 7)):
            for y in range(4):
                value, turned = finish_cell(total, n * 128 + y * 32, grad_ref[x, y])
                wide[n * 64 + y * 16 : n * 64 + y * 16 + 16, :] = value
                pre_ref[x, y] = turned
        from_pairs(wide, out_ref, (0, 7))
        out_ref[1:7] = out_in[...]
        pre_ref[1:7] = pre_in[...]
        for x in range(8):
            first_ref[x] = pre_ref[x, 0]
            last_ref[x] = pre_ref[x, 3]

    return call(
        kernel,
        (
            shape((2, 192, 512)),
            shape((8, 4, 2048)),
            shape(PIECE),
            shape((8, 16, 128)),
            shape((8, 16, 128)),
        ),
        [(coords, pltpu.SMEM)]
        + [(a, None) for a in (field, x_before, x_after, fore, grad, out_inner, pre_inner)],
        [pltpu.VMEM((256, 256), F32), pltpu.VMEM((128, 128), F32)],
        2_000_000_000,
        6_000_000,
    )


def stacked_depth(v):
    even, odd = v[:, :64], v[:, 64:]
    zero = jnp.zeros((16, 64), F32)
    return (
        (jnp.concatenate([odd, even], axis=1), jnp.concatenate([down(odd), zero], axis=1)),
        (jnp.concatenate([up(even), odd], axis=1), jnp.concatenate([even, zero], axis=1)),
    )


def filter_grad(coords, field, rim, pre_grad):
    def kernel(co, field_ref, rim_ref, pre_ref, keep_ref, send_ref, first, second, turned):
        core = co[2]

        def place(x, carry):
            for y in range(4):
                low, high = stacked_depth(pre_ref[x, y].astype(F32))
                first[y * 32 : y * 32 + 16, :] = low[0]
                second[y * 32 : y * 32 + 16, :] = low[1]
                first[y * 32 + 16 : y * 32 + 32, :] = high[0]
                second[y * 32 + 16 : y * 32 + 32, :] = high[1]
            lanes = pl.ds(pl.multiple_of(x * 128, 128), 128)
            turned[0:128, lanes] = first[...].T.astype(BF)
            turned[128:192, lanes] = second[...].T[0:64].astype(BF)
            return carry

        lax.fori_loop(0, 8, place, 0)

        def layer(x, rows, lanes):
            if x in (0, 9):
                return rim_ref[x // 9, rows, lanes]
            return field_ref[x - 1, rows, lanes]

        def multiply(j, carry):
            rows = pl.ds(pl.multiple_of(j * 32, 32), 128)
            for i in range(3):
                for half in range(2):
                    lanes = slice(half * 256, half * 256 + 256)
                    cells = [layer(x + i, rows, lanes) for x in range(8)]
                    got = jnp.dot(
                        turned[...], jnp.concatenate(cells, axis=0), preferred_element_type=F32
                    ) * SCALE
                    left, right = got[:, :128], got[:, 128:]
                    keep_ref[half, i * 3 + j] = jnp.where(core == 0, left, right)
                    send_ref[half, i * 3 + j] = jnp.where(core == 0, right, left).astype(BF)
            return carry

        lax.fori_loop(0, 3, multiply, 0)

    return call(
        kernel,
        (shape((2, 9, 192, 128), F32), shape((2, 9, 192, 128))),
        [(coords, pltpu.SMEM), (field, None), (rim, None), (pre_grad, None)],
        [pltpu.VMEM((128, 128), F32), pltpu.VMEM((128, 128), F32), pltpu.VMEM((192, 1024), BF)],
        5_000_000_000,
        6_000_000,
    )


def add_cores(coords, keep, got):
    def kernel(co, keep_ref, got_ref, stay_ref, send_ref):
        far = co[3]
        stay_ref[...] = keep_ref[far] + got_ref[far].astype(F32)
        send_ref[...] = (keep_ref[1 - far] + got_ref[1 - far].astype(F32)).astype(BF)

    return call(
        kernel,
        (shape((9, 192, 128), F32), shape((9, 192, 128))),
        [(coords, pltpu.SMEM), (keep, None), (got, None)],
        (),
        0,
        4_000_000,
    )


def add_far(coords, stay, got):
    def kernel(co, stay_ref, got_ref, *refs):
        outs, (total, turned) = refs[:8], refs[8:]
        sy = co[4]
        total[...] = (stay_ref[...] + got_ref[...].astype(F32)).reshape(1728, 128)
        for t in range(14):
            width = min(128, 1728 - t * 128)
            block = total[t * 128 : t * 128 + width, :].T.astype(BF).reshape(8, 16, width)
            turned[:, :, t * 128 : t * 128 + width] = block
        for d in range(8):
            outs[d][...] = turned[(sy + d) & 7]

    return call(
        kernel,
        (shape((16, 1728)),) * 8,
        [(coords, pltpu.SMEM), (stay, None), (got, None)],
        [pltpu.VMEM((1728, 128), F32), pltpu.VMEM((8, 16, 1728), BF)],
        0,
        2_000_000,
    )


def add_regions(parts):
    def kernel(*refs):
        ins, (out_ref, total, pairs) = refs[:8], refs[8:]
        for t in range(14):
            width = min(128, 1728 - t * 128)
            lanes = slice(t * 128, t * 128 + width)
            s = ins[0][:, lanes].astype(F32)
            for ref in ins[1:]:
                s = s + ref[:, lanes].astype(F32)
            total[:, 0:width] = s
            even, odd = total[pl.ds(0, 8, stride=2), :], total[pl.ds(1, 8, stride=2), :]
            for u in range(width // 64):
                pick = slice(u * 64, u * 64 + 64)
                at = (2 * t + u) * 8
                pairs[at : at + 8, :] = jnp.concatenate([even[:, pick], odd[:, pick]], axis=1)
        for cp in range(8):
            out_ref[:, cp * 128 : cp * 128 + 128] = pairs[pl.ds(cp, 27, stride=8), :]

    return call(
        kernel,
        shape((27, 1024), F32),
        [(part, None) for part in parts],
        [pltpu.VMEM((16, 128), F32), pltpu.VMEM((216, 128), F32)],
        0,
        600_000,
    )


def place_grad(rim, x, y, v):
    low, high = stacked_depth(v.astype(F32))
    for half in range(2):
        lanes = slice(half * 128, half * 128 + 128)
        rim[x, y * 32 : y * 32 + 16, lanes] = low[half].astype(BF)
        rim[x, y * 32 + 16 : y * 32 + 32, lanes] = high[half].astype(BF)


def input_layers(rows, back_ref, total, store):
    for n in range(2):
        lanes = slice(n * 256, n * 256 + 256)
        acc = jnp.zeros((256, 256), F32)
        for i in range(3):
            for j in range(3):
                acc = acc + jnp.dot(
                    jnp.concatenate([rows(u, 2 - i, (2 - j) * 32) for u in range(2)], axis=0),
                    back_ref[i * 3 + j, :, lanes],
                    preferred_element_type=F32,
                )
        total[:, lanes] = acc
    for u in range(2):
        for y in range(4):
            at = u * 128 + y * 32
            for f in range(8):
                lanes = slice(f * 64, f * 64 + 64)
                pair = jnp.concatenate([total[at : at + 16, lanes], total[at + 16 : at + 32, lanes]], axis=1)
                store(f, u, y, pair.astype(BF))


def input_grad_inner(coords, pre_grad, y_before, y_after, back):
    def kernel(co, pre_ref, yb, ya, back_ref, out_ref, rim, total):
        y_low, y_high = co[4] > 0, co[4] < 7

        def place(x, carry):
            place_grad(rim, x, 0, masked(yb[x], y_low))
            place_grad(rim, x, 5, masked(ya[x], y_high))
            for y in range(4):
                place_grad(rim, x, y + 1, pre_ref[x, y])
            return carry

        lax.fori_loop(0, 8, place, 0)

        def multiply(h, carry):
            def store(f, u, y, block):
                out_ref[f, 2 * h + u, y] = block

            input_layers(lambda u, d, at: rim[2 * h + u + d, at : at + 128, :], back_ref, total, store)
            return carry

        lax.fori_loop(0, 3, multiply, 0)

    return call(
        kernel,
        shape((8, 6, 4, 16, 128)),
        [(coords, pltpu.SMEM)] + [(a, None) for a in (pre_grad, y_before, y_after, back)],
        [pltpu.VMEM((8, 192, 256), BF), pltpu.VMEM((256, 512), F32)],
        4_000_000_000,
        5_000_000,
    )


def input_grad_outer(coords, pre_grad, y_before, y_after, x_before, x_after, back, inner):
    def kernel(co, pre_ref, yb, ya, xb, xa, back_ref, inner_ref, out_ref, rim, total):
        y_low, y_high, x_low, x_high = co[4] > 0, co[4] < 7, co[5] > 0, co[5] < 3
        for y in range(6):
            beside = {0: y_low, 5: y_high}.get(y, True)
            place_grad(rim, 0, y, masked(xb[y], jnp.logical_and(x_low, beside)))
            place_grad(rim, 5, y, masked(xa[y], jnp.logical_and(x_high, beside)))
        for at, x in ((1, 0), (2, 1), (3, 6), (4, 7)):
            place_grad(rim, at, 0, masked(yb[x], y_low))
            place_grad(rim, at, 5, masked(ya[x], y_high))
            for y in range(4):
                place_grad(rim, at, y + 1, pre_ref[x, y])

        def store(f, u, y, block):
            out_ref[f, 7 * u, y] = block

        input_layers(lambda u, d, at: rim[3 * u + d, at : at + 128, :], back_ref, total, store)
        for f in range(8):
            out_ref[f, 1:7] = inner_ref[f]

    return call(
        kernel,
        shape((8,) + PIECE),
        [(coords, pltpu.SMEM)]
        + [(a, None) for a in (pre_grad, y_before, y_after, x_before, x_after, back, inner)],
        [pltpu.VMEM((6, 192, 256), BF), pltpu.VMEM((256, 512), F32)],
        2_000_000_000,
        5_000_000,
    )


def add_blocks(parts):
    def kernel(parts_ref, out_ref, wide):
        s = parts_ref[0].astype(F32)
        for f in range(1, 8):
            s = s + parts_ref[f].astype(F32)
        wide[...] = s.reshape(512, 128)
        from_pairs(wide, out_ref, range(8))

    return call(
        kernel,
        shape((8, 4, 2048)),
        [(parts, None)],
        [pltpu.VMEM((512, 128), F32)],
        0,
        1_200_000,
    )


def both_ways(last, first, axis, size):
    return (
        lax.ppermute(last, axis, [(i, (i + 1) % size) for i in range(size)]),
        lax.ppermute(first, axis, [((i + 1) % size, i) for i in range(size)]),
    )


def exchange(parts, axis):
    return lax.all_to_all(parts, axis, 0, 0)


def per_device(activations, weights, out_grad):
    filt, sx, sy = (lax.axis_index(a) for a in ("filt", "sx", "sy"))
    coords = jnp.stack([filt // 4, filt % 4, sx % 2, sx // 2, sy, sx, 0, 0]).astype(jnp.int32)
    cells = prepare_gather(activations[0, 0])
    cells, weights, out_grad = lax.optimization_barrier((cells, weights, out_grad))
    cells = exchange(cells, "filt")
    fore, back = prepare_weights(weights[0])
    grad = prepare_field(out_grad[0, 0])
    cells, fore, back, grad = lax.optimization_barrier((cells, fore, back, grad))
    y_before, y_after = both_ways(cells[:, 3], cells[:, 0], "sy", 8)
    x_last, x_first = gather_edges(cells, y_before, y_after)
    x_last, x_first, cells = lax.optimization_barrier((x_last, x_first, cells))
    x_before, x_after = both_ways(x_last, x_first, "sx", 4)
    field, out_inner, pre_inner = forward_inner(coords, cells, y_before, y_after, fore, grad)
    rim, outputs, pre_grad, g_first, g_last = forward_outer(
        coords, field, x_before, x_after, fore, grad, out_inner, pre_inner
    )

    gy_before, gy_after = both_ways(g_last, g_first, "sy", 8)
    keep, send = filter_grad(coords, field, rim, pre_grad)
    got = lax.ppermute(send, "sx", [(i, i ^ 1) for i in range(4)])
    stay, send = add_cores(coords, keep, got)
    send, pre_grad, gy_before, gy_after = lax.optimization_barrier((send, pre_grad, gy_before, gy_after))
    got = lax.ppermute(send, "sx", [(i, i ^ 2) for i in range(4)])
    gx_before, gx_after = both_ways(*grad_edges(pre_grad, gy_before, gy_after), "sx", 4)

    inner = input_grad_inner(coords, pre_grad, gy_before, gy_after, back)
    parts = input_grad_outer(coords, pre_grad, gy_before, gy_after, gx_before, gx_after, back, inner)
    parts, got = lax.optimization_barrier((parts, got))
    parts = exchange(parts, "filt")
    turned = add_far(coords, stay, got)
    regions = {0: turned[0]}
    for d in (4, 3, 5, 2, 6, 1, 7):
        regions[d] = lax.ppermute(turned[d], "sy", [(i, (i + d) % 8) for i in range(8)])
    weight_grad = add_regions([regions[d] for d in range(8)])
    input_grad = add_blocks(parts)
    return outputs[None, None], input_grad[None, None], weight_grad[None]


def solution(mesh):
    in_specs = (
        P("filt", None, "sx", "sy", None),
        P("filt", None, None),
        P("filt", None, "sx", "sy", None),
    )
    out_specs = (
        P("filt", None, "sx", "sy", None),
        P("filt", None, "sx", "sy", None),
        P("filt", None, ("sx", "sy")),
    )
    return jax.shard_map(
        per_device, mesh=mesh, in_specs=in_specs, out_specs=out_specs, check_vma=False
    )
```

time: 116 us -> 102 us (0.88)
  the two profiles are of different devices: /device:TPU:2 before, /device:TPU:1 now
where the time goes in v3:
time: 102 us; the launch traced here: 101 us
  starting transfers between devices  38.7 us (38%)
  Pallas kernels  29.1 us (29%)
  waiting for transfers between devices  27.2 us (27%)
  local copies, waits for them, and re-layouts  5.04 us (5%)
    pallas_call x14, Pallas kernels, call(): pl.pallas_call(kernel, out_shape=outs, in_specs=[pl.BlockSpec(memory_spac...  29.1 us
    ppermute x7, starting transfers between devices, per_device(): lax.ppermute(turned[d], 'sy', [(i, (i + d) % 8) for i in range(8)])  11.5 us
    all_to_all x2, starting transfers between devices, exchange(): return lax.all_to_all(parts, axis, 0, 0)  9.5 us
    ppermute x4, starting transfers between devices, both_ways(): lax.ppermute(first, axis, [((i + 1) % size, i) for i in range(size)])  8.35 us
    ppermute x4, starting transfers between devices, both_ways(): lax.ppermute(last, axis, [(i, (i + 1) % size) for i in range(size)])  8.11 us
    ppermute x7, waiting for transfers between devices, per_device(): lax.ppermute(turned[d], 'sy', [(i, (i + d) % 8) for i in range(8)])  6.79 us
    all_to_all x2, waiting for transfers between devices, exchange(): return lax.all_to_all(parts, axis, 0, 0)  5.62 us
    ppermute x4, waiting for transfers between devices, both_ways(): lax.ppermute(first, axis, [((i + 1) % size, i) for i in range(size)])  5.57 us
  transfers between devices with their start and end apart: 19, of which 11 were waited for; matrix products, arithmetic and copies ran while one was open for 1% of the time, Pallas kernels for 20%

profile of v3, /device:TPU:1, one launch (start us, length us, event | category | flops | bytes accessed | tf_op | source)
XLA Modules:
  0.0 100.7 jit_solution(3205103142465021929)
XLA Ops:
  0.6 0.0 copy-start
  0.6 0.0 copy-start.1
  0.7 1.0 %copy-done.1 = bf16[1,1,8,4,2048]{4,3,2,1,0:T(4,128)(2,1)S(1)} copy-done((bf16[1,1,8,4,2048]{4,3,2,1,0:T(4,128)(2,1)S(1)}, bf16[1,1,8,4,2048]{4,3,2,1,0:T(4,128)(2,1)}, u32[]{:S(2)}) %copy-start.1) | copy-done | bytes 131096
  1.7 0.0 copy-start.2
  1.7 1.2 %shard_map.58 = bf16[8,4,8,16,128]{4,3,2,1,0:T(8,128)(2,1)} custom-call(bf16[8,4,2048]{2,1,0:T(4,128)(2,1)S(1)} %bitcast.18), custom_call_target="tpu_custom_call" | custom-call | bytes 1300000 | tf_op jit(solution)/shard_map/pallas_call | solution.py:18
  2.9 5.9 %all-to-all-start = ((bf16[8,4,8,16,128]{4,3,2,1,0:T(8,128)(2,1)}), bf16[8,4,8,16,128]{4,3,2,1,0:T(8,128)(2,1)S(1)}, u32[]{:S(2)}, u32[]{:S(2)}) async-start(bf16[8,4,8,16,128]{4,3,2,1,0:T(8,128)(2,1)} %shard_map.58), calls=%async_computation | async-start | bytes 2097152 | tf_op jit(solution)/shard_map/all_to_all | solution.py:523
  8.9 0.0 copy-done.2
  8.9 0.1 shard_map.60.grad_ref
  9.0 0.0 copy-done
  9.0 7.8 %shard_map.59 = (bf16[9,512,256]{2,1,0:T(8,128)(2,1)S(1)}, bf16[9,256,512]{2,1,0:T(8,128)(2,1)}) custom-call(bf16[27,32768]{1,0:T(8,128)(2,1)S(1)} %bitcast.16), custom_call_target="tpu_custom_call" | custom-call | bytes 8000000 | tf_op jit(solution)/shard_map/pallas_call | solution.py:18
  16.7 0.0 copy-start.4
  16.7 1.4 %copy-done.4 = bf16[9,512,256]{2,1,0:T(8,128)(2,1)} copy-done((bf16[9,512,256]{2,1,0:T(8,128)(2,1)}, bf16[9,512,256]{2,1,0:T(8,128)(2,1)S(1)}, u32[]{:S(2)}) %copy-start.4) | copy-done | bytes 2359320
  18.2 5.6 %all-to-all-done.cells_ref = bf16[8,4,8,16,128]{4,3,2,1,0:T(8,128)(2,1)S(1)} async-done(((bf16[8,4,8,16,128]{4,3,2,1,0:T(8,128)(2,1)}), bf16[8,4,8,16,128]{4,3,2,1,0:T(8,128)(2,1)S(1)}, u32[]{:S(2)}, u32[]{:S(2)}) %all-to-all-start) | async-done | bytes 1048608 | tf_op jit(solution)/shard_map/all_to_all | solution.py:523
  23.8 5.7 %collective-permute-start.1 = (bf16[8,8,16,128]{3,2,1,0:T(8,128)(2,1)S(1)}, bf16[8,8,16,128]{3,2,1,0:T(8,128)(2,1)S(1)}, u32[]{:S(2)}, u32[]{:S(2)}) collective-permute-start(bf16[8,8,16,128]{3,2,1,0:T(8,128)(2,1)S(1)} %get-tuple-element.93), channel_id=1, source_target_pairs={{1,0},{2,1},{3,2},{4,3},{5,4},{6,5},{7,6},{0,7},{9,8},{10,9},{11,1... | collective-permute-start | bytes 786440 | tf_op jit(solution)/shard_map/ppermute | solution.py:518
  29.5 0.0 collective-permute-start
  29.5 0.1 stack.27.co
  29.6 4.7 %collective-permute-done.1.ya = bf16[8,8,16,128]{3,2,1,0:T(8,128)(2,1)S(1)} collective-permute-done((bf16[8,8,16,128]{3,2,1,0:T(8,128)(2,1)S(1)}, bf16[8,8,16,128]{3,2,1,0:T(8,128)(2,1)S(1)}, u32[]{:S(2)}, u32[]{:S(2)}) %collective-permute-start.1) | collective-permute-done | bytes 262176 | tf_op jit(solution)/shard_map/ppermute | solution.py:518
  34.3 3.1 %collective-permute-done.yb = bf16[8,8,16,128]{3,2,1,0:T(8,128)(2,1)S(1)} collective-permute-done((bf16[8,8,16,128]{3,2,1,0:T(8,128)(2,1)S(1)}, bf16[8,8,16,128]{3,2,1,0:T(8,128)(2,1)S(1)}, u32[]{:S(2)}, u32[]{:S(2)}) %collective-permute-start) | collective-permute-done | bytes 262176 | tf_op jit(solution)/shard_map/ppermute | solution.py:517
  37.4 4.5 %collective-permute-start.2 = (bf16[8,6,16,128]{3,2,1,0:T(8,128)(2,1)S(1)}, bf16[8,6,16,128]{3,2,1,0:T(8,128)(2,1)S(1)}, u32[]{:S(2)}, u32[]{:S(2)}) collective-permute-start(bf16[8,6,16,128]{3,2,1,0:T(8,128)(2,1)S(1)} %get-tuple-element.57), channel_id=1, source_target_pairs={{0,8},{8,16},{16,24},{24,0},{1,9},{9,17},{17,25},{25,1},{2,10},{10... | collective-permute-start | bytes 589832 | tf_op jit(solution)/shard_map/ppermute | solution.py:517
  41.9 0.0 collective-permute-start.3
  41.9 0.0 copy-start.5
  41.9 1.7 %copy-done.5 = bf16[9,512,256]{2,1,0:T(8,128)(2,1)S(1)} copy-done((bf16[9,512,256]{2,1,0:T(8,128)(2,1)S(1)}, bf16[9,512,256]{2,1,0:T(8,128)(2,1)}, u32[]{:S(2)}) %copy-start.5) | copy-done | bytes 2359320
  43.5 4.6 %shard_map.62 = (bf16[8,192,512]{2,1,0:T(8,128)(2,1)S(1)}, bf16[6,4,2048]{2,1,0:T(4,128)(2,1)S(1)}, bf16[6,4,16,128]{3,2,1,0:T(8,128)(2,1)S(1)}) custom-call(s32[8]{0:T(128)S(1)} %stack.27.co, bf16[8,4,8,16,128]{4,3,2,1,0:T(8,128)(2,1)S(1)} %all-to-all-done.cells_ref, bf16[8,8,16,128]{3,2,1,0:T(8,128)(2,1)S(1)} %collective-permute-done.yb, ...), custom_call_target="tpu_custom_call" | custom-call | flops 4000000000 | bytes 6000000 | tf_op jit(solution)/shard_map/pallas_call | solution.py:18
  48.2 0.0 collective-permute-done.2.xb
  48.2 0.3 collective-permute-done.3.xa
  48.5 2.1 %shard_map.63 = (bf16[2,192,512]{2,1,0:T(8,128)(2,1)S(1)}, bf16[8,4,2048]{2,1,0:T(4,128)(2,1)}, bf16[8,4,16,128]{3,2,1,0:T(8,128)(2,1)S(1)}, bf16[8,16,128]{2,1,0:T(8,128)(2,1)S(1)}, bf16[8,16,128]{2,1,0:T(8,128)(2,1)S(1)}) custom-call(s32[8]{0:T(128)S(1)} %stack.27.co, bf16[8,192,512]{2,1,0:T(8,128)(2,1)S(1)} %get-tuple-element.56.field_ref, ...), custom_call_target="tpu_custom_call" | custom-call | flops 2000000000 | bytes 6000000 | tf_op jit(solution)/shard_map/pallas_call | solution.py:18
  50.6 4.4 %shard_map.64 = (f32[2,9,192,128]{3,2,1,0:T(8,128)S(1)}, bf16[2,9,192,128]{3,2,1,0:T(8,128)(2,1)S(1)}) custom-call(s32[8]{0:T(128)S(1)} %stack.27.co, bf16[8,192,512]{2,1,0:T(8,128)(2,1)S(1)} %get-tuple-element.56.field_ref, bf16[2,192,512]{2,1,0:T(8,128)(2,1)S(1)} %get-tuple-element.62.rim_ref, bf16[8,4,16,128]{3,2,1,0:T(8,128)(2,1)S(1)} %get-tuple-element.69.pre_ref), custom_call_target="tpu_custom_call" | custom-call | flops 5000000000 | bytes 6000000 | tf_op jit(solution)/shard_map/pallas_call | solution.py:18
  55.0 0.0 copy-start.3
  55.0 0.7 collective-permute-start.4
  55.7 0.0 collective-permute-start.5
  55.7 2.7 %collective-permute-start.6 = (bf16[8,16,128]{2,1,0:T(8,128)(2,1)S(1)}, bf16[8,16,128]{2,1,0:T(8,128)(2,1)S(1)}, u32[]{:S(2)}, u32[]{:S(2)}) collective-permute-start(bf16[8,16,128]{2,1,0:T(8,128)(2,1)S(1)} %get-tuple-element.68), channel_id=1, source_target_pairs={{1,0},{2,1},{3,2},{4,3},{5,4},{6,5},{7,6},{0,7},{9,8},{10,9},{11,1... | collective-permute-start | bytes 98312 | tf_op jit(solution)/shard_map/ppermute | solution.py:518
  58.4 0.0 collective-permute-done.4.got_ref
  58.4 0.7 shard_map.65
  59.1 0.6 collective-permute-done.5.yb
  59.7 0.0 collective-permute-done.6.ya
  59.7 3.7 %collective-permute-start.7 = (bf16[6,16,128]{2,1,0:T(8,128)(2,1)S(1)}, bf16[6,16,128]{2,1,0:T(8,128)(2,1)S(1)}, u32[]{:S(2)}, u32[]{:S(2)}) collective-permute-start(bf16[6,16,128]{2,1,0:T(8,128)(2,1)S(1)} %get-tuple-element.72), channel_id=1, source_target_pairs={{0,8},{8,16},{16,24},{24,0},{1,9},{9,17},{17,25},{25,1},{2,10},{10... | collective-permute-start | bytes 73736 | tf_op jit(solution)/shard_map/ppermute | solution.py:517
  63.4 0.0 collective-permute-start.8
  63.4 0.5 collective-permute-start.9
  63.9 0.0 copy-done.3
  63.9 3.8 %shard_map.67.inner_ref = bf16[8,6,4,16,128]{4,3,2,1,0:T(8,128)(2,1)S(1)} custom-call(s32[8]{0:T(128)S(1)} %stack.27.co, bf16[8,4,16,128]{3,2,1,0:T(8,128)(2,1)S(1)} %get-tuple-element.69.pre_ref, bf16[8,16,128]{2,1,0:T(8,128)(2,1)S(1)} %collective-permute-done.5.yb, bf16[8,16,128]{2,1,0:T(8,128)(2,1)S(1)} %collective-permute-done.6.ya, ...), custom_call_target="tpu_custom_call" | custom-call | flops 4000000000 | bytes 5000000 | tf_op jit(solution)/shard_map/pallas_call | solution.py:18
  67.7 0.0 collective-permute-done.7.xb
  67.7 0.6 collective-permute-done.8.xa
  68.3 2.5 %shard_map.68 = bf16[8,8,4,16,128]{4,3,2,1,0:T(8,128)(2,1)} custom-call(s32[8]{0:T(128)S(1)} %stack.27.co, bf16[8,4,16,128]{3,2,1,0:T(8,128)(2,1)S(1)} %get-tuple-element.69.pre_ref, bf16[8,16,128]{2,1,0:T(8,128)(2,1)S(1)} %collective-permute-done.5.yb, bf16[8,16,128]{2,1,0:T(8,128)(2,1)S(1)} %collective-permute-done.6.ya, ...), custom_call_target="tpu_custom_call" | custom-call | flops 2000000000 | bytes 5000000 | tf_op jit(solution)/shard_map/pallas_call | solution.py:18
  70.8 5.5 %collective-permute-done.9.got_ref = bf16[9,192,128]{2,1,0:T(8,128)(2,1)S(1)} collective-permute-done((bf16[9,192,128]{2,1,0:T(8,128)(2,1)S(1)}, bf16[9,192,128]{2,1,0:T(8,128)(2,1)S(1)}, u32[]{:S(2)}, u32[]{:S(2)}) %collective-permute-start.9) | collective-permute-done | bytes 442400 | tf_op jit(solution)/shard_map/ppermute | solution.py:549
  76.3 3.6 %all-to-all-start.1 = ((bf16[8,8,4,16,128]{4,3,2,1,0:T(8,128)(2,1)}), bf16[8,8,4,16,128]{4,3,2,1,0:T(8,128)(2,1)S(1)}, u32[]{:S(2)}, u32[]{:S(2)}) async-start(bf16[8,8,4,16,128]{4,3,2,1,0:T(8,128)(2,1)} %shard_map.68), calls=%async_computation.1 | async-start | bytes 2097152 | tf_op jit(solution)/shard_map/all_to_all | solution.py:523
  79.8 0.8 shard_map.70
  80.6 0.3 collective-permute-start.10
  80.9 2.2 %collective-permute-start.11 = (bf16[16,1728]{1,0:T(8,128)(2,1)S(1)}, bf16[16,1728]{1,0:T(8,128)(2,1)S(1)}, u32[]{:S(2)}, u32[]{:S(2)}) collective-permute-start(bf16[16,1728]{1,0:T(8,128)(2,1)S(1)} %get-tuple-element.81), channel_id=1, source_target_pairs={{0,2},{1,3},{2,4},{3,5},{4,6},{5,7},{6,0},{7,1},{8,10},{9,11},{10,... | collective-permute-start | bytes 165896 | tf_op jit(solution)/shard_map/ppermute | solution.py:559
  83.0 1.3 %collective-permute-start.12 = (bf16[16,1728]{1,0:T(8,128)(2,1)S(1)}, bf16[16,1728]{1,0:T(8,128)(2,1)S(1)}, u32[]{:S(2)}, u32[]{:S(2)}) collective-permute-start(bf16[16,1728]{1,0:T(8,128)(2,1)S(1)} %get-tuple-element.82), channel_id=1, source_target_pairs={{0,3},{1,4},{2,5},{3,6},{4,7},{5,0},{6,1},{7,2},{8,11},{9,12},{10,... | collective-permute-start | bytes 165896 | tf_op jit(solution)/shard_map/ppermute | solution.py:559
  84.3 2.7 %collective-permute-start.13 = (bf16[16,1728]{1,0:T(8,128)(2,1)S(1)}, bf16[16,1728]{1,0:T(8,128)(2,1)S(1)}, u32[]{:S(2)}, u32[]{:S(2)}) collective-permute-start(bf16[16,1728]{1,0:T(8,128)(2,1)S(1)} %get-tuple-element.83), channel_id=1, source_target_pairs={{0,4},{1,5},{2,6},{3,7},{4,0},{5,1},{6,2},{7,3},{8,12},{9,13},{10,... | collective-permute-start | bytes 165896 | tf_op jit(solution)/shard_map/ppermute | solution.py:559
  87.0 4.5 %collective-permute-start.14 = (bf16[16,1728]{1,0:T(8,128)(2,1)S(1)}, bf16[16,1728]{1,0:T(8,128)(2,1)S(1)}, u32[]{:S(2)}, u32[]{:S(2)}) collective-permute-start(bf16[16,1728]{1,0:T(8,128)(2,1)S(1)} %get-tuple-element.84), channel_id=1, source_target_pairs={{0,5},{1,6},{2,7},{3,0},{4,1},{5,2},{6,3},{7,4},{8,13},{9,14},{10,... | collective-permute-start | bytes 165896 | tf_op jit(solution)/shard_map/ppermute | solution.py:559
  91.5 0.0 collective-permute-done.10.refs_1_
  91.5 0.0 collective-permute-start.15
  91.5 0.0 collective-permute-done.11.refs_2_
  91.5 0.6 collective-permute-start.16
  92.1 0.0 collective-permute-done.12.refs_3_
  92.1 2.6 %collective-permute-done.13.refs_4_ = bf16[16,1728]{1,0:T(8,128)(2,1)S(1)} collective-permute-done((bf16[16,1728]{1,0:T(8,128)(2,1)S(1)}, bf16[16,1728]{1,0:T(8,128)(2,1)S(1)}, u32[]{:S(2)}, u32[]{:S(2)}) %collective-permute-start.13) | collective-permute-done | bytes 55328 | tf_op jit(solution)/shard_map/ppermute | solution.py:559
  94.7 0.2 collective-permute-done.14.refs_5_
  94.9 3.2 %collective-permute-done.15.refs_6_ = bf16[16,1728]{1,0:T(8,128)(2,1)S(1)} collective-permute-done((bf16[16,1728]{1,0:T(8,128)(2,1)S(1)}, bf16[16,1728]{1,0:T(8,128)(2,1)S(1)}, u32[]{:S(2)}, u32[]{:S(2)}) %collective-permute-start.15) | collective-permute-done | bytes 55328 | tf_op jit(solution)/shard_map/ppermute | solution.py:559
  98.0 0.9 collective-permute-done.16.refs_7_
  98.9 0.2 shard_map.71
  99.1 0.8 copy.12
  99.8 0.0 all-to-all-done.1.parts_ref
  99.8 0.9 shard_map.69
  (4 shorter events, 0.1 us)
Async XLA Ops:
  0.6 8.3 %copy-start = (bf16[1,27,32768]{2,1,0:T(8,128)(2,1)S(1)}, bf16[1,27,32768]{2,1,0:T(8,128)(2,1)}, u32[]{:S(2)}) copy-start(bf16[1,27,32768]{2,1,0:T(8,128)(2,1)} %param.4) | copy-start | bytes 5308420
  0.6 1.1 %copy-start.1 = (bf16[1,1,8,4,2048]{4,3,2,1,0:T(4,128)(2,1)S(1)}, bf16[1,1,8,4,2048]{4,3,2,1,0:T(4,128)(2,1)}, u32[]{:S(2)}) copy-start(bf16[1,1,8,4,2048]{4,3,2,1,0:T(4,128)(2,1)} %param.3) | copy-start | bytes 393220
  1.7 7.2 %copy-start.2 = (bf16[1,1,8,4,2048]{4,3,2,1,0:T(4,128)(2,1)S(1)}, bf16[1,1,8,4,2048]{4,3,2,1,0:T(4,128)(2,1)}, u32[]{:S(2)}) copy-start(bf16[1,1,8,4,2048]{4,3,2,1,0:T(4,128)(2,1)} %param.5) | copy-start | bytes 393220
  2.9 20.9 %all-to-all-start = ((bf16[8,4,8,16,128]{4,3,2,1,0:T(8,128)(2,1)}), bf16[8,4,8,16,128]{4,3,2,1,0:T(8,128)(2,1)S(1)}, u32[]{:S(2)}, u32[]{:S(2)}) async-start(bf16[8,4,8,16,128]{4,3,2,1,0:T(8,128)(2,1)} %shard_map.58), calls=%async_computation | async-start | bytes 2097152 | tf_op jit(solution)/shard_map/all_to_all | solution.py:523
  16.7 1.4 %copy-start.4 = (bf16[9,512,256]{2,1,0:T(8,128)(2,1)}, bf16[9,512,256]{2,1,0:T(8,128)(2,1)S(1)}, u32[]{:S(2)}) copy-start(bf16[9,512,256]{2,1,0:T(8,128)(2,1)S(1)} %get-tuple-element.54.fore_ref) | copy-start | bytes 7077892
  23.8 10.4 %collective-permute-start.1 = (bf16[8,8,16,128]{3,2,1,0:T(8,128)(2,1)S(1)}, bf16[8,8,16,128]{3,2,1,0:T(8,128)(2,1)S(1)}, u32[]{:S(2)}, u32[]{:S(2)}) collective-permute-start(bf16[8,8,16,128]{3,2,1,0:T(8,128)(2,1)S(1)} %get-tuple-element.93), channel_id=1, source_target_pairs={{1,0},{2,1},{3,2},{4,3},{5,4},{6,5},{7,6},{0,7},{9,8},{10,9},{11,1... | collective-permute-start | bytes 786440 | tf_op jit(solution)/shard_map/ppermute | solution.py:518
  29.5 7.9 %collective-permute-start = (bf16[8,8,16,128]{3,2,1,0:T(8,128)(2,1)S(1)}, bf16[8,8,16,128]{3,2,1,0:T(8,128)(2,1)S(1)}, u32[]{:S(2)}, u32[]{:S(2)}) collective-permute-start(bf16[8,8,16,128]{3,2,1,0:T(8,128)(2,1)S(1)} %get-tuple-element.94), channel_id=1, source_target_pairs={{0,1},{1,2},{2,3},{3,4},{4,5},{5,6},{6,7},{7,0},{8,9},{9,10},{10,1... | collective-permute-start | bytes 786440 | tf_op jit(solution)/shard_map/ppermute | solution.py:517
  37.4 10.8 %collective-permute-start.2 = (bf16[8,6,16,128]{3,2,1,0:T(8,128)(2,1)S(1)}, bf16[8,6,16,128]{3,2,1,0:T(8,128)(2,1)S(1)}, u32[]{:S(2)}, u32[]{:S(2)}) collective-permute-start(bf16[8,6,16,128]{3,2,1,0:T(8,128)(2,1)S(1)} %get-tuple-element.57), channel_id=1, source_target_pairs={{0,8},{8,16},{16,24},{24,0},{1,9},{9,17},{17,25},{25,1},{2,10},{10... | collective-permute-start | bytes 589832 | tf_op jit(solution)/shard_map/ppermute | solution.py:517
  41.9 6.6 %collective-permute-start.3 = (bf16[8,6,16,128]{3,2,1,0:T(8,128)(2,1)S(1)}, bf16[8,6,16,128]{3,2,1,0:T(8,128)(2,1)S(1)}, u32[]{:S(2)}, u32[]{:S(2)}) collective-permute-start(bf16[8,6,16,128]{3,2,1,0:T(8,128)(2,1)S(1)} %get-tuple-element.58), channel_id=1, source_target_pairs={{8,0},{16,8},{24,16},{0,24},{9,1},{17,9},{25,17},{1,25},{10,2},{18... | collective-permute-start | bytes 589832 | tf_op jit(solution)/shard_map/ppermute | solution.py:518
  41.9 1.7 %copy-start.5 = (bf16[9,512,256]{2,1,0:T(8,128)(2,1)S(1)}, bf16[9,512,256]{2,1,0:T(8,128)(2,1)}, u32[]{:S(2)}) copy-start(bf16[9,512,256]{2,1,0:T(8,128)(2,1)} %copy-done.4) | copy-start | bytes 7077892
  55.0 8.9 %copy-start.3 = (bf16[9,256,512]{2,1,0:T(8,128)(2,1)S(1)}, bf16[9,256,512]{2,1,0:T(8,128)(2,1)}, u32[]{:S(2)}) copy-start(bf16[9,256,512]{2,1,0:T(8,128)(2,1)} %get-tuple-element.74.back_ref) | copy-start | bytes 7077892
  55.0 3.4 %collective-permute-start.4 = (bf16[2,9,192,128]{3,2,1,0:T(8,128)(2,1)S(1)}, bf16[2,9,192,128]{3,2,1,0:T(8,128)(2,1)S(1)}, u32[]{:S(2)}, u32[]{:S(2)}) collective-permute-start(bf16[2,9,192,128]{3,2,1,0:T(8,128)(2,1)S(1)} %get-tuple-element.65), channel_id=1, source_target_pairs={{0,8},{8,0},{16,24},{24,16},{1,9},{9,1},{17,25},{25,17},{2,10},{10... | collective-permute-start | bytes 2654216 | tf_op jit(solution)/shard_map/ppermute | solution.py:546
  55.7 4.0 %collective-permute-start.5 = (bf16[8,16,128]{2,1,0:T(8,128)(2,1)S(1)}, bf16[8,16,128]{2,1,0:T(8,128)(2,1)S(1)}, u32[]{:S(2)}, u32[]{:S(2)}) collective-permute-start(bf16[8,16,128]{2,1,0:T(8,128)(2,1)S(1)} %get-tuple-element.67), channel_id=1, source_target_pairs={{0,1},{1,2},{2,3},{3,4},{4,5},{5,6},{6,7},{7,0},{8,9},{9,10},{10,1... | collective-permute-start | bytes 98312 | tf_op jit(solution)/shard_map/ppermute | solution.py:517
  55.7 4.0 %collective-permute-start.6 = (bf16[8,16,128]{2,1,0:T(8,128)(2,1)S(1)}, bf16[8,16,128]{2,1,0:T(8,128)(2,1)S(1)}, u32[]{:S(2)}, u32[]{:S(2)}) collective-permute-start(bf16[8,16,128]{2,1,0:T(8,128)(2,1)S(1)} %get-tuple-element.68), channel_id=1, source_target_pairs={{1,0},{2,1},{3,2},{4,3},{5,4},{6,5},{7,6},{0,7},{9,8},{10,9},{11,1... | collective-permute-start | bytes 98312 | tf_op jit(solution)/shard_map/ppermute | solution.py:518
  59.7 8.0 %collective-permute-start.7 = (bf16[6,16,128]{2,1,0:T(8,128)(2,1)S(1)}, bf16[6,16,128]{2,1,0:T(8,128)(2,1)S(1)}, u32[]{:S(2)}, u32[]{:S(2)}) collective-permute-start(bf16[6,16,128]{2,1,0:T(8,128)(2,1)S(1)} %get-tuple-element.72), channel_id=1, source_target_pairs={{0,8},{8,16},{16,24},{24,0},{1,9},{9,17},{17,25},{25,1},{2,10},{10... | collective-permute-start | bytes 73736 | tf_op jit(solution)/shard_map/ppermute | solution.py:517
  63.4 5.0 %collective-permute-start.8 = (bf16[6,16,128]{2,1,0:T(8,128)(2,1)S(1)}, bf16[6,16,128]{2,1,0:T(8,128)(2,1)S(1)}, u32[]{:S(2)}, u32[]{:S(2)}) collective-permute-start(bf16[6,16,128]{2,1,0:T(8,128)(2,1)S(1)} %get-tuple-element.73), channel_id=1, source_target_pairs={{8,0},{16,8},{24,16},{0,24},{9,1},{17,9},{25,17},{1,25},{10,2},{18... | collective-permute-start | bytes 73736 | tf_op jit(solution)/shard_map/ppermute | solution.py:518
  63.4 12.9 %collective-permute-start.9 = (bf16[9,192,128]{2,1,0:T(8,128)(2,1)S(1)}, bf16[9,192,128]{2,1,0:T(8,128)(2,1)S(1)}, u32[]{:S(2)}, u32[]{:S(2)}) collective-permute-start(bf16[9,192,128]{2,1,0:T(8,128)(2,1)S(1)} %get-tuple-element.75), channel_id=1, source_target_pairs={{0,16},{8,24},{16,0},{24,8},{1,17},{9,25},{17,1},{25,9},{2,18},{10... | collective-permute-start | bytes 1327112 | tf_op jit(solution)/shard_map/ppermute | solution.py:549
  76.3 23.6 %all-to-all-start.1 = ((bf16[8,8,4,16,128]{4,3,2,1,0:T(8,128)(2,1)}), bf16[8,8,4,16,128]{4,3,2,1,0:T(8,128)(2,1)S(1)}, u32[]{:S(2)}, u32[]{:S(2)}) async-start(bf16[8,8,4,16,128]{4,3,2,1,0:T(8,128)(2,1)} %shard_map.68), calls=%async_computation.1 | async-start | bytes 2097152 | tf_op jit(solution)/shard_map/all_to_all | solution.py:523
  80.6 10.9 %collective-permute-start.10 = (bf16[16,1728]{1,0:T(8,128)(2,1)S(1)}, bf16[16,1728]{1,0:T(8,128)(2,1)S(1)}, u32[]{:S(2)}, u32[]{:S(2)}) collective-permute-start(bf16[16,1728]{1,0:T(8,128)(2,1)S(1)} %get-tuple-element.80), channel_id=1, source_target_pairs={{0,1},{1,2},{2,3},{3,4},{4,5},{5,6},{6,7},{7,0},{8,9},{9,10},{10,1... | collective-permute-start | bytes 165896 | tf_op jit(solution)/shard_map/ppermute | solution.py:559
  80.9 10.6 %collective-permute-start.11 = (bf16[16,1728]{1,0:T(8,128)(2,1)S(1)}, bf16[16,1728]{1,0:T(8,128)(2,1)S(1)}, u32[]{:S(2)}, u32[]{:S(2)}) collective-permute-start(bf16[16,1728]{1,0:T(8,128)(2,1)S(1)} %get-tuple-element.81), channel_id=1, source_target_pairs={{0,2},{1,3},{2,4},{3,5},{4,6},{5,7},{6,0},{7,1},{8,10},{9,11},{10,... | collective-permute-start | bytes 165896 | tf_op jit(solution)/shard_map/ppermute | solution.py:559
  83.0 9.1 %collective-permute-start.12 = (bf16[16,1728]{1,0:T(8,128)(2,1)S(1)}, bf16[16,1728]{1,0:T(8,128)(2,1)S(1)}, u32[]{:S(2)}, u32[]{:S(2)}) collective-permute-start(bf16[16,1728]{1,0:T(8,128)(2,1)S(1)} %get-tuple-element.82), channel_id=1, source_target_pairs={{0,3},{1,4},{2,5},{3,6},{4,7},{5,0},{6,1},{7,2},{8,11},{9,12},{10,... | collective-permute-start | bytes 165896 | tf_op jit(solution)/shard_map/ppermute | solution.py:559
  84.3 10.3 %collective-permute-start.13 = (bf16[16,1728]{1,0:T(8,128)(2,1)S(1)}, bf16[16,1728]{1,0:T(8,128)(2,1)S(1)}, u32[]{:S(2)}, u32[]{:S(2)}) collective-permute-start(bf16[16,1728]{1,0:T(8,128)(2,1)S(1)} %get-tuple-element.83), channel_id=1, source_target_pairs={{0,4},{1,5},{2,6},{3,7},{4,0},{5,1},{6,2},{7,3},{8,12},{9,13},{10,... | collective-permute-start | bytes 165896 | tf_op jit(solution)/shard_map/ppermute | solution.py:559
  87.0 7.9 %collective-permute-start.14 = (bf16[16,1728]{1,0:T(8,128)(2,1)S(1)}, bf16[16,1728]{1,0:T(8,128)(2,1)S(1)}, u32[]{:S(2)}, u32[]{:S(2)}) collective-permute-start(bf16[16,1728]{1,0:T(8,128)(2,1)S(1)} %get-tuple-element.84), channel_id=1, source_target_pairs={{0,5},{1,6},{2,7},{3,0},{4,1},{5,2},{6,3},{7,4},{8,13},{9,14},{10,... | collective-permute-start | bytes 165896 | tf_op jit(solution)/shard_map/ppermute | solution.py:559
  91.5 6.5 %collective-permute-start.15 = (bf16[16,1728]{1,0:T(8,128)(2,1)S(1)}, bf16[16,1728]{1,0:T(8,128)(2,1)S(1)}, u32[]{:S(2)}, u32[]{:S(2)}) collective-permute-start(bf16[16,1728]{1,0:T(8,128)(2,1)S(1)} %get-tuple-element.85), channel_id=1, source_target_pairs={{0,6},{1,7},{2,0},{3,1},{4,2},{5,3},{6,4},{7,5},{8,14},{9,15},{10,... | collective-permute-start | bytes 165896 | tf_op jit(solution)/shard_map/ppermute | solution.py:559
  91.5 7.4 %collective-permute-start.16 = (bf16[16,1728]{1,0:T(8,128)(2,1)S(1)}, bf16[16,1728]{1,0:T(8,128)(2,1)S(1)}, u32[]{:S(2)}, u32[]{:S(2)}) collective-permute-start(bf16[16,1728]{1,0:T(8,128)(2,1)S(1)} %get-tuple-element.86), channel_id=1, source_target_pairs={{0,7},{1,0},{2,1},{3,2},{4,3},{5,4},{6,5},{7,6},{8,15},{9,8},{10,9... | collective-permute-start | bytes 165896 | tf_op jit(solution)/shard_map/ppermute | solution.py:559

commit v4 on v3

--- a/solution.py
+++ b/solution.py
@@ -11,6 +11,8 @@
 F32 = jnp.float32
 LEAK = 0.2
 SCALE = 1.0 / math.sqrt(32768.0)
+URGENT = 20_000_000_000
+COST = [20_000_000_000, 4_000_000_000, 500_000_000, 5_000_000_000]
 PIECE = (8, 4, 16, 128)
 
 
@@ -22,9 +24,14 @@
             pl.BlockSpec(memory_space=pltpu.VMEM if space is None else space)
             for _, space in ins
         ],
-        out_specs=jax.tree.map(lambda _: pl.BlockSpec(memory_space=pltpu.VMEM), outs),
+        out_specs=jax.tree.map(
+            lambda out: pl.BlockSpec(
+                memory_space=pltpu.VMEM if isinstance(out, jax.ShapeDtypeStruct) else pl.ANY
+            ),
+            outs,
+        ),
         scratch_shapes=list(scratch),
-        compiler_params=pltpu.CompilerParams(vmem_limit_bytes=48 << 20),
+        compiler_params=pltpu.CompilerParams(vmem_limit_bytes=14 << 20),
         cost_estimate=pl.CostEstimate(flops=flops, bytes_accessed=nbytes, transcendentals=0),
     )(*[array for array, _ in ins])
 
@@ -87,34 +94,54 @@
     )
 
 
-def gather_edges(cells, y_before, y_after):
-    def kernel(cells_ref, yb, ya, last_ref, first_ref):
-        for out_ref, x in ((last_ref, 7), (first_ref, 0)):
-            for f in range(8):
-                out_ref[f, 0] = yb[f, x]
-                out_ref[f, 5] = ya[f, x]
-                for y in range(4):
-                    out_ref[f, y + 1] = cells_ref[f, y, x]
+def gather_sides(cells, prepared):
+    def kernel(cells_ref, prepared_ref, last_ref, first_ref, sems):
+        copies = [
+            pltpu.make_async_copy(cells_ref.at[:, 3], last_ref, sems.at[0]),
+            pltpu.make_async_copy(cells_ref.at[:, 0], first_ref, sems.at[1]),
+        ]
+        for copy in copies:
+            copy.start()
+        for copy in copies:
+            copy.wait()
+
+    out = shape((8, 8, 16, 128))
+    ins = [(cells, pl.ANY), (prepared, None)]
+    return call(kernel, (out, out), ins, [pltpu.SemaphoreType.DMA((2,))], 0, 1_000_000)
+
+
+def gather_edges(coords, cells, y_before, y_after):
+    def kernel(co, cells_ref, yb, ya, near_ref, far_ref):
+        def give(last_ref, first_ref):
+            for out_ref, x in ((last_ref, 7), (first_ref, 0)):
+                for f in range(8):
+                    out_ref[f, 0] = yb[f, x]
+                    out_ref[f, 5] = ya[f, x]
+                    for y in range(4):
+                        out_ref[f, y + 1] = cells_ref[f, y, x]
+
+        pl.when(co[2] == 0)(lambda: give(near_ref, far_ref))
+        pl.when(co[2] == 1)(lambda: give(far_ref, near_ref))
 
     out = shape((8, 6, 16, 128))
-    ins = [(a, None) for a in (cells, y_before, y_after)]
+    ins = [(coords, pltpu.SMEM)] + [(a, None) for a in (cells, y_before, y_after)]
     return call(kernel, (out, out), ins, (), 0, 400_000)
 
 
-def grad_edges(pre_grad, y_before, y_after):
-    def kernel(pre_ref, yb, ya, last_ref, first_ref):
-        for out_ref, x in ((last_ref, 7), (first_ref, 0)):
+def grad_edges(coords, pre_grad, y_before, y_after):
+    def kernel(co, pre_ref, yb, ya, near_ref, far_ref):
+        for out_ref, x in ((near_ref, 7 - 7 * co[2]), (far_ref, 7 * co[2])):
             out_ref[0] = yb[x]
             out_ref[1:5] = pre_ref[x]
             out_ref[5] = ya[x]
 
     out = shape((6, 16, 128))
-    ins = [(a, None) for a in (pre_grad, y_before, y_after)]
-    return call(kernel, (out, out), ins, (), 0, 50_000)
+    ins = [(coords, pltpu.SMEM)] + [(a, None) for a in (pre_grad, y_before, y_after)]
+    return call(kernel, (out, out), ins, (), 0, 0)
 
 
 def prepare_weights(weights):
-    def kernel(w_ref, fore_ref, back_ref, tall, even, odd):
+    def kernel(w_ref, fore_ref, back_out, done_ref, tall, even, odd, back_ref, sems):
         def spread(t, carry):
             lanes = pl.ds(pl.multiple_of(t * 128, 128), 128)
             tall[pl.ds(t, 27, stride=256), :] = w_ref[:, lanes].astype(F32)
@@ -137,15 +164,31 @@
                 rows = slice(c * 128, c * 128 + 128)
                 back_ref[ij, 0:128, rows] = even[rows, :].T.astype(BF)
                 back_ref[ij, 128:256, rows] = odd[rows, :].T.astype(BF)
+            copy_out(ij).start()
+            return carry
+
+        def copy_out(ij):
+            return pltpu.make_async_copy(back_ref.at[ij], back_out.at[ij], sems.at[ij])
+
+        def finish(ij, carry):
+            copy_out(ij).wait()
             return carry
 
         lax.fori_loop(0, 9, place, 0)
-
-    return call(
-        kernel,
-        (shape((9, 512, 256)), shape((9, 256, 512))),
+        lax.fori_loop(0, 9, finish, 0)
+        done_ref[...] = even[0:8, :]
+
+    return call(
+        kernel,
+        (shape((9, 512, 256)), pltpu.HBM((9, 256, 512), BF), shape((8, 128), F32)),
         [(weights, None)],
-        [pltpu.VMEM((27 * 256, 128), F32), pltpu.VMEM((512, 128), F32), pltpu.VMEM((512, 128), F32)],
+        [
+            pltpu.VMEM((27 * 256, 128), F32),
+            pltpu.VMEM((512, 128), F32),
+            pltpu.VMEM((512, 128), F32),
+            pltpu.VMEM((9, 256, 512), BF),
+            pltpu.SemaphoreType.DMA((9,)),
+        ],
         0,
         8_000_000,
     )
@@ -232,16 +275,27 @@
     )
 
 
-def forward_outer(coords, field, x_before, x_after, fore, grad, out_inner, pre_inner):
+def forward_outer(coords, field, x_near, x_far, fore, grad, out_inner, pre_inner):
     def kernel(
-        co, field_ref, xb, xa, fore_ref, grad_ref, out_in, pre_in,
+        co, field_ref, near_ref, far_ref, fore_ref, grad_ref, out_in, pre_in,
         rim_ref, out_ref, pre_ref, first_ref, last_ref, total, wide,
     ):
         y_low, y_high, x_low, x_high = co[4] > 0, co[4] < 7, co[5] > 0, co[5] < 3
+        odd = co[2] > 0
         for y in range(6):
             beside = {0: y_low, 5: y_high}.get(y, True)
-            place_cell(rim_ref, 0, y, lambda f: masked(xb[f, y], jnp.logical_and(x_low, beside)))
-            place_cell(rim_ref, 1, y, lambda f: masked(xa[f, y], jnp.logical_and(x_high, beside)))
+            place_cell(
+                rim_ref,
+                0,
+                y,
+                lambda f: masked(jnp.where(odd, near_ref[f, y], far_ref[f, y]), jnp.logical_and(x_low, beside)),
+            )
+            place_cell(
+                rim_ref,
+                1,
+                y,
+                lambda f: masked(jnp.where(odd, far_ref[f, y], near_ref[f, y]), jnp.logical_and(x_high, beside)),
+            )
 
         def rows(u, i, at):
             if u == 0:
@@ -271,7 +325,7 @@
             shape((8, 16, 128)),
         ),
         [(coords, pltpu.SMEM)]
-        + [(a, None) for a in (field, x_before, x_after, fore, grad, out_inner, pre_inner)],
+        + [(a, None) for a in (field, x_near, x_far, fore, grad, out_inner, pre_inner)],
         [pltpu.VMEM((256, 256), F32), pltpu.VMEM((128, 128), F32)],
         2_000_000_000,
         6_000_000,
@@ -331,8 +385,8 @@
         (shape((2, 9, 192, 128), F32), shape((2, 9, 192, 128))),
         [(coords, pltpu.SMEM), (field, None), (rim, None), (pre_grad, None)],
         [pltpu.VMEM((128, 128), F32), pltpu.VMEM((128, 128), F32), pltpu.VMEM((192, 1024), BF)],
-        5_000_000_000,
-        6_000_000,
+        COST[3],
+        0,
     )
 
 
@@ -347,36 +401,53 @@
         (shape((9, 192, 128), F32), shape((9, 192, 128))),
         [(coords, pltpu.SMEM), (keep, None), (got, None)],
         (),
-        0,
+        COST[0],
         4_000_000,
     )
 
 
 def add_far(coords, stay, got):
-    def kernel(co, stay_ref, got_ref, *refs):
-        outs, (total, turned) = refs[:8], refs[8:]
-        sy = co[4]
+    def kernel(co, stay_ref, got_ref, keep_ref, send_ref, total, turned):
+        parity = co[4] & 1
         total[...] = (stay_ref[...] + got_ref[...].astype(F32)).reshape(1728, 128)
         for t in range(14):
             width = min(128, 1728 - t * 128)
-            block = total[t * 128 : t * 128 + width, :].T.astype(BF).reshape(8, 16, width)
+            block = total[t * 128 : t * 128 + width, :].T.reshape(8, 16, width)
             turned[:, :, t * 128 : t * 128 + width] = block
-        for d in range(8):
-            outs[d][...] = turned[(sy + d) & 7]
-
-    return call(
-        kernel,
-        (shape((16, 1728)),) * 8,
+        for m in range(4):
+            keep_ref[m] = turned[2 * m + parity]
+            send_ref[m] = turned[2 * m + 1 - parity].astype(BF)
+
+    return call(
+        kernel,
+        (shape((4, 16, 1728), F32), shape((4, 16, 1728))),
         [(coords, pltpu.SMEM), (stay, None), (got, None)],
-        [pltpu.VMEM((1728, 128), F32), pltpu.VMEM((8, 16, 1728), BF)],
-        0,
+        [pltpu.VMEM((1728, 128), F32), pltpu.VMEM((8, 16, 1728), F32)],
+        URGENT,
         2_000_000,
+    )
+
+
+def add_near(coords, keep, got):
+    def kernel(co, keep_ref, got_ref, *outs):
+        own = co[4] // 2
+        for d in range(4):
+            at = (own + d) & 3
+            outs[d][...] = (keep_ref[at] + got_ref[at].astype(F32)).astype(outs[d].dtype)
+
+    return call(
+        kernel,
+        (shape((16, 1728), F32),) + (shape((16, 1728)),) * 3,
+        [(coords, pltpu.SMEM), (keep, None), (got, None)],
+        (),
+        URGENT,
+        1_000_000,
     )
 
 
 def add_regions(parts):
     def kernel(*refs):
-        ins, (out_ref, total, pairs) = refs[:8], refs[8:]
+        ins, (out_ref, total, pairs) = refs[:4], refs[4:]
         for t in range(14):
             width = min(128, 1728 - t * 128)
             lanes = slice(t * 128, t * 128 + width)
@@ -389,15 +460,14 @@
                 pick = slice(u * 64, u * 64 + 64)
                 at = (2 * t + u) * 8
                 pairs[at : at + 8, :] = jnp.concatenate([even[:, pick], odd[:, pick]], axis=1)
-        for cp in range(8):
-            out_ref[:, cp * 128 : cp * 128 + 128] = pairs[pl.ds(cp, 27, stride=8), :]
-
-    return call(
-        kernel,
-        shape((27, 1024), F32),
+        out_ref[...] = pairs[...].reshape(27, 8, 128)
+
+    return call(
+        kernel,
+        shape((27, 8, 128), F32),
         [(part, None) for part in parts],
         [pltpu.VMEM((16, 128), F32), pltpu.VMEM((216, 128), F32)],
-        0,
+        URGENT,
         600_000,
     )
 
@@ -458,18 +528,21 @@
         shape((8, 6, 4, 16, 128)),
         [(coords, pltpu.SMEM)] + [(a, None) for a in (pre_grad, y_before, y_after, back)],
         [pltpu.VMEM((8, 192, 256), BF), pltpu.VMEM((256, 512), F32)],
-        4_000_000_000,
-        5_000_000,
-    )
-
-
-def input_grad_outer(coords, pre_grad, y_before, y_after, x_before, x_after, back, inner):
-    def kernel(co, pre_ref, yb, ya, xb, xa, back_ref, inner_ref, out_ref, rim, total):
+        COST[1],
+        0,
+    )
+
+
+def input_grad_outer(coords, pre_grad, y_before, y_after, x_near, x_far, back, inner):
+    def kernel(co, pre_ref, yb, ya, near_ref, far_ref, back_ref, inner_ref, out_ref, rim, total):
         y_low, y_high, x_low, x_high = co[4] > 0, co[4] < 7, co[5] > 0, co[5] < 3
+        odd = co[2] > 0
         for y in range(6):
             beside = {0: y_low, 5: y_high}.get(y, True)
-            place_grad(rim, 0, y, masked(xb[y], jnp.logical_and(x_low, beside)))
-            place_grad(rim, 5, y, masked(xa[y], jnp.logical_and(x_high, beside)))
+            near, far = near_ref[y], far_ref[y]
+            before, after = jnp.where(odd, near, far), jnp.where(odd, far, near)
+            place_grad(rim, 0, y, masked(before, jnp.logical_and(x_low, beside)))
+            place_grad(rim, 5, y, masked(after, jnp.logical_and(x_high, beside)))
         for at, x in ((1, 0), (2, 1), (3, 6), (4, 7)):
             place_grad(rim, at, 0, masked(yb[x], y_low))
             place_grad(rim, at, 5, masked(ya[x], y_high))
@@ -487,10 +560,10 @@
         kernel,
         shape((8,) + PIECE),
         [(coords, pltpu.SMEM)]
-        + [(a, None) for a in (pre_grad, y_before, y_after, x_before, x_after, back, inner)],
+        + [(a, None) for a in (pre_grad, y_before, y_after, x_near, x_far, back, inner)],
         [pltpu.VMEM((6, 192, 256), BF), pltpu.VMEM((256, 512), F32)],
-        2_000_000_000,
-        5_000_000,
+        COST[2],
+        0,
     )
 
 
@@ -519,6 +592,13 @@
     )
 
 
+def x_rims(near, far):
+    return (
+        lax.ppermute(near, "sx", [(i, i ^ 1) for i in range(4)]),
+        lax.ppermute(far, "sx", [(1, 2), (2, 1)]),
+    )
+
+
 def exchange(parts, axis):
     return lax.all_to_all(parts, axis, 0, 0)
 
@@ -529,37 +609,38 @@
     cells = prepare_gather(activations[0, 0])
     cells, weights, out_grad = lax.optimization_barrier((cells, weights, out_grad))
     cells = exchange(cells, "filt")
-    fore, back = prepare_weights(weights[0])
+    fore, back, prepared = prepare_weights(weights[0])
     grad = prepare_field(out_grad[0, 0])
-    cells, fore, back, grad = lax.optimization_barrier((cells, fore, back, grad))
-    y_before, y_after = both_ways(cells[:, 3], cells[:, 0], "sy", 8)
-    x_last, x_first = gather_edges(cells, y_before, y_after)
-    x_last, x_first, cells = lax.optimization_barrier((x_last, x_first, cells))
-    x_before, x_after = both_ways(x_last, x_first, "sx", 4)
+    y_before, y_after = both_ways(*gather_sides(cells, prepared), "sy", 8)
+    near, far = gather_edges(coords, cells, y_before, y_after)
+    near, far, cells = lax.optimization_barrier((near, far, cells))
+    x_near, x_far = x_rims(near, far)
     field, out_inner, pre_inner = forward_inner(coords, cells, y_before, y_after, fore, grad)
     rim, outputs, pre_grad, g_first, g_last = forward_outer(
-        coords, field, x_before, x_after, fore, grad, out_inner, pre_inner
+        coords, field, x_near, x_far, fore, grad, out_inner, pre_inner
     )
 
     gy_before, gy_after = both_ways(g_last, g_first, "sy", 8)
     keep, send = filter_grad(coords, field, rim, pre_grad)
     got = lax.ppermute(send, "sx", [(i, i ^ 1) for i in range(4)])
     stay, send = add_cores(coords, keep, got)
-    send, pre_grad, gy_before, gy_after = lax.optimization_barrier((send, pre_grad, gy_before, gy_after))
+    stay, pre_grad, gy_before, gy_after = lax.optimization_barrier((stay, pre_grad, gy_before, gy_after))
     got = lax.ppermute(send, "sx", [(i, i ^ 2) for i in range(4)])
-    gx_before, gx_after = both_ways(*grad_edges(pre_grad, gy_before, gy_after), "sx", 4)
+    gx_near, gx_far = x_rims(*grad_edges(coords, pre_grad, gy_before, gy_after))
 
     inner = input_grad_inner(coords, pre_grad, gy_before, gy_after, back)
-    parts = input_grad_outer(coords, pre_grad, gy_before, gy_after, gx_before, gx_after, back, inner)
+    parts = input_grad_outer(coords, pre_grad, gy_before, gy_after, gx_near, gx_far, back, inner)
     parts, got = lax.optimization_barrier((parts, got))
     parts = exchange(parts, "filt")
-    turned = add_far(coords, stay, got)
-    regions = {0: turned[0]}
-    for d in (4, 3, 5, 2, 6, 1, 7):
-        regions[d] = lax.ppermute(turned[d], "sy", [(i, (i + d) % 8) for i in range(8)])
-    weight_grad = add_regions([regions[d] for d in range(8)])
+    keep, send = add_far(coords, stay, got)
+    got = lax.ppermute(send, "sy", [(i, i ^ 1) for i in range(8)])
+    regions = list(add_near(coords, keep, got))
+    for d in (2, 1, 3):
+        regions[d] = lax.ppermute(regions[d], "sy", [(i, (i + 2 * d) % 8) for i in range(8)])
     input_grad = add_blocks(parts)
-    return outputs[None, None], input_grad[None, None], weight_grad[None]
+    input_grad, regions = lax.optimization_barrier((input_grad, regions))
+    weight_grad = add_regions(regions)
+    return outputs[None, None], input_grad[None, None], weight_grad.reshape(1, 27, 1024)
 
 
 def solution(mesh):

time: 102 us -> 95.1 us (0.932)
  waiting for transfers between devices: 27.2 us -> 20.4 us
  Pallas kernels: 29.1 us -> 31 us
    ppermute x7 -> x8, starting transfers between devices: 11.5 us -> 18.5 us  [the longest x2 8.28 us: x_rims(): lax.ppermute(far, 'sx', [(1, 2), (2, 1)])]
    ppermute x4 -> x2, starting transfers between devices: 8.11 us -> 1.8 us  [both_ways(): lax.ppermute(last, axis, [(i, (i + 1) % size) for i in range(size)])]
    ppermute x4 -> x2, waiting for transfers between devices: 5.57 us -> 0.01 us  [both_ways(): lax.ppermute(first, axis, [((i + 1) % size, i) for i in range(size)])]
    ppermute x1, waiting for transfers between devices: 5.47 us -> 0.01 us  [per_device(): got = lax.ppermute(send, 'sx', [(i, i ^ 2) for i in range(4)])]
    all_to_all x2, waiting for transfers between devices: 5.62 us -> 9.08 us  [exchange(): return lax.all_to_all(parts, axis, 0, 0)]
    pallas_call x14 -> x16, Pallas kernels: 29.1 us -> 31 us  [call(): pl.pallas_call(kernel, out_shape=outs, in_specs=[pl.BlockSpec(memory_spac...]
    ppermute x4 -> x2, waiting for transfers between devices: 3.71 us -> 5.54 us  [both_ways(): lax.ppermute(last, axis, [(i, (i + 1) % size) for i in range(size)])]
    ppermute x4 -> x2, starting transfers between devices: 8.35 us -> 6.87 us  [both_ways(): lax.ppermute(first, axis, [((i + 1) % size, i) for i in range(size)])]
  transfers between devices with their start and end apart: 19 -> 16, of which waited for: 11 -> 5; matrix products, arithmetic and copies ran while one was open for 1% -> 0% of each run, Pallas kernels for 20% -> 22%
where the time goes in v4:
time: 95.1 us; the launch traced here: 94.3 us
  starting transfers between devices  37.7 us (40%)
  Pallas kernels  31 us (33%)
  waiting for transfers between devices  20.4 us (21%)
  local copies, waits for them, and re-layouts  4.24 us (4%)
    pallas_call x16, Pallas kernels, call(): pl.pallas_call(kernel, out_shape=outs, in_specs=[pl.BlockSpec(memory_spac...  31 us
    all_to_all x2, starting transfers between devices, exchange(): return lax.all_to_all(parts, axis, 0, 0)  9.52 us
    all_to_all x2, waiting for transfers between devices, exchange(): return lax.all_to_all(parts, axis, 0, 0)  9.08 us
    ppermute x2, starting transfers between devices, x_rims(): lax.ppermute(far, 'sx', [(1, 2), (2, 1)])  8.28 us
    ppermute x3, starting transfers between devices, per_device(): lax.ppermute(regions[d], 'sy', [(i, (i + 2 * d) % 8) for i in range(8)])  7.56 us
    ppermute x2, starting transfers between devices, both_ways(): lax.ppermute(first, axis, [((i + 1) % size, i) for i in range(size)])  6.87 us
    ppermute x2, waiting for transfers between devices, both_ways(): lax.ppermute(last, axis, [(i, (i + 1) % size) for i in range(size)])  5.54 us
    unnamed x12, local copies, waits for them, and re-layouts  4.15 us
  transfers between devices with their start and end apart: 16, of which 5 were waited for; matrix products, arithmetic and copies ran while one was open for 0% of the time, Pallas kernels for 22%

profile of v4, /device:TPU:1, one launch (start us, length us, event | category | flops | bytes accessed | tf_op | source)
XLA Modules:
  0.0 94.3 jit_solution(213939540345223819)
XLA Ops:
  0.6 0.0 copy-start.1
  0.6 0.0 copy-start.2
  0.6 1.0 %copy-done.2 = bf16[1,1,8,4,2048]{4,3,2,1,0:T(4,128)(2,1)S(1)} copy-done((bf16[1,1,8,4,2048]{4,3,2,1,0:T(4,128)(2,1)S(1)}, bf16[1,1,8,4,2048]{4,3,2,1,0:T(4,128)(2,1)}, u32[]{:S(2)}) %copy-start.2) | copy-done | bytes 131096
  1.7 1.2 %shard_map.58 = bf16[8,4,8,16,128]{4,3,2,1,0:T(8,128)(2,1)} custom-call(bf16[8,4,2048]{2,1,0:T(4,128)(2,1)S(1)} %bitcast.13), custom_call_target="tpu_custom_call" | custom-call | bytes 1300000 | tf_op jit(solution)/shard_map/pallas_call | solution.py:20
  2.9 5.9 %all-to-all-start = ((bf16[8,4,8,16,128]{4,3,2,1,0:T(8,128)(2,1)}), bf16[8,4,8,16,128]{4,3,2,1,0:T(8,128)(2,1)S(1)}, u32[]{:S(2)}, u32[]{:S(2)}) async-start(bf16[8,4,8,16,128]{4,3,2,1,0:T(8,128)(2,1)} %shard_map.58), calls=%async_computation | async-start | bytes 2097152 | tf_op jit(solution)/shard_map/all_to_all | solution.py:603
  8.9 0.0 copy-start.3
  8.9 0.0 copy-done.1
  8.9 7.1 %shard_map.59 = (bf16[9,512,256]{2,1,0:T(8,128)(2,1)S(1)}, bf16[9,256,512]{2,1,0:T(8,128)(2,1)}, f32[8,128]{1,0:T(8,128)S(1)}) custom-call(bf16[27,32768]{1,0:T(8,128)(2,1)S(1)} %bitcast.12), custom_call_target="tpu_custom_call" | custom-call | bytes 8000000 | tf_op jit(solution)/shard_map/pallas_call | solution.py:20
  16.0 0.0 copy-start.4
  16.0 1.4 %copy-done.4 = bf16[9,512,256]{2,1,0:T(8,128)(2,1)} copy-done((bf16[9,512,256]{2,1,0:T(8,128)(2,1)}, bf16[9,512,256]{2,1,0:T(8,128)(2,1)S(1)}, u32[]{:S(2)}) %copy-start.4) | copy-done | bytes 2359320
  17.5 6.3 %all-to-all-done.cells_ref = bf16[8,4,8,16,128]{4,3,2,1,0:T(8,128)(2,1)S(1)} async-done(((bf16[8,4,8,16,128]{4,3,2,1,0:T(8,128)(2,1)}), bf16[8,4,8,16,128]{4,3,2,1,0:T(8,128)(2,1)S(1)}, u32[]{:S(2)}, u32[]{:S(2)}) %all-to-all-start) | async-done | bytes 1048608 | tf_op jit(solution)/shard_map/all_to_all | solution.py:603
  23.8 0.1 shard_map.60
  23.8 1.7 %collective-permute-start = (bf16[8,8,16,128]{3,2,1,0:T(8,128)(2,1)S(1)}, bf16[8,8,16,128]{3,2,1,0:T(8,128)(2,1)S(1)}, u32[]{:S(2)}, u32[]{:S(2)}) collective-permute-start(bf16[8,8,16,128]{3,2,1,0:T(8,128)(2,1)S(1)} %get-tuple-element.50), channel_id=1, source_target_pairs={{0,1},{1,2},{2,3},{3,4},{4,5},{5,6},{6,7},{7,0},{8,9},{9,10},{10,1... | collective-permute-start | bytes 786440 | tf_op jit(solution)/shard_map/ppermute | solution.py:590
  25.6 4.0 %collective-permute-start.1 = (bf16[8,8,16,128]{3,2,1,0:T(8,128)(2,1)S(1)}, bf16[8,8,16,128]{3,2,1,0:T(8,128)(2,1)S(1)}, u32[]{:S(2)}, u32[]{:S(2)}) collective-permute-start(bf16[8,8,16,128]{3,2,1,0:T(8,128)(2,1)S(1)} %get-tuple-element.51), channel_id=1, source_target_pairs={{1,0},{2,1},{3,2},{4,3},{5,4},{6,5},{7,6},{0,7},{9,8},{10,9},{11,1... | collective-permute-start | bytes 786440 | tf_op jit(solution)/shard_map/ppermute | solution.py:591
  29.6 0.0 copy-done.3
  29.6 0.1 shard_map.62.grad_ref
  29.7 0.1 stack.27.co
  29.8 5.5 %collective-permute-done.yb = bf16[8,8,16,128]{3,2,1,0:T(8,128)(2,1)S(1)} collective-permute-done((bf16[8,8,16,128]{3,2,1,0:T(8,128)(2,1)S(1)}, bf16[8,8,16,128]{3,2,1,0:T(8,128)(2,1)S(1)}, u32[]{:S(2)}, u32[]{:S(2)}) %collective-permute-start) | collective-permute-done | bytes 262176 | tf_op jit(solution)/shard_map/ppermute | solution.py:590
  35.3 0.0 collective-permute-done.1.ya
  35.3 0.6 shard_map.61
  35.9 1.5 %collective-permute-start.2 = (bf16[8,6,16,128]{3,2,1,0:T(8,128)(2,1)S(1)}, bf16[8,6,16,128]{3,2,1,0:T(8,128)(2,1)S(1)}, u32[]{:S(2)}, u32[]{:S(2)}) collective-permute-start(bf16[8,6,16,128]{3,2,1,0:T(8,128)(2,1)S(1)} %get-tuple-element.58), channel_id=1, source_target_pairs={{0,8},{8,0},{16,24},{24,16},{1,9},{9,1},{17,25},{25,17},{2,10},{10... | collective-permute-start | bytes 589832 | tf_op jit(solution)/shard_map/ppermute | solution.py:597
  37.4 4.3 %collective-permute-start.3 = (bf16[8,6,16,128]{3,2,1,0:T(8,128)(2,1)S(1)}, bf16[8,6,16,128]{3,2,1,0:T(8,128)(2,1)S(1)}, u32[]{:S(2)}, u32[]{:S(2)}) collective-permute-start(bf16[8,6,16,128]{3,2,1,0:T(8,128)(2,1)S(1)} %get-tuple-element.59), channel_id=1, source_target_pairs={{8,16},{16,8},{9,17},{17,9},{10,18},{18,10},{11,19},{19,11},{12,20... | collective-permute-start | bytes 589832 | tf_op jit(solution)/shard_map/ppermute | solution.py:598
  41.7 0.0 copy-start.5
  41.7 1.7 %copy-done.5 = bf16[9,512,256]{2,1,0:T(8,128)(2,1)S(1)} copy-done((bf16[9,512,256]{2,1,0:T(8,128)(2,1)S(1)}, bf16[9,512,256]{2,1,0:T(8,128)(2,1)}, u32[]{:S(2)}) %copy-start.5) | copy-done | bytes 2359320
  43.4 4.6 %shard_map.63 = (bf16[8,192,512]{2,1,0:T(8,128)(2,1)S(1)}, bf16[6,4,2048]{2,1,0:T(4,128)(2,1)S(1)}, bf16[6,4,16,128]{3,2,1,0:T(8,128)(2,1)S(1)}) custom-call(s32[8]{0:T(128)S(1)} %stack.27.co, bf16[8,4,8,16,128]{4,3,2,1,0:T(8,128)(2,1)S(1)} %all-to-all-done.cells_ref, bf16[8,8,16,128]{3,2,1,0:T(8,128)(2,1)S(1)} %collective-permute-done.yb, ...), custom_call_target="tpu_custom_call" | custom-call | flops 4000000000 | bytes 6000000 | tf_op jit(solution)/shard_map/pallas_call | solution.py:20
  48.0 0.0 collective-permute-done.2.near_ref
  48.0 0.0 collective-permute-done.3.far_ref
  48.0 2.1 %shard_map.64 = (bf16[2,192,512]{2,1,0:T(8,128)(2,1)S(1)}, bf16[8,4,2048]{2,1,0:T(4,128)(2,1)}, bf16[8,4,16,128]{3,2,1,0:T(8,128)(2,1)S(1)}, bf16[8,16,128]{2,1,0:T(8,128)(2,1)S(1)}, bf16[8,16,128]{2,1,0:T(8,128)(2,1)S(1)}) custom-call(s32[8]{0:T(128)S(1)} %stack.27.co, bf16[8,192,512]{2,1,0:T(8,128)(2,1)S(1)} %get-tuple-element.57.field_ref, ...), custom_call_target="tpu_custom_call" | custom-call | flops 2000000000 | bytes 6000000 | tf_op jit(solution)/shard_map/pallas_call | solution.py:20
  50.2 4.4 %shard_map.65 = (f32[2,9,192,128]{3,2,1,0:T(8,128)S(1)}, bf16[2,9,192,128]{3,2,1,0:T(8,128)(2,1)S(1)}) custom-call(s32[8]{0:T(128)S(1)} %stack.27.co, bf16[8,192,512]{2,1,0:T(8,128)(2,1)S(1)} %get-tuple-element.57.field_ref, bf16[2,192,512]{2,1,0:T(8,128)(2,1)S(1)} %get-tuple-element.63.rim_ref, bf16[8,4,16,128]{3,2,1,0:T(8,128)(2,1)S(1)} %get-tuple-element.70.pre_ref), custom_call_target="tpu_custom_call" | custom-call | flops 5000000000 | tf_op jit(solution)/shard_map/pallas_call | solution.py:20
  54.6 0.1 collective-permute-start.4
  54.7 0.1 collective-permute-start.5
  54.8 2.8 %collective-permute-start.6 = (bf16[8,16,128]{2,1,0:T(8,128)(2,1)S(1)}, bf16[8,16,128]{2,1,0:T(8,128)(2,1)S(1)}, u32[]{:S(2)}, u32[]{:S(2)}) collective-permute-start(bf16[8,16,128]{2,1,0:T(8,128)(2,1)S(1)} %get-tuple-element.69), channel_id=1, source_target_pairs={{1,0},{2,1},{3,2},{4,3},{5,4},{6,5},{7,6},{0,7},{9,8},{10,9},{11,1... | collective-permute-start | bytes 98312 | tf_op jit(solution)/shard_map/ppermute | solution.py:591
  57.6 0.0 collective-permute-done.4.got_ref
  57.6 0.0 copy-start
  57.6 0.8 shard_map.66
  58.4 0.9 collective-permute-start.9
  59.3 0.0 collective-permute-done.5.yb
  59.3 0.0 collective-permute-done.6.ya
  59.3 0.6 shard_map.67
  59.8 1.1 %collective-permute-start.7 = (bf16[6,16,128]{2,1,0:T(8,128)(2,1)S(1)}, bf16[6,16,128]{2,1,0:T(8,128)(2,1)S(1)}, u32[]{:S(2)}, u32[]{:S(2)}) collective-permute-start(bf16[6,16,128]{2,1,0:T(8,128)(2,1)S(1)} %get-tuple-element.73), channel_id=1, source_target_pairs={{0,8},{8,0},{16,24},{24,16},{1,9},{9,1},{17,25},{25,17},{2,10},{10... | collective-permute-start | bytes 73736 | tf_op jit(solution)/shard_map/ppermute | solution.py:597
  60.9 4.0 %collective-permute-start.8 = (bf16[6,16,128]{2,1,0:T(8,128)(2,1)S(1)}, bf16[6,16,128]{2,1,0:T(8,128)(2,1)S(1)}, u32[]{:S(2)}, u32[]{:S(2)}) collective-permute-start(bf16[6,16,128]{2,1,0:T(8,128)(2,1)S(1)} %get-tuple-element.74), channel_id=1, source_target_pairs={{8,16},{16,8},{9,17},{17,9},{10,18},{18,10},{11,19},{19,11},{12,20... | collective-permute-start | bytes 73736 | tf_op jit(solution)/shard_map/ppermute | solution.py:598
  65.0 0.0 copy-done
  65.0 3.8 %shard_map.68.inner_ref = bf16[8,6,4,16,128]{4,3,2,1,0:T(8,128)(2,1)S(1)} custom-call(s32[8]{0:T(128)S(1)} %stack.27.co, bf16[8,4,16,128]{3,2,1,0:T(8,128)(2,1)S(1)} %get-tuple-element.70.pre_ref, bf16[8,16,128]{2,1,0:T(8,128)(2,1)S(1)} %collective-permute-done.5.yb, bf16[8,16,128]{2,1,0:T(8,128)(2,1)S(1)} %collective-permute-done.6.ya, ...), custom_call_target="tpu_custom_call" | custom-call | flops 4000000000 | tf_op jit(solution)/shard_map/pallas_call | solution.py:20
  68.8 0.0 collective-permute-done.7.near_ref
  68.8 3.3 %collective-permute-done.8.far_ref = bf16[6,16,128]{2,1,0:T(8,128)(2,1)S(1)} collective-permute-done((bf16[6,16,128]{2,1,0:T(8,128)(2,1)S(1)}, bf16[6,16,128]{2,1,0:T(8,128)(2,1)S(1)}, u32[]{:S(2)}, u32[]{:S(2)}) %collective-permute-start.8) | collective-permute-done | bytes 24608 | tf_op jit(solution)/shard_map/ppermute | solution.py:598
  72.1 2.4 %shard_map.69 = bf16[8,8,4,16,128]{4,3,2,1,0:T(8,128)(2,1)} custom-call(s32[8]{0:T(128)S(1)} %stack.27.co, bf16[8,4,16,128]{3,2,1,0:T(8,128)(2,1)S(1)} %get-tuple-element.70.pre_ref, bf16[8,16,128]{2,1,0:T(8,128)(2,1)S(1)} %collective-permute-done.5.yb, bf16[8,16,128]{2,1,0:T(8,128)(2,1)S(1)} %collective-permute-done.6.ya, ...), custom_call_target="tpu_custom_call" | custom-call | flops 500000000 | tf_op jit(solution)/shard_map/pallas_call | solution.py:20
  74.6 0.0 collective-permute-done.9.got_ref
  74.6 0.9 shard_map.71
  75.5 0.1 collective-permute-start.10
  75.6 3.6 %all-to-all-start.1 = ((bf16[8,8,4,16,128]{4,3,2,1,0:T(8,128)(2,1)}), bf16[8,8,4,16,128]{4,3,2,1,0:T(8,128)(2,1)S(1)}, u32[]{:S(2)}, u32[]{:S(2)}) async-start(bf16[8,8,4,16,128]{4,3,2,1,0:T(8,128)(2,1)} %shard_map.69), calls=%async_computation.1 | async-start | bytes 2097152 | tf_op jit(solution)/shard_map/all_to_all | solution.py:603
  79.2 2.4 %collective-permute-done.10.got_ref = bf16[4,16,1728]{2,1,0:T(8,128)(2,1)S(1)} collective-permute-done((bf16[4,16,1728]{2,1,0:T(8,128)(2,1)S(1)}, bf16[4,16,1728]{2,1,0:T(8,128)(2,1)S(1)}, u32[]{:S(2)}, u32[]{:S(2)}) %collective-permute-start.10) | collective-permute-done | bytes 221216 | tf_op jit(solution)/shard_map/ppermute | solution.py:636
  81.6 0.6 shard_map.72
  82.2 2.1 %collective-permute-start.11 = (bf16[16,1728]{1,0:T(8,128)(2,1)S(1)}, bf16[16,1728]{1,0:T(8,128)(2,1)S(1)}, u32[]{:S(2)}, u32[]{:S(2)}) collective-permute-start(bf16[16,1728]{1,0:T(8,128)(2,1)S(1)} %get-tuple-element.83), channel_id=1, source_target_pairs={{0,2},{1,3},{2,4},{3,5},{4,6},{5,7},{6,0},{7,1},{8,10},{9,11},{10,... | collective-permute-start | bytes 165896 | tf_op jit(solution)/shard_map/ppermute | solution.py:639
  84.3 2.0 %collective-permute-start.12 = (bf16[16,1728]{1,0:T(8,128)(2,1)S(1)}, bf16[16,1728]{1,0:T(8,128)(2,1)S(1)}, u32[]{:S(2)}, u32[]{:S(2)}) collective-permute-start(bf16[16,1728]{1,0:T(8,128)(2,1)S(1)} %get-tuple-element.84), channel_id=1, source_target_pairs={{0,4},{1,5},{2,6},{3,7},{4,0},{5,1},{6,2},{7,3},{8,12},{9,13},{10,... | collective-permute-start | bytes 165896 | tf_op jit(solution)/shard_map/ppermute | solution.py:639
  86.3 3.5 %collective-permute-start.13 = (bf16[16,1728]{1,0:T(8,128)(2,1)S(1)}, bf16[16,1728]{1,0:T(8,128)(2,1)S(1)}, u32[]{:S(2)}, u32[]{:S(2)}) collective-permute-start(bf16[16,1728]{1,0:T(8,128)(2,1)S(1)} %get-tuple-element.85), channel_id=1, source_target_pairs={{0,6},{1,7},{2,0},{3,1},{4,2},{5,3},{6,4},{7,5},{8,14},{9,15},{10,... | collective-permute-start | bytes 165896 | tf_op jit(solution)/shard_map/ppermute | solution.py:639
  89.8 2.8 %all-to-all-done.1.parts_ref = bf16[8,8,4,16,128]{4,3,2,1,0:T(8,128)(2,1)S(1)} async-done(((bf16[8,8,4,16,128]{4,3,2,1,0:T(8,128)(2,1)}), bf16[8,8,4,16,128]{4,3,2,1,0:T(8,128)(2,1)S(1)}, u32[]{:S(2)}, u32[]{:S(2)}) %all-to-all-start.1) | async-done | bytes 1048608 | tf_op jit(solution)/shard_map/all_to_all | solution.py:603
  92.6 0.9 shard_map.70
  93.5 0.0 collective-permute-done.11.refs_1_
  93.5 0.0 collective-permute-done.12.refs_2_
  93.5 0.0 collective-permute-done.13.refs_3_
  93.5 0.8 shard_map.73
  (1 shorter events, 0.0 us)
Async XLA Ops:
  0.6 8.2 %copy-start.1 = (bf16[1,27,32768]{2,1,0:T(8,128)(2,1)S(1)}, bf16[1,27,32768]{2,1,0:T(8,128)(2,1)}, u32[]{:S(2)}) copy-start(bf16[1,27,32768]{2,1,0:T(8,128)(2,1)} %param.4) | copy-start | bytes 5308420
  0.6 1.1 %copy-start.2 = (bf16[1,1,8,4,2048]{4,3,2,1,0:T(4,128)(2,1)S(1)}, bf16[1,1,8,4,2048]{4,3,2,1,0:T(4,128)(2,1)}, u32[]{:S(2)}) copy-start(bf16[1,1,8,4,2048]{4,3,2,1,0:T(4,128)(2,1)} %param.3) | copy-start | bytes 393220
  2.9 20.9 %all-to-all-start = ((bf16[8,4,8,16,128]{4,3,2,1,0:T(8,128)(2,1)}), bf16[8,4,8,16,128]{4,3,2,1,0:T(8,128)(2,1)S(1)}, u32[]{:S(2)}, u32[]{:S(2)}) async-start(bf16[8,4,8,16,128]{4,3,2,1,0:T(8,128)(2,1)} %shard_map.58), calls=%async_computation | async-start | bytes 2097152 | tf_op jit(solution)/shard_map/all_to_all | solution.py:603
  8.9 20.7 %copy-start.3 = (bf16[1,1,8,4,2048]{4,3,2,1,0:T(4,128)(2,1)S(1)}, bf16[1,1,8,4,2048]{4,3,2,1,0:T(4,128)(2,1)}, u32[]{:S(2)}) copy-start(bf16[1,1,8,4,2048]{4,3,2,1,0:T(4,128)(2,1)} %param.5) | copy-start | bytes 393220
  16.0 1.4 %copy-start.4 = (bf16[9,512,256]{2,1,0:T(8,128)(2,1)}, bf16[9,512,256]{2,1,0:T(8,128)(2,1)S(1)}, u32[]{:S(2)}) copy-start(bf16[9,512,256]{2,1,0:T(8,128)(2,1)S(1)} %get-tuple-element.55.fore_ref) | copy-start | bytes 7077892
  23.8 11.5 %collective-permute-start = (bf16[8,8,16,128]{3,2,1,0:T(8,128)(2,1)S(1)}, bf16[8,8,16,128]{3,2,1,0:T(8,128)(2,1)S(1)}, u32[]{:S(2)}, u32[]{:S(2)}) collective-permute-start(bf16[8,8,16,128]{3,2,1,0:T(8,128)(2,1)S(1)} %get-tuple-element.50), channel_id=1, source_target_pairs={{0,1},{1,2},{2,3},{3,4},{4,5},{5,6},{6,7},{7,0},{8,9},{9,10},{10,1... | collective-permute-start | bytes 786440 | tf_op jit(solution)/shard_map/ppermute | solution.py:590
  25.6 9.8 %collective-permute-start.1 = (bf16[8,8,16,128]{3,2,1,0:T(8,128)(2,1)S(1)}, bf16[8,8,16,128]{3,2,1,0:T(8,128)(2,1)S(1)}, u32[]{:S(2)}, u32[]{:S(2)}) collective-permute-start(bf16[8,8,16,128]{3,2,1,0:T(8,128)(2,1)S(1)} %get-tuple-element.51), channel_id=1, source_target_pairs={{1,0},{2,1},{3,2},{4,3},{5,4},{6,5},{7,6},{0,7},{9,8},{10,9},{11,1... | collective-permute-start | bytes 786440 | tf_op jit(solution)/shard_map/ppermute | solution.py:591
  35.9 12.1 %collective-permute-start.2 = (bf16[8,6,16,128]{3,2,1,0:T(8,128)(2,1)S(1)}, bf16[8,6,16,128]{3,2,1,0:T(8,128)(2,1)S(1)}, u32[]{:S(2)}, u32[]{:S(2)}) collective-permute-start(bf16[8,6,16,128]{3,2,1,0:T(8,128)(2,1)S(1)} %get-tuple-element.58), channel_id=1, source_target_pairs={{0,8},{8,0},{16,24},{24,16},{1,9},{9,1},{17,25},{25,17},{2,10},{10... | collective-permute-start | bytes 589832 | tf_op jit(solution)/shard_map/ppermute | solution.py:597
  37.4 10.6 %collective-permute-start.3 = (bf16[8,6,16,128]{3,2,1,0:T(8,128)(2,1)S(1)}, bf16[8,6,16,128]{3,2,1,0:T(8,128)(2,1)S(1)}, u32[]{:S(2)}, u32[]{:S(2)}) collective-permute-start(bf16[8,6,16,128]{3,2,1,0:T(8,128)(2,1)S(1)} %get-tuple-element.59), channel_id=1, source_target_pairs={{8,16},{16,8},{9,17},{17,9},{10,18},{18,10},{11,19},{19,11},{12,20... | collective-permute-start | bytes 589832 | tf_op jit(solution)/shard_map/ppermute | solution.py:598
  41.7 1.7 %copy-start.5 = (bf16[9,512,256]{2,1,0:T(8,128)(2,1)S(1)}, bf16[9,512,256]{2,1,0:T(8,128)(2,1)}, u32[]{:S(2)}) copy-start(bf16[9,512,256]{2,1,0:T(8,128)(2,1)} %copy-done.4) | copy-start | bytes 7077892
  54.6 3.0 %collective-permute-start.4 = (bf16[2,9,192,128]{3,2,1,0:T(8,128)(2,1)S(1)}, bf16[2,9,192,128]{3,2,1,0:T(8,128)(2,1)S(1)}, u32[]{:S(2)}, u32[]{:S(2)}) collective-permute-start(bf16[2,9,192,128]{3,2,1,0:T(8,128)(2,1)S(1)} %get-tuple-element.66), channel_id=1, source_target_pairs={{0,8},{8,0},{16,24},{24,16},{1,9},{9,1},{17,25},{25,17},{2,10},{10... | collective-permute-start | bytes 2654216 | tf_op jit(solution)/shard_map/ppermute | solution.py:625
  54.7 4.6 %collective-permute-start.5 = (bf16[8,16,128]{2,1,0:T(8,128)(2,1)S(1)}, bf16[8,16,128]{2,1,0:T(8,128)(2,1)S(1)}, u32[]{:S(2)}, u32[]{:S(2)}) collective-permute-start(bf16[8,16,128]{2,1,0:T(8,128)(2,1)S(1)} %get-tuple-element.68), channel_id=1, source_target_pairs={{0,1},{1,2},{2,3},{3,4},{4,5},{5,6},{6,7},{7,0},{8,9},{9,10},{10,1... | collective-permute-start | bytes 98312 | tf_op jit(solution)/shard_map/ppermute | solution.py:590
  54.8 4.5 %collective-permute-start.6 = (bf16[8,16,128]{2,1,0:T(8,128)(2,1)S(1)}, bf16[8,16,128]{2,1,0:T(8,128)(2,1)S(1)}, u32[]{:S(2)}, u32[]{:S(2)}) collective-permute-start(bf16[8,16,128]{2,1,0:T(8,128)(2,1)S(1)} %get-tuple-element.69), channel_id=1, source_target_pairs={{1,0},{2,1},{3,2},{4,3},{5,4},{6,5},{7,6},{0,7},{9,8},{10,9},{11,1... | collective-permute-start | bytes 98312 | tf_op jit(solution)/shard_map/ppermute | solution.py:591
  57.6 7.4 %copy-start = (bf16[9,256,512]{2,1,0:T(8,128)(2,1)S(1)}, bf16[9,256,512]{2,1,0:T(8,128)(2,1)}, u32[]{:S(2)}) copy-start(bf16[9,256,512]{2,1,0:T(8,128)(2,1)} %get-tuple-element.75.back_ref) | copy-start | bytes 7077892
  58.4 16.2 %collective-permute-start.9 = (bf16[9,192,128]{2,1,0:T(8,128)(2,1)S(1)}, bf16[9,192,128]{2,1,0:T(8,128)(2,1)S(1)}, u32[]{:S(2)}, u32[]{:S(2)}) collective-permute-start(bf16[9,192,128]{2,1,0:T(8,128)(2,1)S(1)} %get-tuple-element.76), channel_id=1, source_target_pairs={{0,16},{8,24},{16,0},{24,8},{1,17},{9,25},{17,1},{25,9},{2,18},{10... | collective-permute-start | bytes 1327112 | tf_op jit(solution)/shard_map/ppermute | solution.py:628
  59.8 8.9 %collective-permute-start.7 = (bf16[6,16,128]{2,1,0:T(8,128)(2,1)S(1)}, bf16[6,16,128]{2,1,0:T(8,128)(2,1)S(1)}, u32[]{:S(2)}, u32[]{:S(2)}) collective-permute-start(bf16[6,16,128]{2,1,0:T(8,128)(2,1)S(1)} %get-tuple-element.73), channel_id=1, source_target_pairs={{0,8},{8,0},{16,24},{24,16},{1,9},{9,1},{17,25},{25,17},{2,10},{10... | collective-permute-start | bytes 73736 | tf_op jit(solution)/shard_map/ppermute | solution.py:597
  60.9 11.2 %collective-permute-start.8 = (bf16[6,16,128]{2,1,0:T(8,128)(2,1)S(1)}, bf16[6,16,128]{2,1,0:T(8,128)(2,1)S(1)}, u32[]{:S(2)}, u32[]{:S(2)}) collective-permute-start(bf16[6,16,128]{2,1,0:T(8,128)(2,1)S(1)} %get-tuple-element.74), channel_id=1, source_target_pairs={{8,16},{16,8},{9,17},{17,9},{10,18},{18,10},{11,19},{19,11},{12,20... | collective-permute-start | bytes 73736 | tf_op jit(solution)/shard_map/ppermute | solution.py:598
  75.5 6.1 %collective-permute-start.10 = (bf16[4,16,1728]{2,1,0:T(8,128)(2,1)S(1)}, bf16[4,16,1728]{2,1,0:T(8,128)(2,1)S(1)}, u32[]{:S(2)}, u32[]{:S(2)}) collective-permute-start(bf16[4,16,1728]{2,1,0:T(8,128)(2,1)S(1)} %get-tuple-element.81), channel_id=1, source_target_pairs={{0,1},{1,0},{2,3},{3,2},{4,5},{5,4},{6,7},{7,6},{8,9},{9,8},{10,11... | collective-permute-start | bytes 663560 | tf_op jit(solution)/shard_map/ppermute | solution.py:636
  75.6 17.0 %all-to-all-start.1 = ((bf16[8,8,4,16,128]{4,3,2,1,0:T(8,128)(2,1)}), bf16[8,8,4,16,128]{4,3,2,1,0:T(8,128)(2,1)S(1)}, u32[]{:S(2)}, u32[]{:S(2)}) async-start(bf16[8,8,4,16,128]{4,3,2,1,0:T(8,128)(2,1)} %shard_map.69), calls=%async_computation.1 | async-start | bytes 2097152 | tf_op jit(solution)/shard_map/all_to_all | solution.py:603
  82.2 11.2 %collective-permute-start.11 = (bf16[16,1728]{1,0:T(8,128)(2,1)S(1)}, bf16[16,1728]{1,0:T(8,128)(2,1)S(1)}, u32[]{:S(2)}, u32[]{:S(2)}) collective-permute-start(bf16[16,1728]{1,0:T(8,128)(2,1)S(1)} %get-tuple-element.83), channel_id=1, source_target_pairs={{0,2},{1,3},{2,4},{3,5},{4,6},{5,7},{6,0},{7,1},{8,10},{9,11},{10,... | collective-permute-start | bytes 165896 | tf_op jit(solution)/shard_map/ppermute | solution.py:639
  84.3 9.2 %collective-permute-start.12 = (bf16[16,1728]{1,0:T(8,128)(2,1)S(1)}, bf16[16,1728]{1,0:T(8,128)(2,1)S(1)}, u32[]{:S(2)}, u32[]{:S(2)}) collective-permute-start(bf16[16,1728]{1,0:T(8,128)(2,1)S(1)} %get-tuple-element.84), channel_id=1, source_target_pairs={{0,4},{1,5},{2,6},{3,7},{4,0},{5,1},{6,2},{7,3},{8,12},{9,13},{10,... | collective-permute-start | bytes 165896 | tf_op jit(solution)/shard_map/ppermute | solution.py:639
  86.3 7.2 %collective-permute-start.13 = (bf16[16,1728]{1,0:T(8,128)(2,1)S(1)}, bf16[16,1728]{1,0:T(8,128)(2,1)S(1)}, u32[]{:S(2)}, u32[]{:S(2)}) collective-permute-start(bf16[16,1728]{1,0:T(8,128)(2,1)S(1)} %get-tuple-element.85), channel_id=1, source_target_pairs={{0,6},{1,7},{2,0},{3,1},{4,2},{5,3},{6,4},{7,5},{8,14},{9,15},{10,... | collective-permute-start | bytes 165896 | tf_op jit(solution)/shard_map/ppermute | solution.py:639

commit v5 on v4

--- a/solution.py
+++ b/solution.py
@@ -40,6 +40,9 @@
     return jax.ShapeDtypeStruct(dims, dtype)
 
 
+TOKEN = shape((8, 128), F32)
+
+
 def down(v):
     rows = lax.broadcasted_iota(jnp.int32, v.shape, 0)
     return jnp.where(rows == 0, 0.0, pltpu.roll(v, 1, 0))
@@ -95,7 +98,8 @@
 
 
 def gather_sides(cells, prepared):
-    def kernel(cells_ref, prepared_ref, last_ref, first_ref, sems):
+    def kernel(cells_ref, prepared_ref, last_ref, first_ref, token_ref, sems):
+        token_ref[...] = prepared_ref[...]
         copies = [
             pltpu.make_async_copy(cells_ref.at[:, 3], last_ref, sems.at[0]),
             pltpu.make_async_copy(cells_ref.at[:, 0], first_ref, sems.at[1]),
@@ -107,11 +111,11 @@
 
     out = shape((8, 8, 16, 128))
     ins = [(cells, pl.ANY), (prepared, None)]
-    return call(kernel, (out, out), ins, [pltpu.SemaphoreType.DMA((2,))], 0, 1_000_000)
-
-
-def gather_edges(coords, cells, y_before, y_after):
-    def kernel(co, cells_ref, yb, ya, near_ref, far_ref):
+    return call(kernel, (out, out, TOKEN), ins, [pltpu.SemaphoreType.DMA((2,))], 0, 1_000_000)
+
+
+def gather_edges(coords, cells, y_before, y_after, token):
+    def kernel(co, cells_ref, yb, ya, token_ref, near_ref, far_ref):
         def give(last_ref, first_ref):
             for out_ref, x in ((last_ref, 7), (first_ref, 0)):
                 for f in range(8):
@@ -124,7 +128,7 @@
         pl.when(co[2] == 1)(lambda: give(far_ref, near_ref))
 
     out = shape((8, 6, 16, 128))
-    ins = [(coords, pltpu.SMEM)] + [(a, None) for a in (cells, y_before, y_after)]
+    ins = [(coords, pltpu.SMEM)] + [(a, None) for a in (cells, y_before, y_after, token)]
     return call(kernel, (out, out), ins, (), 0, 400_000)
 
 
@@ -180,7 +184,7 @@
 
     return call(
         kernel,
-        (shape((9, 512, 256)), pltpu.HBM((9, 256, 512), BF), shape((8, 128), F32)),
+        (shape((9, 512, 256)), pltpu.HBM((9, 256, 512), BF), TOKEN),
         [(weights, None)],
         [
             pltpu.VMEM((27 * 256, 128), F32),
@@ -232,32 +236,69 @@
     return value, (grad.astype(F32) * (LEAK + (1.0 - LEAK) * slope)).astype(BF)
 
 
-def forward_inner(coords, cells, y_before, y_after, fore, grad):
-    def kernel(co, cells_ref, yb, ya, fore_ref, grad_ref, field_ref, out_ref, pre_ref, total, wide):
+def forward_own(cells, fore, token):
+    def kernel(cells_ref, fore_ref, token_ref, field_ref, total_ref, done_ref):
+        def place(x, carry):
+            field_ref[x, 0:32, :] = jnp.zeros((32, 512), BF)
+            field_ref[x, 160:192, :] = jnp.zeros((32, 512), BF)
+            for y in range(4):
+                place_cell(field_ref, x, y + 1, lambda f: cells_ref[f, y, x])
+            return carry
+
+        lax.fori_loop(0, 8, place, 0)
+
+        def multiply(h, carry):
+            start = pl.multiple_of(h * 256, 256)
+            total_ref[pl.ds(start, 256), :] = convolved(
+                lambda u, i, at: field_ref[2 * h + u + i, at : at + 128, :], fore_ref
+            )
+            return carry
+
+        lax.fori_loop(0, 3, multiply, 0)
+        done_ref[...] = token_ref[...]
+
+    return call(
+        kernel,
+        (shape((8, 192, 512)), shape((768, 256), F32), TOKEN),
+        [(a, None) for a in (cells, fore, token)],
+        (),
+        4_000_000_000,
+        5_000_000,
+    )
+
+
+def forward_inner(coords, field, total, y_before, y_after, fore, grad):
+    def kernel(
+        co, own_ref, total_ref, yb, ya, fore_ref, grad_ref, field_ref, out_ref, pre_ref, sides, wide
+    ):
         y_low, y_high = co[4] > 0, co[4] < 7
 
         def place(x, carry):
+            field_ref[x, 32:160, :] = own_ref[x, 32:160, :]
             place_cell(field_ref, x, 0, lambda f: masked(yb[f, x], y_low))
             place_cell(field_ref, x, 5, lambda f: masked(ya[f, x], y_high))
-            for y in range(4):
-                place_cell(field_ref, x, y + 1, lambda f: cells_ref[f, y, x])
             return carry
 
         lax.fori_loop(0, 8, place, 0)
 
-        def multiply(h, carry):
-            start = pl.multiple_of(h * 256, 256)
-            total[pl.ds(start, 256), :] = convolved(
-                lambda u, i, at: field_ref[2 * h + u + i, at : at + 128, :], fore_ref
+        for side, (at, j, y) in enumerate(((0, 0, 0), (160, 2, 3))):
+            acc = jnp.concatenate(
+                [total_ref[x * 128 + y * 32 : x * 128 + y * 32 + 32, :] for x in range(6)], axis=0
             )
-            return carry
-
-        lax.fori_loop(0, 3, multiply, 0)
+            for i in range(3):
+                rows = [field_ref[x + i, at : at + 32, :] for x in range(6)]
+                acc = acc + jnp.dot(
+                    jnp.concatenate(rows, axis=0), fore_ref[i * 3 + j], preferred_element_type=F32
+                )
+            sides[side] = acc
 
         def finish(x, carry):
             for y in range(4):
-                start = pl.multiple_of(x * 128 + y * 32, 32)
-                value, turned = finish_cell(total, start, grad_ref[x + 1, y])
+                if y in (0, 3):
+                    source, start = sides.at[y // 3], pl.multiple_of(x * 32, 32)
+                else:
+                    source, start = total_ref, pl.multiple_of(x * 128 + y * 32, 32)
+                value, turned = finish_cell(source, start, grad_ref[x + 1, y])
                 wide[pl.ds(pl.multiple_of(x * 64 + y * 16, 16), 16), :] = value
                 pre_ref[x, y] = turned
             return carry
@@ -268,16 +309,17 @@
     return call(
         kernel,
         (shape((8, 192, 512)), shape((6, 4, 2048)), shape((6, 4, 16, 128))),
-        [(coords, pltpu.SMEM)] + [(a, None) for a in (cells, y_before, y_after, fore, grad)],
-        [pltpu.VMEM((768, 256), F32), pltpu.VMEM((384, 128), F32)],
-        4_000_000_000,
+        [(coords, pltpu.SMEM)]
+        + [(a, None) for a in (field, total, y_before, y_after, fore, grad)],
+        [pltpu.VMEM((2, 192, 256), F32), pltpu.VMEM((384, 128), F32)],
+        1_000_000_000,
         6_000_000,
     )
 
 
-def forward_outer(coords, field, x_near, x_far, fore, grad, out_inner, pre_inner):
+def forward_outer(coords, field, x_near, x_far, fore, grad, out_inner, pre_inner, token):
     def kernel(
-        co, field_ref, near_ref, far_ref, fore_ref, grad_ref, out_in, pre_in,
+        co, field_ref, near_ref, far_ref, fore_ref, grad_ref, out_in, pre_in, token_ref,
         rim_ref, out_ref, pre_ref, first_ref, last_ref, total, wide,
     ):
         y_low, y_high, x_low, x_high = co[4] > 0, co[4] < 7, co[5] > 0, co[5] < 3
@@ -325,7 +367,7 @@
             shape((8, 16, 128)),
         ),
         [(coords, pltpu.SMEM)]
-        + [(a, None) for a in (field, x_near, x_far, fore, grad, out_inner, pre_inner)],
+        + [(a, None) for a in (field, x_near, x_far, fore, grad, out_inner, pre_inner, token)],
         [pltpu.VMEM((256, 256), F32), pltpu.VMEM((128, 128), F32)],
         2_000_000_000,
         6_000_000,
@@ -341,38 +383,63 @@
     )
 
 
-def filter_grad(coords, field, rim, pre_grad):
-    def kernel(co, field_ref, rim_ref, pre_ref, keep_ref, send_ref, first, second, turned):
-        core = co[2]
-
-        def place(x, carry):
-            for y in range(4):
-                low, high = stacked_depth(pre_ref[x, y].astype(F32))
-                first[y * 32 : y * 32 + 16, :] = low[0]
-                second[y * 32 : y * 32 + 16, :] = low[1]
-                first[y * 32 + 16 : y * 32 + 32, :] = high[0]
-                second[y * 32 + 16 : y * 32 + 32, :] = high[1]
-            lanes = pl.ds(pl.multiple_of(x * 128, 128), 128)
-            turned[0:128, lanes] = first[...].T.astype(BF)
-            turned[128:192, lanes] = second[...].T[0:64].astype(BF)
-            return carry
-
-        lax.fori_loop(0, 8, place, 0)
-
-        def layer(x, rows, lanes):
-            if x in (0, 9):
-                return rim_ref[x // 9, rows, lanes]
-            return field_ref[x - 1, rows, lanes]
+def turn_grad(pre_ref, layers, first, second, turned):
+    for n, x in enumerate(layers):
+        for y in range(4):
+            low, high = stacked_depth(pre_ref[x, y].astype(F32))
+            first[y * 32 : y * 32 + 16, :] = low[0]
+            second[y * 32 : y * 32 + 16, :] = low[1]
+            first[y * 32 + 16 : y * 32 + 32, :] = high[0]
+            second[y * 32 + 16 : y * 32 + 32, :] = high[1]
+        turned[0:128, n * 128 : n * 128 + 128] = first[...].T.astype(BF)
+        turned[128:192, n * 128 : n * 128 + 128] = second[...].T[0:64].astype(BF)
+
+
+def filter_grad_inner(field, pre_inner):
+    def kernel(field_ref, pre_ref, part_ref, done_ref, first, second, turned):
+        turn_grad(pre_ref, range(6), first, second, turned)
 
         def multiply(j, carry):
             rows = pl.ds(pl.multiple_of(j * 32, 32), 128)
             for i in range(3):
                 for half in range(2):
                     lanes = slice(half * 256, half * 256 + 256)
-                    cells = [layer(x + i, rows, lanes) for x in range(8)]
+                    cells = [field_ref[x + i, rows, lanes] for x in range(6)]
                     got = jnp.dot(
                         turned[...], jnp.concatenate(cells, axis=0), preferred_element_type=F32
-                    ) * SCALE
+                    )
+                    part_ref[i * 3 + j, :, lanes] = got.astype(part_ref.dtype)
+            return carry
+
+        lax.fori_loop(0, 3, multiply, 0)
+        done_ref[...] = first[0:8, :]
+
+    return call(
+        kernel,
+        (shape((9, 192, 512)), TOKEN),
+        [(field, None), (pre_inner, None)],
+        [pltpu.VMEM((128, 128), F32), pltpu.VMEM((128, 128), F32), pltpu.VMEM((192, 768), BF)],
+        3_000_000_000,
+        0,
+    )
+
+
+def filter_grad(coords, field, rim, pre_grad, part):
+    def kernel(co, field_ref, rim_ref, pre_ref, part_ref, keep_ref, send_ref, first, second, turned):
+        core = co[2]
+        turn_grad(pre_ref, (0, 7), first, second, turned)
+
+        def multiply(j, carry):
+            rows = pl.ds(pl.multiple_of(j * 32, 32), 128)
+            for i in range(3):
+                for half in range(2):
+                    lanes = slice(half * 256, half * 256 + 256)
+                    low = field_ref[i - 1, rows, lanes] if i else rim_ref[0, rows, lanes]
+                    high = field_ref[6 + i, rows, lanes] if i < 2 else rim_ref[1, rows, lanes]
+                    got = jnp.dot(
+                        turned[...], jnp.concatenate([low, high], axis=0), preferred_element_type=F32
+                    )
+                    got = (got + part_ref[i * 3 + j, :, lanes].astype(F32)) * SCALE
                     left, right = got[:, :128], got[:, 128:]
                     keep_ref[half, i * 3 + j] = jnp.where(core == 0, left, right)
                     send_ref[half, i * 3 + j] = jnp.where(core == 0, right, left).astype(BF)
@@ -383,8 +450,8 @@
     return call(
         kernel,
         (shape((2, 9, 192, 128), F32), shape((2, 9, 192, 128))),
-        [(coords, pltpu.SMEM), (field, None), (rim, None), (pre_grad, None)],
-        [pltpu.VMEM((128, 128), F32), pltpu.VMEM((128, 128), F32), pltpu.VMEM((192, 1024), BF)],
+        [(coords, pltpu.SMEM)] + [(a, None) for a in (field, rim, pre_grad, part)],
+        [pltpu.VMEM((128, 128), F32), pltpu.VMEM((128, 128), F32), pltpu.VMEM((192, 256), BF)],
         COST[3],
         0,
     )
@@ -611,17 +678,20 @@
     cells = exchange(cells, "filt")
     fore, back, prepared = prepare_weights(weights[0])
     grad = prepare_field(out_grad[0, 0])
-    y_before, y_after = both_ways(*gather_sides(cells, prepared), "sy", 8)
-    near, far = gather_edges(coords, cells, y_before, y_after)
-    near, far, cells = lax.optimization_barrier((near, far, cells))
+    last, first, token = gather_sides(cells, prepared)
+    y_before, y_after = both_ways(last, first, "sy", 8)
+    field, total, token = forward_own(cells, fore, token)
+    near, far = gather_edges(coords, cells, y_before, y_after, token)
+    near, far, total = lax.optimization_barrier((near, far, total))
     x_near, x_far = x_rims(near, far)
-    field, out_inner, pre_inner = forward_inner(coords, cells, y_before, y_after, fore, grad)
+    field, out_inner, pre_inner = forward_inner(coords, field, total, y_before, y_after, fore, grad)
+    part, token = filter_grad_inner(field, pre_inner)
     rim, outputs, pre_grad, g_first, g_last = forward_outer(
-        coords, field, x_near, x_far, fore, grad, out_inner, pre_inner
+        coords, field, x_near, x_far, fore, grad, out_inner, pre_inner, token
     )
 
     gy_before, gy_after = both_ways(g_last, g_first, "sy", 8)
-    keep, send = filter_grad(coords, field, rim, pre_grad)
+    keep, send = filter_grad(coords, field, rim, pre_grad, part)
     got = lax.ppermute(send, "sx", [(i, i ^ 1) for i in range(4)])
     stay, send = add_cores(coords, keep, got)
     stay, pre_grad, gy_before, gy_after = lax.optimization_barrier((stay, pre_grad, gy_before, gy_after))

time: 95.1 us -> 90.7 us (0.954)
  waiting for transfers between devices: 20.4 us -> 17.1 us
  local copies, waits for them, and re-layouts: 4.24 us -> 2.58 us
    ppermute x2, waiting for transfers between devices: 5.54 us -> 2.6 us  [both_ways(): lax.ppermute(last, axis, [(i, (i + 1) % size) for i in range(size)])]
    unnamed x12 -> x8, local copies, waits for them, and re-layouts: 4.15 us -> 2.49 us
    pallas_call x16 -> x18, Pallas kernels: 31 us -> 31.6 us  [call(): pl.pallas_call(kernel, out_shape=outs, in_specs=[pl.BlockSpec(memory_spac...]
  transfers between devices with their start and end apart: 16 -> 16, of which waited for: 5 -> 5; matrix products, arithmetic and copies ran while one was open for 0% -> 0% of each run, Pallas kernels for 22% -> 27%
where the time goes in v5:
time: 90.7 us; the launch traced here: 89.9 us
  starting transfers between devices  37.7 us (42%)
  Pallas kernels  31.6 us (35%)
  waiting for transfers between devices  17.1 us (19%)
  local copies, waits for them, and re-layouts  2.58 us (3%)
    pallas_call x18, Pallas kernels, call(): pl.pallas_call(kernel, out_shape=outs, in_specs=[pl.BlockSpec(memory_spac...  31.6 us
    all_to_all x2, starting transfers between devices, exchange(): return lax.all_to_all(parts, axis, 0, 0)  9.52 us
    all_to_all x2, waiting for transfers between devices, exchange(): return lax.all_to_all(parts, axis, 0, 0)  8.74 us
    ppermute x2, starting transfers between devices, x_rims(): lax.ppermute(far, 'sx', [(1, 2), (2, 1)])  7.6 us
    ppermute x3, starting transfers between devices, per_device(): lax.ppermute(regions[d], 'sy', [(i, (i + 2 * d) % 8) for i in range(8)])  7.58 us
    ppermute x2, starting transfers between devices, both_ways(): lax.ppermute(first, axis, [((i + 1) % size, i) for i in range(size)])  6.86 us
    ppermute x2, waiting for transfers between devices, x_rims(): lax.ppermute(far, 'sx', [(1, 2), (2, 1)])  3.34 us
    ppermute x2, waiting for transfers between devices, both_ways(): lax.ppermute(last, axis, [(i, (i + 1) % size) for i in range(size)])  2.6 us
  transfers between devices with their start and end apart: 16, of which 5 were waited for; matrix products, arithmetic and copies ran while one was open for 0% of the time, Pallas kernels for 27%

profile of v5, /device:TPU:1, one launch (start us, length us, event | category | flops | bytes accessed | tf_op | source)
XLA Modules:
  0.0 89.9 jit_solution(6870976006248560769)
XLA Ops:
  0.6 0.0 copy-start.2
  0.6 0.9 copy-done.2
  1.5 0.0 copy-start.3
  1.5 1.2 %shard_map.58 = bf16[8,4,8,16,128]{4,3,2,1,0:T(8,128)(2,1)} custom-call(bf16[8,4,2048]{2,1,0:T(4,128)(2,1)S(1)} %bitcast.13), custom_call_target="tpu_custom_call" | custom-call | bytes 1300000 | tf_op jit(solution)/shard_map/pallas_call | solution.py:20
  2.7 5.9 %all-to-all-start = ((bf16[8,4,8,16,128]{4,3,2,1,0:T(8,128)(2,1)}), bf16[8,4,8,16,128]{4,3,2,1,0:T(8,128)(2,1)S(1)}, u32[]{:S(2)}, u32[]{:S(2)}) async-start(bf16[8,4,8,16,128]{4,3,2,1,0:T(8,128)(2,1)} %shard_map.58), calls=%async_computation | async-start | bytes 2097152 | tf_op jit(solution)/shard_map/all_to_all | solution.py:670
  8.7 0.0 copy-done.3
  8.7 0.1 shard_map.63.grad_ref
  8.8 0.0 copy-start.1
  8.8 1.6 %copy-done.1 = bf16[1,27,32768]{2,1,0:T(8,128)(2,1)S(1)} copy-done((bf16[1,27,32768]{2,1,0:T(8,128)(2,1)S(1)}, bf16[1,27,32768]{2,1,0:T(8,128)(2,1)}, u32[]{:S(2)}) %copy-start.1) | copy-done | bytes 1769496
  10.4 7.1 %shard_map.59 = (bf16[9,512,256]{2,1,0:T(8,128)(2,1)S(1)}, bf16[9,256,512]{2,1,0:T(8,128)(2,1)}, f32[8,128]{1,0:T(8,128)S(1)}) custom-call(bf16[27,32768]{1,0:T(8,128)(2,1)S(1)} %bitcast.12), custom_call_target="tpu_custom_call" | custom-call | bytes 8000000 | tf_op jit(solution)/shard_map/pallas_call | solution.py:20
  17.5 0.1 stack.27.co
  17.6 6.0 %all-to-all-done.cells_ref = bf16[8,4,8,16,128]{4,3,2,1,0:T(8,128)(2,1)S(1)} async-done(((bf16[8,4,8,16,128]{4,3,2,1,0:T(8,128)(2,1)}), bf16[8,4,8,16,128]{4,3,2,1,0:T(8,128)(2,1)S(1)}, u32[]{:S(2)}, u32[]{:S(2)}) %all-to-all-start) | async-done | bytes 1048608 | tf_op jit(solution)/shard_map/all_to_all | solution.py:670
  23.6 0.1 shard_map.60
  23.7 1.7 %collective-permute-start = (bf16[8,8,16,128]{3,2,1,0:T(8,128)(2,1)S(1)}, bf16[8,8,16,128]{3,2,1,0:T(8,128)(2,1)S(1)}, u32[]{:S(2)}, u32[]{:S(2)}) collective-permute-start(bf16[8,8,16,128]{3,2,1,0:T(8,128)(2,1)S(1)} %get-tuple-element.59), channel_id=1, source_target_pairs={{0,1},{1,2},{2,3},{3,4},{4,5},{5,6},{6,7},{7,0},{8,9},{9,10},{10,1... | collective-permute-start | bytes 786440 | tf_op jit(solution)/shard_map/ppermute | solution.py:657
  25.4 4.0 %collective-permute-start.1 = (bf16[8,8,16,128]{3,2,1,0:T(8,128)(2,1)S(1)}, bf16[8,8,16,128]{3,2,1,0:T(8,128)(2,1)S(1)}, u32[]{:S(2)}, u32[]{:S(2)}) collective-permute-start(bf16[8,8,16,128]{3,2,1,0:T(8,128)(2,1)S(1)} %get-tuple-element.60), channel_id=1, source_target_pairs={{1,0},{2,1},{3,2},{4,3},{5,4},{6,5},{7,6},{0,7},{9,8},{10,9},{11,1... | collective-permute-start | bytes 786440 | tf_op jit(solution)/shard_map/ppermute | solution.py:658
  29.4 3.1 %shard_map.61 = (bf16[8,192,512]{2,1,0:T(8,128)(2,1)S(1)}, f32[768,256]{1,0:T(8,128)S(1)}, f32[8,128]{1,0:T(8,128)S(1)}) custom-call(bf16[8,4,8,16,128]{4,3,2,1,0:T(8,128)(2,1)S(1)} %all-to-all-done.cells_ref, bf16[9,512,256]{2,1,0:T(8,128)(2,1)S(1)} %get-tuple-element.55.fore_ref, f32[8,128]{1,0:T(8,128)S(1)} %get-tuple-element.57.token_ref), custom_call_target="tpu_custom_call" | custom-call | flops 4000000000 | bytes 5000000 | tf_op jit(solution)/shard_map/pallas_call | solution.py:20
  32.6 2.6 %collective-permute-done.yb = bf16[8,8,16,128]{3,2,1,0:T(8,128)(2,1)S(1)} collective-permute-done((bf16[8,8,16,128]{3,2,1,0:T(8,128)(2,1)S(1)}, bf16[8,8,16,128]{3,2,1,0:T(8,128)(2,1)S(1)}, u32[]{:S(2)}, u32[]{:S(2)}) %collective-permute-start) | collective-permute-done | bytes 262176 | tf_op jit(solution)/shard_map/ppermute | solution.py:657
  35.1 0.0 collective-permute-done.1.ya
  35.2 0.6 shard_map.62
  35.7 1.5 %collective-permute-start.2 = (bf16[8,6,16,128]{3,2,1,0:T(8,128)(2,1)S(1)}, bf16[8,6,16,128]{3,2,1,0:T(8,128)(2,1)S(1)}, u32[]{:S(2)}, u32[]{:S(2)}) collective-permute-start(bf16[8,6,16,128]{3,2,1,0:T(8,128)(2,1)S(1)} %get-tuple-element.68), channel_id=1, source_target_pairs={{0,8},{8,0},{16,24},{24,16},{1,9},{9,1},{17,25},{25,17},{2,10},{10... | collective-permute-start | bytes 589832 | tf_op jit(solution)/shard_map/ppermute | solution.py:664
  37.2 4.3 %collective-permute-start.3 = (bf16[8,6,16,128]{3,2,1,0:T(8,128)(2,1)S(1)}, bf16[8,6,16,128]{3,2,1,0:T(8,128)(2,1)S(1)}, u32[]{:S(2)}, u32[]{:S(2)}) collective-permute-start(bf16[8,6,16,128]{3,2,1,0:T(8,128)(2,1)S(1)} %get-tuple-element.69), channel_id=1, source_target_pairs={{8,16},{16,8},{9,17},{17,9},{10,18},{18,10},{11,19},{19,11},{12,20... | collective-permute-start | bytes 589832 | tf_op jit(solution)/shard_map/ppermute | solution.py:665
  41.5 2.6 %shard_map.64 = (bf16[8,192,512]{2,1,0:T(8,128)(2,1)S(1)}, bf16[6,4,2048]{2,1,0:T(4,128)(2,1)S(1)}, bf16[6,4,16,128]{3,2,1,0:T(8,128)(2,1)S(1)}) custom-call(s32[8]{0:T(128)S(1)} %stack.27.co, bf16[8,192,512]{2,1,0:T(8,128)(2,1)S(1)} %get-tuple-element.58.own_ref, f32[768,256]{1,0:T(8,128)S(1)} %get-tuple-element.65.total_ref, ...), custom_call_target="tpu_custom_call" | custom-call | flops 1000000000 | bytes 6000000 | tf_op jit(solution)/shard_map/pallas_call | solution.py:20
  44.1 2.2 %shard_map.65 = (bf16[9,192,512]{2,1,0:T(8,128)(2,1)S(1)}, f32[8,128]{1,0:T(8,128)S(1)}) custom-call(bf16[8,192,512]{2,1,0:T(8,128)(2,1)S(1)} %get-tuple-element.67.field_ref, bf16[6,4,16,128]{3,2,1,0:T(8,128)(2,1)S(1)} %get-tuple-element.71.pre_ref.pre_in), custom_call_target="tpu_custom_call" | custom-call | flops 3000000000 | tf_op jit(solution)/shard_map/pallas_call | solution.py:20
  46.3 0.0 collective-permute-done.2.near_ref
  46.3 0.0 collective-permute-done.3.far_ref
  46.3 2.2 %shard_map.66 = (bf16[2,192,512]{2,1,0:T(8,128)(2,1)S(1)}, bf16[8,4,2048]{2,1,0:T(4,128)(2,1)}, bf16[8,4,16,128]{3,2,1,0:T(8,128)(2,1)S(1)}, bf16[8,16,128]{2,1,0:T(8,128)(2,1)S(1)}, bf16[8,16,128]{2,1,0:T(8,128)(2,1)S(1)}) custom-call(s32[8]{0:T(128)S(1)} %stack.27.co, bf16[8,192,512]{2,1,0:T(8,128)(2,1)S(1)} %get-tuple-element.67.field_ref, ...), custom_call_target="tpu_custom_call" | custom-call | flops 2000000000 | bytes 6000000 | tf_op jit(solution)/shard_map/pallas_call | solution.py:20
  48.5 1.8 %shard_map.67 = (f32[2,9,192,128]{3,2,1,0:T(8,128)S(1)}, bf16[2,9,192,128]{3,2,1,0:T(8,128)(2,1)S(1)}) custom-call(s32[8]{0:T(128)S(1)} %stack.27.co, bf16[8,192,512]{2,1,0:T(8,128)(2,1)S(1)} %get-tuple-element.67.field_ref, bf16[2,192,512]{2,1,0:T(8,128)(2,1)S(1)} %get-tuple-element.74.rim_ref, bf16[8,4,16,128]{3,2,1,0:T(8,128)(2,1)S(1)} %get-tuple-element.82.pre_ref, ...), custom_call_target="tpu_custom_call" | custom-call | flops 5000000000 | tf_op jit(solution)/shard_map/pallas_call | solution.py:20
  50.3 0.1 collective-permute-start.4
  50.4 0.1 collective-permute-start.5
  50.5 2.8 %collective-permute-start.6 = (bf16[8,16,128]{2,1,0:T(8,128)(2,1)S(1)}, bf16[8,16,128]{2,1,0:T(8,128)(2,1)S(1)}, u32[]{:S(2)}, u32[]{:S(2)}) collective-permute-start(bf16[8,16,128]{2,1,0:T(8,128)(2,1)S(1)} %get-tuple-element.81), channel_id=1, source_target_pairs={{1,0},{2,1},{3,2},{4,3},{5,4},{6,5},{7,6},{0,7},{9,8},{10,9},{11,1... | collective-permute-start | bytes 98312 | tf_op jit(solution)/shard_map/ppermute | solution.py:658
  53.3 0.0 collective-permute-done.4.got_ref
  53.3 0.0 copy-start
  53.3 0.7 shard_map.68
  54.0 1.8 %collective-permute-start.9 = (bf16[9,192,128]{2,1,0:T(8,128)(2,1)S(1)}, bf16[9,192,128]{2,1,0:T(8,128)(2,1)S(1)}, u32[]{:S(2)}, u32[]{:S(2)}) collective-permute-start(bf16[9,192,128]{2,1,0:T(8,128)(2,1)S(1)} %get-tuple-element.88), channel_id=1, source_target_pairs={{0,16},{8,24},{16,0},{24,8},{1,17},{9,25},{17,1},{25,9},{2,18},{10... | collective-permute-start | bytes 1327112 | tf_op jit(solution)/shard_map/ppermute | solution.py:698
  55.8 0.0 collective-permute-done.5.yb
  55.8 0.0 collective-permute-done.6.ya
  55.8 0.6 shard_map.69
  56.3 0.9 %collective-permute-start.7 = (bf16[6,16,128]{2,1,0:T(8,128)(2,1)S(1)}, bf16[6,16,128]{2,1,0:T(8,128)(2,1)S(1)}, u32[]{:S(2)}, u32[]{:S(2)}) collective-permute-start(bf16[6,16,128]{2,1,0:T(8,128)(2,1)S(1)} %get-tuple-element.85), channel_id=1, source_target_pairs={{0,8},{8,0},{16,24},{24,16},{1,9},{9,1},{17,25},{25,17},{2,10},{10... | collective-permute-start | bytes 73736 | tf_op jit(solution)/shard_map/ppermute | solution.py:664
  57.3 3.3 %collective-permute-start.8 = (bf16[6,16,128]{2,1,0:T(8,128)(2,1)S(1)}, bf16[6,16,128]{2,1,0:T(8,128)(2,1)S(1)}, u32[]{:S(2)}, u32[]{:S(2)}) collective-permute-start(bf16[6,16,128]{2,1,0:T(8,128)(2,1)S(1)} %get-tuple-element.86), channel_id=1, source_target_pairs={{8,16},{16,8},{9,17},{17,9},{10,18},{18,10},{11,19},{19,11},{12,20... | collective-permute-start | bytes 73736 | tf_op jit(solution)/shard_map/ppermute | solution.py:665
  60.6 0.0 copy-done
  60.6 3.8 %shard_map.70.inner_ref = bf16[8,6,4,16,128]{4,3,2,1,0:T(8,128)(2,1)S(1)} custom-call(s32[8]{0:T(128)S(1)} %stack.27.co, bf16[8,4,16,128]{3,2,1,0:T(8,128)(2,1)S(1)} %get-tuple-element.82.pre_ref, bf16[8,16,128]{2,1,0:T(8,128)(2,1)S(1)} %collective-permute-done.5.yb, bf16[8,16,128]{2,1,0:T(8,128)(2,1)S(1)} %collective-permute-done.6.ya, ...), custom_call_target="tpu_custom_call" | custom-call | flops 4000000000 | tf_op jit(solution)/shard_map/pallas_call | solution.py:20
  64.4 0.0 collective-permute-done.7.near_ref
  64.5 3.3 %collective-permute-done.8.far_ref = bf16[6,16,128]{2,1,0:T(8,128)(2,1)S(1)} collective-permute-done((bf16[6,16,128]{2,1,0:T(8,128)(2,1)S(1)}, bf16[6,16,128]{2,1,0:T(8,128)(2,1)S(1)}, u32[]{:S(2)}, u32[]{:S(2)}) %collective-permute-start.8) | collective-permute-done | bytes 24608 | tf_op jit(solution)/shard_map/ppermute | solution.py:665
  67.8 2.4 %shard_map.71 = bf16[8,8,4,16,128]{4,3,2,1,0:T(8,128)(2,1)} custom-call(s32[8]{0:T(128)S(1)} %stack.27.co, bf16[8,4,16,128]{3,2,1,0:T(8,128)(2,1)S(1)} %get-tuple-element.82.pre_ref, bf16[8,16,128]{2,1,0:T(8,128)(2,1)S(1)} %collective-permute-done.5.yb, bf16[8,16,128]{2,1,0:T(8,128)(2,1)S(1)} %collective-permute-done.6.ya, ...), custom_call_target="tpu_custom_call" | custom-call | flops 500000000 | tf_op jit(solution)/shard_map/pallas_call | solution.py:20
  70.2 0.0 collective-permute-done.9.got_ref
  70.2 0.9 %shard_map.73 = (f32[4,16,1728]{2,1,0:T(8,128)S(1)}, bf16[4,16,1728]{2,1,0:T(8,128)(2,1)S(1)}) custom-call(s32[8]{0:T(128)S(1)} %stack.27.co, f32[9,192,128]{2,1,0:T(8,128)S(1)} %get-tuple-element.90.stay_ref, bf16[9,192,128]{2,1,0:T(8,128)(2,1)S(1)} %collective-permute-done.9.got_ref), custom_call_target="tpu_custom_call" | custom-call | flops 20000000000 | bytes 2000000 | tf_op jit(solution)/shard_map/pallas_call | solution.py:20
  71.2 0.1 collective-permute-start.10
  71.3 3.6 %all-to-all-start.1 = ((bf16[8,8,4,16,128]{4,3,2,1,0:T(8,128)(2,1)}), bf16[8,8,4,16,128]{4,3,2,1,0:T(8,128)(2,1)S(1)}, u32[]{:S(2)}, u32[]{:S(2)}) async-start(bf16[8,8,4,16,128]{4,3,2,1,0:T(8,128)(2,1)} %shard_map.71), calls=%async_computation.1 | async-start | bytes 2097152 | tf_op jit(solution)/shard_map/all_to_all | solution.py:670
  74.8 2.4 %collective-permute-done.10.got_ref = bf16[4,16,1728]{2,1,0:T(8,128)(2,1)S(1)} collective-permute-done((bf16[4,16,1728]{2,1,0:T(8,128)(2,1)S(1)}, bf16[4,16,1728]{2,1,0:T(8,128)(2,1)S(1)}, u32[]{:S(2)}, u32[]{:S(2)}) %collective-permute-start.10) | collective-permute-done | bytes 221216 | tf_op jit(solution)/shard_map/ppermute | solution.py:706
  77.3 0.6 shard_map.74
  77.9 2.1 %collective-permute-start.11 = (bf16[16,1728]{1,0:T(8,128)(2,1)S(1)}, bf16[16,1728]{1,0:T(8,128)(2,1)S(1)}, u32[]{:S(2)}, u32[]{:S(2)}) collective-permute-start(bf16[16,1728]{1,0:T(8,128)(2,1)S(1)} %get-tuple-element.95), channel_id=1, source_target_pairs={{0,2},{1,3},{2,4},{3,5},{4,6},{5,7},{6,0},{7,1},{8,10},{9,11},{10,... | collective-permute-start | bytes 165896 | tf_op jit(solution)/shard_map/ppermute | solution.py:709
  80.0 2.0 %collective-permute-start.12 = (bf16[16,1728]{1,0:T(8,128)(2,1)S(1)}, bf16[16,1728]{1,0:T(8,128)(2,1)S(1)}, u32[]{:S(2)}, u32[]{:S(2)}) collective-permute-start(bf16[16,1728]{1,0:T(8,128)(2,1)S(1)} %get-tuple-element.96), channel_id=1, source_target_pairs={{0,4},{1,5},{2,6},{3,7},{4,0},{5,1},{6,2},{7,3},{8,12},{9,13},{10,... | collective-permute-start | bytes 165896 | tf_op jit(solution)/shard_map/ppermute | solution.py:709
  82.0 3.5 %collective-permute-start.13 = (bf16[16,1728]{1,0:T(8,128)(2,1)S(1)}, bf16[16,1728]{1,0:T(8,128)(2,1)S(1)}, u32[]{:S(2)}, u32[]{:S(2)}) collective-permute-start(bf16[16,1728]{1,0:T(8,128)(2,1)S(1)} %get-tuple-element.97), channel_id=1, source_target_pairs={{0,6},{1,7},{2,0},{3,1},{4,2},{5,3},{6,4},{7,5},{8,14},{9,15},{10,... | collective-permute-start | bytes 165896 | tf_op jit(solution)/shard_map/ppermute | solution.py:709
  85.5 2.8 %all-to-all-done.1.parts_ref = bf16[8,8,4,16,128]{4,3,2,1,0:T(8,128)(2,1)S(1)} async-done(((bf16[8,8,4,16,128]{4,3,2,1,0:T(8,128)(2,1)}), bf16[8,8,4,16,128]{4,3,2,1,0:T(8,128)(2,1)S(1)}, u32[]{:S(2)}, u32[]{:S(2)}) %all-to-all-start.1) | async-done | bytes 1048608 | tf_op jit(solution)/shard_map/all_to_all | solution.py:670
  88.2 0.9 %shard_map.72 = bf16[8,4,2048]{2,1,0:T(4,128)(2,1)} custom-call(bf16[8,8,4,16,128]{4,3,2,1,0:T(8,128)(2,1)S(1)} %all-to-all-done.1.parts_ref), custom_call_target="tpu_custom_call" | custom-call | bytes 1200000 | tf_op jit(solution)/shard_map/pallas_call | solution.py:20
  89.1 0.0 collective-permute-done.11.refs_1_
  89.1 0.0 collective-permute-done.12.refs_2_
  89.1 0.0 collective-permute-done.13.refs_3_
  89.1 0.8 shard_map.75
  (1 shorter events, 0.0 us)
Async XLA Ops:
  0.6 0.9 %copy-start.2 = (bf16[1,1,8,4,2048]{4,3,2,1,0:T(4,128)(2,1)S(1)}, bf16[1,1,8,4,2048]{4,3,2,1,0:T(4,128)(2,1)}, u32[]{:S(2)}) copy-start(bf16[1,1,8,4,2048]{4,3,2,1,0:T(4,128)(2,1)} %param.3) | copy-start | bytes 393220
  1.5 7.1 %copy-start.3 = (bf16[1,1,8,4,2048]{4,3,2,1,0:T(4,128)(2,1)S(1)}, bf16[1,1,8,4,2048]{4,3,2,1,0:T(4,128)(2,1)}, u32[]{:S(2)}) copy-start(bf16[1,1,8,4,2048]{4,3,2,1,0:T(4,128)(2,1)} %param.5) | copy-start | bytes 393220
  2.7 20.9 %all-to-all-start = ((bf16[8,4,8,16,128]{4,3,2,1,0:T(8,128)(2,1)}), bf16[8,4,8,16,128]{4,3,2,1,0:T(8,128)(2,1)S(1)}, u32[]{:S(2)}, u32[]{:S(2)}) async-start(bf16[8,4,8,16,128]{4,3,2,1,0:T(8,128)(2,1)} %shard_map.58), calls=%async_computation | async-start | bytes 2097152 | tf_op jit(solution)/shard_map/all_to_all | solution.py:670
  8.8 1.6 %copy-start.1 = (bf16[1,27,32768]{2,1,0:T(8,128)(2,1)S(1)}, bf16[1,27,32768]{2,1,0:T(8,128)(2,1)}, u32[]{:S(2)}) copy-start(bf16[1,27,32768]{2,1,0:T(8,128)(2,1)} %param.4) | copy-start | bytes 5308420
  23.7 11.5 %collective-permute-start = (bf16[8,8,16,128]{3,2,1,0:T(8,128)(2,1)S(1)}, bf16[8,8,16,128]{3,2,1,0:T(8,128)(2,1)S(1)}, u32[]{:S(2)}, u32[]{:S(2)}) collective-permute-start(bf16[8,8,16,128]{3,2,1,0:T(8,128)(2,1)S(1)} %get-tuple-element.59), channel_id=1, source_target_pairs={{0,1},{1,2},{2,3},{3,4},{4,5},{5,6},{6,7},{7,0},{8,9},{9,10},{10,1... | collective-permute-start | bytes 786440 | tf_op jit(solution)/shard_map/ppermute | solution.py:657
  25.4 9.8 %collective-permute-start.1 = (bf16[8,8,16,128]{3,2,1,0:T(8,128)(2,1)S(1)}, bf16[8,8,16,128]{3,2,1,0:T(8,128)(2,1)S(1)}, u32[]{:S(2)}, u32[]{:S(2)}) collective-permute-start(bf16[8,8,16,128]{3,2,1,0:T(8,128)(2,1)S(1)} %get-tuple-element.60), channel_id=1, source_target_pairs={{1,0},{2,1},{3,2},{4,3},{5,4},{6,5},{7,6},{0,7},{9,8},{10,9},{11,1... | collective-permute-start | bytes 786440 | tf_op jit(solution)/shard_map/ppermute | solution.py:658
  35.7 10.6 %collective-permute-start.2 = (bf16[8,6,16,128]{3,2,1,0:T(8,128)(2,1)S(1)}, bf16[8,6,16,128]{3,2,1,0:T(8,128)(2,1)S(1)}, u32[]{:S(2)}, u32[]{:S(2)}) collective-permute-start(bf16[8,6,16,128]{3,2,1,0:T(8,128)(2,1)S(1)} %get-tuple-element.68), channel_id=1, source_target_pairs={{0,8},{8,0},{16,24},{24,16},{1,9},{9,1},{17,25},{25,17},{2,10},{10... | collective-permute-start | bytes 589832 | tf_op jit(solution)/shard_map/ppermute | solution.py:664
  37.2 9.1 %collective-permute-start.3 = (bf16[8,6,16,128]{3,2,1,0:T(8,128)(2,1)S(1)}, bf16[8,6,16,128]{3,2,1,0:T(8,128)(2,1)S(1)}, u32[]{:S(2)}, u32[]{:S(2)}) collective-permute-start(bf16[8,6,16,128]{3,2,1,0:T(8,128)(2,1)S(1)} %get-tuple-element.69), channel_id=1, source_target_pairs={{8,16},{16,8},{9,17},{17,9},{10,18},{18,10},{11,19},{19,11},{12,20... | collective-permute-start | bytes 589832 | tf_op jit(solution)/shard_map/ppermute | solution.py:665
  50.3 3.0 %collective-permute-start.4 = (bf16[2,9,192,128]{3,2,1,0:T(8,128)(2,1)S(1)}, bf16[2,9,192,128]{3,2,1,0:T(8,128)(2,1)S(1)}, u32[]{:S(2)}, u32[]{:S(2)}) collective-permute-start(bf16[2,9,192,128]{3,2,1,0:T(8,128)(2,1)S(1)} %get-tuple-element.78), channel_id=1, source_target_pairs={{0,8},{8,0},{16,24},{24,16},{1,9},{9,1},{17,25},{25,17},{2,10},{10... | collective-permute-start | bytes 2654216 | tf_op jit(solution)/shard_map/ppermute | solution.py:695
  50.4 5.4 %collective-permute-start.5 = (bf16[8,16,128]{2,1,0:T(8,128)(2,1)S(1)}, bf16[8,16,128]{2,1,0:T(8,128)(2,1)S(1)}, u32[]{:S(2)}, u32[]{:S(2)}) collective-permute-start(bf16[8,16,128]{2,1,0:T(8,128)(2,1)S(1)} %get-tuple-element.80), channel_id=1, source_target_pairs={{0,1},{1,2},{2,3},{3,4},{4,5},{5,6},{6,7},{7,0},{8,9},{9,10},{10,1... | collective-permute-start | bytes 98312 | tf_op jit(solution)/shard_map/ppermute | solution.py:657
  50.5 5.3 %collective-permute-start.6 = (bf16[8,16,128]{2,1,0:T(8,128)(2,1)S(1)}, bf16[8,16,128]{2,1,0:T(8,128)(2,1)S(1)}, u32[]{:S(2)}, u32[]{:S(2)}) collective-permute-start(bf16[8,16,128]{2,1,0:T(8,128)(2,1)S(1)} %get-tuple-element.81), channel_id=1, source_target_pairs={{1,0},{2,1},{3,2},{4,3},{5,4},{6,5},{7,6},{0,7},{9,8},{10,9},{11,1... | collective-permute-start | bytes 98312 | tf_op jit(solution)/shard_map/ppermute | solution.py:658
  53.3 7.3 %copy-start = (bf16[9,256,512]{2,1,0:T(8,128)(2,1)S(1)}, bf16[9,256,512]{2,1,0:T(8,128)(2,1)}, u32[]{:S(2)}) copy-start(bf16[9,256,512]{2,1,0:T(8,128)(2,1)} %get-tuple-element.87.back_ref) | copy-start | bytes 7077892
  54.0 16.2 %collective-permute-start.9 = (bf16[9,192,128]{2,1,0:T(8,128)(2,1)S(1)}, bf16[9,192,128]{2,1,0:T(8,128)(2,1)S(1)}, u32[]{:S(2)}, u32[]{:S(2)}) collective-permute-start(bf16[9,192,128]{2,1,0:T(8,128)(2,1)S(1)} %get-tuple-element.88), channel_id=1, source_target_pairs={{0,16},{8,24},{16,0},{24,8},{1,17},{9,25},{17,1},{25,9},{2,18},{10... | collective-permute-start | bytes 1327112 | tf_op jit(solution)/shard_map/ppermute | solution.py:698
  56.3 8.1 %collective-permute-start.7 = (bf16[6,16,128]{2,1,0:T(8,128)(2,1)S(1)}, bf16[6,16,128]{2,1,0:T(8,128)(2,1)S(1)}, u32[]{:S(2)}, u32[]{:S(2)}) collective-permute-start(bf16[6,16,128]{2,1,0:T(8,128)(2,1)S(1)} %get-tuple-element.85), channel_id=1, source_target_pairs={{0,8},{8,0},{16,24},{24,16},{1,9},{9,1},{17,25},{25,17},{2,10},{10... | collective-permute-start | bytes 73736 | tf_op jit(solution)/shard_map/ppermute | solution.py:664
  57.3 10.5 %collective-permute-start.8 = (bf16[6,16,128]{2,1,0:T(8,128)(2,1)S(1)}, bf16[6,16,128]{2,1,0:T(8,128)(2,1)S(1)}, u32[]{:S(2)}, u32[]{:S(2)}) collective-permute-start(bf16[6,16,128]{2,1,0:T(8,128)(2,1)S(1)} %get-tuple-element.86), channel_id=1, source_target_pairs={{8,16},{16,8},{9,17},{17,9},{10,18},{18,10},{11,19},{19,11},{12,20... | collective-permute-start | bytes 73736 | tf_op jit(solution)/shard_map/ppermute | solution.py:665
  71.2 6.1 %collective-permute-start.10 = (bf16[4,16,1728]{2,1,0:T(8,128)(2,1)S(1)}, bf16[4,16,1728]{2,1,0:T(8,128)(2,1)S(1)}, u32[]{:S(2)}, u32[]{:S(2)}) collective-permute-start(bf16[4,16,1728]{2,1,0:T(8,128)(2,1)S(1)} %get-tuple-element.93), channel_id=1, source_target_pairs={{0,1},{1,0},{2,3},{3,2},{4,5},{5,4},{6,7},{7,6},{8,9},{9,8},{10,11... | collective-permute-start | bytes 663560 | tf_op jit(solution)/shard_map/ppermute | solution.py:706
  71.3 17.0 %all-to-all-start.1 = ((bf16[8,8,4,16,128]{4,3,2,1,0:T(8,128)(2,1)}), bf16[8,8,4,16,128]{4,3,2,1,0:T(8,128)(2,1)S(1)}, u32[]{:S(2)}, u32[]{:S(2)}) async-start(bf16[8,8,4,16,128]{4,3,2,1,0:T(8,128)(2,1)} %shard_map.71), calls=%async_computation.1 | async-start | bytes 2097152 | tf_op jit(solution)/shard_map/all_to_all | solution.py:670
  77.9 11.3 %collective-permute-start.11 = (bf16[16,1728]{1,0:T(8,128)(2,1)S(1)}, bf16[16,1728]{1,0:T(8,128)(2,1)S(1)}, u32[]{:S(2)}, u32[]{:S(2)}) collective-permute-start(bf16[16,1728]{1,0:T(8,128)(2,1)S(1)} %get-tuple-element.95), channel_id=1, source_target_pairs={{0,2},{1,3},{2,4},{3,5},{4,6},{5,7},{6,0},{7,1},{8,10},{9,11},{10,... | collective-permute-start | bytes 165896 | tf_op jit(solution)/shard_map/ppermute | solution.py:709
  80.0 9.1 %collective-permute-start.12 = (bf16[16,1728]{1,0:T(8,128)(2,1)S(1)}, bf16[16,1728]{1,0:T(8,128)(2,1)S(1)}, u32[]{:S(2)}, u32[]{:S(2)}) collective-permute-start(bf16[16,1728]{1,0:T(8,128)(2,1)S(1)} %get-tuple-element.96), channel_id=1, source_target_pairs={{0,4},{1,5},{2,6},{3,7},{4,0},{5,1},{6,2},{7,3},{8,12},{9,13},{10,... | collective-permute-start | bytes 165896 | tf_op jit(solution)/shard_map/ppermute | solution.py:709
  82.0 7.2 %collective-permute-start.13 = (bf16[16,1728]{1,0:T(8,128)(2,1)S(1)}, bf16[16,1728]{1,0:T(8,128)(2,1)S(1)}, u32[]{:S(2)}, u32[]{:S(2)}) collective-permute-start(bf16[16,1728]{1,0:T(8,128)(2,1)S(1)} %get-tuple-element.97), channel_id=1, source_target_pairs={{0,6},{1,7},{2,0},{3,1},{4,2},{5,3},{6,4},{7,5},{8,14},{9,15},{10,... | collective-permute-start | bytes 165896 | tf_op jit(solution)/shard_map/ppermute | solution.py:709

commit v6 on v5

--- a/solution.py
+++ b/solution.py
@@ -12,7 +12,7 @@
 LEAK = 0.2
 SCALE = 1.0 / math.sqrt(32768.0)
 URGENT = 20_000_000_000
-COST = [20_000_000_000, 4_000_000_000, 500_000_000, 5_000_000_000]
+COST = [20000000000, 4000000000, 500000000, 5000000000, 0, 20000000000, 20000000000]
 PIECE = (8, 4, 16, 128)
 
 
@@ -490,7 +490,7 @@
         (shape((4, 16, 1728), F32), shape((4, 16, 1728))),
         [(coords, pltpu.SMEM), (stay, None), (got, None)],
         [pltpu.VMEM((1728, 128), F32), pltpu.VMEM((8, 16, 1728), F32)],
-        URGENT,
+        COST[6],
         2_000_000,
     )
 
@@ -507,19 +507,23 @@
         (shape((16, 1728), F32),) + (shape((16, 1728)),) * 3,
         [(coords, pltpu.SMEM), (keep, None), (got, None)],
         (),
-        URGENT,
+        COST[5],
         1_000_000,
     )
 
 
-def add_regions(parts):
-    def kernel(*refs):
-        ins, (out_ref, total, pairs) = refs[:4], refs[4:]
+def last_sums(regions, parts):
+    def kernel(r0, r1, r2, r3, parts_ref, filter_ref, input_ref, total, pairs, wide):
+        s = parts_ref[0].astype(F32)
+        for f in range(1, 8):
+            s = s + parts_ref[f].astype(F32)
+        wide[...] = s.reshape(512, 128)
+        from_pairs(wide, input_ref, range(8))
         for t in range(14):
             width = min(128, 1728 - t * 128)
             lanes = slice(t * 128, t * 128 + width)
-            s = ins[0][:, lanes].astype(F32)
-            for ref in ins[1:]:
+            s = r0[:, lanes].astype(F32)
+            for ref in (r1, r2, r3):
                 s = s + ref[:, lanes].astype(F32)
             total[:, 0:width] = s
             even, odd = total[pl.ds(0, 8, stride=2), :], total[pl.ds(1, 8, stride=2), :]
@@ -527,15 +531,15 @@
                 pick = slice(u * 64, u * 64 + 64)
                 at = (2 * t + u) * 8
                 pairs[at : at + 8, :] = jnp.concatenate([even[:, pick], odd[:, pick]], axis=1)
-        out_ref[...] = pairs[...].reshape(27, 8, 128)
-
-    return call(
-        kernel,
-        shape((27, 8, 128), F32),
-        [(part, None) for part in parts],
-        [pltpu.VMEM((16, 128), F32), pltpu.VMEM((216, 128), F32)],
-        URGENT,
-        600_000,
+        filter_ref[...] = pairs[...].reshape(27, 8, 128)
+
+    return call(
+        kernel,
+        (shape((27, 8, 128), F32), shape((8, 4, 2048))),
+        [(part, None) for part in regions] + [(parts, None)],
+        [pltpu.VMEM((16, 128), F32), pltpu.VMEM((216, 128), F32), pltpu.VMEM((512, 128), F32)],
+        COST[4],
+        1_800_000,
     )
 
 
@@ -634,24 +638,6 @@
     )
 
 
-def add_blocks(parts):
-    def kernel(parts_ref, out_ref, wide):
-        s = parts_ref[0].astype(F32)
-        for f in range(1, 8):
-            s = s + parts_ref[f].astype(F32)
-        wide[...] = s.reshape(512, 128)
-        from_pairs(wide, out_ref, range(8))
-
-    return call(
-        kernel,
-        shape((8, 4, 2048)),
-        [(parts, None)],
-        [pltpu.VMEM((512, 128), F32)],
-        0,
-        1_200_000,
-    )
-
-
 def both_ways(last, first, axis, size):
     return (
         lax.ppermute(last, axis, [(i, (i + 1) % size) for i in range(size)]),
@@ -707,9 +693,7 @@
     regions = list(add_near(coords, keep, got))
     for d in (2, 1, 3):
         regions[d] = lax.ppermute(regions[d], "sy", [(i, (i + 2 * d) % 8) for i in range(8)])
-    input_grad = add_blocks(parts)
-    input_grad, regions = lax.optimization_barrier((input_grad, regions))
-    weight_grad = add_regions(regions)
+    weight_grad, input_grad = last_sums(regions, parts)
     return outputs[None, None], input_grad[None, None], weight_grad.reshape(1, 27, 1024)
 
 

time: 90.7 us -> 90 us (level)
    ppermute x3, waiting for transfers between devices: 0.01 us -> 3.31 us  [per_device(): lax.ppermute(regions[d], 'sy', [(i, (i + 2 * d) % 8) for i in range(8)])]
    all_to_all x2, waiting for transfers between devices: 8.74 us -> 5.98 us  [exchange(): return lax.all_to_all(parts, axis, 0, 0)]
    pallas_call x18 -> x17, Pallas kernels: 31.6 us -> 30.9 us  [call(): pl.pallas_call(kernel, out_shape=outs, in_specs=[pl.BlockSpec(memory_spac...]
  transfers between devices with their start and end apart: 16 -> 16, of which waited for: 5 -> 6; matrix products, arithmetic and copies ran while one was open for 0% -> 0% of each run, Pallas kernels for 27% -> 26%
where the time goes in v6:
time: 90 us; the launch traced here: 89.8 us
  starting transfers between devices  37.7 us (42%)
  Pallas kernels  30.9 us (34%)
  waiting for transfers between devices  17.7 us (20%)
  local copies, waits for them, and re-layouts  2.58 us (3%)
    pallas_call x17, Pallas kernels, call(): pl.pallas_call(kernel, out_shape=outs, in_specs=[pl.BlockSpec(memory_spac...  30.9 us
    all_to_all x2, starting transfers between devices, exchange(): return lax.all_to_all(parts, axis, 0, 0)  9.52 us
    ppermute x2, starting transfers between devices, x_rims(): lax.ppermute(far, 'sx', [(1, 2), (2, 1)])  7.59 us
    ppermute x3, starting transfers between devices, per_device(): lax.ppermute(regions[d], 'sy', [(i, (i + 2 * d) % 8) for i in range(8)])  7.57 us
    ppermute x2, starting transfers between devices, both_ways(): lax.ppermute(first, axis, [((i + 1) % size, i) for i in range(size)])  6.86 us
    all_to_all x2, waiting for transfers between devices, exchange(): return lax.all_to_all(parts, axis, 0, 0)  5.98 us
    ppermute x2, waiting for transfers between devices, x_rims(): lax.ppermute(far, 'sx', [(1, 2), (2, 1)])  3.34 us
    ppermute x3, waiting for transfers between devices, per_device(): lax.ppermute(regions[d], 'sy', [(i, (i + 2 * d) % 8) for i in range(8)])  3.31 us
  transfers between devices with their start and end apart: 16, of which 6 were waited for; matrix products, arithmetic and copies ran while one was open for 0% of the time, Pallas kernels for 26%

profile of v6, /device:TPU:1, one launch (start us, length us, event | category | flops | bytes accessed | tf_op | source)
XLA Modules:
  0.0 89.8 jit_solution(3040787538910046106)
XLA Ops:
  0.6 0.0 copy-start.2
  0.6 0.9 copy-done.2
  1.5 0.0 copy-start.3
  1.5 1.2 %shard_map.58 = bf16[8,4,8,16,128]{4,3,2,1,0:T(8,128)(2,1)} custom-call(bf16[8,4,2048]{2,1,0:T(4,128)(2,1)S(1)} %bitcast.13), custom_call_target="tpu_custom_call" | custom-call | bytes 1300000 | tf_op jit(solution)/shard_map/pallas_call | solution.py:20
  2.7 5.9 %all-to-all-start = ((bf16[8,4,8,16,128]{4,3,2,1,0:T(8,128)(2,1)}), bf16[8,4,8,16,128]{4,3,2,1,0:T(8,128)(2,1)S(1)}, u32[]{:S(2)}, u32[]{:S(2)}) async-start(bf16[8,4,8,16,128]{4,3,2,1,0:T(8,128)(2,1)} %shard_map.58), calls=%async_computation | async-start | bytes 2097152 | tf_op jit(solution)/shard_map/all_to_all | solution.py:656
  8.7 0.0 copy-done.3
  8.7 0.1 shard_map.63.grad_ref
  8.8 0.0 copy-start.1
  8.8 1.6 %copy-done.1 = bf16[1,27,32768]{2,1,0:T(8,128)(2,1)S(1)} copy-done((bf16[1,27,32768]{2,1,0:T(8,128)(2,1)S(1)}, bf16[1,27,32768]{2,1,0:T(8,128)(2,1)}, u32[]{:S(2)}) %copy-start.1) | copy-done | bytes 1769496
  10.4 7.1 %shard_map.59 = (bf16[9,512,256]{2,1,0:T(8,128)(2,1)S(1)}, bf16[9,256,512]{2,1,0:T(8,128)(2,1)}, f32[8,128]{1,0:T(8,128)S(1)}) custom-call(bf16[27,32768]{1,0:T(8,128)(2,1)S(1)} %bitcast.12), custom_call_target="tpu_custom_call" | custom-call | bytes 8000000 | tf_op jit(solution)/shard_map/pallas_call | solution.py:20
  17.5 0.1 stack.27.co
  17.6 6.0 %all-to-all-done.cells_ref = bf16[8,4,8,16,128]{4,3,2,1,0:T(8,128)(2,1)S(1)} async-done(((bf16[8,4,8,16,128]{4,3,2,1,0:T(8,128)(2,1)}), bf16[8,4,8,16,128]{4,3,2,1,0:T(8,128)(2,1)S(1)}, u32[]{:S(2)}, u32[]{:S(2)}) %all-to-all-start) | async-done | bytes 1048608 | tf_op jit(solution)/shard_map/all_to_all | solution.py:656
  23.6 0.1 shard_map.60
  23.6 1.7 %collective-permute-start = (bf16[8,8,16,128]{3,2,1,0:T(8,128)(2,1)S(1)}, bf16[8,8,16,128]{3,2,1,0:T(8,128)(2,1)S(1)}, u32[]{:S(2)}, u32[]{:S(2)}) collective-permute-start(bf16[8,8,16,128]{3,2,1,0:T(8,128)(2,1)S(1)} %get-tuple-element.56), channel_id=1, source_target_pairs={{0,1},{1,2},{2,3},{3,4},{4,5},{5,6},{6,7},{7,0},{8,9},{9,10},{10,1... | collective-permute-start | bytes 786440 | tf_op jit(solution)/shard_map/ppermute | solution.py:643
  25.4 4.0 %collective-permute-start.1 = (bf16[8,8,16,128]{3,2,1,0:T(8,128)(2,1)S(1)}, bf16[8,8,16,128]{3,2,1,0:T(8,128)(2,1)S(1)}, u32[]{:S(2)}, u32[]{:S(2)}) collective-permute-start(bf16[8,8,16,128]{3,2,1,0:T(8,128)(2,1)S(1)} %get-tuple-element.57), channel_id=1, source_target_pairs={{1,0},{2,1},{3,2},{4,3},{5,4},{6,5},{7,6},{0,7},{9,8},{10,9},{11,1... | collective-permute-start | bytes 786440 | tf_op jit(solution)/shard_map/ppermute | solution.py:644
  29.4 3.1 %shard_map.61 = (bf16[8,192,512]{2,1,0:T(8,128)(2,1)S(1)}, f32[768,256]{1,0:T(8,128)S(1)}, f32[8,128]{1,0:T(8,128)S(1)}) custom-call(bf16[8,4,8,16,128]{4,3,2,1,0:T(8,128)(2,1)S(1)} %all-to-all-done.cells_ref, bf16[9,512,256]{2,1,0:T(8,128)(2,1)S(1)} %get-tuple-element.52.fore_ref, f32[8,128]{1,0:T(8,128)S(1)} %get-tuple-element.54.token_ref), custom_call_target="tpu_custom_call" | custom-call | flops 4000000000 | bytes 5000000 | tf_op jit(solution)/shard_map/pallas_call | solution.py:20
  32.5 2.6 %collective-permute-done.yb = bf16[8,8,16,128]{3,2,1,0:T(8,128)(2,1)S(1)} collective-permute-done((bf16[8,8,16,128]{3,2,1,0:T(8,128)(2,1)S(1)}, bf16[8,8,16,128]{3,2,1,0:T(8,128)(2,1)S(1)}, u32[]{:S(2)}, u32[]{:S(2)}) %collective-permute-start) | collective-permute-done | bytes 262176 | tf_op jit(solution)/shard_map/ppermute | solution.py:643
  35.1 0.0 collective-permute-done.1.ya
  35.1 0.6 shard_map.62
  35.7 1.5 %collective-permute-start.2 = (bf16[8,6,16,128]{3,2,1,0:T(8,128)(2,1)S(1)}, bf16[8,6,16,128]{3,2,1,0:T(8,128)(2,1)S(1)}, u32[]{:S(2)}, u32[]{:S(2)}) collective-permute-start(bf16[8,6,16,128]{3,2,1,0:T(8,128)(2,1)S(1)} %get-tuple-element.65), channel_id=1, source_target_pairs={{0,8},{8,0},{16,24},{24,16},{1,9},{9,1},{17,25},{25,17},{2,10},{10... | collective-permute-start | bytes 589832 | tf_op jit(solution)/shard_map/ppermute | solution.py:650
  37.2 4.3 %collective-permute-start.3 = (bf16[8,6,16,128]{3,2,1,0:T(8,128)(2,1)S(1)}, bf16[8,6,16,128]{3,2,1,0:T(8,128)(2,1)S(1)}, u32[]{:S(2)}, u32[]{:S(2)}) collective-permute-start(bf16[8,6,16,128]{3,2,1,0:T(8,128)(2,1)S(1)} %get-tuple-element.66), channel_id=1, source_target_pairs={{8,16},{16,8},{9,17},{17,9},{10,18},{18,10},{11,19},{19,11},{12,20... | collective-permute-start | bytes 589832 | tf_op jit(solution)/shard_map/ppermute | solution.py:651
  41.5 2.6 %shard_map.64 = (bf16[8,192,512]{2,1,0:T(8,128)(2,1)S(1)}, bf16[6,4,2048]{2,1,0:T(4,128)(2,1)S(1)}, bf16[6,4,16,128]{3,2,1,0:T(8,128)(2,1)S(1)}) custom-call(s32[8]{0:T(128)S(1)} %stack.27.co, bf16[8,192,512]{2,1,0:T(8,128)(2,1)S(1)} %get-tuple-element.55.own_ref, f32[768,256]{1,0:T(8,128)S(1)} %get-tuple-element.62.total_ref, ...), custom_call_target="tpu_custom_call" | custom-call | flops 1000000000 | bytes 6000000 | tf_op jit(solution)/shard_map/pallas_call | solution.py:20
  44.1 2.2 %shard_map.65 = (bf16[9,192,512]{2,1,0:T(8,128)(2,1)S(1)}, f32[8,128]{1,0:T(8,128)S(1)}) custom-call(bf16[8,192,512]{2,1,0:T(8,128)(2,1)S(1)} %get-tuple-element.64.field_ref, bf16[6,4,16,128]{3,2,1,0:T(8,128)(2,1)S(1)} %get-tuple-element.68.pre_ref.pre_in), custom_call_target="tpu_custom_call" | custom-call | flops 3000000000 | tf_op jit(solution)/shard_map/pallas_call | solution.py:20
  46.3 0.0 collective-permute-done.2.near_ref
  46.3 0.0 collective-permute-done.3.far_ref
  46.3 2.2 %shard_map.66 = (bf16[2,192,512]{2,1,0:T(8,128)(2,1)S(1)}, bf16[8,4,2048]{2,1,0:T(4,128)(2,1)}, bf16[8,4,16,128]{3,2,1,0:T(8,128)(2,1)S(1)}, bf16[8,16,128]{2,1,0:T(8,128)(2,1)S(1)}, bf16[8,16,128]{2,1,0:T(8,128)(2,1)S(1)}) custom-call(s32[8]{0:T(128)S(1)} %stack.27.co, bf16[8,192,512]{2,1,0:T(8,128)(2,1)S(1)} %get-tuple-element.64.field_ref, ...), custom_call_target="tpu_custom_call" | custom-call | flops 2000000000 | bytes 6000000 | tf_op jit(solution)/shard_map/pallas_call | solution.py:20
  48.5 1.8 %shard_map.67 = (f32[2,9,192,128]{3,2,1,0:T(8,128)S(1)}, bf16[2,9,192,128]{3,2,1,0:T(8,128)(2,1)S(1)}) custom-call(s32[8]{0:T(128)S(1)} %stack.27.co, bf16[8,192,512]{2,1,0:T(8,128)(2,1)S(1)} %get-tuple-element.64.field_ref, bf16[2,192,512]{2,1,0:T(8,128)(2,1)S(1)} %get-tuple-element.71.rim_ref, bf16[8,4,16,128]{3,2,1,0:T(8,128)(2,1)S(1)} %get-tuple-element.80.pre_ref, ...), custom_call_target="tpu_custom_call" | custom-call | flops 5000000000 | tf_op jit(solution)/shard_map/pallas_call | solution.py:20
  50.3 0.1 collective-permute-start.4
  50.4 0.1 collective-permute-start.5
  50.5 2.8 %collective-permute-start.6 = (bf16[8,16,128]{2,1,0:T(8,128)(2,1)S(1)}, bf16[8,16,128]{2,1,0:T(8,128)(2,1)S(1)}, u32[]{:S(2)}, u32[]{:S(2)}) collective-permute-start(bf16[8,16,128]{2,1,0:T(8,128)(2,1)S(1)} %get-tuple-element.78), channel_id=1, source_target_pairs={{1,0},{2,1},{3,2},{4,3},{5,4},{6,5},{7,6},{0,7},{9,8},{10,9},{11,1... | collective-permute-start | bytes 98312 | tf_op jit(solution)/shard_map/ppermute | solution.py:644
  53.3 0.0 collective-permute-done.4.got_ref
  53.3 0.0 copy-start
  53.3 0.7 shard_map.68
  54.0 1.8 %collective-permute-start.9 = (bf16[9,192,128]{2,1,0:T(8,128)(2,1)S(1)}, bf16[9,192,128]{2,1,0:T(8,128)(2,1)S(1)}, u32[]{:S(2)}, u32[]{:S(2)}) collective-permute-start(bf16[9,192,128]{2,1,0:T(8,128)(2,1)S(1)} %get-tuple-element.86), channel_id=1, source_target_pairs={{0,16},{8,24},{16,0},{24,8},{1,17},{9,25},{17,1},{25,9},{2,18},{10... | collective-permute-start | bytes 1327112 | tf_op jit(solution)/shard_map/ppermute | solution.py:684
  55.8 0.0 collective-permute-done.5.yb
  55.8 0.0 collective-permute-done.6.ya
  55.8 0.6 shard_map.69
  56.3 0.9 %collective-permute-start.7 = (bf16[6,16,128]{2,1,0:T(8,128)(2,1)S(1)}, bf16[6,16,128]{2,1,0:T(8,128)(2,1)S(1)}, u32[]{:S(2)}, u32[]{:S(2)}) collective-permute-start(bf16[6,16,128]{2,1,0:T(8,128)(2,1)S(1)} %get-tuple-element.83), channel_id=1, source_target_pairs={{0,8},{8,0},{16,24},{24,16},{1,9},{9,1},{17,25},{25,17},{2,10},{10... | collective-permute-start | bytes 73736 | tf_op jit(solution)/shard_map/ppermute | solution.py:650
  57.3 3.3 %collective-permute-start.8 = (bf16[6,16,128]{2,1,0:T(8,128)(2,1)S(1)}, bf16[6,16,128]{2,1,0:T(8,128)(2,1)S(1)}, u32[]{:S(2)}, u32[]{:S(2)}) collective-permute-start(bf16[6,16,128]{2,1,0:T(8,128)(2,1)S(1)} %get-tuple-element.84), channel_id=1, source_target_pairs={{8,16},{16,8},{9,17},{17,9},{10,18},{18,10},{11,19},{19,11},{12,20... | collective-permute-start | bytes 73736 | tf_op jit(solution)/shard_map/ppermute | solution.py:651
  60.6 0.0 copy-done
  60.6 3.8 %shard_map.70.inner_ref = bf16[8,6,4,16,128]{4,3,2,1,0:T(8,128)(2,1)S(1)} custom-call(s32[8]{0:T(128)S(1)} %stack.27.co, bf16[8,4,16,128]{3,2,1,0:T(8,128)(2,1)S(1)} %get-tuple-element.80.pre_ref, bf16[8,16,128]{2,1,0:T(8,128)(2,1)S(1)} %collective-permute-done.5.yb, bf16[8,16,128]{2,1,0:T(8,128)(2,1)S(1)} %collective-permute-done.6.ya, ...), custom_call_target="tpu_custom_call" | custom-call | flops 4000000000 | tf_op jit(solution)/shard_map/pallas_call | solution.py:20
  64.4 0.0 collective-permute-done.7.near_ref
  64.4 3.3 %collective-permute-done.8.far_ref = bf16[6,16,128]{2,1,0:T(8,128)(2,1)S(1)} collective-permute-done((bf16[6,16,128]{2,1,0:T(8,128)(2,1)S(1)}, bf16[6,16,128]{2,1,0:T(8,128)(2,1)S(1)}, u32[]{:S(2)}, u32[]{:S(2)}) %collective-permute-start.8) | collective-permute-done | bytes 24608 | tf_op jit(solution)/shard_map/ppermute | solution.py:651
  67.8 2.5 %shard_map.71 = bf16[8,8,4,16,128]{4,3,2,1,0:T(8,128)(2,1)} custom-call(s32[8]{0:T(128)S(1)} %stack.27.co, bf16[8,4,16,128]{3,2,1,0:T(8,128)(2,1)S(1)} %get-tuple-element.80.pre_ref, bf16[8,16,128]{2,1,0:T(8,128)(2,1)S(1)} %collective-permute-done.5.yb, bf16[8,16,128]{2,1,0:T(8,128)(2,1)S(1)} %collective-permute-done.6.ya, ...), custom_call_target="tpu_custom_call" | custom-call | flops 500000000 | tf_op jit(solution)/shard_map/pallas_call | solution.py:20
  70.2 0.0 collective-permute-done.9.got_ref
  70.2 0.9 %shard_map.72 = (f32[4,16,1728]{2,1,0:T(8,128)S(1)}, bf16[4,16,1728]{2,1,0:T(8,128)(2,1)S(1)}) custom-call(s32[8]{0:T(128)S(1)} %stack.27.co, f32[9,192,128]{2,1,0:T(8,128)S(1)} %get-tuple-element.79.stay_ref, bf16[9,192,128]{2,1,0:T(8,128)(2,1)S(1)} %collective-permute-done.9.got_ref), custom_call_target="tpu_custom_call" | custom-call | flops 20000000000 | bytes 2000000 | tf_op jit(solution)/shard_map/pallas_call | solution.py:20
  71.2 0.1 collective-permute-start.10
  71.3 3.6 %all-to-all-start.1 = ((bf16[8,8,4,16,128]{4,3,2,1,0:T(8,128)(2,1)}), bf16[8,8,4,16,128]{4,3,2,1,0:T(8,128)(2,1)S(1)}, u32[]{:S(2)}, u32[]{:S(2)}) async-start(bf16[8,8,4,16,128]{4,3,2,1,0:T(8,128)(2,1)} %shard_map.71), calls=%async_computation.1 | async-start | bytes 2097152 | tf_op jit(solution)/shard_map/all_to_all | solution.py:656
  74.8 2.4 %collective-permute-done.10.got_ref = bf16[4,16,1728]{2,1,0:T(8,128)(2,1)S(1)} collective-permute-done((bf16[4,16,1728]{2,1,0:T(8,128)(2,1)S(1)}, bf16[4,16,1728]{2,1,0:T(8,128)(2,1)S(1)}, u32[]{:S(2)}, u32[]{:S(2)}) %collective-permute-start.10) | collective-permute-done | bytes 221216 | tf_op jit(solution)/shard_map/ppermute | solution.py:692
  77.3 0.6 shard_map.73
  77.9 2.1 %collective-permute-start.11 = (bf16[16,1728]{1,0:T(8,128)(2,1)S(1)}, bf16[16,1728]{1,0:T(8,128)(2,1)S(1)}, u32[]{:S(2)}, u32[]{:S(2)}) collective-permute-start(bf16[16,1728]{1,0:T(8,128)(2,1)S(1)} %get-tuple-element.91), channel_id=1, source_target_pairs={{0,2},{1,3},{2,4},{3,5},{4,6},{5,7},{6,0},{7,1},{8,10},{9,11},{10,... | collective-permute-start | bytes 165896 | tf_op jit(solution)/shard_map/ppermute | solution.py:695
  80.0 2.0 %collective-permute-start.12 = (bf16[16,1728]{1,0:T(8,128)(2,1)S(1)}, bf16[16,1728]{1,0:T(8,128)(2,1)S(1)}, u32[]{:S(2)}, u32[]{:S(2)}) collective-permute-start(bf16[16,1728]{1,0:T(8,128)(2,1)S(1)} %get-tuple-element.92), channel_id=1, source_target_pairs={{0,4},{1,5},{2,6},{3,7},{4,0},{5,1},{6,2},{7,3},{8,12},{9,13},{10,... | collective-permute-start | bytes 165896 | tf_op jit(solution)/shard_map/ppermute | solution.py:695
  82.0 3.5 %collective-permute-start.13 = (bf16[16,1728]{1,0:T(8,128)(2,1)S(1)}, bf16[16,1728]{1,0:T(8,128)(2,1)S(1)}, u32[]{:S(2)}, u32[]{:S(2)}) collective-permute-start(bf16[16,1728]{1,0:T(8,128)(2,1)S(1)} %get-tuple-element.93), channel_id=1, source_target_pairs={{0,6},{1,7},{2,0},{3,1},{4,2},{5,3},{6,4},{7,5},{8,14},{9,15},{10,... | collective-permute-start | bytes 165896 | tf_op jit(solution)/shard_map/ppermute | solution.py:695
  85.5 0.0 collective-permute-done.11.r1
  85.5 1.7 %collective-permute-done.12.r2 = bf16[16,1728]{1,0:T(8,128)(2,1)S(1)} collective-permute-done((bf16[16,1728]{1,0:T(8,128)(2,1)S(1)}, bf16[16,1728]{1,0:T(8,128)(2,1)S(1)}, u32[]{:S(2)}, u32[]{:S(2)}) %collective-permute-start.12) | collective-permute-done | bytes 55328 | tf_op jit(solution)/shard_map/ppermute | solution.py:695
  87.1 1.7 %collective-permute-done.13.r3 = bf16[16,1728]{1,0:T(8,128)(2,1)S(1)} collective-permute-done((bf16[16,1728]{1,0:T(8,128)(2,1)S(1)}, bf16[16,1728]{1,0:T(8,128)(2,1)S(1)}, u32[]{:S(2)}, u32[]{:S(2)}) %collective-permute-start.13) | collective-permute-done | bytes 55328 | tf_op jit(solution)/shard_map/ppermute | solution.py:695
  88.8 0.0 all-to-all-done.1.parts_ref
  88.8 1.0 %shard_map.74 = (f32[27,8,128]{2,1,0:T(8,128)}, bf16[8,4,2048]{2,1,0:T(4,128)(2,1)}) custom-call(f32[16,1728]{1,0:T(8,128)S(1)} %get-tuple-element.90.r0, bf16[16,1728]{1,0:T(8,128)(2,1)S(1)} %collective-permute-done.11.r1, bf16[16,1728]{1,0:T(8,128)(2,1)S(1)} %collective-permute-done.12.r2, bf16[16,1728]{1,0:T(8,128)(2,1)S(1)} %collective-permute-done.13.r3, ...), custom_call_target="tpu_custom_call" | custom-call | bytes 1800000 | tf_op jit(solution)/shard_map/pallas_call | solution.py:20
  (1 shorter events, 0.0 us)
Async XLA Ops:
  0.6 0.9 %copy-start.2 = (bf16[1,1,8,4,2048]{4,3,2,1,0:T(4,128)(2,1)S(1)}, bf16[1,1,8,4,2048]{4,3,2,1,0:T(4,128)(2,1)}, u32[]{:S(2)}) copy-start(bf16[1,1,8,4,2048]{4,3,2,1,0:T(4,128)(2,1)} %param.3) | copy-start | bytes 393220
  1.5 7.1 %copy-start.3 = (bf16[1,1,8,4,2048]{4,3,2,1,0:T(4,128)(2,1)S(1)}, bf16[1,1,8,4,2048]{4,3,2,1,0:T(4,128)(2,1)}, u32[]{:S(2)}) copy-start(bf16[1,1,8,4,2048]{4,3,2,1,0:T(4,128)(2,1)} %param.5) | copy-start | bytes 393220
  2.7 20.9 %all-to-all-start = ((bf16[8,4,8,16,128]{4,3,2,1,0:T(8,128)(2,1)}), bf16[8,4,8,16,128]{4,3,2,1,0:T(8,128)(2,1)S(1)}, u32[]{:S(2)}, u32[]{:S(2)}) async-start(bf16[8,4,8,16,128]{4,3,2,1,0:T(8,128)(2,1)} %shard_map.58), calls=%async_computation | async-start | bytes 2097152 | tf_op jit(solution)/shard_map/all_to_all | solution.py:656
  8.8 1.6 %copy-start.1 = (bf16[1,27,32768]{2,1,0:T(8,128)(2,1)S(1)}, bf16[1,27,32768]{2,1,0:T(8,128)(2,1)}, u32[]{:S(2)}) copy-start(bf16[1,27,32768]{2,1,0:T(8,128)(2,1)} %param.4) | copy-start | bytes 5308420
  23.6 11.5 %collective-permute-start = (bf16[8,8,16,128]{3,2,1,0:T(8,128)(2,1)S(1)}, bf16[8,8,16,128]{3,2,1,0:T(8,128)(2,1)S(1)}, u32[]{:S(2)}, u32[]{:S(2)}) collective-permute-start(bf16[8,8,16,128]{3,2,1,0:T(8,128)(2,1)S(1)} %get-tuple-element.56), channel_id=1, source_target_pairs={{0,1},{1,2},{2,3},{3,4},{4,5},{5,6},{6,7},{7,0},{8,9},{9,10},{10,1... | collective-permute-start | bytes 786440 | tf_op jit(solution)/shard_map/ppermute | solution.py:643
  25.4 9.8 %collective-permute-start.1 = (bf16[8,8,16,128]{3,2,1,0:T(8,128)(2,1)S(1)}, bf16[8,8,16,128]{3,2,1,0:T(8,128)(2,1)S(1)}, u32[]{:S(2)}, u32[]{:S(2)}) collective-permute-start(bf16[8,8,16,128]{3,2,1,0:T(8,128)(2,1)S(1)} %get-tuple-element.57), channel_id=1, source_target_pairs={{1,0},{2,1},{3,2},{4,3},{5,4},{6,5},{7,6},{0,7},{9,8},{10,9},{11,1... | collective-permute-start | bytes 786440 | tf_op jit(solution)/shard_map/ppermute | solution.py:644
  35.7 10.6 %collective-permute-start.2 = (bf16[8,6,16,128]{3,2,1,0:T(8,128)(2,1)S(1)}, bf16[8,6,16,128]{3,2,1,0:T(8,128)(2,1)S(1)}, u32[]{:S(2)}, u32[]{:S(2)}) collective-permute-start(bf16[8,6,16,128]{3,2,1,0:T(8,128)(2,1)S(1)} %get-tuple-element.65), channel_id=1, source_target_pairs={{0,8},{8,0},{16,24},{24,16},{1,9},{9,1},{17,25},{25,17},{2,10},{10... | collective-permute-start | bytes 589832 | tf_op jit(solution)/shard_map/ppermute | solution.py:650
  37.2 9.1 %collective-permute-start.3 = (bf16[8,6,16,128]{3,2,1,0:T(8,128)(2,1)S(1)}, bf16[8,6,16,128]{3,2,1,0:T(8,128)(2,1)S(1)}, u32[]{:S(2)}, u32[]{:S(2)}) collective-permute-start(bf16[8,6,16,128]{3,2,1,0:T(8,128)(2,1)S(1)} %get-tuple-element.66), channel_id=1, source_target_pairs={{8,16},{16,8},{9,17},{17,9},{10,18},{18,10},{11,19},{19,11},{12,20... | collective-permute-start | bytes 589832 | tf_op jit(solution)/shard_map/ppermute | solution.py:651
  50.3 3.0 %collective-permute-start.4 = (bf16[2,9,192,128]{3,2,1,0:T(8,128)(2,1)S(1)}, bf16[2,9,192,128]{3,2,1,0:T(8,128)(2,1)S(1)}, u32[]{:S(2)}, u32[]{:S(2)}) collective-permute-start(bf16[2,9,192,128]{3,2,1,0:T(8,128)(2,1)S(1)} %get-tuple-element.75), channel_id=1, source_target_pairs={{0,8},{8,0},{16,24},{24,16},{1,9},{9,1},{17,25},{25,17},{2,10},{10... | collective-permute-start | bytes 2654216 | tf_op jit(solution)/shard_map/ppermute | solution.py:681
  50.4 5.4 %collective-permute-start.5 = (bf16[8,16,128]{2,1,0:T(8,128)(2,1)S(1)}, bf16[8,16,128]{2,1,0:T(8,128)(2,1)S(1)}, u32[]{:S(2)}, u32[]{:S(2)}) collective-permute-start(bf16[8,16,128]{2,1,0:T(8,128)(2,1)S(1)} %get-tuple-element.77), channel_id=1, source_target_pairs={{0,1},{1,2},{2,3},{3,4},{4,5},{5,6},{6,7},{7,0},{8,9},{9,10},{10,1... | collective-permute-start | bytes 98312 | tf_op jit(solution)/shard_map/ppermute | solution.py:643
  50.5 5.3 %collective-permute-start.6 = (bf16[8,16,128]{2,1,0:T(8,128)(2,1)S(1)}, bf16[8,16,128]{2,1,0:T(8,128)(2,1)S(1)}, u32[]{:S(2)}, u32[]{:S(2)}) collective-permute-start(bf16[8,16,128]{2,1,0:T(8,128)(2,1)S(1)} %get-tuple-element.78), channel_id=1, source_target_pairs={{1,0},{2,1},{3,2},{4,3},{5,4},{6,5},{7,6},{0,7},{9,8},{10,9},{11,1... | collective-permute-start | bytes 98312 | tf_op jit(solution)/shard_map/ppermute | solution.py:644
  53.3 7.3 %copy-start = (bf16[9,256,512]{2,1,0:T(8,128)(2,1)S(1)}, bf16[9,256,512]{2,1,0:T(8,128)(2,1)}, u32[]{:S(2)}) copy-start(bf16[9,256,512]{2,1,0:T(8,128)(2,1)} %get-tuple-element.85.back_ref) | copy-start | bytes 7077892
  54.0 16.2 %collective-permute-start.9 = (bf16[9,192,128]{2,1,0:T(8,128)(2,1)S(1)}, bf16[9,192,128]{2,1,0:T(8,128)(2,1)S(1)}, u32[]{:S(2)}, u32[]{:S(2)}) collective-permute-start(bf16[9,192,128]{2,1,0:T(8,128)(2,1)S(1)} %get-tuple-element.86), channel_id=1, source_target_pairs={{0,16},{8,24},{16,0},{24,8},{1,17},{9,25},{17,1},{25,9},{2,18},{10... | collective-permute-start | bytes 1327112 | tf_op jit(solution)/shard_map/ppermute | solution.py:684
  56.3 8.1 %collective-permute-start.7 = (bf16[6,16,128]{2,1,0:T(8,128)(2,1)S(1)}, bf16[6,16,128]{2,1,0:T(8,128)(2,1)S(1)}, u32[]{:S(2)}, u32[]{:S(2)}) collective-permute-start(bf16[6,16,128]{2,1,0:T(8,128)(2,1)S(1)} %get-tuple-element.83), channel_id=1, source_target_pairs={{0,8},{8,0},{16,24},{24,16},{1,9},{9,1},{17,25},{25,17},{2,10},{10... | collective-permute-start | bytes 73736 | tf_op jit(solution)/shard_map/ppermute | solution.py:650
  57.3 10.5 %collective-permute-start.8 = (bf16[6,16,128]{2,1,0:T(8,128)(2,1)S(1)}, bf16[6,16,128]{2,1,0:T(8,128)(2,1)S(1)}, u32[]{:S(2)}, u32[]{:S(2)}) collective-permute-start(bf16[6,16,128]{2,1,0:T(8,128)(2,1)S(1)} %get-tuple-element.84), channel_id=1, source_target_pairs={{8,16},{16,8},{9,17},{17,9},{10,18},{18,10},{11,19},{19,11},{12,20... | collective-permute-start | bytes 73736 | tf_op jit(solution)/shard_map/ppermute | solution.py:651
  71.2 6.1 %collective-permute-start.10 = (bf16[4,16,1728]{2,1,0:T(8,128)(2,1)S(1)}, bf16[4,16,1728]{2,1,0:T(8,128)(2,1)S(1)}, u32[]{:S(2)}, u32[]{:S(2)}) collective-permute-start(bf16[4,16,1728]{2,1,0:T(8,128)(2,1)S(1)} %get-tuple-element.89), channel_id=1, source_target_pairs={{0,1},{1,0},{2,3},{3,2},{4,5},{5,4},{6,7},{7,6},{8,9},{9,8},{10,11... | collective-permute-start | bytes 663560 | tf_op jit(solution)/shard_map/ppermute | solution.py:692
  71.3 17.5 %all-to-all-start.1 = ((bf16[8,8,4,16,128]{4,3,2,1,0:T(8,128)(2,1)}), bf16[8,8,4,16,128]{4,3,2,1,0:T(8,128)(2,1)S(1)}, u32[]{:S(2)}, u32[]{:S(2)}) async-start(bf16[8,8,4,16,128]{4,3,2,1,0:T(8,128)(2,1)} %shard_map.71), calls=%async_computation.1 | async-start | bytes 2097152 | tf_op jit(solution)/shard_map/all_to_all | solution.py:656
  77.9 7.6 %collective-permute-start.11 = (bf16[16,1728]{1,0:T(8,128)(2,1)S(1)}, bf16[16,1728]{1,0:T(8,128)(2,1)S(1)}, u32[]{:S(2)}, u32[]{:S(2)}) collective-permute-start(bf16[16,1728]{1,0:T(8,128)(2,1)S(1)} %get-tuple-element.91), channel_id=1, source_target_pairs={{0,2},{1,3},{2,4},{3,5},{4,6},{5,7},{6,0},{7,1},{8,10},{9,11},{10,... | collective-permute-start | bytes 165896 | tf_op jit(solution)/shard_map/ppermute | solution.py:695
  80.0 7.1 %collective-permute-start.12 = (bf16[16,1728]{1,0:T(8,128)(2,1)S(1)}, bf16[16,1728]{1,0:T(8,128)(2,1)S(1)}, u32[]{:S(2)}, u32[]{:S(2)}) collective-permute-start(bf16[16,1728]{1,0:T(8,128)(2,1)S(1)} %get-tuple-element.92), channel_id=1, source_target_pairs={{0,4},{1,5},{2,6},{3,7},{4,0},{5,1},{6,2},{7,3},{8,12},{9,13},{10,... | collective-permute-start | bytes 165896 | tf_op jit(solution)/shard_map/ppermute | solution.py:695
  82.0 6.8 %collective-permute-start.13 = (bf16[16,1728]{1,0:T(8,128)(2,1)S(1)}, bf16[16,1728]{1,0:T(8,128)(2,1)S(1)}, u32[]{:S(2)}, u32[]{:S(2)}) collective-permute-start(bf16[16,1728]{1,0:T(8,128)(2,1)S(1)} %get-tuple-element.93), channel_id=1, source_target_pairs={{0,6},{1,7},{2,0},{3,1},{4,2},{5,3},{6,4},{7,5},{8,14},{9,15},{10,... | collective-permute-start | bytes 165896 | tf_op jit(solution)/shard_map/ppermute | solution.py:695

commit v7 on v6

--- a/solution.py
+++ b/solution.py
@@ -58,7 +58,7 @@
         rows = field_ref[x].astype(F32)
         for t in range(16):
             wide[pl.ds(x * 64 + t, 4, stride=16), :] = rows[:, t * 128 : (t + 1) * 128]
-    pair_ref[...] = wide[...].reshape(PIECE).astype(BF)
+    pair_ref[...] = wide[0:512, :].reshape(PIECE).astype(BF)
 
 
 def from_pairs(wide, field_ref, layers):
@@ -72,7 +72,7 @@
         to_pairs(field_ref, pair_ref, wide)
 
     return call(
-        kernel, shape(PIECE), [(field, None)], [pltpu.VMEM((512, 128), F32)], 0, 400_000
+        kernel, shape(PIECE), [(field, None)], [pltpu.VMEM((576, 128), F32)], 0, 400_000
     )
 
 
@@ -91,7 +91,7 @@
         kernel,
         shape((8, 4, 8, 16, 128)),
         [(field, None)],
-        [pltpu.VMEM((512, 128), F32)],
+        [pltpu.VMEM((1024, 128), F32)],
         0,
         1_300_000,
     )
@@ -187,7 +187,7 @@
         (shape((9, 512, 256)), pltpu.HBM((9, 256, 512), BF), TOKEN),
         [(weights, None)],
         [
-            pltpu.VMEM((27 * 256, 128), F32),
+            pltpu.VMEM((32 * 256, 128), F32),
             pltpu.VMEM((512, 128), F32),
             pltpu.VMEM((512, 128), F32),
             pltpu.VMEM((9, 256, 512), BF),
@@ -311,7 +311,7 @@
         (shape((8, 192, 512)), shape((6, 4, 2048)), shape((6, 4, 16, 128))),
         [(coords, pltpu.SMEM)]
         + [(a, None) for a in (field, total, y_before, y_after, fore, grad)],
-        [pltpu.VMEM((2, 192, 256), F32), pltpu.VMEM((384, 128), F32)],
+        [pltpu.VMEM((2, 192, 256), F32), pltpu.VMEM((448, 128), F32)],
         1_000_000_000,
         6_000_000,
     )
@@ -368,7 +368,7 @@
         ),
         [(coords, pltpu.SMEM)]
         + [(a, None) for a in (field, x_near, x_far, fore, grad, out_inner, pre_inner, token)],
-        [pltpu.VMEM((256, 256), F32), pltpu.VMEM((128, 128), F32)],
+        [pltpu.VMEM((256, 256), F32), pltpu.VMEM((192, 128), F32)],
         2_000_000_000,
         6_000_000,
     )
@@ -517,7 +517,7 @@
         s = parts_ref[0].astype(F32)
         for f in range(1, 8):
             s = s + parts_ref[f].astype(F32)
-        wide[...] = s.reshape(512, 128)
+        wide[0:512, :] = s.reshape(512, 128)
         from_pairs(wide, input_ref, range(8))
         for t in range(14):
             width = min(128, 1728 - t * 128)
@@ -537,7 +537,7 @@
         kernel,
         (shape((27, 8, 128), F32), shape((8, 4, 2048))),
         [(part, None) for part in regions] + [(parts, None)],
-        [pltpu.VMEM((16, 128), F32), pltpu.VMEM((216, 128), F32), pltpu.VMEM((512, 128), F32)],
+        [pltpu.VMEM((16, 128), F32), pltpu.VMEM((216, 128), F32), pltpu.VMEM((576, 128), F32)],
         COST[4],
         1_800_000,
     )

time: 90 us -> 90 us (level)
  no operation moved by 1% of the time
where the time goes in v7:
time: 90 us; the launch traced here: 89.8 us
  starting transfers between devices  37.7 us (42%)
  Pallas kernels  30.9 us (34%)
  waiting for transfers between devices  17.7 us (20%)
  local copies, waits for them, and re-layouts  2.58 us (3%)
    pallas_call x17, Pallas kernels, call(): pl.pallas_call(kernel, out_shape=outs, in_specs=[pl.BlockSpec(memory_spac...  30.9 us
    all_to_all x2, starting transfers between devices, exchange(): return lax.all_to_all(parts, axis, 0, 0)  9.52 us
    ppermute x2, starting transfers between devices, x_rims(): lax.ppermute(far, 'sx', [(1, 2), (2, 1)])  7.59 us
    ppermute x3, starting transfers between devices, per_device(): lax.ppermute(regions[d], 'sy', [(i, (i + 2 * d) % 8) for i in range(8)])  7.57 us
    ppermute x2, starting transfers between devices, both_ways(): lax.ppermute(first, axis, [((i + 1) % size, i) for i in range(size)])  6.86 us
    all_to_all x2, waiting for transfers between devices, exchange(): return lax.all_to_all(parts, axis, 0, 0)  5.98 us
    ppermute x2, waiting for transfers between devices, x_rims(): lax.ppermute(far, 'sx', [(1, 2), (2, 1)])  3.34 us
    ppermute x3, waiting for transfers between devices, per_device(): lax.ppermute(regions[d], 'sy', [(i, (i + 2 * d) % 8) for i in range(8)])  3.31 us
  transfers between devices with their start and end apart: 16, of which 6 were waited for; matrix products, arithmetic and copies ran while one was open for 0% of the time, Pallas kernels for 26%

profile of v7, /device:TPU:1, one launch (start us, length us, event | category | flops | bytes accessed | tf_op | source)
XLA Modules:
  0.0 89.8 jit_solution(8546383130719323148)
XLA Ops:
  0.6 0.0 copy-start.2
  0.6 0.9 copy-done.2
  1.5 0.0 copy-start.3
  1.5 1.2 %shard_map.58 = bf16[8,4,8,16,128]{4,3,2,1,0:T(8,128)(2,1)} custom-call(bf16[8,4,2048]{2,1,0:T(4,128)(2,1)S(1)} %bitcast.13), custom_call_target="tpu_custom_call" | custom-call | bytes 1300000 | tf_op jit(solution)/shard_map/pallas_call | solution.py:20
  2.7 5.9 %all-to-all-start = ((bf16[8,4,8,16,128]{4,3,2,1,0:T(8,128)(2,1)}), bf16[8,4,8,16,128]{4,3,2,1,0:T(8,128)(2,1)S(1)}, u32[]{:S(2)}, u32[]{:S(2)}) async-start(bf16[8,4,8,16,128]{4,3,2,1,0:T(8,128)(2,1)} %shard_map.58), calls=%async_computation | async-start | bytes 2097152 | tf_op jit(solution)/shard_map/all_to_all | solution.py:656
  8.7 0.0 copy-done.3
  8.7 0.1 shard_map.63.grad_ref
  8.8 0.0 copy-start.1
  8.8 1.6 %copy-done.1 = bf16[1,27,32768]{2,1,0:T(8,128)(2,1)S(1)} copy-done((bf16[1,27,32768]{2,1,0:T(8,128)(2,1)S(1)}, bf16[1,27,32768]{2,1,0:T(8,128)(2,1)}, u32[]{:S(2)}) %copy-start.1) | copy-done | bytes 1769496
  10.4 7.1 %shard_map.59 = (bf16[9,512,256]{2,1,0:T(8,128)(2,1)S(1)}, bf16[9,256,512]{2,1,0:T(8,128)(2,1)}, f32[8,128]{1,0:T(8,128)S(1)}) custom-call(bf16[27,32768]{1,0:T(8,128)(2,1)S(1)} %bitcast.12), custom_call_target="tpu_custom_call" | custom-call | bytes 8000000 | tf_op jit(solution)/shard_map/pallas_call | solution.py:20
  17.5 0.1 stack.27.co
  17.6 6.0 %all-to-all-done.cells_ref = bf16[8,4,8,16,128]{4,3,2,1,0:T(8,128)(2,1)S(1)} async-done(((bf16[8,4,8,16,128]{4,3,2,1,0:T(8,128)(2,1)}), bf16[8,4,8,16,128]{4,3,2,1,0:T(8,128)(2,1)S(1)}, u32[]{:S(2)}, u32[]{:S(2)}) %all-to-all-start) | async-done | bytes 1048608 | tf_op jit(solution)/shard_map/all_to_all | solution.py:656
  23.6 0.1 shard_map.60
  23.6 1.7 %collective-permute-start = (bf16[8,8,16,128]{3,2,1,0:T(8,128)(2,1)S(1)}, bf16[8,8,16,128]{3,2,1,0:T(8,128)(2,1)S(1)}, u32[]{:S(2)}, u32[]{:S(2)}) collective-permute-start(bf16[8,8,16,128]{3,2,1,0:T(8,128)(2,1)S(1)} %get-tuple-element.56), channel_id=1, source_target_pairs={{0,1},{1,2},{2,3},{3,4},{4,5},{5,6},{6,7},{7,0},{8,9},{9,10},{10,1... | collective-permute-start | bytes 786440 | tf_op jit(solution)/shard_map/ppermute | solution.py:643
  25.4 4.0 %collective-permute-start.1 = (bf16[8,8,16,128]{3,2,1,0:T(8,128)(2,1)S(1)}, bf16[8,8,16,128]{3,2,1,0:T(8,128)(2,1)S(1)}, u32[]{:S(2)}, u32[]{:S(2)}) collective-permute-start(bf16[8,8,16,128]{3,2,1,0:T(8,128)(2,1)S(1)} %get-tuple-element.57), channel_id=1, source_target_pairs={{1,0},{2,1},{3,2},{4,3},{5,4},{6,5},{7,6},{0,7},{9,8},{10,9},{11,1... | collective-permute-start | bytes 786440 | tf_op jit(solution)/shard_map/ppermute | solution.py:644
  29.4 3.1 %shard_map.61 = (bf16[8,192,512]{2,1,0:T(8,128)(2,1)S(1)}, f32[768,256]{1,0:T(8,128)S(1)}, f32[8,128]{1,0:T(8,128)S(1)}) custom-call(bf16[8,4,8,16,128]{4,3,2,1,0:T(8,128)(2,1)S(1)} %all-to-all-done.cells_ref, bf16[9,512,256]{2,1,0:T(8,128)(2,1)S(1)} %get-tuple-element.52.fore_ref, f32[8,128]{1,0:T(8,128)S(1)} %get-tuple-element.54.token_ref), custom_call_target="tpu_custom_call" | custom-call | flops 4000000000 | bytes 5000000 | tf_op jit(solution)/shard_map/pallas_call | solution.py:20
  32.5 2.6 %collective-permute-done.yb = bf16[8,8,16,128]{3,2,1,0:T(8,128)(2,1)S(1)} collective-permute-done((bf16[8,8,16,128]{3,2,1,0:T(8,128)(2,1)S(1)}, bf16[8,8,16,128]{3,2,1,0:T(8,128)(2,1)S(1)}, u32[]{:S(2)}, u32[]{:S(2)}) %collective-permute-start) | collective-permute-done | bytes 262176 | tf_op jit(solution)/shard_map/ppermute | solution.py:643
  35.1 0.0 collective-permute-done.1.ya
  35.1 0.6 shard_map.62
  35.7 1.5 %collective-permute-start.2 = (bf16[8,6,16,128]{3,2,1,0:T(8,128)(2,1)S(1)}, bf16[8,6,16,128]{3,2,1,0:T(8,128)(2,1)S(1)}, u32[]{:S(2)}, u32[]{:S(2)}) collective-permute-start(bf16[8,6,16,128]{3,2,1,0:T(8,128)(2,1)S(1)} %get-tuple-element.65), channel_id=1, source_target_pairs={{0,8},{8,0},{16,24},{24,16},{1,9},{9,1},{17,25},{25,17},{2,10},{10... | collective-permute-start | bytes 589832 | tf_op jit(solution)/shard_map/ppermute | solution.py:650
  37.2 4.3 %collective-permute-start.3 = (bf16[8,6,16,128]{3,2,1,0:T(8,128)(2,1)S(1)}, bf16[8,6,16,128]{3,2,1,0:T(8,128)(2,1)S(1)}, u32[]{:S(2)}, u32[]{:S(2)}) collective-permute-start(bf16[8,6,16,128]{3,2,1,0:T(8,128)(2,1)S(1)} %get-tuple-element.66), channel_id=1, source_target_pairs={{8,16},{16,8},{9,17},{17,9},{10,18},{18,10},{11,19},{19,11},{12,20... | collective-permute-start | bytes 589832 | tf_op jit(solution)/shard_map/ppermute | solution.py:651
  41.5 2.6 %shard_map.64 = (bf16[8,192,512]{2,1,0:T(8,128)(2,1)S(1)}, bf16[6,4,2048]{2,1,0:T(4,128)(2,1)S(1)}, bf16[6,4,16,128]{3,2,1,0:T(8,128)(2,1)S(1)}) custom-call(s32[8]{0:T(128)S(1)} %stack.27.co, bf16[8,192,512]{2,1,0:T(8,128)(2,1)S(1)} %get-tuple-element.55.own_ref, f32[768,256]{1,0:T(8,128)S(1)} %get-tuple-element.62.total_ref, ...), custom_call_target="tpu_custom_call" | custom-call | flops 1000000000 | bytes 6000000 | tf_op jit(solution)/shard_map/pallas_call | solution.py:20
  44.1 2.2 %shard_map.65 = (bf16[9,192,512]{2,1,0:T(8,128)(2,1)S(1)}, f32[8,128]{1,0:T(8,128)S(1)}) custom-call(bf16[8,192,512]{2,1,0:T(8,128)(2,1)S(1)} %get-tuple-element.64.field_ref, bf16[6,4,16,128]{3,2,1,0:T(8,128)(2,1)S(1)} %get-tuple-element.68.pre_ref.pre_in), custom_call_target="tpu_custom_call" | custom-call | flops 3000000000 | tf_op jit(solution)/shard_map/pallas_call | solution.py:20
  46.3 0.0 collective-permute-done.2.near_ref
  46.3 0.0 collective-permute-done.3.far_ref
  46.3 2.2 %shard_map.66 = (bf16[2,192,512]{2,1,0:T(8,128)(2,1)S(1)}, bf16[8,4,2048]{2,1,0:T(4,128)(2,1)}, bf16[8,4,16,128]{3,2,1,0:T(8,128)(2,1)S(1)}, bf16[8,16,128]{2,1,0:T(8,128)(2,1)S(1)}, bf16[8,16,128]{2,1,0:T(8,128)(2,1)S(1)}) custom-call(s32[8]{0:T(128)S(1)} %stack.27.co, bf16[8,192,512]{2,1,0:T(8,128)(2,1)S(1)} %get-tuple-element.64.field_ref, ...), custom_call_target="tpu_custom_call" | custom-call | flops 2000000000 | bytes 6000000 | tf_op jit(solution)/shard_map/pallas_call | solution.py:20
  48.5 1.8 %shard_map.67 = (f32[2,9,192,128]{3,2,1,0:T(8,128)S(1)}, bf16[2,9,192,128]{3,2,1,0:T(8,128)(2,1)S(1)}) custom-call(s32[8]{0:T(128)S(1)} %stack.27.co, bf16[8,192,512]{2,1,0:T(8,128)(2,1)S(1)} %get-tuple-element.64.field_ref, bf16[2,192,512]{2,1,0:T(8,128)(2,1)S(1)} %get-tuple-element.71.rim_ref, bf16[8,4,16,128]{3,2,1,0:T(8,128)(2,1)S(1)} %get-tuple-element.80.pre_ref, ...), custom_call_target="tpu_custom_call" | custom-call | flops 5000000000 | tf_op jit(solution)/shard_map/pallas_call | solution.py:20
  50.3 0.1 collective-permute-start.4
  50.4 0.1 collective-permute-start.5
  50.5 2.8 %collective-permute-start.6 = (bf16[8,16,128]{2,1,0:T(8,128)(2,1)S(1)}, bf16[8,16,128]{2,1,0:T(8,128)(2,1)S(1)}, u32[]{:S(2)}, u32[]{:S(2)}) collective-permute-start(bf16[8,16,128]{2,1,0:T(8,128)(2,1)S(1)} %get-tuple-element.78), channel_id=1, source_target_pairs={{1,0},{2,1},{3,2},{4,3},{5,4},{6,5},{7,6},{0,7},{9,8},{10,9},{11,1... | collective-permute-start | bytes 98312 | tf_op jit(solution)/shard_map/ppermute | solution.py:644
  53.3 0.0 collective-permute-done.4.got_ref
  53.3 0.0 copy-start
  53.3 0.7 shard_map.68
  54.0 1.8 %collective-permute-start.9 = (bf16[9,192,128]{2,1,0:T(8,128)(2,1)S(1)}, bf16[9,192,128]{2,1,0:T(8,128)(2,1)S(1)}, u32[]{:S(2)}, u32[]{:S(2)}) collective-permute-start(bf16[9,192,128]{2,1,0:T(8,128)(2,1)S(1)} %get-tuple-element.86), channel_id=1, source_target_pairs={{0,16},{8,24},{16,0},{24,8},{1,17},{9,25},{17,1},{25,9},{2,18},{10... | collective-permute-start | bytes 1327112 | tf_op jit(solution)/shard_map/ppermute | solution.py:684
  55.8 0.0 collective-permute-done.5.yb
  55.8 0.0 collective-permute-done.6.ya
  55.8 0.6 shard_map.69
  56.3 0.9 %collective-permute-start.7 = (bf16[6,16,128]{2,1,0:T(8,128)(2,1)S(1)}, bf16[6,16,128]{2,1,0:T(8,128)(2,1)S(1)}, u32[]{:S(2)}, u32[]{:S(2)}) collective-permute-start(bf16[6,16,128]{2,1,0:T(8,128)(2,1)S(1)} %get-tuple-element.83), channel_id=1, source_target_pairs={{0,8},{8,0},{16,24},{24,16},{1,9},{9,1},{17,25},{25,17},{2,10},{10... | collective-permute-start | bytes 73736 | tf_op jit(solution)/shard_map/ppermute | solution.py:650
  57.3 3.3 %collective-permute-start.8 = (bf16[6,16,128]{2,1,0:T(8,128)(2,1)S(1)}, bf16[6,16,128]{2,1,0:T(8,128)(2,1)S(1)}, u32[]{:S(2)}, u32[]{:S(2)}) collective-permute-start(bf16[6,16,128]{2,1,0:T(8,128)(2,1)S(1)} %get-tuple-element.84), channel_id=1, source_target_pairs={{8,16},{16,8},{9,17},{17,9},{10,18},{18,10},{11,19},{19,11},{12,20... | collective-permute-start | bytes 73736 | tf_op jit(solution)/shard_map/ppermute | solution.py:651
  60.6 0.0 copy-done
  60.6 3.8 %shard_map.70.inner_ref = bf16[8,6,4,16,128]{4,3,2,1,0:T(8,128)(2,1)S(1)} custom-call(s32[8]{0:T(128)S(1)} %stack.27.co, bf16[8,4,16,128]{3,2,1,0:T(8,128)(2,1)S(1)} %get-tuple-element.80.pre_ref, bf16[8,16,128]{2,1,0:T(8,128)(2,1)S(1)} %collective-permute-done.5.yb, bf16[8,16,128]{2,1,0:T(8,128)(2,1)S(1)} %collective-permute-done.6.ya, ...), custom_call_target="tpu_custom_call" | custom-call | flops 4000000000 | tf_op jit(solution)/shard_map/pallas_call | solution.py:20
  64.4 0.0 collective-permute-done.7.near_ref
  64.4 3.3 %collective-permute-done.8.far_ref = bf16[6,16,128]{2,1,0:T(8,128)(2,1)S(1)} collective-permute-done((bf16[6,16,128]{2,1,0:T(8,128)(2,1)S(1)}, bf16[6,16,128]{2,1,0:T(8,128)(2,1)S(1)}, u32[]{:S(2)}, u32[]{:S(2)}) %collective-permute-start.8) | collective-permute-done | bytes 24608 | tf_op jit(solution)/shard_map/ppermute | solution.py:651
  67.8 2.5 %shard_map.71 = bf16[8,8,4,16,128]{4,3,2,1,0:T(8,128)(2,1)} custom-call(s32[8]{0:T(128)S(1)} %stack.27.co, bf16[8,4,16,128]{3,2,1,0:T(8,128)(2,1)S(1)} %get-tuple-element.80.pre_ref, bf16[8,16,128]{2,1,0:T(8,128)(2,1)S(1)} %collective-permute-done.5.yb, bf16[8,16,128]{2,1,0:T(8,128)(2,1)S(1)} %collective-permute-done.6.ya, ...), custom_call_target="tpu_custom_call" | custom-call | flops 500000000 | tf_op jit(solution)/shard_map/pallas_call | solution.py:20
  70.2 0.0 collective-permute-done.9.got_ref
  70.2 0.9 %shard_map.72 = (f32[4,16,1728]{2,1,0:T(8,128)S(1)}, bf16[4,16,1728]{2,1,0:T(8,128)(2,1)S(1)}) custom-call(s32[8]{0:T(128)S(1)} %stack.27.co, f32[9,192,128]{2,1,0:T(8,128)S(1)} %get-tuple-element.79.stay_ref, bf16[9,192,128]{2,1,0:T(8,128)(2,1)S(1)} %collective-permute-done.9.got_ref), custom_call_target="tpu_custom_call" | custom-call | flops 20000000000 | bytes 2000000 | tf_op jit(solution)/shard_map/pallas_call | solution.py:20
  71.2 0.1 collective-permute-start.10
  71.3 3.6 %all-to-all-start.1 = ((bf16[8,8,4,16,128]{4,3,2,1,0:T(8,128)(2,1)}), bf16[8,8,4,16,128]{4,3,2,1,0:T(8,128)(2,1)S(1)}, u32[]{:S(2)}, u32[]{:S(2)}) async-start(bf16[8,8,4,16,128]{4,3,2,1,0:T(8,128)(2,1)} %shard_map.71), calls=%async_computation.1 | async-start | bytes 2097152 | tf_op jit(solution)/shard_map/all_to_all | solution.py:656
  74.8 2.4 %collective-permute-done.10.got_ref = bf16[4,16,1728]{2,1,0:T(8,128)(2,1)S(1)} collective-permute-done((bf16[4,16,1728]{2,1,0:T(8,128)(2,1)S(1)}, bf16[4,16,1728]{2,1,0:T(8,128)(2,1)S(1)}, u32[]{:S(2)}, u32[]{:S(2)}) %collective-permute-start.10) | collective-permute-done | bytes 221216 | tf_op jit(solution)/shard_map/ppermute | solution.py:692
  77.3 0.6 shard_map.73
  77.9 2.1 %collective-permute-start.11 = (bf16[16,1728]{1,0:T(8,128)(2,1)S(1)}, bf16[16,1728]{1,0:T(8,128)(2,1)S(1)}, u32[]{:S(2)}, u32[]{:S(2)}) collective-permute-start(bf16[16,1728]{1,0:T(8,128)(2,1)S(1)} %get-tuple-element.91), channel_id=1, source_target_pairs={{0,2},{1,3},{2,4},{3,5},{4,6},{5,7},{6,0},{7,1},{8,10},{9,11},{10,... | collective-permute-start | bytes 165896 | tf_op jit(solution)/shard_map/ppermute | solution.py:695
  80.0 2.0 %collective-permute-start.12 = (bf16[16,1728]{1,0:T(8,128)(2,1)S(1)}, bf16[16,1728]{1,0:T(8,128)(2,1)S(1)}, u32[]{:S(2)}, u32[]{:S(2)}) collective-permute-start(bf16[16,1728]{1,0:T(8,128)(2,1)S(1)} %get-tuple-element.92), channel_id=1, source_target_pairs={{0,4},{1,5},{2,6},{3,7},{4,0},{5,1},{6,2},{7,3},{8,12},{9,13},{10,... | collective-permute-start | bytes 165896 | tf_op jit(solution)/shard_map/ppermute | solution.py:695
  82.0 3.5 %collective-permute-start.13 = (bf16[16,1728]{1,0:T(8,128)(2,1)S(1)}, bf16[16,1728]{1,0:T(8,128)(2,1)S(1)}, u32[]{:S(2)}, u32[]{:S(2)}) collective-permute-start(bf16[16,1728]{1,0:T(8,128)(2,1)S(1)} %get-tuple-element.93), channel_id=1, source_target_pairs={{0,6},{1,7},{2,0},{3,1},{4,2},{5,3},{6,4},{7,5},{8,14},{9,15},{10,... | collective-permute-start | bytes 165896 | tf_op jit(solution)/shard_map/ppermute | solution.py:695
  85.5 0.0 collective-permute-done.11.r1
  85.5 1.7 %collective-permute-done.12.r2 = bf16[16,1728]{1,0:T(8,128)(2,1)S(1)} collective-permute-done((bf16[16,1728]{1,0:T(8,128)(2,1)S(1)}, bf16[16,1728]{1,0:T(8,128)(2,1)S(1)}, u32[]{:S(2)}, u32[]{:S(2)}) %collective-permute-start.12) | collective-permute-done | bytes 55328 | tf_op jit(solution)/shard_map/ppermute | solution.py:695
  87.1 1.7 %collective-permute-done.13.r3 = bf16[16,1728]{1,0:T(8,128)(2,1)S(1)} collective-permute-done((bf16[16,1728]{1,0:T(8,128)(2,1)S(1)}, bf16[16,1728]{1,0:T(8,128)(2,1)S(1)}, u32[]{:S(2)}, u32[]{:S(2)}) %collective-permute-start.13) | collective-permute-done | bytes 55328 | tf_op jit(solution)/shard_map/ppermute | solution.py:695
  88.8 0.0 all-to-all-done.1.parts_ref
  88.8 1.0 %shard_map.74 = (f32[27,8,128]{2,1,0:T(8,128)}, bf16[8,4,2048]{2,1,0:T(4,128)(2,1)}) custom-call(f32[16,1728]{1,0:T(8,128)S(1)} %get-tuple-element.90.r0, bf16[16,1728]{1,0:T(8,128)(2,1)S(1)} %collective-permute-done.11.r1, bf16[16,1728]{1,0:T(8,128)(2,1)S(1)} %collective-permute-done.12.r2, bf16[16,1728]{1,0:T(8,128)(2,1)S(1)} %collective-permute-done.13.r3, ...), custom_call_target="tpu_custom_call" | custom-call | bytes 1800000 | tf_op jit(solution)/shard_map/pallas_call | solution.py:20
  (1 shorter events, 0.0 us)
Async XLA Ops:
  0.6 0.9 %copy-start.2 = (bf16[1,1,8,4,2048]{4,3,2,1,0:T(4,128)(2,1)S(1)}, bf16[1,1,8,4,2048]{4,3,2,1,0:T(4,128)(2,1)}, u32[]{:S(2)}) copy-start(bf16[1,1,8,4,2048]{4,3,2,1,0:T(4,128)(2,1)} %param.3) | copy-start | bytes 393220
  1.5 7.1 %copy-start.3 = (bf16[1,1,8,4,2048]{4,3,2,1,0:T(4,128)(2,1)S(1)}, bf16[1,1,8,4,2048]{4,3,2,1,0:T(4,128)(2,1)}, u32[]{:S(2)}) copy-start(bf16[1,1,8,4,2048]{4,3,2,1,0:T(4,128)(2,1)} %param.5) | copy-start | bytes 393220
  2.7 20.9 %all-to-all-start = ((bf16[8,4,8,16,128]{4,3,2,1,0:T(8,128)(2,1)}), bf16[8,4,8,16,128]{4,3,2,1,0:T(8,128)(2,1)S(1)}, u32[]{:S(2)}, u32[]{:S(2)}) async-start(bf16[8,4,8,16,128]{4,3,2,1,0:T(8,128)(2,1)} %shard_map.58), calls=%async_computation | async-start | bytes 2097152 | tf_op jit(solution)/shard_map/all_to_all | solution.py:656
  8.8 1.6 %copy-start.1 = (bf16[1,27,32768]{2,1,0:T(8,128)(2,1)S(1)}, bf16[1,27,32768]{2,1,0:T(8,128)(2,1)}, u32[]{:S(2)}) copy-start(bf16[1,27,32768]{2,1,0:T(8,128)(2,1)} %param.4) | copy-start | bytes 5308420
  23.6 11.5 %collective-permute-start = (bf16[8,8,16,128]{3,2,1,0:T(8,128)(2,1)S(1)}, bf16[8,8,16,128]{3,2,1,0:T(8,128)(2,1)S(1)}, u32[]{:S(2)}, u32[]{:S(2)}) collective-permute-start(bf16[8,8,16,128]{3,2,1,0:T(8,128)(2,1)S(1)} %get-tuple-element.56), channel_id=1, source_target_pairs={{0,1},{1,2},{2,3},{3,4},{4,5},{5,6},{6,7},{7,0},{8,9},{9,10},{10,1... | collective-permute-start | bytes 786440 | tf_op jit(solution)/shard_map/ppermute | solution.py:643
  25.4 9.8 %collective-permute-start.1 = (bf16[8,8,16,128]{3,2,1,0:T(8,128)(2,1)S(1)}, bf16[8,8,16,128]{3,2,1,0:T(8,128)(2,1)S(1)}, u32[]{:S(2)}, u32[]{:S(2)}) collective-permute-start(bf16[8,8,16,128]{3,2,1,0:T(8,128)(2,1)S(1)} %get-tuple-element.57), channel_id=1, source_target_pairs={{1,0},{2,1},{3,2},{4,3},{5,4},{6,5},{7,6},{0,7},{9,8},{10,9},{11,1... | collective-permute-start | bytes 786440 | tf_op jit(solution)/shard_map/ppermute | solution.py:644
  35.7 10.6 %collective-permute-start.2 = (bf16[8,6,16,128]{3,2,1,0:T(8,128)(2,1)S(1)}, bf16[8,6,16,128]{3,2,1,0:T(8,128)(2,1)S(1)}, u32[]{:S(2)}, u32[]{:S(2)}) collective-permute-start(bf16[8,6,16,128]{3,2,1,0:T(8,128)(2,1)S(1)} %get-tuple-element.65), channel_id=1, source_target_pairs={{0,8},{8,0},{16,24},{24,16},{1,9},{9,1},{17,25},{25,17},{2,10},{10... | collective-permute-start | bytes 589832 | tf_op jit(solution)/shard_map/ppermute | solution.py:650
  37.2 9.1 %collective-permute-start.3 = (bf16[8,6,16,128]{3,2,1,0:T(8,128)(2,1)S(1)}, bf16[8,6,16,128]{3,2,1,0:T(8,128)(2,1)S(1)}, u32[]{:S(2)}, u32[]{:S(2)}) collective-permute-start(bf16[8,6,16,128]{3,2,1,0:T(8,128)(2,1)S(1)} %get-tuple-element.66), channel_id=1, source_target_pairs={{8,16},{16,8},{9,17},{17,9},{10,18},{18,10},{11,19},{19,11},{12,20... | collective-permute-start | bytes 589832 | tf_op jit(solution)/shard_map/ppermute | solution.py:651
  50.3 3.0 %collective-permute-start.4 = (bf16[2,9,192,128]{3,2,1,0:T(8,128)(2,1)S(1)}, bf16[2,9,192,128]{3,2,1,0:T(8,128)(2,1)S(1)}, u32[]{:S(2)}, u32[]{:S(2)}) collective-permute-start(bf16[2,9,192,128]{3,2,1,0:T(8,128)(2,1)S(1)} %get-tuple-element.75), channel_id=1, source_target_pairs={{0,8},{8,0},{16,24},{24,16},{1,9},{9,1},{17,25},{25,17},{2,10},{10... | collective-permute-start | bytes 2654216 | tf_op jit(solution)/shard_map/ppermute | solution.py:681
  50.4 5.4 %collective-permute-start.5 = (bf16[8,16,128]{2,1,0:T(8,128)(2,1)S(1)}, bf16[8,16,128]{2,1,0:T(8,128)(2,1)S(1)}, u32[]{:S(2)}, u32[]{:S(2)}) collective-permute-start(bf16[8,16,128]{2,1,0:T(8,128)(2,1)S(1)} %get-tuple-element.77), channel_id=1, source_target_pairs={{0,1},{1,2},{2,3},{3,4},{4,5},{5,6},{6,7},{7,0},{8,9},{9,10},{10,1... | collective-permute-start | bytes 98312 | tf_op jit(solution)/shard_map/ppermute | solution.py:643
  50.5 5.3 %collective-permute-start.6 = (bf16[8,16,128]{2,1,0:T(8,128)(2,1)S(1)}, bf16[8,16,128]{2,1,0:T(8,128)(2,1)S(1)}, u32[]{:S(2)}, u32[]{:S(2)}) collective-permute-start(bf16[8,16,128]{2,1,0:T(8,128)(2,1)S(1)} %get-tuple-element.78), channel_id=1, source_target_pairs={{1,0},{2,1},{3,2},{4,3},{5,4},{6,5},{7,6},{0,7},{9,8},{10,9},{11,1... | collective-permute-start | bytes 98312 | tf_op jit(solution)/shard_map/ppermute | solution.py:644
  53.3 7.3 %copy-start = (bf16[9,256,512]{2,1,0:T(8,128)(2,1)S(1)}, bf16[9,256,512]{2,1,0:T(8,128)(2,1)}, u32[]{:S(2)}) copy-start(bf16[9,256,512]{2,1,0:T(8,128)(2,1)} %get-tuple-element.85.back_ref) | copy-start | bytes 7077892
  54.0 16.2 %collective-permute-start.9 = (bf16[9,192,128]{2,1,0:T(8,128)(2,1)S(1)}, bf16[9,192,128]{2,1,0:T(8,128)(2,1)S(1)}, u32[]{:S(2)}, u32[]{:S(2)}) collective-permute-start(bf16[9,192,128]{2,1,0:T(8,128)(2,1)S(1)} %get-tuple-element.86), channel_id=1, source_target_pairs={{0,16},{8,24},{16,0},{24,8},{1,17},{9,25},{17,1},{25,9},{2,18},{10... | collective-permute-start | bytes 1327112 | tf_op jit(solution)/shard_map/ppermute | solution.py:684
  56.3 8.1 %collective-permute-start.7 = (bf16[6,16,128]{2,1,0:T(8,128)(2,1)S(1)}, bf16[6,16,128]{2,1,0:T(8,128)(2,1)S(1)}, u32[]{:S(2)}, u32[]{:S(2)}) collective-permute-start(bf16[6,16,128]{2,1,0:T(8,128)(2,1)S(1)} %get-tuple-element.83), channel_id=1, source_target_pairs={{0,8},{8,0},{16,24},{24,16},{1,9},{9,1},{17,25},{25,17},{2,10},{10... | collective-permute-start | bytes 73736 | tf_op jit(solution)/shard_map/ppermute | solution.py:650
  57.3 10.5 %collective-permute-start.8 = (bf16[6,16,128]{2,1,0:T(8,128)(2,1)S(1)}, bf16[6,16,128]{2,1,0:T(8,128)(2,1)S(1)}, u32[]{:S(2)}, u32[]{:S(2)}) collective-permute-start(bf16[6,16,128]{2,1,0:T(8,128)(2,1)S(1)} %get-tuple-element.84), channel_id=1, source_target_pairs={{8,16},{16,8},{9,17},{17,9},{10,18},{18,10},{11,19},{19,11},{12,20... | collective-permute-start | bytes 73736 | tf_op jit(solution)/shard_map/ppermute | solution.py:651
  71.2 6.1 %collective-permute-start.10 = (bf16[4,16,1728]{2,1,0:T(8,128)(2,1)S(1)}, bf16[4,16,1728]{2,1,0:T(8,128)(2,1)S(1)}, u32[]{:S(2)}, u32[]{:S(2)}) collective-permute-start(bf16[4,16,1728]{2,1,0:T(8,128)(2,1)S(1)} %get-tuple-element.89), channel_id=1, source_target_pairs={{0,1},{1,0},{2,3},{3,2},{4,5},{5,4},{6,7},{7,6},{8,9},{9,8},{10,11... | collective-permute-start | bytes 663560 | tf_op jit(solution)/shard_map/ppermute | solution.py:692
  71.3 17.5 %all-to-all-start.1 = ((bf16[8,8,4,16,128]{4,3,2,1,0:T(8,128)(2,1)}), bf16[8,8,4,16,128]{4,3,2,1,0:T(8,128)(2,1)S(1)}, u32[]{:S(2)}, u32[]{:S(2)}) async-start(bf16[8,8,4,16,128]{4,3,2,1,0:T(8,128)(2,1)} %shard_map.71), calls=%async_computation.1 | async-start | bytes 2097152 | tf_op jit(solution)/shard_map/all_to_all | solution.py:656
  77.9 7.6 %collective-permute-start.11 = (bf16[16,1728]{1,0:T(8,128)(2,1)S(1)}, bf16[16,1728]{1,0:T(8,128)(2,1)S(1)}, u32[]{:S(2)}, u32[]{:S(2)}) collective-permute-start(bf16[16,1728]{1,0:T(8,128)(2,1)S(1)} %get-tuple-element.91), channel_id=1, source_target_pairs={{0,2},{1,3},{2,4},{3,5},{4,6},{5,7},{6,0},{7,1},{8,10},{9,11},{10,... | collective-permute-start | bytes 165896 | tf_op jit(solution)/shard_map/ppermute | solution.py:695
  80.0 7.1 %collective-permute-start.12 = (bf16[16,1728]{1,0:T(8,128)(2,1)S(1)}, bf16[16,1728]{1,0:T(8,128)(2,1)S(1)}, u32[]{:S(2)}, u32[]{:S(2)}) collective-permute-start(bf16[16,1728]{1,0:T(8,128)(2,1)S(1)} %get-tuple-element.92), channel_id=1, source_target_pairs={{0,4},{1,5},{2,6},{3,7},{4,0},{5,1},{6,2},{7,3},{8,12},{9,13},{10,... | collective-permute-start | bytes 165896 | tf_op jit(solution)/shard_map/ppermute | solution.py:695
  82.0 6.8 %collective-permute-start.13 = (bf16[16,1728]{1,0:T(8,128)(2,1)S(1)}, bf16[16,1728]{1,0:T(8,128)(2,1)S(1)}, u32[]{:S(2)}, u32[]{:S(2)}) collective-permute-start(bf16[16,1728]{1,0:T(8,128)(2,1)S(1)} %get-tuple-element.93), channel_id=1, source_target_pairs={{0,6},{1,7},{2,0},{3,1},{4,2},{5,3},{6,4},{7,5},{8,14},{9,15},{10,... | collective-permute-start | bytes 165896 | tf_op jit(solution)/shard_map/ppermute | solution.py:695

commit v8 on v7

--- a/solution.py
+++ b/solution.py
@@ -691,7 +691,7 @@
     keep, send = add_far(coords, stay, got)
     got = lax.ppermute(send, "sy", [(i, i ^ 1) for i in range(8)])
     regions = list(add_near(coords, keep, got))
-    for d in (2, 1, 3):
+    for d in (2, 3, 1):
         regions[d] = lax.ppermute(regions[d], "sy", [(i, (i + 2 * d) % 8) for i in range(8)])
     weight_grad, input_grad = last_sums(regions, parts)
     return outputs[None, None], input_grad[None, None], weight_grad.reshape(1, 27, 1024)

time: 90 us -> 90 us (level)
  no operation moved by 1% of the time
where the time goes in v8:
time: 90 us; the launch traced here: 89.8 us
  starting transfers between devices  37.7 us (42%)
  Pallas kernels  30.9 us (34%)
  waiting for transfers between devices  17.7 us (20%)
  local copies, waits for them, and re-layouts  2.58 us (3%)
    pallas_call x17, Pallas kernels, call(): pl.pallas_call(kernel, out_shape=outs, in_specs=[pl.BlockSpec(memory_spac...  30.9 us
    all_to_all x2, starting transfers between devices, exchange(): return lax.all_to_all(parts, axis, 0, 0)  9.52 us
    ppermute x2, starting transfers between devices, x_rims(): lax.ppermute(far, 'sx', [(1, 2), (2, 1)])  7.59 us
    ppermute x3, starting transfers between devices, per_device(): lax.ppermute(regions[d], 'sy', [(i, (i + 2 * d) % 8) for i in range(8)])  7.57 us
    ppermute x2, starting transfers between devices, both_ways(): lax.ppermute(first, axis, [((i + 1) % size, i) for i in range(size)])  6.86 us
    all_to_all x2, waiting for transfers between devices, exchange(): return lax.all_to_all(parts, axis, 0, 0)  5.98 us
    ppermute x2, waiting for transfers between devices, x_rims(): lax.ppermute(far, 'sx', [(1, 2), (2, 1)])  3.34 us
    ppermute x3, waiting for transfers between devices, per_device(): lax.ppermute(regions[d], 'sy', [(i, (i + 2 * d) % 8) for i in range(8)])  3.31 us
  transfers between devices with their start and end apart: 16, of which 6 were waited for; matrix products, arithmetic and copies ran while one was open for 0% of the time, Pallas kernels for 26%

profile of v8, /device:TPU:1, one launch (start us, length us, event | category | flops | bytes accessed | tf_op | source)
XLA Modules:
  0.0 89.8 jit_solution(8546383130719323148)
XLA Ops:
  0.6 0.0 copy-start.2
  0.6 0.9 copy-done.2
  1.5 0.0 copy-start.3
  1.5 1.2 %shard_map.58 = bf16[8,4,8,16,128]{4,3,2,1,0:T(8,128)(2,1)} custom-call(bf16[8,4,2048]{2,1,0:T(4,128)(2,1)S(1)} %bitcast.13), custom_call_target="tpu_custom_call" | custom-call | bytes 1300000 | tf_op jit(solution)/shard_map/pallas_call | solution.py:20
  2.7 5.9 %all-to-all-start = ((bf16[8,4,8,16,128]{4,3,2,1,0:T(8,128)(2,1)}), bf16[8,4,8,16,128]{4,3,2,1,0:T(8,128)(2,1)S(1)}, u32[]{:S(2)}, u32[]{:S(2)}) async-start(bf16[8,4,8,16,128]{4,3,2,1,0:T(8,128)(2,1)} %shard_map.58), calls=%async_computation | async-start | bytes 2097152 | tf_op jit(solution)/shard_map/all_to_all | solution.py:656
  8.7 0.0 copy-done.3
  8.7 0.1 shard_map.63.grad_ref
  8.8 0.0 copy-start.1
  8.8 1.6 %copy-done.1 = bf16[1,27,32768]{2,1,0:T(8,128)(2,1)S(1)} copy-done((bf16[1,27,32768]{2,1,0:T(8,128)(2,1)S(1)}, bf16[1,27,32768]{2,1,0:T(8,128)(2,1)}, u32[]{:S(2)}) %copy-start.1) | copy-done | bytes 1769496
  10.4 7.1 %shard_map.59 = (bf16[9,512,256]{2,1,0:T(8,128)(2,1)S(1)}, bf16[9,256,512]{2,1,0:T(8,128)(2,1)}, f32[8,128]{1,0:T(8,128)S(1)}) custom-call(bf16[27,32768]{1,0:T(8,128)(2,1)S(1)} %bitcast.12), custom_call_target="tpu_custom_call" | custom-call | bytes 8000000 | tf_op jit(solution)/shard_map/pallas_call | solution.py:20
  17.5 0.1 stack.27.co
  17.6 6.0 %all-to-all-done.cells_ref = bf16[8,4,8,16,128]{4,3,2,1,0:T(8,128)(2,1)S(1)} async-done(((bf16[8,4,8,16,128]{4,3,2,1,0:T(8,128)(2,1)}), bf16[8,4,8,16,128]{4,3,2,1,0:T(8,128)(2,1)S(1)}, u32[]{:S(2)}, u32[]{:S(2)}) %all-to-all-start) | async-done | bytes 1048608 | tf_op jit(solution)/shard_map/all_to_all | solution.py:656
  23.6 0.1 shard_map.60
  23.6 1.7 %collective-permute-start = (bf16[8,8,16,128]{3,2,1,0:T(8,128)(2,1)S(1)}, bf16[8,8,16,128]{3,2,1,0:T(8,128)(2,1)S(1)}, u32[]{:S(2)}, u32[]{:S(2)}) collective-permute-start(bf16[8,8,16,128]{3,2,1,0:T(8,128)(2,1)S(1)} %get-tuple-element.56), channel_id=1, source_target_pairs={{0,1},{1,2},{2,3},{3,4},{4,5},{5,6},{6,7},{7,0},{8,9},{9,10},{10,1... | collective-permute-start | bytes 786440 | tf_op jit(solution)/shard_map/ppermute | solution.py:643
  25.4 4.0 %collective-permute-start.1 = (bf16[8,8,16,128]{3,2,1,0:T(8,128)(2,1)S(1)}, bf16[8,8,16,128]{3,2,1,0:T(8,128)(2,1)S(1)}, u32[]{:S(2)}, u32[]{:S(2)}) collective-permute-start(bf16[8,8,16,128]{3,2,1,0:T(8,128)(2,1)S(1)} %get-tuple-element.57), channel_id=1, source_target_pairs={{1,0},{2,1},{3,2},{4,3},{5,4},{6,5},{7,6},{0,7},{9,8},{10,9},{11,1... | collective-permute-start | bytes 786440 | tf_op jit(solution)/shard_map/ppermute | solution.py:644
  29.4 3.1 %shard_map.61 = (bf16[8,192,512]{2,1,0:T(8,128)(2,1)S(1)}, f32[768,256]{1,0:T(8,128)S(1)}, f32[8,128]{1,0:T(8,128)S(1)}) custom-call(bf16[8,4,8,16,128]{4,3,2,1,0:T(8,128)(2,1)S(1)} %all-to-all-done.cells_ref, bf16[9,512,256]{2,1,0:T(8,128)(2,1)S(1)} %get-tuple-element.52.fore_ref, f32[8,128]{1,0:T(8,128)S(1)} %get-tuple-element.54.token_ref), custom_call_target="tpu_custom_call" | custom-call | flops 4000000000 | bytes 5000000 | tf_op jit(solution)/shard_map/pallas_call | solution.py:20
  32.5 2.6 %collective-permute-done.yb = bf16[8,8,16,128]{3,2,1,0:T(8,128)(2,1)S(1)} collective-permute-done((bf16[8,8,16,128]{3,2,1,0:T(8,128)(2,1)S(1)}, bf16[8,8,16,128]{3,2,1,0:T(8,128)(2,1)S(1)}, u32[]{:S(2)}, u32[]{:S(2)}) %collective-permute-start) | collective-permute-done | bytes 262176 | tf_op jit(solution)/shard_map/ppermute | solution.py:643
  35.1 0.0 collective-permute-done.1.ya
  35.1 0.6 shard_map.62
  35.7 1.5 %collective-permute-start.2 = (bf16[8,6,16,128]{3,2,1,0:T(8,128)(2,1)S(1)}, bf16[8,6,16,128]{3,2,1,0:T(8,128)(2,1)S(1)}, u32[]{:S(2)}, u32[]{:S(2)}) collective-permute-start(bf16[8,6,16,128]{3,2,1,0:T(8,128)(2,1)S(1)} %get-tuple-element.65), channel_id=1, source_target_pairs={{0,8},{8,0},{16,24},{24,16},{1,9},{9,1},{17,25},{25,17},{2,10},{10... | collective-permute-start | bytes 589832 | tf_op jit(solution)/shard_map/ppermute | solution.py:650
  37.2 4.3 %collective-permute-start.3 = (bf16[8,6,16,128]{3,2,1,0:T(8,128)(2,1)S(1)}, bf16[8,6,16,128]{3,2,1,0:T(8,128)(2,1)S(1)}, u32[]{:S(2)}, u32[]{:S(2)}) collective-permute-start(bf16[8,6,16,128]{3,2,1,0:T(8,128)(2,1)S(1)} %get-tuple-element.66), channel_id=1, source_target_pairs={{8,16},{16,8},{9,17},{17,9},{10,18},{18,10},{11,19},{19,11},{12,20... | collective-permute-start | bytes 589832 | tf_op jit(solution)/shard_map/ppermute | solution.py:651
  41.5 2.6 %shard_map.64 = (bf16[8,192,512]{2,1,0:T(8,128)(2,1)S(1)}, bf16[6,4,2048]{2,1,0:T(4,128)(2,1)S(1)}, bf16[6,4,16,128]{3,2,1,0:T(8,128)(2,1)S(1)}) custom-call(s32[8]{0:T(128)S(1)} %stack.27.co, bf16[8,192,512]{2,1,0:T(8,128)(2,1)S(1)} %get-tuple-element.55.own_ref, f32[768,256]{1,0:T(8,128)S(1)} %get-tuple-element.62.total_ref, ...), custom_call_target="tpu_custom_call" | custom-call | flops 1000000000 | bytes 6000000 | tf_op jit(solution)/shard_map/pallas_call | solution.py:20
  44.1 2.2 %shard_map.65 = (bf16[9,192,512]{2,1,0:T(8,128)(2,1)S(1)}, f32[8,128]{1,0:T(8,128)S(1)}) custom-call(bf16[8,192,512]{2,1,0:T(8,128)(2,1)S(1)} %get-tuple-element.64.field_ref, bf16[6,4,16,128]{3,2,1,0:T(8,128)(2,1)S(1)} %get-tuple-element.68.pre_ref.pre_in), custom_call_target="tpu_custom_call" | custom-call | flops 3000000000 | tf_op jit(solution)/shard_map/pallas_call | solution.py:20
  46.3 0.0 collective-permute-done.2.near_ref
  46.3 0.0 collective-permute-done.3.far_ref
  46.3 2.2 %shard_map.66 = (bf16[2,192,512]{2,1,0:T(8,128)(2,1)S(1)}, bf16[8,4,2048]{2,1,0:T(4,128)(2,1)}, bf16[8,4,16,128]{3,2,1,0:T(8,128)(2,1)S(1)}, bf16[8,16,128]{2,1,0:T(8,128)(2,1)S(1)}, bf16[8,16,128]{2,1,0:T(8,128)(2,1)S(1)}) custom-call(s32[8]{0:T(128)S(1)} %stack.27.co, bf16[8,192,512]{2,1,0:T(8,128)(2,1)S(1)} %get-tuple-element.64.field_ref, ...), custom_call_target="tpu_custom_call" | custom-call | flops 2000000000 | bytes 6000000 | tf_op jit(solution)/shard_map/pallas_call | solution.py:20
  48.5 1.8 %shard_map.67 = (f32[2,9,192,128]{3,2,1,0:T(8,128)S(1)}, bf16[2,9,192,128]{3,2,1,0:T(8,128)(2,1)S(1)}) custom-call(s32[8]{0:T(128)S(1)} %stack.27.co, bf16[8,192,512]{2,1,0:T(8,128)(2,1)S(1)} %get-tuple-element.64.field_ref, bf16[2,192,512]{2,1,0:T(8,128)(2,1)S(1)} %get-tuple-element.71.rim_ref, bf16[8,4,16,128]{3,2,1,0:T(8,128)(2,1)S(1)} %get-tuple-element.80.pre_ref, ...), custom_call_target="tpu_custom_call" | custom-call | flops 5000000000 | tf_op jit(solution)/shard_map/pallas_call | solution.py:20
  50.3 0.1 collective-permute-start.4
  50.4 0.1 collective-permute-start.5
  50.5 2.8 %collective-permute-start.6 = (bf16[8,16,128]{2,1,0:T(8,128)(2,1)S(1)}, bf16[8,16,128]{2,1,0:T(8,128)(2,1)S(1)}, u32[]{:S(2)}, u32[]{:S(2)}) collective-permute-start(bf16[8,16,128]{2,1,0:T(8,128)(2,1)S(1)} %get-tuple-element.78), channel_id=1, source_target_pairs={{1,0},{2,1},{3,2},{4,3},{5,4},{6,5},{7,6},{0,7},{9,8},{10,9},{11,1... | collective-permute-start | bytes 98312 | tf_op jit(solution)/shard_map/ppermute | solution.py:644
  53.3 0.0 collective-permute-done.4.got_ref
  53.3 0.0 copy-start
  53.3 0.7 shard_map.68
  54.0 1.8 %collective-permute-start.9 = (bf16[9,192,128]{2,1,0:T(8,128)(2,1)S(1)}, bf16[9,192,128]{2,1,0:T(8,128)(2,1)S(1)}, u32[]{:S(2)}, u32[]{:S(2)}) collective-permute-start(bf16[9,192,128]{2,1,0:T(8,128)(2,1)S(1)} %get-tuple-element.86), channel_id=1, source_target_pairs={{0,16},{8,24},{16,0},{24,8},{1,17},{9,25},{17,1},{25,9},{2,18},{10... | collective-permute-start | bytes 1327112 | tf_op jit(solution)/shard_map/ppermute | solution.py:684
  55.8 0.0 collective-permute-done.5.yb
  55.8 0.0 collective-permute-done.6.ya
  55.8 0.6 shard_map.69
  56.3 0.9 %collective-permute-start.7 = (bf16[6,16,128]{2,1,0:T(8,128)(2,1)S(1)}, bf16[6,16,128]{2,1,0:T(8,128)(2,1)S(1)}, u32[]{:S(2)}, u32[]{:S(2)}) collective-permute-start(bf16[6,16,128]{2,1,0:T(8,128)(2,1)S(1)} %get-tuple-element.83), channel_id=1, source_target_pairs={{0,8},{8,0},{16,24},{24,16},{1,9},{9,1},{17,25},{25,17},{2,10},{10... | collective-permute-start | bytes 73736 | tf_op jit(solution)/shard_map/ppermute | solution.py:650
  57.3 3.3 %collective-permute-start.8 = (bf16[6,16,128]{2,1,0:T(8,128)(2,1)S(1)}, bf16[6,16,128]{2,1,0:T(8,128)(2,1)S(1)}, u32[]{:S(2)}, u32[]{:S(2)}) collective-permute-start(bf16[6,16,128]{2,1,0:T(8,128)(2,1)S(1)} %get-tuple-element.84), channel_id=1, source_target_pairs={{8,16},{16,8},{9,17},{17,9},{10,18},{18,10},{11,19},{19,11},{12,20... | collective-permute-start | bytes 73736 | tf_op jit(solution)/shard_map/ppermute | solution.py:651
  60.6 0.0 copy-done
  60.6 3.8 %shard_map.70.inner_ref = bf16[8,6,4,16,128]{4,3,2,1,0:T(8,128)(2,1)S(1)} custom-call(s32[8]{0:T(128)S(1)} %stack.27.co, bf16[8,4,16,128]{3,2,1,0:T(8,128)(2,1)S(1)} %get-tuple-element.80.pre_ref, bf16[8,16,128]{2,1,0:T(8,128)(2,1)S(1)} %collective-permute-done.5.yb, bf16[8,16,128]{2,1,0:T(8,128)(2,1)S(1)} %collective-permute-done.6.ya, ...), custom_call_target="tpu_custom_call" | custom-call | flops 4000000000 | tf_op jit(solution)/shard_map/pallas_call | solution.py:20
  64.4 0.0 collective-permute-done.7.near_ref
  64.4 3.3 %collective-permute-done.8.far_ref = bf16[6,16,128]{2,1,0:T(8,128)(2,1)S(1)} collective-permute-done((bf16[6,16,128]{2,1,0:T(8,128)(2,1)S(1)}, bf16[6,16,128]{2,1,0:T(8,128)(2,1)S(1)}, u32[]{:S(2)}, u32[]{:S(2)}) %collective-permute-start.8) | collective-permute-done | bytes 24608 | tf_op jit(solution)/shard_map/ppermute | solution.py:651
  67.8 2.5 %shard_map.71 = bf16[8,8,4,16,128]{4,3,2,1,0:T(8,128)(2,1)} custom-call(s32[8]{0:T(128)S(1)} %stack.27.co, bf16[8,4,16,128]{3,2,1,0:T(8,128)(2,1)S(1)} %get-tuple-element.80.pre_ref, bf16[8,16,128]{2,1,0:T(8,128)(2,1)S(1)} %collective-permute-done.5.yb, bf16[8,16,128]{2,1,0:T(8,128)(2,1)S(1)} %collective-permute-done.6.ya, ...), custom_call_target="tpu_custom_call" | custom-call | flops 500000000 | tf_op jit(solution)/shard_map/pallas_call | solution.py:20
  70.2 0.0 collective-permute-done.9.got_ref
  70.2 0.9 %shard_map.72 = (f32[4,16,1728]{2,1,0:T(8,128)S(1)}, bf16[4,16,1728]{2,1,0:T(8,128)(2,1)S(1)}) custom-call(s32[8]{0:T(128)S(1)} %stack.27.co, f32[9,192,128]{2,1,0:T(8,128)S(1)} %get-tuple-element.79.stay_ref, bf16[9,192,128]{2,1,0:T(8,128)(2,1)S(1)} %collective-permute-done.9.got_ref), custom_call_target="tpu_custom_call" | custom-call | flops 20000000000 | bytes 2000000 | tf_op jit(solution)/shard_map/pallas_call | solution.py:20
  71.2 0.1 collective-permute-start.10
  71.3 3.6 %all-to-all-start.1 = ((bf16[8,8,4,16,128]{4,3,2,1,0:T(8,128)(2,1)}), bf16[8,8,4,16,128]{4,3,2,1,0:T(8,128)(2,1)S(1)}, u32[]{:S(2)}, u32[]{:S(2)}) async-start(bf16[8,8,4,16,128]{4,3,2,1,0:T(8,128)(2,1)} %shard_map.71), calls=%async_computation.1 | async-start | bytes 2097152 | tf_op jit(solution)/shard_map/all_to_all | solution.py:656
  74.8 2.4 %collective-permute-done.10.got_ref = bf16[4,16,1728]{2,1,0:T(8,128)(2,1)S(1)} collective-permute-done((bf16[4,16,1728]{2,1,0:T(8,128)(2,1)S(1)}, bf16[4,16,1728]{2,1,0:T(8,128)(2,1)S(1)}, u32[]{:S(2)}, u32[]{:S(2)}) %collective-permute-start.10) | collective-permute-done | bytes 221216 | tf_op jit(solution)/shard_map/ppermute | solution.py:692
  77.3 0.6 shard_map.73
  77.9 2.1 %collective-permute-start.11 = (bf16[16,1728]{1,0:T(8,128)(2,1)S(1)}, bf16[16,1728]{1,0:T(8,128)(2,1)S(1)}, u32[]{:S(2)}, u32[]{:S(2)}) collective-permute-start(bf16[16,1728]{1,0:T(8,128)(2,1)S(1)} %get-tuple-element.91), channel_id=1, source_target_pairs={{0,2},{1,3},{2,4},{3,5},{4,6},{5,7},{6,0},{7,1},{8,10},{9,11},{10,... | collective-permute-start | bytes 165896 | tf_op jit(solution)/shard_map/ppermute | solution.py:695
  80.0 2.0 %collective-permute-start.12 = (bf16[16,1728]{1,0:T(8,128)(2,1)S(1)}, bf16[16,1728]{1,0:T(8,128)(2,1)S(1)}, u32[]{:S(2)}, u32[]{:S(2)}) collective-permute-start(bf16[16,1728]{1,0:T(8,128)(2,1)S(1)} %get-tuple-element.92), channel_id=1, source_target_pairs={{0,4},{1,5},{2,6},{3,7},{4,0},{5,1},{6,2},{7,3},{8,12},{9,13},{10,... | collective-permute-start | bytes 165896 | tf_op jit(solution)/shard_map/ppermute | solution.py:695
  82.0 3.5 %collective-permute-start.13 = (bf16[16,1728]{1,0:T(8,128)(2,1)S(1)}, bf16[16,1728]{1,0:T(8,128)(2,1)S(1)}, u32[]{:S(2)}, u32[]{:S(2)}) collective-permute-start(bf16[16,1728]{1,0:T(8,128)(2,1)S(1)} %get-tuple-element.93), channel_id=1, source_target_pairs={{0,6},{1,7},{2,0},{3,1},{4,2},{5,3},{6,4},{7,5},{8,14},{9,15},{10,... | collective-permute-start | bytes 165896 | tf_op jit(solution)/shard_map/ppermute | solution.py:695
  85.5 0.0 collective-permute-done.11.r1
  85.5 1.7 %collective-permute-done.12.r2 = bf16[16,1728]{1,0:T(8,128)(2,1)S(1)} collective-permute-done((bf16[16,1728]{1,0:T(8,128)(2,1)S(1)}, bf16[16,1728]{1,0:T(8,128)(2,1)S(1)}, u32[]{:S(2)}, u32[]{:S(2)}) %collective-permute-start.12) | collective-permute-done | bytes 55328 | tf_op jit(solution)/shard_map/ppermute | solution.py:695
  87.1 1.7 %collective-permute-done.13.r3 = bf16[16,1728]{1,0:T(8,128)(2,1)S(1)} collective-permute-done((bf16[16,1728]{1,0:T(8,128)(2,1)S(1)}, bf16[16,1728]{1,0:T(8,128)(2,1)S(1)}, u32[]{:S(2)}, u32[]{:S(2)}) %collective-permute-start.13) | collective-permute-done | bytes 55328 | tf_op jit(solution)/shard_map/ppermute | solution.py:695
  88.8 0.0 all-to-all-done.1.parts_ref
  88.8 1.0 %shard_map.74 = (f32[27,8,128]{2,1,0:T(8,128)}, bf16[8,4,2048]{2,1,0:T(4,128)(2,1)}) custom-call(f32[16,1728]{1,0:T(8,128)S(1)} %get-tuple-element.90.r0, bf16[16,1728]{1,0:T(8,128)(2,1)S(1)} %collective-permute-done.11.r1, bf16[16,1728]{1,0:T(8,128)(2,1)S(1)} %collective-permute-done.12.r2, bf16[16,1728]{1,0:T(8,128)(2,1)S(1)} %collective-permute-done.13.r3, ...), custom_call_target="tpu_custom_call" | custom-call | bytes 1800000 | tf_op jit(solution)/shard_map/pallas_call | solution.py:20
  (1 shorter events, 0.0 us)
Async XLA Ops:
  0.6 0.9 %copy-start.2 = (bf16[1,1,8,4,2048]{4,3,2,1,0:T(4,128)(2,1)S(1)}, bf16[1,1,8,4,2048]{4,3,2,1,0:T(4,128)(2,1)}, u32[]{:S(2)}) copy-start(bf16[1,1,8,4,2048]{4,3,2,1,0:T(4,128)(2,1)} %param.3) | copy-start | bytes 393220
  1.5 7.1 %copy-start.3 = (bf16[1,1,8,4,2048]{4,3,2,1,0:T(4,128)(2,1)S(1)}, bf16[1,1,8,4,2048]{4,3,2,1,0:T(4,128)(2,1)}, u32[]{:S(2)}) copy-start(bf16[1,1,8,4,2048]{4,3,2,1,0:T(4,128)(2,1)} %param.5) | copy-start | bytes 393220
  2.7 20.9 %all-to-all-start = ((bf16[8,4,8,16,128]{4,3,2,1,0:T(8,128)(2,1)}), bf16[8,4,8,16,128]{4,3,2,1,0:T(8,128)(2,1)S(1)}, u32[]{:S(2)}, u32[]{:S(2)}) async-start(bf16[8,4,8,16,128]{4,3,2,1,0:T(8,128)(2,1)} %shard_map.58), calls=%async_computation | async-start | bytes 2097152 | tf_op jit(solution)/shard_map/all_to_all | solution.py:656
  8.8 1.6 %copy-start.1 = (bf16[1,27,32768]{2,1,0:T(8,128)(2,1)S(1)}, bf16[1,27,32768]{2,1,0:T(8,128)(2,1)}, u32[]{:S(2)}) copy-start(bf16[1,27,32768]{2,1,0:T(8,128)(2,1)} %param.4) | copy-start | bytes 5308420
  23.6 11.5 %collective-permute-start = (bf16[8,8,16,128]{3,2,1,0:T(8,128)(2,1)S(1)}, bf16[8,8,16,128]{3,2,1,0:T(8,128)(2,1)S(1)}, u32[]{:S(2)}, u32[]{:S(2)}) collective-permute-start(bf16[8,8,16,128]{3,2,1,0:T(8,128)(2,1)S(1)} %get-tuple-element.56), channel_id=1, source_target_pairs={{0,1},{1,2},{2,3},{3,4},{4,5},{5,6},{6,7},{7,0},{8,9},{9,10},{10,1... | collective-permute-start | bytes 786440 | tf_op jit(solution)/shard_map/ppermute | solution.py:643
  25.4 9.8 %collective-permute-start.1 = (bf16[8,8,16,128]{3,2,1,0:T(8,128)(2,1)S(1)}, bf16[8,8,16,128]{3,2,1,0:T(8,128)(2,1)S(1)}, u32[]{:S(2)}, u32[]{:S(2)}) collective-permute-start(bf16[8,8,16,128]{3,2,1,0:T(8,128)(2,1)S(1)} %get-tuple-element.57), channel_id=1, source_target_pairs={{1,0},{2,1},{3,2},{4,3},{5,4},{6,5},{7,6},{0,7},{9,8},{10,9},{11,1... | collective-permute-start | bytes 786440 | tf_op jit(solution)/shard_map/ppermute | solution.py:644
  35.7 10.6 %collective-permute-start.2 = (bf16[8,6,16,128]{3,2,1,0:T(8,128)(2,1)S(1)}, bf16[8,6,16,128]{3,2,1,0:T(8,128)(2,1)S(1)}, u32[]{:S(2)}, u32[]{:S(2)}) collective-permute-start(bf16[8,6,16,128]{3,2,1,0:T(8,128)(2,1)S(1)} %get-tuple-element.65), channel_id=1, source_target_pairs={{0,8},{8,0},{16,24},{24,16},{1,9},{9,1},{17,25},{25,17},{2,10},{10... | collective-permute-start | bytes 589832 | tf_op jit(solution)/shard_map/ppermute | solution.py:650
  37.2 9.1 %collective-permute-start.3 = (bf16[8,6,16,128]{3,2,1,0:T(8,128)(2,1)S(1)}, bf16[8,6,16,128]{3,2,1,0:T(8,128)(2,1)S(1)}, u32[]{:S(2)}, u32[]{:S(2)}) collective-permute-start(bf16[8,6,16,128]{3,2,1,0:T(8,128)(2,1)S(1)} %get-tuple-element.66), channel_id=1, source_target_pairs={{8,16},{16,8},{9,17},{17,9},{10,18},{18,10},{11,19},{19,11},{12,20... | collective-permute-start | bytes 589832 | tf_op jit(solution)/shard_map/ppermute | solution.py:651
  50.3 3.0 %collective-permute-start.4 = (bf16[2,9,192,128]{3,2,1,0:T(8,128)(2,1)S(1)}, bf16[2,9,192,128]{3,2,1,0:T(8,128)(2,1)S(1)}, u32[]{:S(2)}, u32[]{:S(2)}) collective-permute-start(bf16[2,9,192,128]{3,2,1,0:T(8,128)(2,1)S(1)} %get-tuple-element.75), channel_id=1, source_target_pairs={{0,8},{8,0},{16,24},{24,16},{1,9},{9,1},{17,25},{25,17},{2,10},{10... | collective-permute-start | bytes 2654216 | tf_op jit(solution)/shard_map/ppermute | solution.py:681
  50.4 5.4 %collective-permute-start.5 = (bf16[8,16,128]{2,1,0:T(8,128)(2,1)S(1)}, bf16[8,16,128]{2,1,0:T(8,128)(2,1)S(1)}, u32[]{:S(2)}, u32[]{:S(2)}) collective-permute-start(bf16[8,16,128]{2,1,0:T(8,128)(2,1)S(1)} %get-tuple-element.77), channel_id=1, source_target_pairs={{0,1},{1,2},{2,3},{3,4},{4,5},{5,6},{6,7},{7,0},{8,9},{9,10},{10,1... | collective-permute-start | bytes 98312 | tf_op jit(solution)/shard_map/ppermute | solution.py:643
  50.5 5.3 %collective-permute-start.6 = (bf16[8,16,128]{2,1,0:T(8,128)(2,1)S(1)}, bf16[8,16,128]{2,1,0:T(8,128)(2,1)S(1)}, u32[]{:S(2)}, u32[]{:S(2)}) collective-permute-start(bf16[8,16,128]{2,1,0:T(8,128)(2,1)S(1)} %get-tuple-element.78), channel_id=1, source_target_pairs={{1,0},{2,1},{3,2},{4,3},{5,4},{6,5},{7,6},{0,7},{9,8},{10,9},{11,1... | collective-permute-start | bytes 98312 | tf_op jit(solution)/shard_map/ppermute | solution.py:644
  53.3 7.3 %copy-start = (bf16[9,256,512]{2,1,0:T(8,128)(2,1)S(1)}, bf16[9,256,512]{2,1,0:T(8,128)(2,1)}, u32[]{:S(2)}) copy-start(bf16[9,256,512]{2,1,0:T(8,128)(2,1)} %get-tuple-element.85.back_ref) | copy-start | bytes 7077892
  54.0 16.2 %collective-permute-start.9 = (bf16[9,192,128]{2,1,0:T(8,128)(2,1)S(1)}, bf16[9,192,128]{2,1,0:T(8,128)(2,1)S(1)}, u32[]{:S(2)}, u32[]{:S(2)}) collective-permute-start(bf16[9,192,128]{2,1,0:T(8,128)(2,1)S(1)} %get-tuple-element.86), channel_id=1, source_target_pairs={{0,16},{8,24},{16,0},{24,8},{1,17},{9,25},{17,1},{25,9},{2,18},{10... | collective-permute-start | bytes 1327112 | tf_op jit(solution)/shard_map/ppermute | solution.py:684
  56.3 8.1 %collective-permute-start.7 = (bf16[6,16,128]{2,1,0:T(8,128)(2,1)S(1)}, bf16[6,16,128]{2,1,0:T(8,128)(2,1)S(1)}, u32[]{:S(2)}, u32[]{:S(2)}) collective-permute-start(bf16[6,16,128]{2,1,0:T(8,128)(2,1)S(1)} %get-tuple-element.83), channel_id=1, source_target_pairs={{0,8},{8,0},{16,24},{24,16},{1,9},{9,1},{17,25},{25,17},{2,10},{10... | collective-permute-start | bytes 73736 | tf_op jit(solution)/shard_map/ppermute | solution.py:650
  57.3 10.5 %collective-permute-start.8 = (bf16[6,16,128]{2,1,0:T(8,128)(2,1)S(1)}, bf16[6,16,128]{2,1,0:T(8,128)(2,1)S(1)}, u32[]{:S(2)}, u32[]{:S(2)}) collective-permute-start(bf16[6,16,128]{2,1,0:T(8,128)(2,1)S(1)} %get-tuple-element.84), channel_id=1, source_target_pairs={{8,16},{16,8},{9,17},{17,9},{10,18},{18,10},{11,19},{19,11},{12,20... | collective-permute-start | bytes 73736 | tf_op jit(solution)/shard_map/ppermute | solution.py:651
  71.2 6.1 %collective-permute-start.10 = (bf16[4,16,1728]{2,1,0:T(8,128)(2,1)S(1)}, bf16[4,16,1728]{2,1,0:T(8,128)(2,1)S(1)}, u32[]{:S(2)}, u32[]{:S(2)}) collective-permute-start(bf16[4,16,1728]{2,1,0:T(8,128)(2,1)S(1)} %get-tuple-element.89), channel_id=1, source_target_pairs={{0,1},{1,0},{2,3},{3,2},{4,5},{5,4},{6,7},{7,6},{8,9},{9,8},{10,11... | collective-permute-start | bytes 663560 | tf_op jit(solution)/shard_map/ppermute | solution.py:692
  71.3 17.5 %all-to-all-start.1 = ((bf16[8,8,4,16,128]{4,3,2,1,0:T(8,128)(2,1)}), bf16[8,8,4,16,128]{4,3,2,1,0:T(8,128)(2,1)S(1)}, u32[]{:S(2)}, u32[]{:S(2)}) async-start(bf16[8,8,4,16,128]{4,3,2,1,0:T(8,128)(2,1)} %shard_map.71), calls=%async_computation.1 | async-start | bytes 2097152 | tf_op jit(solution)/shard_map/all_to_all | solution.py:656
  77.9 7.6 %collective-permute-start.11 = (bf16[16,1728]{1,0:T(8,128)(2,1)S(1)}, bf16[16,1728]{1,0:T(8,128)(2,1)S(1)}, u32[]{:S(2)}, u32[]{:S(2)}) collective-permute-start(bf16[16,1728]{1,0:T(8,128)(2,1)S(1)} %get-tuple-element.91), channel_id=1, source_target_pairs={{0,2},{1,3},{2,4},{3,5},{4,6},{5,7},{6,0},{7,1},{8,10},{9,11},{10,... | collective-permute-start | bytes 165896 | tf_op jit(solution)/shard_map/ppermute | solution.py:695
  80.0 7.1 %collective-permute-start.12 = (bf16[16,1728]{1,0:T(8,128)(2,1)S(1)}, bf16[16,1728]{1,0:T(8,128)(2,1)S(1)}, u32[]{:S(2)}, u32[]{:S(2)}) collective-permute-start(bf16[16,1728]{1,0:T(8,128)(2,1)S(1)} %get-tuple-element.92), channel_id=1, source_target_pairs={{0,4},{1,5},{2,6},{3,7},{4,0},{5,1},{6,2},{7,3},{8,12},{9,13},{10,... | collective-permute-start | bytes 165896 | tf_op jit(solution)/shard_map/ppermute | solution.py:695
  82.0 6.8 %collective-permute-start.13 = (bf16[16,1728]{1,0:T(8,128)(2,1)S(1)}, bf16[16,1728]{1,0:T(8,128)(2,1)S(1)}, u32[]{:S(2)}, u32[]{:S(2)}) collective-permute-start(bf16[16,1728]{1,0:T(8,128)(2,1)S(1)} %get-tuple-element.93), channel_id=1, source_target_pairs={{0,6},{1,7},{2,0},{3,1},{4,2},{5,3},{6,4},{7,5},{8,14},{9,15},{10,... | collective-permute-start | bytes 165896 | tf_op jit(solution)/shard_map/ppermute | solution.py:695
